TPU v7x, 32 devices: a whole 2x2x4 slice. The times are simulated.
32 devices in a mesh: fsdp: 8 (over z, x), ctx: 2 (over y), tp: 2 (over core).
Axes of the slice: x: 2, y: 2, z: 4, core: 2. Of those that a mesh axis runs over, the one named last changes fastest.
Arguments:
- inputs: bfloat16 [8, 640, 1536], P('fsdp', 'ctx'), may hold values from -6 to 6
- conditioning: bfloat16 [8, 130, 768], P('fsdp'), may hold values from -6 to 6
- query_matrix: bfloat16 [1536, 1536], P(('fsdp', 'ctx'), 'tp'), may hold values from -0.15625 to 0.15625
- key_matrix: bfloat16 [1536, 1536], P(('fsdp', 'ctx'), 'tp'), may hold values from -0.15625 to 0.15625
- value_matrix: bfloat16 [1536, 1536], P(('fsdp', 'ctx'), 'tp'), may hold values from -0.15625 to 0.15625
- output_matrix: bfloat16 [1536, 1536], P('tp', ('fsdp', 'ctx')), may hold values from -1.25 to 1.25
- cross_query: bfloat16 [1536, 1536], P(('fsdp', 'ctx'), 'tp'), may hold values from -0.15625 to 0.15625
- cross_key: bfloat16 [768, 1536], P(('fsdp', 'ctx'), 'tp'), may hold values from -0.21875 to 0.21875
- cross_value: bfloat16 [768, 1536], P(('fsdp', 'ctx'), 'tp'), may hold values from -0.21875 to 0.21875
- cross_output: bfloat16 [1536, 1536], P('tp', ('fsdp', 'ctx')), may hold values from -0.625 to 0.625
- gate_matrix: bfloat16 [1536, 6144], P(('fsdp', 'ctx'), 'tp'), may hold values from -0.15625 to 0.15625
- up_matrix: bfloat16 [1536, 6144], P(('fsdp', 'ctx'), 'tp'), may hold values from -0.15625 to 0.15625
- down_matrix: bfloat16 [6144, 1536], P('tp', ('fsdp', 'ctx')), may hold values from -0.078125 to 0.078125
- first_gain: bfloat16 [1536], P(('fsdp', 'ctx')), may hold values from 0.099609375 to 1.8984375
- second_gain: bfloat16 [1536], P(('fsdp', 'ctx')), may hold values from 0.099609375 to 1.8984375
- third_gain: bfloat16 [1536], P(('fsdp', 'ctx')), may hold values from 0.099609375 to 1.8984375
- cotangent: bfloat16 [8, 640, 1536], P('fsdp', 'ctx'), may hold values from -6 to 6
Outputs:
- layer_output: float32 [8, 640, 1536], P('fsdp', 'ctx')
- inputs_gradient: float32 [8, 640, 1536], P('fsdp', 'ctx')
- conditioning_gradient: float32 [8, 130, 768], P('fsdp')
- query_gradient: float32 [1536, 1536], P(('fsdp', 'ctx'), 'tp')
- key_gradient: float32 [1536, 1536], P(('fsdp', 'ctx'), 'tp')
- value_gradient: float32 [1536, 1536], P(('fsdp', 'ctx'), 'tp')
- output_gradient: float32 [1536, 1536], P('tp', ('fsdp', 'ctx'))
- cross_query_gradient: float32 [1536, 1536], P(('fsdp', 'ctx'), 'tp')
- cross_key_gradient: float32 [768, 1536], P(('fsdp', 'ctx'), 'tp')
- cross_value_gradient: float32 [768, 1536], P(('fsdp', 'ctx'), 'tp')
- cross_output_gradient: float32 [1536, 1536], P('tp', ('fsdp', 'ctx'))
- gate_gradient: float32 [1536, 6144], P(('fsdp', 'ctx'), 'tp')
- up_gradient: float32 [1536, 6144], P(('fsdp', 'ctx'), 'tp')
- down_gradient: float32 [6144, 1536], P('tp', ('fsdp', 'ctx'))
- first_gain_gradient: float32 [1536], P(('fsdp', 'ctx'))
- second_gain_gradient: float32 [1536], P(('fsdp', 'ctx'))
- third_gain_gradient: float32 [1536], P(('fsdp', 'ctx'))
All inputs are finite; a program needn't handle non-finite values.
Results may differ from a plain program's by a relative error of at most 0.02.
Values may be sent and summed in bfloat16 or wider, within the bound.
No kernel may reach another device: no remote copies, remote signals or barrier semaphores. Data moves between devices by JAX's collectives and lax.ppermute only.
A program may use at most 256 MiB of HBM per device.

v0:
```python
import math

import jax
import jax.numpy as jnp
from jax import lax
from jax.sharding import PartitionSpec as P

HDIM = 64


EPSILON = 1e-05
HIGHEST = lax.Precision.HIGHEST


def matmul(left, right):
    return jnp.dot(left, right, preferred_element_type=jnp.float32)


def inner_rows(left, right):
    return lax.dot_general(
        left, right, (((0,), (0,)), ((), ())), preferred_element_type=jnp.float32
    )


def outer_cols(left, right):
    return lax.dot_general(
        left, right, (((1,), (1,)), ((), ())), preferred_element_type=jnp.float32
    )


def inner_exact(left, right):
    return lax.dot_general(
        left, right, (((0,), (0,)), ((), ())), precision=HIGHEST, preferred_element_type=jnp.float32
    )


def outer_exact(left, right):
    return lax.dot_general(
        left, right, (((1,), (1,)), ((), ())), precision=HIGHEST, preferred_element_type=jnp.float32
    )


def layer_norm(values, norm_gain):
    center = values - jnp.mean(values, axis=-1, keepdims=True)
    spread = jnp.mean(center * center, axis=-1, keepdims=True)
    return center * lax.rsqrt(spread + EPSILON) * norm_gain


def norm_backward(values, norm_gain, upstream):
    result, pullback = jax.vjp(layer_norm, values, norm_gain)
    return pullback(upstream)


def rotary_tables(offset, length, head_size):
    position = (offset + lax.iota(jnp.int32, length)).astype(jnp.float32)
    rotated = head_size // 2
    middle = rotated // 2
    frequency = jnp.exp(
        -(2.0 * jnp.arange(middle).astype(jnp.float32) / rotated) * math.log(10000.0)
    )
    angles = position[:, None] * frequency[None, :]
    return (jnp.cos(angles)[:, None, :], jnp.sin(angles)[:, None, :])


def rotate(values, cosine, sine_table):
    middle = cosine.shape[-1]
    first_half = values[..., :middle]
    second_half = values[..., middle : 2 * middle]
    passing = values[..., 2 * middle :]
    return jnp.concatenate(
        [
            first_half * cosine - second_half * sine_table,
            second_half * cosine + first_half * sine_table,
            passing,
        ],
        axis=-1,
    )


def group_width(local_heads, head_size):
    group_size = max(1, min(local_heads, 128 // head_size))
    while local_heads % group_size:
        group_size -= 1
    return group_size


def head_sum(values):
    return lax.psum(values, "tp")


def attend_forward(queries, keys, values, group_size, head_size):
    row_count = queries.shape[0]
    key_count = keys.shape[0]
    group_cols = group_size * head_size
    groups = queries.shape[1] // group_cols
    score_scale = head_size ** (-0.5)

    def one_group(group_index):
        first_col = group_index * group_cols
        query_part = lax.dynamic_slice_in_dim(queries, first_col, group_cols, 1).reshape(
            row_count, group_size, head_size
        )
        key_part = lax.dynamic_slice_in_dim(keys, first_col, group_cols, 1).reshape(
            key_count, group_size, head_size
        )
        value_part = lax.dynamic_slice_in_dim(values, first_col, group_cols, 1).reshape(
            key_count, group_size, head_size
        )
        scores = (
            jnp.einsum("qhd,khd->hqk", query_part, key_part, preferred_element_type=jnp.float32)
            * score_scale
        )
        row_peak = jnp.max(scores, axis=-1, keepdims=True)
        shifted = jnp.exp(scores - row_peak)
        row_total = jnp.sum(shifted, axis=-1, keepdims=True)
        probability = (shifted / row_total).astype(jnp.bfloat16)
        mixture = jnp.einsum(
            "hqk,khd->qhd", probability, value_part, preferred_element_type=jnp.float32
        )
        return (mixture.reshape(row_count, group_cols), (row_peak + jnp.log(row_total))[..., 0])

    mixture, logsum = lax.map(one_group, jnp.arange(groups))
    return (jnp.transpose(mixture, (1, 0, 2)).reshape(row_count, groups * group_cols), logsum)


def attend_backward(queries, keys, values, out_grad, logsum, group_size, head_size):
    row_count = queries.shape[0]
    key_count = keys.shape[0]
    group_cols = group_size * head_size
    groups = queries.shape[1] // group_cols
    score_scale = head_size ** (-0.5)

    def one_group(items):
        group_index, logsum_part = items
        first_col = group_index * group_cols
        query_part = lax.dynamic_slice_in_dim(queries, first_col, group_cols, 1).reshape(
            row_count, group_size, head_size
        )
        key_part = lax.dynamic_slice_in_dim(keys, first_col, group_cols, 1).reshape(
            key_count, group_size, head_size
        )
        value_part = lax.dynamic_slice_in_dim(values, first_col, group_cols, 1).reshape(
            key_count, group_size, head_size
        )
        grad_part = lax.dynamic_slice_in_dim(out_grad, first_col, group_cols, 1).reshape(
            row_count, group_size, head_size
        )
        scores = (
            jnp.einsum("qhd,khd->hqk", query_part, key_part, preferred_element_type=jnp.float32)
            * score_scale
        )
        probability = jnp.exp(scores - logsum_part[..., None])
        prob_low = probability.astype(jnp.bfloat16)
        prob_grad = jnp.einsum(
            "qhd,khd->hqk", grad_part, value_part, preferred_element_type=jnp.float32
        )
        score_grad = (
            probability * (prob_grad - jnp.sum(probability * prob_grad, axis=-1, keepdims=True))
        ).astype(jnp.bfloat16)
        query_grad = (
            jnp.einsum("hqk,khd->qhd", score_grad, key_part, preferred_element_type=jnp.float32)
            * score_scale
        )
        key_grad = (
            jnp.einsum("hqk,qhd->khd", score_grad, query_part, preferred_element_type=jnp.float32)
            * score_scale
        )
        value_grad = jnp.einsum(
            "hqk,qhd->khd", prob_low, grad_part, preferred_element_type=jnp.float32
        )
        return (
            query_grad.reshape(row_count, group_cols),
            key_grad.reshape(key_count, group_cols),
            value_grad.reshape(key_count, group_cols),
        )

    query_grads, key_grads, value_grads = lax.map(one_group, (jnp.arange(groups), logsum))
    return (
        jnp.transpose(query_grads, (1, 0, 2)).reshape(row_count, groups * group_cols),
        jnp.transpose(key_grads, (1, 0, 2)).reshape(key_count, groups * group_cols),
        jnp.transpose(value_grads, (1, 0, 2)).reshape(key_count, groups * group_cols),
    )


def on_device(
    inputs,
    conditioning,
    query_matrix,
    key_matrix,
    value_matrix,
    output_matrix,
    cross_query,
    cross_key,
    cross_value,
    cross_output,
    gate_matrix,
    up_matrix,
    down_matrix,
    first_gain,
    second_gain,
    third_gain,
    cotangent,
):
    (
        query_full,
        key_full,
        value_full,
        cross_query_full,
        cross_key_full,
        cross_value_full,
        gate_full,
        up_full,
        first_full,
        second_full,
        third_full,
    ) = (
        lax.all_gather(query_matrix, ("fsdp", "ctx"), axis=0, tiled=True),
        lax.all_gather(key_matrix, ("fsdp", "ctx"), axis=0, tiled=True),
        lax.all_gather(value_matrix, ("fsdp", "ctx"), axis=0, tiled=True),
        lax.all_gather(cross_query, ("fsdp", "ctx"), axis=0, tiled=True),
        lax.all_gather(cross_key, ("fsdp", "ctx"), axis=0, tiled=True),
        lax.all_gather(cross_value, ("fsdp", "ctx"), axis=0, tiled=True),
        lax.all_gather(gate_matrix, ("fsdp", "ctx"), axis=0, tiled=True),
        lax.all_gather(up_matrix, ("fsdp", "ctx"), axis=0, tiled=True),
        lax.all_gather(first_gain, ("fsdp", "ctx"), axis=0, tiled=True),
        lax.all_gather(second_gain, ("fsdp", "ctx"), axis=0, tiled=True),
        lax.all_gather(third_gain, ("fsdp", "ctx"), axis=0, tiled=True),
    )
    output_full, cross_output_full, down_full = (
        lax.all_gather(output_matrix, ("fsdp", "ctx"), axis=1, tiled=True),
        lax.all_gather(cross_output, ("fsdp", "ctx"), axis=1, tiled=True),
        lax.all_gather(down_matrix, ("fsdp", "ctx"), axis=1, tiled=True),
    )
    first_norm = first_full.astype(jnp.float32)
    second_norm = second_full.astype(jnp.float32)
    third_norm = third_full.astype(jnp.float32)
    tokens = inputs[0].astype(jnp.float32)
    row_count = tokens.shape[0]
    head_size = HDIM
    local_heads = query_full.shape[1] // head_size
    group_size = group_width(local_heads, head_size)
    cosine, sine_table = rotary_tables(lax.axis_index("ctx") * row_count, row_count, head_size)
    normed_one = layer_norm(tokens, first_norm).astype(jnp.bfloat16)
    query_rot = (
        rotate(
            matmul(normed_one, query_full).reshape(row_count, local_heads, head_size),
            cosine,
            sine_table,
        )
        .reshape(row_count, -1)
        .astype(jnp.bfloat16)
    )
    key_rot = (
        rotate(
            matmul(normed_one, key_full).reshape(row_count, local_heads, head_size),
            cosine,
            sine_table,
        )
        .reshape(row_count, -1)
        .astype(jnp.bfloat16)
    )
    value_low = matmul(normed_one, value_full).astype(jnp.bfloat16)
    key_all, value_all = (
        lax.all_gather(key_rot, "ctx", axis=0, tiled=True),
        lax.all_gather(value_low, "ctx", axis=0, tiled=True),
    )
    self_out, self_logsum = attend_forward(query_rot, key_all, value_all, group_size, head_size)
    self_low = self_out.astype(jnp.bfloat16)
    hidden_one = tokens + head_sum(matmul(self_low, output_full))
    normed_two = layer_norm(hidden_one, second_norm).astype(jnp.bfloat16)
    cross_query_low = matmul(normed_two, cross_query_full).astype(jnp.bfloat16)
    context = conditioning[0]
    cross_key_low = matmul(context, cross_key_full).astype(jnp.bfloat16)
    cross_value_low = matmul(context, cross_value_full).astype(jnp.bfloat16)
    cross_out, cross_logsum = attend_forward(
        cross_query_low, cross_key_low, cross_value_low, group_size, head_size
    )
    cross_low = cross_out.astype(jnp.bfloat16)
    hidden_two = hidden_one + head_sum(matmul(cross_low, cross_output_full))
    normed_three = layer_norm(hidden_two, third_norm).astype(jnp.bfloat16)
    gate_value = matmul(normed_three, gate_full)
    up_value = matmul(normed_three, up_full)
    sigmoid_gate = jax.nn.sigmoid(gate_value)
    silu_gate = gate_value * sigmoid_gate
    feed_low = (silu_gate * up_value).astype(jnp.bfloat16)
    layer_result = hidden_two + head_sum(matmul(feed_low, down_full))
    upstream = cotangent[0]
    down_grad = inner_rows(feed_low, upstream)
    feed_grad = lax.optimization_barrier(
        outer_cols(upstream, down_full).astype(jnp.bfloat16)
    ).astype(jnp.float32)
    gate_grad = (
        feed_grad * up_value * sigmoid_gate * (1.0 + gate_value * (1.0 - sigmoid_gate))
    ).astype(jnp.bfloat16)
    up_grad = (feed_grad * silu_gate).astype(jnp.bfloat16)
    gate_weight_grad = inner_rows(normed_three, gate_grad)
    up_weight_grad = inner_rows(normed_three, up_grad)
    third_grad = head_sum(outer_cols(gate_grad, gate_full) + outer_cols(up_grad, up_full))
    norm_three_back, third_gain_grad = norm_backward(hidden_two, third_norm, third_grad)
    hidden_two_grad = upstream.astype(jnp.float32) + norm_three_back
    branch_two = hidden_two_grad.astype(jnp.bfloat16)
    cross_output_grad = inner_rows(cross_low, branch_two)
    cross_out_grad = outer_cols(branch_two, cross_output_full).astype(jnp.bfloat16)
    cross_query_back, cross_key_back, cross_value_back = attend_backward(
        cross_query_low,
        cross_key_low,
        cross_value_low,
        cross_out_grad,
        cross_logsum,
        group_size,
        head_size,
    )
    cross_query_round = cross_query_back.astype(jnp.bfloat16)
    cross_query_grad = inner_rows(normed_two, cross_query_round)
    context_float = context.astype(jnp.float32)
    cross_key_grad = inner_exact(context_float, cross_key_back)
    cross_value_grad = inner_exact(context_float, cross_value_back)
    context_term = outer_exact(cross_key_back, cross_key_full.astype(jnp.float32)) + outer_exact(
        cross_value_back, cross_value_full.astype(jnp.float32)
    )
    context_grad = lax.psum(context_term.astype(jnp.bfloat16), ("ctx", "tp")).astype(jnp.float32)
    second_grad = head_sum(outer_cols(cross_query_round, cross_query_full))
    norm_two_back, second_gain_grad = norm_backward(hidden_one, second_norm, second_grad)
    hidden_one_grad = hidden_two_grad + norm_two_back
    branch_one = hidden_one_grad.astype(jnp.bfloat16)
    output_grad = inner_rows(self_low, branch_one)
    self_out_grad = outer_cols(branch_one, output_full).astype(jnp.bfloat16)
    query_back, key_back_all, value_back_all = attend_backward(
        query_rot, key_all, value_all, self_out_grad, self_logsum, group_size, head_size
    )
    key_back, value_back = (
        lax.psum_scatter(
            key_back_all.astype(jnp.bfloat16), "ctx", scatter_dimension=0, tiled=True
        ).astype(jnp.float32),
        lax.psum_scatter(
            value_back_all.astype(jnp.bfloat16), "ctx", scatter_dimension=0, tiled=True
        ).astype(jnp.float32),
    )
    query_round = (
        rotate(query_back.reshape(row_count, local_heads, head_size), cosine, -sine_table)
        .reshape(row_count, -1)
        .astype(jnp.bfloat16)
    )
    key_round = (
        rotate(key_back.reshape(row_count, local_heads, head_size), cosine, -sine_table)
        .reshape(row_count, -1)
        .astype(jnp.bfloat16)
    )
    value_round = value_back.astype(jnp.bfloat16)
    query_grad = inner_rows(normed_one, query_round)
    key_grad = inner_rows(normed_one, key_round)
    value_grad = inner_rows(normed_one, value_round)
    first_grad = head_sum(
        outer_cols(query_round, query_full)
        + outer_cols(key_round, key_full)
        + outer_cols(value_round, value_full)
    )
    norm_one_back, first_gain_grad = norm_backward(tokens, first_norm, first_grad)
    inputs_grad = hidden_one_grad + norm_one_back
    (
        query_sum,
        key_sum,
        value_sum,
        cross_query_sum,
        cross_key_sum,
        cross_value_sum,
        gate_sum,
        up_sum,
        first_sum,
        second_sum,
        third_sum,
    ) = (
        lax.psum_scatter(query_grad, ("fsdp", "ctx"), scatter_dimension=0, tiled=True),
        lax.psum_scatter(key_grad, ("fsdp", "ctx"), scatter_dimension=0, tiled=True),
        lax.psum_scatter(value_grad, ("fsdp", "ctx"), scatter_dimension=0, tiled=True),
        lax.psum_scatter(cross_query_grad, ("fsdp", "ctx"), scatter_dimension=0, tiled=True),
        lax.psum_scatter(cross_key_grad, ("fsdp", "ctx"), scatter_dimension=0, tiled=True),
        lax.psum_scatter(cross_value_grad, ("fsdp", "ctx"), scatter_dimension=0, tiled=True),
        lax.psum_scatter(gate_weight_grad, ("fsdp", "ctx"), scatter_dimension=0, tiled=True),
        lax.psum_scatter(up_weight_grad, ("fsdp", "ctx"), scatter_dimension=0, tiled=True),
        lax.psum_scatter(first_gain_grad, ("fsdp", "ctx"), scatter_dimension=0, tiled=True),
        lax.psum_scatter(second_gain_grad, ("fsdp", "ctx"), scatter_dimension=0, tiled=True),
        lax.psum_scatter(third_gain_grad, ("fsdp", "ctx"), scatter_dimension=0, tiled=True),
    )
    output_sum, cross_output_sum, down_sum = (
        lax.psum_scatter(output_grad, ("fsdp", "ctx"), scatter_dimension=1, tiled=True),
        lax.psum_scatter(cross_output_grad, ("fsdp", "ctx"), scatter_dimension=1, tiled=True),
        lax.psum_scatter(down_grad, ("fsdp", "ctx"), scatter_dimension=1, tiled=True),
    )
    return (
        layer_result[None],
        inputs_grad[None],
        context_grad[None],
        query_sum,
        key_sum,
        value_sum,
        output_sum,
        cross_query_sum,
        cross_key_sum,
        cross_value_sum,
        cross_output_sum,
        gate_sum,
        up_sum,
        down_sum,
        first_sum,
        second_sum,
        third_sum,
    )


def solution(mesh):
    return jax.shard_map(
        on_device,
        mesh=mesh,
        in_specs=(
            P("fsdp", "ctx", None),
            P("fsdp", None, None),
            P(("fsdp", "ctx"), "tp"),
            P(("fsdp", "ctx"), "tp"),
            P(("fsdp", "ctx"), "tp"),
            P("tp", ("fsdp", "ctx")),
            P(("fsdp", "ctx"), "tp"),
            P(("fsdp", "ctx"), "tp"),
            P(("fsdp", "ctx"), "tp"),
            P("tp", ("fsdp", "ctx")),
            P(("fsdp", "ctx"), "tp"),
            P(("fsdp", "ctx"), "tp"),
            P("tp", ("fsdp", "ctx")),
            P(("fsdp", "ctx")),
            P(("fsdp", "ctx")),
            P(("fsdp", "ctx")),
            P("fsdp", "ctx", None),
        ),
        out_specs=(
            P("fsdp", "ctx", None),
            P("fsdp", "ctx", None),
            P("fsdp", None, None),
            P(("fsdp", "ctx"), "tp"),
            P(("fsdp", "ctx"), "tp"),
            P(("fsdp", "ctx"), "tp"),
            P("tp", ("fsdp", "ctx")),
            P(("fsdp", "ctx"), "tp"),
            P(("fsdp", "ctx"), "tp"),
            P(("fsdp", "ctx"), "tp"),
            P("tp", ("fsdp", "ctx")),
            P(("fsdp", "ctx"), "tp"),
            P(("fsdp", "ctx"), "tp"),
            P("tp", ("fsdp", "ctx")),
            P(("fsdp", "ctx")),
            P(("fsdp", "ctx")),
            P(("fsdp", "ctx")),
        ),
        check_vma=False,
    )
```

profile of v0, /device:TPU:0, one launch (start us, length us, event | category | flops | bytes accessed | tf_op | source)
XLA Modules:
  0.0 3237.6 jit_solution(107725008281151993)
XLA Ops:
  16.6 79.0 %all-reduce.8 = (bf16[1536]{0:T(1024)(128)(2,1)S(1)}, bf16[1536]{0:T(1024)(128)(2,1)S(1)}, bf16[1536]{0:T(1024)(128)(2,1)S(1)}) all-reduce(bf16[1536]{0:T(1024)(128)(2,1)S(1)} %dynamic-update-slice, bf16[1536]{0:T(1024)(128)(2,1)S(1)} %dynamic-update-slice.1, ...), channel_id=1, replica_groups=mesh['fsdp'=8,'ctx'=2,'tp'=2] {'fsdp','ctx'}, use_global_device_ids=true, to_apply=%add | all-reduce | flops 4608 | bytes 18432
  99.0 4.3 copy.50
  103.3 36.9 %all-gather.14.cloned.1.call-done = bf16[1536,768]{1,0:T(8,128)(2,1)} async-done(((bf16[96,768]{1,0:T(8,128)(2,1)}), bf16[1536,768]{1,0:T(8,128)(2,1)}) %all-gather.14.cloned.1.call-update) | async-done | bytes 2359312 | tf_op jit(solution)/shard_map/all_gather | solution.py:217
  140.2 4.3 copy.49
  144.5 3.3 fusion.37
  150.0 14.1 all_gather.53
  165.4 38.7 %all-gather.12.cloned.1.call-done = bf16[1536,768]{1,0:T(8,128)(2,1)} async-done(((bf16[96,768]{1,0:T(8,128)(2,1)}), bf16[1536,768]{1,0:T(8,128)(2,1)}) %all-gather.12.cloned.1.call-update) | async-done | bytes 2359312 | tf_op jit(solution)/shard_map/all_gather | solution.py:219
  206.8 14.1 all_gather.50
  223.1 32.7 %while.56 = (s32[]{:T(128)}, bf16[6,320,128]{1,2,0:T(8,128)(2,1)}, f32[6,2,320]{2,1,0:T(2,128)S(1)}, s32[6]{0:T(128)S(1)}, bf16[640,768]{0,1:T(8,128)(2,1)}, /*i...) while((s32[]{:T(128)}, bf16[6,320,128]{1,2,0:T(8,128)(2,1)}, ...), condition=%wide.region_5.6_spmd.clone, body=%wide.region_2.5_spmd.sunk.clone | while | flops 108543360 | bytes 6428827 | solution.py:122
  255.8 12.9 all-gather.18.cloned.1.call-done
  268.7 4.4 fusion.78
  276.8 49.4 %all-gather.20.cloned.1.call-done = bf16[768,768]{1,0:T(8,128)(2,1)} async-done(((bf16[48,768]{1,0:T(8,128)(2,1)}), bf16[768,768]{1,0:T(8,128)(2,1)}) %all-gather.20.cloned.1.call-update) | async-done | bytes 1179664 | tf_op jit(solution)/shard_map/all_gather | solution.py:222
  328.7 55.1 %all-gather.24.cloned.1.call-done = bf16[768,768]{1,0:T(8,128)(2,1)} async-done(((bf16[48,768]{1,0:T(8,128)(2,1)}), bf16[768,768]{1,0:T(8,128)(2,1)}) %all-gather.24.cloned.1.call-update) | async-done | bytes 1179664 | tf_op jit(solution)/shard_map/all_gather | solution.py:221
  386.4 20.3 all-reduce.16.cloned.1.call-done
  409.0 64.5 %all-gather.22.cloned.1.call-done = bf16[1536,768]{1,0:T(8,128)(2,1)} async-done(((bf16[96,768]{1,0:T(8,128)(2,1)}), bf16[1536,768]{1,0:T(8,128)(2,1)}) %all-gather.22.cloned.1.call-update) | async-done | bytes 2359312 | tf_op jit(solution)/shard_map/all_gather | solution.py:220
  473.4 3.5 convolution_convert_fusion.3
  479.0 26.0 while.57
  505.0 32.8 %all-gather.26.cloned.1.call-done = bf16[768,1536]{0,1:T(8,128)(2,1)} async-done(((bf16[768,96]{0,1:T(8,128)(2,1)}), bf16[768,1536]{0,1:T(8,128)(2,1)}) %all-gather.26.cloned.1.call-update) | async-done | bytes 2359312 | tf_op jit(solution)/shard_map/all_gather | solution.py:231
  537.9 4.4 fusion.79
  544.4 17.9 all-reduce.18.cloned.1.call-done
  566.4 122.4 %all-gather.32.cloned.1.call-done = bf16[3072,1536]{0,1:T(8,128)(2,1)} async-done(((bf16[3072,96]{0,1:T(8,128)(2,1)}), bf16[3072,1536]{0,1:T(8,128)(2,1)}) %all-gather.32.cloned.1.call-update) | async-done | bytes 9437200 | tf_op jit(solution)/shard_map/all_gather | solution.py:232
  688.7 8.5 convolution_convert_fusion
  697.2 114.8 %all-gather.28.cloned.1.call-done = bf16[1536,3072]{1,0:T(8,128)(2,1)} async-done(((bf16[96,3072]{1,0:T(8,128)(2,1)}), bf16[1536,3072]{1,0:T(8,128)(2,1)}) %all-gather.28.cloned.1.call-update) | async-done | bytes 9437200 | tf_op jit(solution)/shard_map/all_gather | solution.py:223
  812.0 9.1 fusion.80
  821.1 114.4 %all-gather.30.cloned.1.call-done = bf16[1536,3072]{1,0:T(8,128)(2,1)} async-done(((bf16[96,3072]{1,0:T(8,128)(2,1)}), bf16[1536,3072]{1,0:T(8,128)(2,1)}) %all-gather.30.cloned.1.call-update) | async-done | bytes 9437200 | tf_op jit(solution)/shard_map/all_gather | solution.py:224
  935.5 11.4 fusion.13
  948.2 3.3 fusion.82
  951.5 17.2 convolution_add_fusion.2
  968.8 19.3 all-reduce.20.cloned.1.call-done
  995.2 45.3 %while.58 = (s32[]{:T(128)}, bf16[6,320,128]{1,2,0:T(8,128)(2,1)}, f32[6,130,128]{1,2,0:T(8,128)}, f32[6,130,128]{1,2,0:T(8,128)}, s32[6]{0:T(128)S(1)}, /*index...) while((s32[]{:T(128)}, bf16[6,320,128]{1,2,0:T(8,128)(2,1)}, ...), condition=%wide.region_22.23_spmd.clone, body=%wide.region_20.22_spmd.sunk.clone | while | flops 54011524 | bytes 4352699 | solution.py:177
  1040.5 4.4 fusion.83
  1045.0 22.3 all-reduce.22.cloned.1.call-done
  1067.3 2.9 multiply_reduce_fusion.4
  1075.8 53.1 %while.59 = (s32[]{:T(128)}, f32[6,320,128]{1,2,0:T(8,128)}, bf16[6,640,128]{1,2,0:T(8,128)(2,1)}, bf16[6,640,128]{1,2,0:T(8,128)(2,1)}, s32[6]{0:T(128)S(1)}, /...) while((s32[]{:T(128)}, f32[6,320,128]{1,2,0:T(8,128)}, ...), condition=%wide.region_28.29_spmd.clone, body=%wide.region_26.28_spmd.sunk.clone | while | flops 265624960 | bytes 15775419 | solution.py:177
  1133.7 8.9 fusion.81
  1148.6 3.4 reduce-scatter.40.cloned.1.call-done
  1161.7 12.8 reduce-scatter.42.cloned.1.call-done
  1174.5 4.6 convolution_add_fusion
  1179.2 3.7 convolution_bitcast_fusion.1
  1182.8 3.1 copy.71
  1186.4 3.7 convolution_bitcast_fusion
  1190.0 3.1 copy.73
  1193.2 5.4 fusion.60
  1198.7 5.0 fusion.86
  1203.7 5.3 fusion.45
  1209.7 4.9 fusion.43
  1214.6 5.0 fusion.41
  1219.7 4.8 fusion.56
  1224.8 12.1 fusion.87
  1236.9 11.5 fusion.65
  1248.5 10.7 fusion.34
  1265.0 76.5 %all-reduce.6 = (f32[1536]{0:T(1024)S(1)}, f32[1536]{0:T(1024)S(1)}, f32[1536]{0:T(1024)S(1)}) all-reduce(f32[1536]{0:T(1024)S(1)} %get-tuple-element.317, f32[1536]{0:T(1024)S(1)} %get-tuple-element.315, f32[1536]{0:T(1024)S(1)} %get-tuple-element.313), channel_id=15, replica_groups=mesh['fsdp'=8,'ctx'=2,'tp'=2] {'fsdp','ctx'}, use_global_device_ids=true, to_apply=%region_47.48.clone | all-reduce | flops 4608 | bytes 36864
  1343.3 3.4 add_bitcast_fusion.1
  1348.7 22.0 reduce-scatter.44.cloned.1.call-done
  1370.7 133.2 %reduce-scatter.46.cloned.1.call-done = f32[48,768]{1,0:T(8,128)} async-done(((f32[768,768]{1,0:T(8,128)}), f32[48,768]{1,0:T(8,128)}) %reduce-scatter.46.cloned.1.call-update) | async-done | bytes 147472
  1503.9 142.7 %reduce-scatter.30.cloned.1.call-done = f32[96,768]{1,0:T(8,128)} async-done(((f32[1536,768]{1,0:T(8,128)}), f32[96,768]{1,0:T(8,128)}) %reduce-scatter.30.cloned.1.call-update) | async-done | bytes 294928 | tf_op jit(solution)/shard_map/reduce_scatter | solution.py:376
  1646.5 143.2 %reduce-scatter.32.cloned.1.call-done = f32[768,96]{0,1:T(8,128)} async-done(((f32[768,1536]{0,1:T(8,128)}), f32[768,96]{0,1:T(8,128)}) %reduce-scatter.32.cloned.1.call-update) | async-done | bytes 294928 | tf_op jit(solution)/shard_map/reduce_scatter | solution.py:387
  1789.7 142.2 %reduce-scatter.28.cloned.1.call-done = f32[768,96]{0,1:T(8,128)} async-done(((f32[768,1536]{0,1:T(8,128)}), f32[768,96]{0,1:T(8,128)}) %reduce-scatter.28.cloned.1.call-update) | async-done | bytes 294928 | tf_op jit(solution)/shard_map/reduce_scatter | solution.py:386
  1931.9 143.0 %reduce-scatter.22.cloned.1.call-done = f32[96,768]{1,0:T(8,128)} async-done(((f32[1536,768]{1,0:T(8,128)}), f32[96,768]{1,0:T(8,128)}) %reduce-scatter.22.cloned.1.call-update) | async-done | bytes 294928 | tf_op jit(solution)/shard_map/reduce_scatter | solution.py:373
  2074.9 142.0 %reduce-scatter.24.cloned.1.call-done = f32[96,768]{1,0:T(8,128)} async-done(((f32[1536,768]{1,0:T(8,128)}), f32[96,768]{1,0:T(8,128)}) %reduce-scatter.24.cloned.1.call-update) | async-done | bytes 294928 | tf_op jit(solution)/shard_map/reduce_scatter | solution.py:374
  2216.9 142.8 %reduce-scatter.26.cloned.1.call-done = f32[96,768]{1,0:T(8,128)} async-done(((f32[1536,768]{1,0:T(8,128)}), f32[96,768]{1,0:T(8,128)}) %reduce-scatter.26.cloned.1.call-update) | async-done | bytes 294928 | tf_op jit(solution)/shard_map/reduce_scatter | solution.py:375
  2359.6 290.3 %reduce-scatter.34.cloned.1.call-done = f32[96,3072]{1,0:T(8,128)} async-done(((f32[1536,3072]{1,0:T(8,128)}), f32[96,3072]{1,0:T(8,128)}) %reduce-scatter.34.cloned.1.call-update) | async-done | bytes 1179664 | tf_op jit(solution)/shard_map/reduce_scatter | solution.py:379
  2650.0 290.2 %reduce-scatter.36.cloned.1.call-done = f32[96,3072]{1,0:T(8,128)} async-done(((f32[1536,3072]{1,0:T(8,128)}), f32[96,3072]{1,0:T(8,128)}) %reduce-scatter.36.cloned.1.call-update) | async-done | bytes 1179664 | tf_op jit(solution)/shard_map/reduce_scatter | solution.py:380
  2940.1 290.4 %reduce-scatter.38.cloned.1.call-done = f32[3072,96]{0,1:T(8,128)} async-done(((f32[3072,1536]{0,1:T(8,128)}), f32[3072,96]{0,1:T(8,128)}) %reduce-scatter.38.cloned.1.call-update) | async-done | bytes 1179664 | tf_op jit(solution)/shard_map/reduce_scatter | solution.py:388
  (504 shorter events, 225.1 us)
Async XLA Ops:
  7.2 319.0 %copy-start = (bf16[1,130,768]{2,1,0:T(8,128)(2,1)S(1)}, bf16[1,130,768]{2,1,0:T(8,128)(2,1)}, u32[]{:S(2)}) copy-start(bf16[1,130,768]{2,1,0:T(8,128)(2,1)} %param.26) | copy-start | bytes 599044
  7.2 88.5 %copy-start.1 = (bf16[1,320,1536]{2,1,0:T(8,128)(2,1)S(1)}, bf16[1,320,1536]{2,1,0:T(8,128)(2,1)}, u32[]{:S(2)}) copy-start(bf16[1,320,1536]{2,1,0:T(8,128)(2,1)} %param.25) | copy-start | bytes 2949124
  7.2 91.8 %all-gather.16.cloned.1.call-start = ((), (), s32[]{:S(2)}) async-start(), calls=%async_computation.15 | async-start | bytes 2506752 | tf_op jit(solution)/shard_map/all_gather | solution.py:218
  7.9 132.2 %all-gather.14.cloned.1.call-start = ((), (), s32[]{:S(2)}) async-start(), calls=%async_computation.14 | async-start | bytes 2506752 | tf_op jit(solution)/shard_map/all_gather | solution.py:217
  8.7 195.4 %all-gather.12.cloned.1.call-start = ((), (), s32[]{:S(2)}) async-start(), calls=%async_computation.13 | async-start | bytes 2506752 | tf_op jit(solution)/shard_map/all_gather | solution.py:219
  9.4 259.2 %all-gather.18.cloned.1.call-start = ((), (), s32[]{:S(2)}) async-start(), calls=%async_computation.16 | async-start | bytes 2506752 | tf_op jit(solution)/shard_map/all_gather | solution.py:230
  10.0 316.2 %all-gather.20.cloned.1.call-start = ((), (), s32[]{:S(2)}) async-start(), calls=%async_computation.18 | async-start | bytes 1253376 | tf_op jit(solution)/shard_map/all_gather | solution.py:222
  10.6 373.3 %all-gather.24.cloned.1.call-start = ((), (), s32[]{:S(2)}) async-start(), calls=%async_computation.20 | async-start | bytes 1253376 | tf_op jit(solution)/shard_map/all_gather | solution.py:221
  11.2 395.5 %all-reduce.16.cloned.1.call-start = ((), (), s32[]{:S(2)}) async-start(), calls=%async_computation.17 | async-start | bytes 3932160 | tf_op jit(solution)/shard_map/psum | solution.py:88
  95.7 108.4 %copy-start.26 = (f32[1536]{0:T(1024)}, f32[1536]{0:T(1024)S(1)}, u32[]{:S(2)}) copy-start(f32[1536]{0:T(1024)S(1)} %convert_element_type.201) | copy-start | bytes 18436
  95.9 108.2 %copy-start.28 = (f32[320]{0:T(512)}, f32[320]{0:T(512)S(1)}, u32[]{:S(2)}) copy-start(f32[320]{0:T(512)S(1)} %broadcast_multiply_fusion.2) | copy-start | bytes 3844
  96.4 107.7 %copy-start.30 = (f32[320]{0:T(512)}, f32[320]{0:T(512)S(1)}, u32[]{:S(2)}) copy-start(f32[320]{0:T(512)S(1)} %fusion.53) | copy-start | bytes 3844
  144.5 3.3 copy-start.23
  273.1 200.4 %all-gather.22.cloned.1.call-start = ((), (), s32[]{:S(2)}) async-start(), calls=%async_computation.19 | async-start | bytes 2506752 | tf_op jit(solution)/shard_map/all_gather | solution.py:220
  273.8 264.0 %all-gather.26.cloned.1.call-start = ((), (), s32[]{:S(2)}) async-start(), calls=%async_computation.21 | async-start | bytes 2506752 | tf_op jit(solution)/shard_map/all_gather | solution.py:231
  274.6 287.7 %all-reduce.18.cloned.1.call-start = ((), (), s32[]{:S(2)}) async-start(), calls=%async_computation.22 | async-start | bytes 3932160 | tf_op jit(solution)/shard_map/psum | solution.py:88
  408.6 68.3 %copy-start.2 = (f32[320,1536]{1,0:T(8,128)}, f32[320,1536]{1,0:T(8,128)S(1)}, u32[]{:S(2)}) copy-start(f32[320,1536]{1,0:T(8,128)S(1)} %get-tuple-element.402) | copy-start | bytes 5898244
  542.3 146.4 %all-gather.32.cloned.1.call-start = ((), (), s32[]{:S(2)}) async-start(), calls=%async_computation.25 | async-start | bytes 10027008 | tf_op jit(solution)/shard_map/all_gather | solution.py:232
  543.0 269.0 %all-gather.28.cloned.1.call-start = ((), (), s32[]{:S(2)}) async-start(), calls=%async_computation.23 | async-start | bytes 10027008 | tf_op jit(solution)/shard_map/all_gather | solution.py:223
  543.6 391.9 %all-gather.30.cloned.1.call-start = ((), (), s32[]{:S(2)}) async-start(), calls=%async_computation.24 | async-start | bytes 10027008 | tf_op jit(solution)/shard_map/all_gather | solution.py:224
  544.3 443.7 %all-reduce.20.cloned.1.call-start = ((), (), s32[]{:S(2)}) async-start(), calls=%async_computation.26 | async-start | bytes 3932160 | tf_op jit(solution)/shard_map/psum | solution.py:88
  935.5 12.7 copy-start.34
  946.9 1.3 copy-start.25
  948.2 3.3 copy-start.37
  948.2 3.3 copy-start.38
  968.7 98.6 %all-reduce.22.cloned.1.call-start = ((), (), s32[]{:S(2)}) async-start(), calls=%async_computation.27 | async-start | bytes 3932160 | tf_op jit(solution)/shard_map/psum | solution.py:88
  988.1 2.4 copy-start.13
  991.2 1.3 copy-start.4
  991.7 1.8 copy-start.36
  993.5 1.7 copy-start.18
  1044.9 107.1 %reduce-scatter.40.cloned.1.call-start = ((), (), s32[]{:S(2)}) async-start(), calls=%async_computation.38 | async-start | bytes 1474560
  1067.3 3.0 copy-start.3
  1067.3 3.3 copy-start.14
  1070.6 1.5 copy-start.5
  1070.6 1.8 copy-start.12
  1072.4 1.7 copy-start.35
  1074.1 1.7 copy-start.6
  1131.1 43.3 %reduce-scatter.42.cloned.1.call-start = ((), (), s32[]{:S(2)}) async-start(), calls=%async_computation.39 | async-start | bytes 1474560
  1133.7 126.2 %all-reduce.24.cloned.1.call-start = ((), (), s32[]{:S(2)}) async-start(), calls=%async_computation.28 | async-start | bytes 417792 | tf_op jit(solution)/shard_map/psum | solution.py:321
  1133.7 9.0 copy-start.17
  1133.7 9.0 copy-start.20
  1142.7 2.0 copy-start.16
  1142.7 2.0 copy-start.21
  1147.5 114.4 %all-reduce.26.cloned.1.call-start = ((), (), s32[]{:S(2)}) async-start(), calls=%async_computation.42 | async-start | bytes 7864320 | tf_op jit(solution)/shard_map/psum | solution.py:88
  1154.1 1.2 copy-start.19
  1155.4 1.8 copy-start.22
  1157.0 1.5 copy-start.24
  1157.1 1.5 copy-start.15
  1157.3 1.9 copy-start.10
  1179.1 191.6 %reduce-scatter.44.cloned.1.call-start = ((), (), s32[]{:S(2)}) async-start(), calls=%async_computation.40 | async-start | bytes 2506752
  1185.9 317.9 %reduce-scatter.46.cloned.1.call-start = ((), (), s32[]{:S(2)}) async-start(), calls=%async_computation.41 | async-start | bytes 2506752
  1193.2 453.4 %reduce-scatter.30.cloned.1.call-start = ((), (), s32[]{:S(2)}) async-start(), calls=%async_computation.33 | async-start | bytes 5013504 | tf_op jit(solution)/shard_map/reduce_scatter | solution.py:376
  1198.6 591.1 %reduce-scatter.32.cloned.1.call-start = ((), (), s32[]{:S(2)}) async-start(), calls=%async_computation.34 | async-start | bytes 5013504 | tf_op jit(solution)/shard_map/reduce_scatter | solution.py:387
  1203.6 728.2 %reduce-scatter.28.cloned.1.call-start = ((), (), s32[]{:S(2)}) async-start(), calls=%async_computation.32 | async-start | bytes 5013504 | tf_op jit(solution)/shard_map/reduce_scatter | solution.py:386
  1209.0 865.9 %reduce-scatter.22.cloned.1.call-start = ((), (), s32[]{:S(2)}) async-start(), calls=%async_computation.29 | async-start | bytes 5013504 | tf_op jit(solution)/shard_map/reduce_scatter | solution.py:373
  1214.6 1002.3 %reduce-scatter.24.cloned.1.call-start = ((), (), s32[]{:S(2)}) async-start(), calls=%async_computation.30 | async-start | bytes 5013504 | tf_op jit(solution)/shard_map/reduce_scatter | solution.py:374
  1219.7 1140.0 %reduce-scatter.26.cloned.1.call-start = ((), (), s32[]{:S(2)}) async-start(), calls=%async_computation.31 | async-start | bytes 5013504 | tf_op jit(solution)/shard_map/reduce_scatter | solution.py:375
  1224.5 1425.4 %reduce-scatter.34.cloned.1.call-start = ((), (), s32[]{:S(2)}) async-start(), calls=%async_computation.35 | async-start | bytes 20054016 | tf_op jit(solution)/shard_map/reduce_scatter | solution.py:379
  1236.9 1703.2 %reduce-scatter.36.cloned.1.call-start = ((), (), s32[]{:S(2)}) async-start(), calls=%async_computation.36 | async-start | bytes 20054016 | tf_op jit(solution)/shard_map/reduce_scatter | solution.py:380
  1248.5 1982.1 %reduce-scatter.38.cloned.1.call-start = ((), (), s32[]{:S(2)}) async-start(), calls=%async_computation.37 | async-start | bytes 20054016 | tf_op jit(solution)/shard_map/reduce_scatter | solution.py:388
  1259.2 4.9 copy-start.33
  1261.9 2.2 copy-start.8
  1343.3 3.4 copy-start.7
  1343.3 3.4 copy-start.9
  (5 other events, 3.9 us)
Sparse Core Ops, SparseCore 0:
  10.8 65.2 all-gather.15
  79.0 61.1 all-gather.13
  143.0 61.0 all-gather.11
  206.7 61.8 all-gather.17
  271.3 54.8 all-gather.19
  328.9 54.9 all-gather.23
  386.8 19.8 all-reduce.15
  409.9 63.5 all-gather.21
  476.6 61.1 all-gather.25
  542.4 19.8 all-reduce.17
  565.1 123.6 all-gather.31
  691.4 120.6 all-gather.27
  814.8 120.6 all-gather.29
  968.8 19.2 all-reduce.19
  1045.1 22.1 all-reduce.21
  1131.3 20.7 reduce-scatter.39
  1154.8 19.5 reduce-scatter.41
  1177.2 31.0 all-reduce.23
  1210.8 25.5 all-reduce.25
  1241.7 128.9 reduce-scatter.43
  1377.0 126.8 reduce-scatter.45
  1509.6 136.8 reduce-scatter.29
  1653.1 136.5 reduce-scatter.31
  1795.3 136.5 reduce-scatter.27
  1938.4 136.4 reduce-scatter.21
  2080.5 136.3 reduce-scatter.23
  2223.3 136.3 reduce-scatter.25
  2366.0 283.9 reduce-scatter.33
  2656.3 283.7 reduce-scatter.35
  2946.3 284.1 reduce-scatter.37
where the time goes:
time: 3240 us
  waiting for transfers between devices  2630 us (81%)
  matrix products  203 us (6%)
  blocking collectives  184 us (6%)
  local copies, waits for them, and re-layouts  155 us (5%)
  other arithmetic  33 us (1%)
    reduce_scatter x1, waiting for transfers between devices, on_device(): lax.psum_scatter(down_grad, ('fsdp', 'ctx'), scatter_dimension=1, tiled=T...  290 us
    reduce_scatter x1, waiting for transfers between devices, on_device(): lax.psum_scatter(gate_weight_grad, ('fsdp', 'ctx'), scatter_dimension=0,...  290 us
    reduce_scatter x1, waiting for transfers between devices, on_device(): lax.psum_scatter(up_weight_grad, ('fsdp', 'ctx'), scatter_dimension=0, ti...  290 us
    unnamed x34, waiting for transfers between devices  179 us
    unnamed x2, blocking collectives  156 us
    reduce_scatter x1, waiting for transfers between devices, on_device(): lax.psum_scatter(cross_output_grad, ('fsdp', 'ctx'), scatter_dimension=1,...  143 us
    reduce_scatter x1, waiting for transfers between devices, on_device(): lax.psum_scatter(query_grad, ('fsdp', 'ctx'), scatter_dimension=0, tiled=...  143 us
    reduce_scatter x1, waiting for transfers between devices, on_device(): lax.psum_scatter(value_grad, ('fsdp', 'ctx'), scatter_dimension=0, tiled=...  143 us
  transfers between devices with their start and end apart: 30, of which 27 were waited for; matrix products, arithmetic and copies ran while one was open for 7% of the time, Pallas kernels for 0%

commit v1 on v0

v1 whole, which is shorter than its diff:
```python
import functools
import math

import jax
import jax.numpy as jnp
from jax import lax
from jax.experimental import pallas as pl
from jax.experimental.pallas import tpu as pltpu
from jax.sharding import PartitionSpec as P

HDIM = 64
EPSILON = 1e-05
F32 = jnp.float32
BF16 = jnp.bfloat16
SCALE = HDIM ** (-0.5)
PAIR = 2 * HDIM
VMEM_LIMIT = 48 * 1024 * 1024


def mm(left, right):
    return lax.dot_general(left, right, (((1,), (0,)), ((), ())), preferred_element_type=F32)


def mm_tn(left, right):
    return lax.dot_general(left, right, (((0,), (0,)), ((), ())), preferred_element_type=F32)


def mm_nt(left, right):
    return lax.dot_general(left, right, (((1,), (1,)), ((), ())), preferred_element_type=F32)


def norm_stats(values):
    center = values - jnp.mean(values, axis=-1, keepdims=True)
    rate = lax.rsqrt(jnp.mean(center * center, axis=-1, keepdims=True) + EPSILON)
    return center * rate, rate


def norm_low(values, gain):
    return (norm_stats(values)[0] * gain).astype(BF16)


def norm_backward(values, gain, upstream):
    unit, rate = norm_stats(values)
    scaled = upstream * gain
    back = rate * (
        scaled
        - jnp.mean(scaled, axis=-1, keepdims=True)
        - unit * jnp.mean(scaled * unit, axis=-1, keepdims=True)
    )
    return back, jnp.sum(upstream * unit, axis=0)


def turned(values, cosine, upper, lower):
    width = values.shape[1]
    return (
        values * cosine
        + pltpu.roll(values, width - HDIM // 4, 1) * upper
        + pltpu.roll(values, HDIM // 4, 1) * lower
    )


def chunk_of(rows):
    return 128 if rows % 128 == 0 else rows


def scores_of(query, key, valid):
    scores = mm_nt(query, key) * SCALE
    if valid < key.shape[0]:
        column = lax.broadcasted_iota(jnp.int32, scores.shape, 1)
        scores = jnp.where(column < valid, scores, -1e30)
    return scores


def forward_heads(q_ref, k_ref, v_ref, o_ref, lse_ref, valid):
    rows = q_ref.shape[0]
    step = chunk_of(rows)
    for head in range(2):
        cols = slice(head * HDIM, (head + 1) * HDIM)
        key, value = k_ref[:, cols], v_ref[:, cols]
        for first in range(0, rows, step):
            part = slice(first, first + step)
            scores = scores_of(q_ref[part, cols], key, valid)
            peak = jnp.max(scores, axis=-1, keepdims=True)
            shifted = jnp.exp(scores - peak)
            total = jnp.sum(shifted, axis=-1, keepdims=True)
            probability = (shifted * (1.0 / total)).astype(BF16)
            o_ref[part, cols] = mm(probability, value).astype(BF16)
            lse_ref[part, cols] = jnp.broadcast_to(peak + jnp.log(total), (step, HDIM))


def self_forward_kernel(
    q_ref, k_ref, v_ref, cos_ref, up_ref, low_ref, qr_ref, kr_ref, o_ref, lse_ref
):
    tables = cos_ref[...], up_ref[...], low_ref[...]
    qr_ref[...] = turned(q_ref[...], *tables).astype(BF16)
    kr_ref[...] = turned(k_ref[...], *tables).astype(BF16)
    forward_heads(qr_ref, kr_ref, v_ref, o_ref, lse_ref, kr_ref.shape[0])


def cross_forward_kernel(valid, q_ref, k_ref, v_ref, o_ref, lse_ref):
    forward_heads(q_ref, k_ref, v_ref, o_ref, lse_ref, valid)


def backward_heads(q_ref, k_ref, v_ref, do_ref, lse_ref, dq_ref, dk_ref, dv_ref, valid):
    rows = q_ref.shape[0]
    step = chunk_of(rows)
    for head in range(2):
        cols = slice(head * HDIM, (head + 1) * HDIM)
        key, value = k_ref[:, cols], v_ref[:, cols]
        for first in range(0, rows, step):
            part = slice(first, first + step)
            query, grad = q_ref[part, cols], do_ref[part, cols]
            scores = scores_of(query, key, valid)
            probability = jnp.exp(scores - lse_ref[part, cols][:, :1])
            prob_grad = mm_nt(grad, value)
            mean_grad = jnp.sum(probability * prob_grad, axis=-1, keepdims=True)
            score_grad = (probability * (prob_grad - mean_grad)).astype(BF16)
            dq_ref[part, cols] = mm(score_grad, key) * SCALE
            key_term = mm_tn(score_grad, query) * SCALE
            value_term = mm_tn(probability.astype(BF16), grad)
            if first == 0:
                dk_ref[:, cols] = key_term
                dv_ref[:, cols] = value_term
            else:
                dk_ref[:, cols] += key_term
                dv_ref[:, cols] += value_term


def self_backward_kernel(
    q_ref, k_ref, v_ref, do_ref, lse_ref, cos_ref, up_ref, low_ref,
    dq_ref, dk_ref, dv_ref, dq_acc, dk_acc, dv_acc,
):
    backward_heads(
        q_ref, k_ref, v_ref, do_ref, lse_ref, dq_acc, dk_acc, dv_acc, k_ref.shape[0]
    )
    tables = cos_ref[...], -up_ref[...], -low_ref[...]
    dq_ref[...] = turned(dq_acc[...], *tables).astype(BF16)
    dk_ref[...] = turned(dk_acc[...], *tables).astype(BF16)
    dv_ref[...] = dv_acc[...].astype(BF16)


def cross_backward_kernel(
    valid, q_ref, k_ref, v_ref, do_ref, lse_ref, dq_ref, dk_ref, dv_ref, dq_acc
):
    backward_heads(q_ref, k_ref, v_ref, do_ref, lse_ref, dq_acc, dk_ref, dv_ref, valid)
    dq_ref[...] = dq_acc[...].astype(BF16)


def pair_block(rows):
    return pl.BlockSpec((rows, PAIR), lambda pair: (0, pair))


def fixed_block(rows):
    return pl.BlockSpec((rows, PAIR), lambda pair: (0, 0))


def shape(rows, cols, kind):
    return jax.ShapeDtypeStruct((rows, cols), kind)


def attention_call(kernel, cols, rows_in, fixed, outs, scratch=(), flops=0):
    return pl.pallas_call(
        kernel,
        grid=(cols // PAIR,),
        in_specs=[pair_block(r) for r in rows_in] + [fixed_block(r) for r in fixed],
        out_specs=[pair_block(r) for r, _ in outs],
        out_shape=[shape(r, cols, kind) for r, kind in outs],
        scratch_shapes=[pltpu.VMEM((r, PAIR), F32) for r in scratch],
        compiler_params=pltpu.CompilerParams(vmem_limit_bytes=VMEM_LIMIT),
        cost_estimate=pl.CostEstimate(
            flops=flops, bytes_accessed=sum(r * cols * 4 for r in rows_in), transcendentals=flops // 256
        ),
    )


def self_forward(query, key, value, tables):
    rows, cols = query.shape
    return attention_call(
        self_forward_kernel, cols, (rows,) * 3, (rows,) * 3,
        ((rows, BF16), (rows, BF16), (rows, BF16), (rows, F32)),
        flops=4 * rows * rows * cols,
    )(query, key, value, *tables)


def self_backward(query, key, value, grad, lse, tables):
    rows, cols = query.shape
    return attention_call(
        self_backward_kernel, cols, (rows,) * 5, (rows,) * 3,
        ((rows, BF16),) * 3, (rows,) * 3, flops=10 * rows * rows * cols,
    )(query, key, value, grad, lse, *tables)


def cross_forward(query, key, value, valid):
    rows, cols = query.shape
    keys = key.shape[0]
    return attention_call(
        functools.partial(cross_forward_kernel, valid), cols, (rows, keys, keys), (),
        ((rows, BF16), (rows, F32)), flops=4 * rows * keys * cols,
    )(query, key, value)


def cross_backward(query, key, value, grad, lse, valid):
    rows, cols = query.shape
    keys = key.shape[0]
    return attention_call(
        functools.partial(cross_backward_kernel, valid), cols, (rows, keys, keys, rows, rows), (),
        ((rows, BF16), (keys, F32), (keys, F32)), (rows,), flops=10 * rows * keys * cols,
    )(query, key, value, grad, lse)


def rotary_tables(position):
    quarter = HDIM // 4
    frequency = jnp.exp(
        -(2.0 * jnp.arange(quarter).astype(F32) / (2 * quarter)) * math.log(10000.0)
    )
    angles = position.astype(F32)[:, None] * frequency[None, :]
    cosine, sine = jnp.cos(angles), jnp.sin(angles)
    none = jnp.zeros_like(sine)
    rest = jnp.zeros((position.shape[0], HDIM // 2), F32)
    return tuple(
        jnp.concatenate(parts + parts, axis=1)
        for parts in (
            [cosine, cosine, rest + 1.0],
            [-sine, none, rest],
            [none, sine, rest],
        )
    )


class Links:
    def __init__(self, mesh):
        self.fsdp = mesh.shape["fsdp"]
        self.ring = 4 if self.fsdp % 4 == 0 else 1
        self.width = self.fsdp // self.ring
        index = lax.axis_index("fsdp")
        self.at = index // self.width
        self.lane = index % self.width
        self.half = lax.axis_index("ctx")
        self.core = lax.axis_index("tp")

    def over_ring(self, value, hops=1):
        z, r = self.ring, self.width
        pairs = [(a * r + b, (a + hops) % z * r + b) for a in range(z) for b in range(r)]
        return lax.ppermute(value, "fsdp", pairs)

    def over_lanes(self, value, hops=1):
        z, r = self.ring, self.width
        pairs = [(a * r + b, a * r + (b + hops) % r) for a in range(z) for b in range(r)]
        return lax.ppermute(value, "fsdp", pairs)

    def over_half(self, value):
        return lax.ppermute(value, "ctx", [(0, 1), (1, 0)])

    def over_core(self, value):
        return lax.ppermute(value, "tp", [(0, 1), (1, 0)])

    def ring_at(self, back):
        return (self.at - back) % self.ring

    def lane_at(self, back):
        return (self.lane - back) % self.width


    def share(self, own):
        pair = jnp.concatenate([own, self.over_half(own)], axis=0)
        return jnp.concatenate([pair, self.over_core(pair)], axis=0)

    def reduce(self, partial):
        rows = partial.shape[0] // 2
        mine = partial[:rows] + self.over_core(partial[rows:].astype(BF16)).astype(F32)
        rows //= 2
        return mine[:rows] + self.over_half(mine[rows:].astype(BF16)).astype(F32)

    def both_cores(self, own):
        other = self.over_core(own)
        first = jnp.where(self.core == 0, own, other)
        second = jnp.where(self.core == 0, other, own)
        return jnp.concatenate([first, second], axis=0)


    def share_ring(self, own):
        parts = [own]
        for _ in range(self.ring - 1):
            parts.append(self.over_ring(parts[-1]))
        mine = jnp.concatenate(parts, axis=0)
        return jnp.concatenate([mine, self.over_core(mine)], axis=0)

    def reduce_ring(self, partial):
        rows = partial.shape[0] // 2
        mine = partial[:rows] + self.over_core(partial[rows:].astype(BF16)).astype(F32)
        rows //= self.ring
        parts = [mine[k * rows : (k + 1) * rows] for k in range(self.ring)]
        total = None
        for back in list(range(1, self.ring)) + [0]:
            total = parts[back] if total is None else total + parts[back]
            if back:
                total = self.over_ring(total.astype(BF16)).astype(F32)
        return total


    def gather_pack(self, shards):
        m, rows, cols = shards.shape
        cols //= 2
        halves = shards.reshape(m, rows, 2, cols)
        keep = lax.dynamic_index_in_dim(halves, self.half, 2, keepdims=False)
        send = lax.dynamic_index_in_dim(halves, 1 - self.half, 2, keepdims=False)
        recv = self.over_half(send)
        unit = jnp.where(
            self.half == 0, jnp.stack([keep, recv], 1), jnp.stack([recv, keep], 1)
        ).reshape(m, 1, 2 * rows, cols)
        whole = jnp.zeros((m, self.fsdp, 2 * rows, cols), shards.dtype)
        for back in range(self.ring):
            piece = unit
            for turn in range(self.width):
                place = self.ring_at(back) * self.width + self.lane_at(turn)
                whole = lax.dynamic_update_slice(whole, piece, (0, place, 0, 0))
                if turn < self.width - 1:
                    piece = self.over_lanes(piece)
            if back < self.ring - 1:
                unit = self.over_ring(unit)
        return whole

    def scatter_pack(self, grads):
        m, _, rows, cols = grads.shape

        def block(back, turn):
            place = self.ring_at(back) * self.width + self.lane_at(turn)
            return lax.dynamic_slice(grads, (0, place, 0, 0), (m, 1, rows, cols))

        def over_width(back):
            total = None
            for turn in list(range(1, self.width)) + [0]:
                term = block(back, turn)
                total = term if total is None else total.astype(F32) + term.astype(F32)
                if turn:
                    total = self.over_lanes(total.astype(BF16))
            return total.astype(F32)

        sums = {back: over_width(back) for back in list(range(1, self.ring)) + [0]}
        total = None
        for back in list(range(1, self.ring)) + [0]:
            total = sums[back] if total is None else total + sums[back]
            if back:
                total = self.over_ring(total.astype(BF16)).astype(F32)
        total = total.reshape(m, 2, rows // 2, cols)
        keep = lax.dynamic_index_in_dim(total, self.half, 1, keepdims=False)
        send = lax.dynamic_index_in_dim(total, 1 - self.half, 1, keepdims=False).astype(BF16)
        recv = self.over_half(send).astype(F32)
        return jnp.where(
            self.half == 0,
            jnp.concatenate([keep, recv], -1),
            jnp.concatenate([recv, keep], -1),
        )


    def gather_feed(self, shards):
        m, rows, cols = shards.shape
        cols //= self.ring
        parts = shards.reshape(m, rows, self.ring, cols)

        def part(ahead):
            index = (self.at + ahead) % self.ring
            return lax.dynamic_index_in_dim(parts, index, 2, keepdims=False)

        pieces = [part(0)] + [self.over_ring(part(k), k) for k in range(1, self.ring)]
        group = max(1, self.ring // 2)
        whole = jnp.zeros((m, self.ring, self.width, 2, rows, cols), shards.dtype)

        def put(whole, values, backs, turn, half):
            for n, back in enumerate(backs):
                spot = (0, self.ring_at(back), self.lane_at(turn), half, 0, 0)
                whole = lax.dynamic_update_slice(whole, values[n][:, None, None, None], spot)
            return whole

        for first in range(0, self.ring, group):
            backs = list(range(first, first + group))
            values = jnp.stack([pieces[b] for b in backs])
            if first == 0:
                for turn in range(self.width):
                    whole = put(whole, values, backs, turn, self.half)
                    whole = put(whole, self.over_half(values), backs, turn, 1 - self.half)
                    if turn < self.width - 1:
                        values = self.over_lanes(values)
            else:
                for half in (self.half, 1 - self.half):
                    there = values
                    for turn in range(self.width):
                        whole = put(whole, there, backs, turn, half)
                        if turn < self.width - 1:
                            there = self.over_lanes(there)
                    values = self.over_half(values)
        return whole.reshape(m, self.ring * self.width * 2 * rows, cols)

    def scatter_feed(self, grads):
        m, rows, cols = grads.shape
        rows //= self.fsdp * 2
        blocks = grads.reshape(m, self.ring, self.width, 2, rows, cols)
        group = max(1, self.ring // 2)

        def over_width(values):
            total = None
            for turn in list(range(1, self.width)) + [0]:
                term = lax.dynamic_index_in_dim(values, self.lane_at(turn), 2, keepdims=False)
                total = term if total is None else total.astype(F32) + term.astype(F32)
                if turn:
                    total = self.over_lanes(total.astype(BF16))
            return total.astype(F32)

        def over_halves(values, dim):
            keep = lax.dynamic_index_in_dim(values, self.half, dim, keepdims=False)
            send = lax.dynamic_index_in_dim(values, 1 - self.half, dim, keepdims=False)
            return keep.astype(F32) + self.over_half(send.astype(BF16)).astype(F32)

        sums = []
        for first in range(0, self.ring, group):
            values = blocks[:, first : first + group]
            if first == 0:
                sums.append(over_halves(over_width(values), 2))
            else:
                sums.append(over_width(over_halves(values, 3)))
        mine = jnp.concatenate(sums, 1).astype(BF16)
        result = jnp.zeros((m, rows, self.ring, cols), F32)
        for k in range(self.ring):
            piece = lax.dynamic_index_in_dim(mine, (self.at + k) % self.ring, 1, keepdims=False)
            if k:
                piece = self.over_ring(piece, k)
            result = lax.dynamic_update_slice(
                result, piece.astype(F32)[:, :, None], (0, 0, self.ring_at(k), 0)
            )
        return result.reshape(m, rows, self.ring * cols)

    def scatter_gains(self, grads):
        grads = grads + self.over_core(grads)
        count, width = grads.shape
        blocks = grads.reshape(count, self.ring, self.width, 2, width // (self.fsdp * 2))
        keep = lax.dynamic_index_in_dim(blocks, self.half, 3, keepdims=False)
        send = lax.dynamic_index_in_dim(blocks, 1 - self.half, 3, keepdims=False)
        blocks = keep + self.over_half(send)
        total = None
        for turn in list(range(1, self.width)) + [0]:
            term = lax.dynamic_index_in_dim(blocks, self.lane_at(turn), 2, keepdims=False)
            total = term if total is None else total + term
            if turn:
                total = self.over_lanes(total)
        blocks, total = total, None
        for back in list(range(1, self.ring)) + [0]:
            term = lax.dynamic_index_in_dim(blocks, self.ring_at(back), 1, keepdims=False)
            total = term if total is None else total + term
            if back:
                total = self.over_ring(total)
        return total

    def gather_gains(self, gains):
        count, part = gains.shape
        other = self.over_half(gains)
        unit = jnp.where(
            self.half == 0,
            jnp.concatenate([gains, other], 1),
            jnp.concatenate([other, gains], 1),
        )[:, None]
        whole = jnp.zeros((count, self.fsdp, 2 * part), gains.dtype)
        for back in range(self.ring):
            piece = unit
            for turn in range(self.width):
                place = self.ring_at(back) * self.width + self.lane_at(turn)
                whole = lax.dynamic_update_slice(whole, piece, (0, place, 0))
                if turn < self.width - 1:
                    piece = self.over_lanes(piece)
            if back < self.ring - 1:
                unit = self.over_ring(unit)
        return whole.reshape(count, self.fsdp * 2 * part)


def on_device(
    mesh,
    inputs,
    conditioning,
    query_matrix,
    key_matrix,
    value_matrix,
    output_matrix,
    cross_query,
    cross_key,
    cross_value,
    cross_output,
    gate_matrix,
    up_matrix,
    down_matrix,
    first_gain,
    second_gain,
    third_gain,
    cotangent,
):
    links = Links(mesh)
    core, half = links.core, links.half
    rows = inputs.shape[1]
    own_rows = rows // 2
    width = inputs.shape[2]

    gains = links.gather_gains(jnp.stack([first_gain, second_gain, third_gain])).astype(F32)
    first_norm, second_norm, third_norm = gains[0], gains[1], gains[2]
    early = links.gather_pack(jnp.stack([query_matrix, key_matrix, value_matrix]))
    late = links.gather_pack(
        jnp.stack(
            [
                output_matrix.T,
                cross_query,
                cross_output.T,
                jnp.concatenate([cross_key, cross_value], axis=0),
            ]
        )
    )
    cols = early.shape[-1]
    query_full, key_full, value_full = (early[n].reshape(width, cols) for n in range(3))
    output_full, cross_query_full, cross_output_full = (
        late[n].reshape(width, cols) for n in range(3)
    )
    context_rows = cross_key.shape[0]
    context_pack = late[3].reshape(2 * links.fsdp, 2, context_rows, cols)
    cross_key_full = context_pack[:, 0].reshape(-1, cols)
    cross_value_full = context_pack[:, 1].reshape(-1, cols)
    feed = links.gather_feed(jnp.stack([gate_matrix, up_matrix, down_matrix.T]))
    gate_full, up_full, down_full = feed[0], feed[1], feed[2]

    own = lax.dynamic_slice_in_dim(inputs[0], core * own_rows, own_rows, 0)
    sequence = links.share(own)
    tokens = own.astype(F32)
    upstream = lax.dynamic_slice_in_dim(cotangent[0], core * own_rows, own_rows, 0)
    row = lax.iota(jnp.int32, own_rows)
    position = jnp.concatenate(
        [
            row + (half ^ there) * rows + (core ^ other) * own_rows
            for other in (0, 1)
            for there in (0, 1)
        ]
    )
    tables = rotary_tables(position)

    normed_one = norm_low(sequence.astype(F32), first_norm)
    query_rot, key_rot, value_low, self_low = None, None, None, None
    value_low = mm(normed_one, value_full).astype(BF16)
    query_rot, key_rot, self_low, self_logsum = self_forward(
        mm(normed_one, query_full), mm(normed_one, key_full), value_low, tables
    )
    hidden_one = tokens + links.reduce(mm_nt(self_low, output_full))

    normed_two = links.share(norm_low(hidden_one, second_norm))
    cross_query_low = mm(normed_two, cross_query_full).astype(BF16)
    context_count = conditioning.shape[1]
    padded = -(-context_count // 128) * 128
    context = jnp.pad(conditioning[0], ((0, padded - context_count), (0, 0)))
    cross_key_low = mm(context, cross_key_full).astype(BF16)
    cross_value_low = mm(context, cross_value_full).astype(BF16)
    cross_low, cross_logsum = cross_forward(
        cross_query_low, cross_key_low, cross_value_low, context_count
    )
    hidden_two = hidden_one + links.reduce(mm_nt(cross_low, cross_output_full))

    normed_three = links.share_ring(norm_low(hidden_two, third_norm))
    upstream_all = links.share_ring(upstream)
    gate_value = mm(normed_three, gate_full)
    up_value = mm(normed_three, up_full)
    sigmoid_gate = jax.nn.sigmoid(gate_value)
    silu_gate = gate_value * sigmoid_gate
    feed_low = (silu_gate * up_value).astype(BF16)
    feed_grad = mm_nt_down(upstream_all, down_full)
    gate_grad = (
        feed_grad * up_value * sigmoid_gate * (1.0 + gate_value * (1.0 - sigmoid_gate))
    ).astype(BF16)
    up_grad = (feed_grad * silu_gate).astype(BF16)
    third_grad = links.reduce_ring(mm_nt(gate_grad, gate_full) + mm_nt(up_grad, up_full))
    layer_result = hidden_two + links.reduce_ring(mm_nt(feed_low, down_full))
    feed_grads = jnp.stack(
        [
            mm_tn(normed_three, gate_grad).astype(BF16),
            mm_tn(normed_three, up_grad).astype(BF16),
            mm_tn(upstream_all, feed_low).astype(BF16),
        ]
    )
    gate_sum, up_sum, down_sum = links.scatter_feed(feed_grads)

    norm_three_back, third_gain_grad = norm_backward(hidden_two, third_norm, third_grad)
    hidden_two_grad = upstream.astype(F32) + norm_three_back
    branch_two = links.share(hidden_two_grad.astype(BF16))
    cross_out_grad = mm(branch_two, cross_output_full).astype(BF16)
    cross_query_round, cross_key_back, cross_value_back = cross_backward(
        cross_query_low, cross_key_low, cross_value_low, cross_out_grad, cross_logsum, context_count
    )
    second_grad = links.reduce(mm_nt(cross_query_round, cross_query_full))
    cross_key_low_back = cross_key_back.astype(BF16)
    cross_value_low_back = cross_value_back.astype(BF16)
    context_term = (
        mm_nt(cross_key_low_back, cross_key_full) + mm_nt(cross_value_low_back, cross_value_full)
    )[:context_count]
    context_term = context_term + links.over_core(context_term.astype(BF16)).astype(F32)
    context_low = context_term.astype(BF16)
    context_grad = context_low.astype(F32) + links.over_half(context_low).astype(F32)

    norm_two_back, second_gain_grad = norm_backward(hidden_one, second_norm, second_grad)
    hidden_one_grad = hidden_two_grad + norm_two_back
    branch_one = links.share(hidden_one_grad.astype(BF16))
    self_out_grad = mm(branch_one, output_full).astype(BF16)
    context_grads = jnp.stack(
        [
            mm_tn(context, cross_key_low_back).reshape(-1, context_rows, cols),
            mm_tn(context, cross_value_low_back).reshape(-1, context_rows, cols),
        ],
        axis=1,
    )
    late_grads = jnp.stack(
        [
            mm_tn(branch_one, self_low).astype(BF16),
            mm_tn(normed_two, cross_query_round).astype(BF16),
            mm_tn(branch_two, cross_low).astype(BF16),
            context_grads.reshape(width, cols).astype(BF16),
        ]
    )
    unit_rows = width // links.fsdp
    late_sums = links.scatter_pack(late_grads.reshape(4, links.fsdp, unit_rows, cols))
    query_round, key_round, value_round = self_backward(
        query_rot, key_rot, value_low, self_out_grad, self_logsum, tables
    )
    first_grad = links.reduce(
        mm_nt(query_round, query_full)
        + mm_nt(key_round, key_full)
        + mm_nt(value_round, value_full)
    )
    early_grads = jnp.stack(
        [
            mm_tn(normed_one, query_round).astype(BF16),
            mm_tn(normed_one, key_round).astype(BF16),
            mm_tn(normed_one, value_round).astype(BF16),
        ]
    )
    early_sums = links.scatter_pack(early_grads.reshape(3, links.fsdp, unit_rows, cols))
    norm_one_back, first_gain_grad = norm_backward(tokens, first_norm, first_grad)
    inputs_grad = hidden_one_grad + norm_one_back
    gain_sums = links.scatter_gains(
        jnp.stack([first_gain_grad, second_gain_grad, third_gain_grad])
    )
    return (
        links.both_cores(layer_result)[None],
        links.both_cores(inputs_grad)[None],
        context_grad[None],
        early_sums[0],
        early_sums[1],
        early_sums[2],
        late_sums[0].T,
        late_sums[1],
        late_sums[3][:context_rows],
        late_sums[3][context_rows:],
        late_sums[2].T,
        gate_sum,
        up_sum,
        down_sum.T,
        gain_sums[0],
        gain_sums[1],
        gain_sums[2],
    )


def mm_nt_down(upstream, down_rows):
    return mm(upstream, down_rows).astype(BF16).astype(F32)


def solution(mesh):
    row = P(("fsdp", "ctx"), "tp")
    col = P("tp", ("fsdp", "ctx"))
    gain = P(("fsdp", "ctx"))
    token = P("fsdp", "ctx", None)
    context = P("fsdp", None, None)
    weights = (row, row, row, col, row, row, row, col, row, row, col, gain, gain, gain)
    return jax.shard_map(
        functools.partial(on_device, mesh),
        mesh=mesh,
        in_specs=(token, context) + weights + (token,),
        out_specs=(token, token, context) + weights,
        check_vma=False,
    )
```

time: 3240 us -> 878 us (0.27)
  waiting for transfers between devices: 2630 us -> 412 us
  blocking collectives: 184 us -> 0 us
  matrix products: 203 us -> 71.6 us
  starting transfers between devices: 2.25 us -> 90.9 us
  Pallas kernels: 0 us -> 48.2 us
  local copies, waits for them, and re-layouts: 155 us -> 192 us
    reduce_scatter x9 -> x0, waiting for transfers between devices: 1730 us -> none  [the longest x1 290 us: on_device(): lax.psum_scatter(down_grad, ('fsdp', 'ctx'), scatter_dimension=1, tiled=T...]
    all_gather x11 -> x0, waiting for transfers between devices: 642 us -> none  [the longest x1 122 us: on_device(): lax.all_gather(down_matrix, ('fsdp', 'ctx'), axis=1, tiled=True)]
    ppermute x0 -> x98, waiting for transfers between devices: none -> 412 us  [the longest x36 226 us: over_ring(): return lax.ppermute(value, 'fsdp', pairs)]
    unnamed x34 -> x0, waiting for transfers between devices: 179 us -> none
    unnamed x2 -> x0, blocking collectives: 156 us -> none
    dot_general x117 -> x33, matrix products: 203 us -> 71.6 us  [the longest x11 27.1 us: mm_nt(): lax.dot_general(left, right, (((1,), (1,)), ((), ())), preferred_element_...]
    ppermute x0 -> x98, starting transfers between devices: none -> 90.9 us  [the longest x36 43 us: over_ring(): return lax.ppermute(value, 'fsdp', pairs)]
    psum x6 -> x0, waiting for transfers between devices: 79.7 us -> none  [the longest x5 79.7 us: head_sum(): return lax.psum(values, 'tp')]
  transfers between devices with their start and end apart: 30 -> 98, of which waited for: 27 -> 44; matrix products, arithmetic and copies ran while one was open for 7% -> 31% of each run, Pallas kernels for 0% -> 4%
where the time goes in v1:
time: 878 us; the launch traced here: 872 us
  waiting for transfers between devices  412 us (47%)
  local copies, waits for them, and re-layouts  192 us (22%)
  starting transfers between devices  90.9 us (10%)
  matrix products  71.6 us (8%)
  other arithmetic  52.9 us (6%)
  Pallas kernels  48.2 us (5%)
    ppermute x36, waiting for transfers between devices, over_ring(): return lax.ppermute(value, 'fsdp', pairs)  226 us
    ppermute x20, waiting for transfers between devices, over_half(): return lax.ppermute(value, 'ctx', [(0, 1), (1, 0)])  127 us
    dynamic_update_slice x4, local copies, waits for them, and re-layouts, scatter_feed(): lax.dynamic_update_slice(result, piece.astype(F32)[:, :, None], (0, 0, se...  70.2 us
    ppermute x26, waiting for transfers between devices, over_lanes(): return lax.ppermute(value, 'fsdp', pairs)  58.1 us
    ppermute x36, starting transfers between devices, over_ring(): return lax.ppermute(value, 'fsdp', pairs)  43 us
    unnamed x212, local copies, waits for them, and re-layouts  31.3 us
    dot_general x11, matrix products, mm_nt(): lax.dot_general(left, right, (((1,), (1,)), ((), ())), preferred_element_...  27.1 us
    ppermute x26, starting transfers between devices, over_lanes(): return lax.ppermute(value, 'fsdp', pairs)  24.5 us
  transfers between devices with their start and end apart: 98, of which 44 were waited for; matrix products, arithmetic and copies ran while one was open for 31% of the time, Pallas kernels for 4%

profile of v1, /device:TPU:0, one launch (start us, length us, event | category | flops | bytes accessed | tf_op | source)
XLA Modules:
  0.0 871.7 jit_solution(12407265383739891540)
XLA Ops:
  33.3 5.2 constant_dynamic-slice_fusion.18
  58.1 3.2 collective-permute-done.6
  62.2 4.7 collective-permute-done.8
  67.5 3.0 collective-permute-done.9
  77.4 9.6 %collective-permute-done.12 = bf16[3,1,192,384]{3,2,0,1:T(8,128)(2,1)S(1)} collective-permute-done((bf16[3,1,192,384]{3,2,0,1:T(8,128)(2,1)S(1)}, bf16[3,1,192,384]{3,2,0,1:T(8,128)(2,1)S(1)}, u32[]{:S(2)}, u32[]{:S(2)}) %collective-permute-start.12) | collective-permute-done | bytes 442400 | tf_op jit(solution)/shard_map/ppermute | solution.py:244
  87.7 11.9 %collective-permute-done.20 = bf16[4,1,192,384]{3,2,0,1:T(8,128)(2,1)S(1)} collective-permute-done((bf16[4,1,192,384]{3,2,0,1:T(8,128)(2,1)S(1)}, bf16[4,1,192,384]{3,2,0,1:T(8,128)(2,1)S(1)}, u32[]{:S(2)}, u32[]{:S(2)}) %collective-permute-start.20) | collective-permute-done | bytes 589856 | tf_op jit(solution)/shard_map/ppermute | solution.py:244
  99.9 9.2 %collective-permute-done.14 = bf16[3,1,192,384]{3,2,0,1:T(8,128)(2,1)S(1)} collective-permute-done((bf16[3,1,192,384]{3,2,0,1:T(8,128)(2,1)S(1)}, bf16[3,1,192,384]{3,2,0,1:T(8,128)(2,1)S(1)}, u32[]{:S(2)}, u32[]{:S(2)}) %collective-permute-start.14) | collective-permute-done | bytes 442400 | tf_op jit(solution)/shard_map/ppermute | solution.py:244
  113.1 5.9 collective-permute-done.21
  119.4 21.5 %collective-permute-done.16 = bf16[3,1,192,384]{3,2,0,1:T(8,128)(2,1)S(1)} collective-permute-done((bf16[3,1,192,384]{3,2,0,1:T(8,128)(2,1)S(1)}, bf16[3,1,192,384]{3,2,0,1:T(8,128)(2,1)S(1)}, u32[]{:S(2)}, u32[]{:S(2)}) %collective-permute-start.16) | collective-permute-done | bytes 442400 | tf_op jit(solution)/shard_map/ppermute | solution.py:244
  143.3 8.8 %collective-permute-start.24 = (bf16[4,1,192,384]{3,2,0,1:T(8,128)(2,1)S(1)}, bf16[4,1,192,384]{3,2,0,1:T(8,128)(2,1)S(1)}, u32[]{:S(2)}, u32[]{:S(2)}) collective-permute-start(bf16[4,1,192,384]{3,2,0,1:T(8,128)(2,1)S(1)} %collective-permute-done.22), channel_id=1, source_target_pairs={{0,8},{4,12},{8,16},{12,20},{16,24},{20,28},{24,0},{28,4},{1,9},{5... | collective-permute-start | bytes 1769480 | tf_op jit(solution)/shard_map/ppermute | solution.py:244
  156.8 12.0 %collective-permute-done.24 = bf16[4,1,192,384]{3,2,0,1:T(8,128)(2,1)S(1)} collective-permute-done((bf16[4,1,192,384]{3,2,0,1:T(8,128)(2,1)S(1)}, bf16[4,1,192,384]{3,2,0,1:T(8,128)(2,1)S(1)}, u32[]{:S(2)}, u32[]{:S(2)}) %collective-permute-start.24) | collective-permute-done | bytes 589856 | tf_op jit(solution)/shard_map/ppermute | solution.py:244
  171.5 14.5 %shard_map.296 = (bf16[640,384]{1,0:T(8,128)(2,1)S(1)}, bf16[640,384]{1,0:T(8,128)(2,1)S(1)}, bf16[640,384]{1,0:T(8,128)(2,1)S(1)}, f32[640,384]{1,0:T(8,128)S(1)}) custom-call(f32[640,384]{1,0:T(8,128)S(1)} %fusion.94.q_ref, f32[640,384]{1,0:T(8,128)S(1)} %fusion.95.k_ref, bf16[640,384]{1,0:T(8,128)(2,1)S(1)} %convolution_convert_fusion.15.v_ref, ...), custom_call_target="tpu_custom_call" | custom-call | flops 629145600 | bytes 2949120 | tf_op jit(solution)/shard_map/pallas_call | solution.py:178
  186.1 12.9 %collective-permute-start.50 = (bf16[160,1536]{1,0:T(8,128)(2,1)}, bf16[160,1536]{1,0:T(8,128)(2,1)}, u32[]{:S(2)}, u32[]{:S(2)}) collective-permute-start(bf16[160,1536]{1,0:T(8,128)(2,1)} %get-tuple-element.145), channel_id=1, source_target_pairs={{0,8},{4,12},{8,16},{12,20},{16,24},{20,28},{24,0},{28,4},{1,9},{5... | collective-permute-start | bytes 1474568 | tf_op jit(solution)/shard_map/ppermute | solution.py:244
  206.5 3.8 broadcast_in_dim.75
  226.8 7.4 collective-permute-done.51
  235.5 20.4 %collective-permute-done.43 = bf16[2,3,96,768]{3,2,1,0:T(8,128)(2,1)} collective-permute-done((bf16[2,3,96,768]{3,2,1,0:T(8,128)(2,1)S(1)}, bf16[2,3,96,768]{3,2,1,0:T(8,128)(2,1)}, u32[]{:S(2)}, u32[]{:S(2)}) %collective-permute-start.43) | collective-permute-done | bytes 884768 | tf_op jit(solution)/shard_map/ppermute | solution.py:252
  261.1 5.1 collective-permute-done.27
  270.4 24.5 %collective-permute-done.28 = bf16[160,1536]{1,0:T(8,128)(2,1)S(1)} collective-permute-done((bf16[160,1536]{1,0:T(8,128)(2,1)S(1)}, bf16[160,1536]{1,0:T(8,128)(2,1)S(1)}, u32[]{:S(2)}, u32[]{:S(2)}) %collective-permute-start.28) | collective-permute-done | bytes 491552 | tf_op jit(solution)/shard_map/ppermute | solution.py:252
  298.9 4.6 shard_map.297
  316.9 8.1 collective-permute-done.31
  332.6 8.2 collective-permute-done.32
  345.0 9.0 %collective-permute-done.33 = bf16[160,1536]{1,0:T(8,128)(2,1)S(1)} collective-permute-done((bf16[160,1536]{1,0:T(8,128)(2,1)S(1)}, bf16[160,1536]{1,0:T(8,128)(2,1)S(1)}, u32[]{:S(2)}, u32[]{:S(2)}) %collective-permute-start.33) | collective-permute-done | bytes 491552 | tf_op jit(solution)/shard_map/ppermute | solution.py:244
  357.7 8.7 collective-permute-done.34
  366.6 3.6 fusion.89
  371.8 6.0 convolution_convert_fusion.3
  378.1 3.3 fusion.98
  381.4 4.4 convolution_convert_fusion.1
  385.9 4.5 fusion.7
  390.3 3.6 convolution_convert_fusion.2
  394.0 5.6 fusion.100
  399.6 3.6 convolution_convert_fusion
  409.8 10.1 %convolution_add_fusion = f32[1280,1536]{1,0:T(8,128)} fusion(f32[1280,1536]{1,0:T(8,128)} %fusion.100, bf16[1536,768]{1,0:T(8,128)(2,1)S(1)} %bitcast.317, bf16[1280,768]{1,0:T(8,128)(2,1)} %copy-done.89, f32[1280,768]{1,0:T(8,128)S(1)} %copy-done.88), kind=kOutput, calls=%fused_computation | convolution fusion | flops 3028746240 | bytes 23986176 | tf_op jit(solution)/shard_map/dot_general | solution.py:29
  422.7 3.3 fusion.99
  426.6 22.4 %collective-permute-done.87 = bf16[3,2,2,96,768]{4,3,2,1,0:T(8,128)(2,1)S(1)} collective-permute-done((bf16[3,2,2,96,768]{4,3,2,1,0:T(8,128)(2,1)}, bf16[3,2,2,96,768]{4,3,2,1,0:T(8,128)(2,1)S(1)}, u32[]{:S(2)}, u32[]{:S(2)}) %collective-permute-start.87) | collective-permute-done | bytes 1769504 | tf_op jit(solution)/shard_map/ppermute | solution.py:252
  458.7 15.2 %collective-permute-done.55 = bf16[160,1536]{1,0:T(8,128)(2,1)S(1)} collective-permute-done((bf16[160,1536]{1,0:T(8,128)(2,1)S(1)}, bf16[160,1536]{1,0:T(8,128)(2,1)S(1)}, u32[]{:S(2)}, u32[]{:S(2)}) %collective-permute-start.55) | collective-permute-done | bytes 491552 | tf_op jit(solution)/shard_map/ppermute | solution.py:244
  474.0 10.4 %collective-permute-done.46 = bf16[160,1536]{1,0:T(8,128)(2,1)S(1)} collective-permute-done((bf16[160,1536]{1,0:T(8,128)(2,1)S(1)}, bf16[160,1536]{1,0:T(8,128)(2,1)S(1)}, u32[]{:S(2)}, u32[]{:S(2)}) %collective-permute-start.46) | collective-permute-done | bytes 491552 | tf_op jit(solution)/shard_map/ppermute | solution.py:244
  484.6 10.4 %collective-permute-done.56 = bf16[160,1536]{1,0:T(8,128)(2,1)S(1)} collective-permute-done((bf16[160,1536]{1,0:T(8,128)(2,1)S(1)}, bf16[160,1536]{1,0:T(8,128)(2,1)S(1)}, u32[]{:S(2)}, u32[]{:S(2)}) %collective-permute-start.56) | collective-permute-done | bytes 491552 | tf_op jit(solution)/shard_map/ppermute | solution.py:244
  495.1 10.4 %collective-permute-done.47 = bf16[160,1536]{1,0:T(8,128)(2,1)S(1)} collective-permute-done((bf16[160,1536]{1,0:T(8,128)(2,1)S(1)}, bf16[160,1536]{1,0:T(8,128)(2,1)S(1)}, u32[]{:S(2)}, u32[]{:S(2)}) %collective-permute-start.47) | collective-permute-done | bytes 491552 | tf_op jit(solution)/shard_map/ppermute | solution.py:244
  505.6 10.4 %collective-permute-done.57 = bf16[160,1536]{1,0:T(8,128)(2,1)S(1)} collective-permute-done((bf16[160,1536]{1,0:T(8,128)(2,1)S(1)}, bf16[160,1536]{1,0:T(8,128)(2,1)S(1)}, u32[]{:S(2)}, u32[]{:S(2)}) %collective-permute-start.57) | collective-permute-done | bytes 491552 | tf_op jit(solution)/shard_map/ppermute | solution.py:244
  516.5 8.1 collective-permute-done.48
  529.7 9.2 %collective-permute-done.58 = bf16[160,1536]{1,0:T(8,128)(2,1)S(1)} collective-permute-done((bf16[160,1536]{1,0:T(8,128)(2,1)S(1)}, bf16[160,1536]{1,0:T(8,128)(2,1)S(1)}, u32[]{:S(2)}, u32[]{:S(2)}) %collective-permute-start.58) | collective-permute-done | bytes 491552 | tf_op jit(solution)/shard_map/ppermute | solution.py:252
  543.3 3.9 collective-permute-start.91
  547.2 3.0 copy.85
  552.5 17.5 %dynamic_update_slice.172 = f32[3,96,4,768]{3,2,1,0:T(4,128)} dynamic-update-slice(f32[3,96,4,768]{3,2,1,0:T(4,128)} %broadcast_in_dim.79, f32[3,96,1,768]{3,2,1,0:T(1,128)} %copy.85, s32[]{:T(128)} %constant.455.clone.1, s32[]{:T(128)} %constant.455.clone.1, s32[]{:T(128)S(6)} %select_n.590, s32[]{:T(128)} %constant.455.clone.1) | dynamic-update-slice | bytes 1769476 | tf_op jit(solution)/shard_map/dynamic_update_slice | solution.py:427
  572.5 17.5 %dynamic_update_slice.173 = f32[3,96,4,768]{3,2,1,0:T(4,128)} dynamic-update-slice(f32[3,96,4,768]{3,2,1,0:T(4,128)} %dynamic_update_slice.172, f32[3,96,1,768]{3,2,1,0:T(1,128)} %reshape.357, s32[]{:T(128)} %constant.455.clone.1, s32[]{:T(128)} %constant.455.clone.1, s32[]{:T(128)S(6)} %select_n.594, s32[]{:T(128)} %constant.455.clone.1) | dynamic-update-slice | bytes 1769476 | tf_op jit(solution)/shard_map/dynamic_update_slice | solution.py:427
  592.4 17.5 %dynamic_update_slice.174 = f32[3,96,4,768]{3,2,1,0:T(4,128)} dynamic-update-slice(f32[3,96,4,768]{3,2,1,0:T(4,128)} %dynamic_update_slice.173, f32[3,96,1,768]{3,2,1,0:T(1,128)} %reshape.358, s32[]{:T(128)} %constant.455.clone.1, s32[]{:T(128)} %constant.455.clone.1, s32[]{:T(128)S(6)} %select_n.598, s32[]{:T(128)} %constant.455.clone.1) | dynamic-update-slice | bytes 1769476 | tf_op jit(solution)/shard_map/dynamic_update_slice | solution.py:427
  612.3 17.5 %dynamic_update_slice.175 = f32[3,96,4,768]{3,2,1,0:T(4,128)} dynamic-update-slice(f32[3,96,4,768]{3,2,1,0:T(4,128)} %dynamic_update_slice.174, f32[3,96,1,768]{3,2,1,0:T(1,128)} %reshape.359, s32[]{:T(128)} %constant.455.clone.1, s32[]{:T(128)} %constant.455.clone.1, s32[]{:T(128)S(6)} %select_n.601, s32[]{:T(128)} %constant.455.clone.1) | dynamic-update-slice | bytes 1769476 | tf_op jit(solution)/shard_map/dynamic_update_slice | solution.py:427
  638.6 11.7 %shard_map.298 = (bf16[640,384]{1,0:T(8,128)(2,1)S(1)}, f32[256,384]{1,0:T(8,128)S(1)}, f32[256,384]{1,0:T(8,128)S(1)}) custom-call(bf16[640,384]{1,0:T(8,128)(2,1)S(1)} %copy-done.7, bf16[256,384]{1,0:T(8,128)(2,1)S(1)} %convolution_convert_fusion.17.k_ref, bf16[256,384]{1,0:T(8,128)(2,1)S(1)} %convolution_convert_fusion.16.v_ref, ...), custom_call_target="tpu_custom_call" | custom-call | flops 629145600 | bytes 3735552 | tf_op jit(solution)/shard_map/pallas_call | solution.py:205
  657.4 12.1 %collective-permute-done.61 = bf16[160,1536]{1,0:T(8,128)(2,1)S(1)} collective-permute-done((bf16[160,1536]{1,0:T(8,128)(2,1)S(1)}, bf16[160,1536]{1,0:T(8,128)(2,1)S(1)}, u32[]{:S(2)}, u32[]{:S(2)}) %collective-permute-start.61) | collective-permute-done | bytes 491552 | tf_op jit(solution)/shard_map/ppermute | solution.py:252
  674.1 8.8 %collective-permute-done.62 = bf16[160,1536]{1,0:T(8,128)(2,1)S(1)} collective-permute-done((bf16[160,1536]{1,0:T(8,128)(2,1)S(1)}, bf16[160,1536]{1,0:T(8,128)(2,1)S(1)}, u32[]{:S(2)}, u32[]{:S(2)}) %collective-permute-start.62) | collective-permute-done | bytes 491552 | tf_op jit(solution)/shard_map/ppermute | solution.py:252
  685.4 5.7 collective-permute-done.68
  694.2 17.5 %shard_map.299 = (bf16[640,384]{1,0:T(8,128)(2,1)S(1)}, bf16[640,384]{1,0:T(8,128)(2,1)S(1)}, bf16[640,384]{1,0:T(8,128)(2,1)S(1)}) custom-call(bf16[640,384]{1,0:T(8,128)(2,1)S(1)} %copy-done.11, bf16[640,384]{1,0:T(8,128)(2,1)S(1)} %copy-done.13, bf16[640,384]{1,0:T(8,128)(2,1)S(1)} %copy-done.9, bf16[640,384]{1,0:T(8,128)(2,1)S(1)} %convolution_convert_fusion.12.do_ref, ...), custom_call_target="tpu_custom_call" | custom-call | flops 1572864000 | bytes 4915200 | tf_op jit(solution)/shard_map/pallas_call | solution.py:187
  731.2 3.3 collective-permute-done.69
  735.1 40.0 %collective-permute-done.77 = bf16[4,1,192,384]{3,2,0,1:T(8,128)(2,1)S(1)} collective-permute-done((bf16[4,1,192,384]{3,2,0,1:T(8,128)(2,1)S(1)}, bf16[4,1,192,384]{3,2,0,1:T(8,128)(2,1)S(1)}, u32[]{:S(2)}, u32[]{:S(2)}) %collective-permute-start.77) | collective-permute-done | bytes 589856 | tf_op jit(solution)/shard_map/ppermute | solution.py:249
  780.8 11.7 %collective-permute-done.70 = bf16[3,1,192,384]{3,2,0,1:T(8,128)(2,1)S(1)} collective-permute-done((bf16[3,1,192,384]{3,2,0,1:T(8,128)(2,1)S(1)}, bf16[3,1,192,384]{3,2,0,1:T(8,128)(2,1)S(1)}, u32[]{:S(2)}, u32[]{:S(2)}) %collective-permute-start.70) | collective-permute-done | bytes 442400 | tf_op jit(solution)/shard_map/ppermute | solution.py:244
  794.5 10.8 %collective-permute-done.78 = bf16[4,1,192,384]{3,2,0,1:T(8,128)(2,1)} collective-permute-done((bf16[4,1,192,384]{3,2,0,1:T(8,128)(2,1)}, bf16[4,1,192,384]{3,2,0,1:T(8,128)(2,1)}, u32[]{:S(2)}, u32[]{:S(2)}) %collective-permute-start.78) | collective-permute-done | bytes 589856 | tf_op jit(solution)/shard_map/ppermute | solution.py:244
  809.6 5.2 collective-permute-done.72
  816.7 5.7 collective-permute-done.94
  823.0 4.9 collective-permute-done.95
  827.9 5.4 collective-permute-done.96
  833.9 4.9 collective-permute-done.97
  840.2 12.1 %collective-permute-done.74 = bf16[3,1,192,384]{3,2,0,1:T(8,128)(2,1)S(1)} collective-permute-done((bf16[3,1,192,384]{3,2,0,1:T(8,128)(2,1)S(1)}, bf16[3,1,192,384]{3,2,0,1:T(8,128)(2,1)S(1)}, u32[]{:S(2)}, u32[]{:S(2)}) %collective-permute-start.74) | collective-permute-done | bytes 442400 | tf_op jit(solution)/shard_map/ppermute | solution.py:244
  854.9 4.8 collective-permute-done.76
  865.1 4.5 collective-permute-done.84
  (599 shorter events, 255.5 us)
Async XLA Ops:
  2.1 40.1 %collective-permute-start.2 = (bf16[3,96]{1,0:T(4,128)(2,1)}, bf16[3,96]{1,0:T(4,128)(2,1)}, u32[]{:S(2)}, u32[]{:S(2)}) collective-permute-start(bf16[3,96]{1,0:T(4,128)(2,1)} %pad_maximum_fusion.24), channel_id=1, source_target_pairs={{0,2},{2,0},{1,3},{3,1},{4,6},{6,4},{5,7},{7,5},{8,10},{10,8},{9,1... | collective-permute-start | bytes 1736 | tf_op jit(solution)/shard_map/ppermute | solution.py:252
  10.7 60.0 %collective-permute-start.10 = (bf16[3,96,384]{2,1,0:T(8,128)(2,1)}, bf16[3,96,384]{2,1,0:T(8,128)(2,1)}, u32[]{:S(2)}, u32[]{:S(2)}) collective-permute-start(bf16[3,96,384]{2,1,0:T(8,128)(2,1)} %bitcast.287), channel_id=1, source_target_pairs={{0,2},{2,0},{1,3},{3,1},{4,6},{6,4},{5,7},{7,5},{8,10},{10,8},{9,1... | collective-permute-start | bytes 663560 | tf_op jit(solution)/shard_map/ppermute | solution.py:252
  11.5 64.4 %collective-permute-start = (bf16[160,1536]{1,0:T(8,128)(2,1)S(1)}, bf16[160,1536]{1,0:T(8,128)(2,1)S(1)}, u32[]{:S(2)}, u32[]{:S(2)}) collective-permute-start(bf16[160,1536]{1,0:T(8,128)(2,1)S(1)} %get-tuple-element.141), channel_id=1, source_target_pairs={{0,2},{2,0},{1,3},{3,1},{4,6},{6,4},{5,7},{7,5},{8,10},{10,8},{9,1... | collective-permute-start | bytes 1474568 | tf_op jit(solution)/shard_map/ppermute | solution.py:252
  18.8 53.9 %collective-permute-start.18 = (bf16[4,96,384]{2,1,0:T(8,128)(2,1)}, bf16[4,96,384]{2,1,0:T(8,128)(2,1)}, u32[]{:S(2)}, u32[]{:S(2)}) collective-permute-start(bf16[4,96,384]{2,1,0:T(8,128)(2,1)} %bitcast.285), channel_id=1, source_target_pairs={{0,2},{2,0},{1,3},{3,1},{4,6},{6,4},{5,7},{7,5},{8,10},{10,8},{9,1... | collective-permute-start | bytes 884744 | tf_op jit(solution)/shard_map/ppermute | solution.py:252
  72.1 15.0 %collective-permute-start.12 = (bf16[3,1,192,384]{3,2,0,1:T(8,128)(2,1)S(1)}, bf16[3,1,192,384]{3,2,0,1:T(8,128)(2,1)S(1)}, u32[]{:S(2)}, u32[]{:S(2)}) collective-permute-start(bf16[3,1,192,384]{3,2,0,1:T(8,128)(2,1)S(1)} %bitcast.332), channel_id=1, source_target_pairs={{0,8},{4,12},{8,16},{12,20},{16,24},{20,28},{24,0},{28,4},{1,9},{5... | collective-permute-start | bytes 1327112 | tf_op jit(solution)/shard_map/ppermute | solution.py:244
  72.2 14.9 %collective-permute-start.11 = (bf16[3,1,192,384]{3,2,0,1:T(8,128)(2,1)S(1)}, bf16[3,1,192,384]{3,2,0,1:T(8,128)(2,1)S(1)}, u32[]{:S(2)}, u32[]{:S(2)}) collective-permute-start(bf16[3,1,192,384]{3,2,0,1:T(8,128)(2,1)S(1)} %bitcast.333), channel_id=1, source_target_pairs={{0,4},{4,0},{8,12},{12,8},{16,20},{20,16},{24,28},{28,24},{1,5},{5... | collective-permute-start | bytes 1327112 | tf_op jit(solution)/shard_map/ppermute | solution.py:249
  74.2 25.5 %collective-permute-start.20 = (bf16[4,1,192,384]{3,2,0,1:T(8,128)(2,1)S(1)}, bf16[4,1,192,384]{3,2,0,1:T(8,128)(2,1)S(1)}, u32[]{:S(2)}, u32[]{:S(2)}) collective-permute-start(bf16[4,1,192,384]{3,2,0,1:T(8,128)(2,1)S(1)} %bitcast.327), channel_id=1, source_target_pairs={{0,8},{4,12},{8,16},{12,20},{16,24},{20,28},{24,0},{28,4},{1,9},{5... | collective-permute-start | bytes 1769480 | tf_op jit(solution)/shard_map/ppermute | solution.py:244
  74.3 25.4 %collective-permute-start.19 = (bf16[4,1,192,384]{3,2,0,1:T(8,128)(2,1)S(1)}, bf16[4,1,192,384]{3,2,0,1:T(8,128)(2,1)S(1)}, u32[]{:S(2)}, u32[]{:S(2)}) collective-permute-start(bf16[4,1,192,384]{3,2,0,1:T(8,128)(2,1)S(1)} %bitcast.328), channel_id=1, source_target_pairs={{0,4},{4,0},{8,12},{12,8},{16,20},{20,16},{24,28},{28,24},{1,5},{5... | collective-permute-start | bytes 1769480 | tf_op jit(solution)/shard_map/ppermute | solution.py:249
  75.9 34.0 %collective-permute-start.1 = (bf16[320,1536]{1,0:T(8,128)(2,1)S(1)}, bf16[320,1536]{1,0:T(8,128)(2,1)S(1)}, u32[]{:S(2)}, u32[]{:S(2)}) collective-permute-start(bf16[320,1536]{1,0:T(8,128)(2,1)S(1)} %pad_maximum_fusion.10), channel_id=1, source_target_pairs={{0,1},{1,0},{2,3},{3,2},{4,5},{5,4},{6,7},{7,6},{8,9},{9,8},{10,11... | collective-permute-start | bytes 2949128 | tf_op jit(solution)/shard_map/ppermute | solution.py:255
  87.0 22.1 %collective-permute-start.14 = (bf16[3,1,192,384]{3,2,0,1:T(8,128)(2,1)S(1)}, bf16[3,1,192,384]{3,2,0,1:T(8,128)(2,1)S(1)}, u32[]{:S(2)}, u32[]{:S(2)}) collective-permute-start(bf16[3,1,192,384]{3,2,0,1:T(8,128)(2,1)S(1)} %collective-permute-done.12), channel_id=1, source_target_pairs={{0,8},{4,12},{8,16},{12,20},{16,24},{20,28},{24,0},{28,4},{1,9},{5... | collective-permute-start | bytes 1327112 | tf_op jit(solution)/shard_map/ppermute | solution.py:244
  87.0 22.7 %collective-permute-start.13 = (bf16[3,1,192,384]{3,2,0,1:T(8,128)(2,1)S(1)}, bf16[3,1,192,384]{3,2,0,1:T(8,128)(2,1)S(1)}, u32[]{:S(2)}, u32[]{:S(2)}) collective-permute-start(bf16[3,1,192,384]{3,2,0,1:T(8,128)(2,1)S(1)} %collective-permute-done.12), channel_id=1, source_target_pairs={{0,4},{4,0},{8,12},{12,8},{16,20},{20,16},{24,28},{28,24},{1,5},{5... | collective-permute-start | bytes 1327112 | tf_op jit(solution)/shard_map/ppermute | solution.py:249
  99.7 111.6 %collective-permute-start.36 = (bf16[3,96,768]{2,1,0:T(8,128)(2,1)}, bf16[3,96,768]{2,1,0:T(8,128)(2,1)}, u32[]{:S(2)}, u32[]{:S(2)}) collective-permute-start(bf16[3,96,768]{2,1,0:T(8,128)(2,1)} %bitcast.284), channel_id=1, source_target_pairs={{0,8},{4,12},{8,16},{12,20},{16,24},{20,28},{24,0},{28,4},{1,9},{5... | collective-permute-start | bytes 1327112 | tf_op jit(solution)/shard_map/ppermute | solution.py:244
  99.7 41.8 %collective-permute-start.22 = (bf16[4,1,192,384]{3,2,0,1:T(8,128)(2,1)S(1)}, bf16[4,1,192,384]{3,2,0,1:T(8,128)(2,1)S(1)}, u32[]{:S(2)}, u32[]{:S(2)}) collective-permute-start(bf16[4,1,192,384]{3,2,0,1:T(8,128)(2,1)S(1)} %collective-permute-done.20), channel_id=1, source_target_pairs={{0,8},{4,12},{8,16},{12,20},{16,24},{20,28},{24,0},{28,4},{1,9},{5... | collective-permute-start | bytes 1769480 | tf_op jit(solution)/shard_map/ppermute | solution.py:244
  109.7 31.2 %collective-permute-start.16 = (bf16[3,1,192,384]{3,2,0,1:T(8,128)(2,1)S(1)}, bf16[3,1,192,384]{3,2,0,1:T(8,128)(2,1)S(1)}, u32[]{:S(2)}, u32[]{:S(2)}) collective-permute-start(bf16[3,1,192,384]{3,2,0,1:T(8,128)(2,1)S(1)} %collective-permute-done.14), channel_id=1, source_target_pairs={{0,8},{4,12},{8,16},{12,20},{16,24},{20,28},{24,0},{28,4},{1,9},{5... | collective-permute-start | bytes 1327112 | tf_op jit(solution)/shard_map/ppermute | solution.py:244
  109.9 33.5 %collective-permute-start.15 = (bf16[3,1,192,384]{3,2,0,1:T(8,128)(2,1)S(1)}, bf16[3,1,192,384]{3,2,0,1:T(8,128)(2,1)S(1)}, u32[]{:S(2)}, u32[]{:S(2)}) collective-permute-start(bf16[3,1,192,384]{3,2,0,1:T(8,128)(2,1)S(1)} %collective-permute-done.14), channel_id=1, source_target_pairs={{0,4},{4,0},{8,12},{12,8},{16,20},{20,16},{24,28},{28,24},{1,5},{5... | collective-permute-start | bytes 1327112 | tf_op jit(solution)/shard_map/ppermute | solution.py:249
  119.0 95.2 %collective-permute-start.40 = (bf16[3,96,768]{2,1,0:T(8,128)(2,1)}, bf16[3,96,768]{2,1,0:T(8,128)(2,1)}, u32[]{:S(2)}, u32[]{:S(2)}) collective-permute-start(bf16[3,96,768]{2,1,0:T(8,128)(2,1)} %bitcast.283), channel_id=1, source_target_pairs={{0,16},{4,20},{8,24},{12,28},{16,0},{20,4},{24,8},{28,12},{1,17},{... | collective-permute-start | bytes 1327112 | tf_op jit(solution)/shard_map/ppermute | solution.py:244
  141.5 74.3 %collective-permute-start.41 = (bf16[3,96,768]{2,1,0:T(8,128)(2,1)}, bf16[3,96,768]{2,1,0:T(8,128)(2,1)}, u32[]{:S(2)}, u32[]{:S(2)}) collective-permute-start(bf16[3,96,768]{2,1,0:T(8,128)(2,1)} %bitcast.282), channel_id=1, source_target_pairs={{0,24},{4,28},{8,0},{12,4},{16,8},{20,12},{24,16},{28,20},{1,25},{... | collective-permute-start | bytes 1327112 | tf_op jit(solution)/shard_map/ppermute | solution.py:244
  143.3 25.5 %collective-permute-start.24 = (bf16[4,1,192,384]{3,2,0,1:T(8,128)(2,1)S(1)}, bf16[4,1,192,384]{3,2,0,1:T(8,128)(2,1)S(1)}, u32[]{:S(2)}, u32[]{:S(2)}) collective-permute-start(bf16[4,1,192,384]{3,2,0,1:T(8,128)(2,1)S(1)} %collective-permute-done.22), channel_id=1, source_target_pairs={{0,8},{4,12},{8,16},{12,20},{16,24},{20,28},{24,0},{28,4},{1,9},{5... | collective-permute-start | bytes 1769480 | tf_op jit(solution)/shard_map/ppermute | solution.py:244
  152.3 33.7 %collective-permute-start.23 = (bf16[4,1,192,384]{3,2,0,1:T(8,128)(2,1)S(1)}, bf16[4,1,192,384]{3,2,0,1:T(8,128)(2,1)S(1)}, u32[]{:S(2)}, u32[]{:S(2)}) collective-permute-start(bf16[4,1,192,384]{3,2,0,1:T(8,128)(2,1)S(1)} %collective-permute-done.22), channel_id=1, source_target_pairs={{0,4},{4,0},{8,12},{12,8},{16,20},{20,16},{24,28},{28,24},{1,5},{5... | collective-permute-start | bytes 1769480 | tf_op jit(solution)/shard_map/ppermute | solution.py:249
  168.8 30.4 %collective-permute-start.25 = (bf16[4,1,192,384]{3,2,0,1:T(8,128)(2,1)S(1)}, bf16[4,1,192,384]{3,2,0,1:T(8,128)(2,1)S(1)}, u32[]{:S(2)}, u32[]{:S(2)}) collective-permute-start(bf16[4,1,192,384]{3,2,0,1:T(8,128)(2,1)S(1)} %collective-permute-done.24), channel_id=1, source_target_pairs={{0,4},{4,0},{8,12},{12,8},{16,20},{20,16},{24,28},{28,24},{1,5},{5... | collective-permute-start | bytes 1769480 | tf_op jit(solution)/shard_map/ppermute | solution.py:249
  186.1 33.4 %collective-permute-start.50 = (bf16[160,1536]{1,0:T(8,128)(2,1)}, bf16[160,1536]{1,0:T(8,128)(2,1)}, u32[]{:S(2)}, u32[]{:S(2)}) collective-permute-start(bf16[160,1536]{1,0:T(8,128)(2,1)} %get-tuple-element.145), channel_id=1, source_target_pairs={{0,8},{4,12},{8,16},{12,20},{16,24},{20,28},{24,0},{28,4},{1,9},{5... | collective-permute-start | bytes 1474568 | tf_op jit(solution)/shard_map/ppermute | solution.py:244
  205.7 16.2 %collective-permute-start.26 = (bf16[320,1536]{1,0:T(8,128)(2,1)}, bf16[320,1536]{1,0:T(8,128)(2,1)}, u32[]{:S(2)}, u32[]{:S(2)}) collective-permute-start(bf16[320,1536]{1,0:T(8,128)(2,1)} %slice.507), channel_id=1, source_target_pairs={{0,1},{1,0},{2,3},{3,2},{4,5},{5,4},{6,7},{7,6},{8,9},{9,8},{10,11... | collective-permute-start | bytes 2949128 | tf_op jit(solution)/shard_map/ppermute | solution.py:255
  212.7 45.6 %collective-permute-start.38 = (bf16[2,3,96,768]{3,2,1,0:T(8,128)(2,1)S(1)}, bf16[2,3,96,768]{3,2,1,0:T(8,128)(2,1)S(1)}, u32[]{:S(2)}, u32[]{:S(2)}) collective-permute-start(bf16[2,3,96,768]{3,2,1,0:T(8,128)(2,1)S(1)} %pad_maximum_fusion.14), channel_id=1, source_target_pairs={{0,4},{4,0},{8,12},{12,8},{16,20},{20,16},{24,28},{28,24},{1,5},{5... | collective-permute-start | bytes 2654216 | tf_op jit(solution)/shard_map/ppermute | solution.py:249
  214.3 44.6 %collective-permute-start.37 = (bf16[2,3,96,768]{3,2,1,0:T(8,128)(2,1)S(1)}, bf16[2,3,96,768]{3,2,1,0:T(8,128)(2,1)S(1)}, u32[]{:S(2)}, u32[]{:S(2)}) collective-permute-start(bf16[2,3,96,768]{3,2,1,0:T(8,128)(2,1)S(1)} %pad_maximum_fusion.14), channel_id=1, source_target_pairs={{0,2},{2,0},{1,3},{3,1},{4,6},{6,4},{5,7},{7,5},{8,10},{10,8},{9,1... | collective-permute-start | bytes 2654216 | tf_op jit(solution)/shard_map/ppermute | solution.py:252
  217.0 38.8 %collective-permute-start.43 = (bf16[2,3,96,768]{3,2,1,0:T(8,128)(2,1)S(1)}, bf16[2,3,96,768]{3,2,1,0:T(8,128)(2,1)}, u32[]{:S(2)}, u32[]{:S(2)}) collective-permute-start(bf16[2,3,96,768]{3,2,1,0:T(8,128)(2,1)S(1)} %pad_maximum_fusion.15), channel_id=1, source_target_pairs={{0,2},{2,0},{1,3},{3,1},{4,6},{6,4},{5,7},{7,5},{8,10},{10,8},{9,1... | collective-permute-start | bytes 2654216 | tf_op jit(solution)/shard_map/ppermute | solution.py:252
  223.4 42.9 %collective-permute-start.27 = (bf16[160,1536]{1,0:T(8,128)(2,1)S(1)}, bf16[160,1536]{1,0:T(8,128)(2,1)S(1)}, u32[]{:S(2)}, u32[]{:S(2)}) collective-permute-start(bf16[160,1536]{1,0:T(8,128)(2,1)S(1)} %slice.513), channel_id=1, source_target_pairs={{0,2},{2,0},{1,3},{3,1},{4,6},{6,4},{5,7},{7,5},{8,10},{10,8},{9,1... | collective-permute-start | bytes 1474568 | tf_op jit(solution)/shard_map/ppermute | solution.py:252
  234.2 94.8 %collective-permute-start.42 = (bf16[2,3,96,768]{3,2,1,0:T(8,128)(2,1)S(1)}, bf16[2,3,96,768]{3,2,1,0:T(8,128)(2,1)}, u32[]{:S(2)}, u32[]{:S(2)}) collective-permute-start(bf16[2,3,96,768]{3,2,1,0:T(8,128)(2,1)S(1)} %pad_maximum_fusion.15), channel_id=1, source_target_pairs={{0,4},{4,0},{8,12},{12,8},{16,20},{20,16},{24,28},{28,24},{1,5},{5... | collective-permute-start | bytes 2654216 | tf_op jit(solution)/shard_map/ppermute | solution.py:249
  255.8 49.3 %collective-permute-start.52 = (bf16[160,1536]{1,0:T(8,128)(2,1)S(1)}, bf16[160,1536]{1,0:T(8,128)(2,1)S(1)}, u32[]{:S(2)}, u32[]{:S(2)}) collective-permute-start(bf16[160,1536]{1,0:T(8,128)(2,1)S(1)} %collective-permute-done.51), channel_id=1, source_target_pairs={{0,8},{4,12},{8,16},{12,20},{16,24},{20,28},{24,0},{28,4},{1,9},{5... | collective-permute-start | bytes 1474568 | tf_op jit(solution)/shard_map/ppermute | solution.py:244
  258.3 95.8 %collective-permute-start.44 = (bf16[2,3,96,768]{3,2,1,0:T(8,128)(2,1)}, bf16[2,3,96,768]{3,2,1,0:T(8,128)(2,1)}, u32[]{:S(2)}, u32[]{:S(2)}) collective-permute-start(bf16[2,3,96,768]{3,2,1,0:T(8,128)(2,1)} %collective-permute-done.43), channel_id=1, source_target_pairs={{0,4},{4,0},{8,12},{12,8},{16,20},{20,16},{24,28},{28,24},{1,5},{5... | collective-permute-start | bytes 2654216 | tf_op jit(solution)/shard_map/ppermute | solution.py:249
  258.9 48.8 %collective-permute-start.39 = (bf16[2,3,96,768]{3,2,1,0:T(8,128)(2,1)S(1)}, bf16[2,3,96,768]{3,2,1,0:T(8,128)(2,1)}, u32[]{:S(2)}, u32[]{:S(2)}) collective-permute-start(bf16[2,3,96,768]{3,2,1,0:T(8,128)(2,1)S(1)} %collective-permute-done.38), channel_id=1, source_target_pairs={{0,2},{2,0},{1,3},{3,1},{4,6},{6,4},{5,7},{7,5},{8,10},{10,8},{9,1... | collective-permute-start | bytes 2654216 | tf_op jit(solution)/shard_map/ppermute | solution.py:252
  267.2 27.8 %collective-permute-start.28 = (bf16[160,1536]{1,0:T(8,128)(2,1)S(1)}, bf16[160,1536]{1,0:T(8,128)(2,1)S(1)}, u32[]{:S(2)}, u32[]{:S(2)}) collective-permute-start(bf16[160,1536]{1,0:T(8,128)(2,1)S(1)} %multiply_convert_fusion.2), channel_id=1, source_target_pairs={{0,2},{2,0},{1,3},{3,1},{4,6},{6,4},{5,7},{7,5},{8,10},{10,8},{9,1... | collective-permute-start | bytes 1474568 | tf_op jit(solution)/shard_map/ppermute | solution.py:252
  306.4 63.8 %collective-permute-start.53 = (bf16[640,1536]{1,0:T(8,128)(2,1)S(1)}, bf16[640,1536]{1,0:T(8,128)(2,1)S(1)}, u32[]{:S(2)}, u32[]{:S(2)}) collective-permute-start(bf16[640,1536]{1,0:T(8,128)(2,1)S(1)} %pad_maximum_fusion.6), channel_id=1, source_target_pairs={{0,1},{1,0},{2,3},{3,2},{4,5},{5,4},{6,7},{7,6},{8,9},{9,8},{10,11... | collective-permute-start | bytes 5898248 | tf_op jit(solution)/shard_map/ppermute | solution.py:255
  407.7 41.2 %collective-permute-start.87 = (bf16[3,2,2,96,768]{4,3,2,1,0:T(8,128)(2,1)}, bf16[3,2,2,96,768]{4,3,2,1,0:T(8,128)(2,1)S(1)}, u32[]{:S(2)}, u32[]{:S(2)}) collective-permute-start(bf16[3,2,2,96,768]{4,3,2,1,0:T(8,128)(2,1)} %dynamic-slice_bitcast_fusion), channel_id=1, source_target_pairs={{0,2},{2,0},{1,3},{3,1},{4,6},{6,4},{5,7},{7,5},{8,10},{10,8},{9,1... | collective-permute-start | bytes 5308424 | tf_op jit(solution)/shard_map/ppermute | solution.py:252
  409.2 40.9 %collective-permute-start.85 = (bf16[3,2,2,96,768]{4,3,1,0,2:T(8,128)(2,1)}, bf16[3,2,2,96,768]{4,3,1,0,2:T(8,128)(2,1)S(1)}, u32[]{:S(2)}, u32[]{:S(2)}) collective-permute-start(bf16[3,2,2,96,768]{4,3,1,0,2:T(8,128)(2,1)} %bitcast.281), channel_id=1, source_target_pairs={{0,4},{4,0},{8,12},{12,8},{16,20},{20,16},{24,28},{28,24},{1,5},{5... | collective-permute-start | bytes 5308424 | tf_op jit(solution)/shard_map/ppermute | solution.py:249
  422.3 32.8 %collective-permute-start.54 = (bf16[640,1536]{1,0:T(8,128)(2,1)S(1)}, bf16[640,1536]{1,0:T(8,128)(2,1)S(1)}, u32[]{:S(2)}, u32[]{:S(2)}) collective-permute-start(bf16[640,1536]{1,0:T(8,128)(2,1)S(1)} %slice.502), channel_id=1, source_target_pairs={{0,1},{1,0},{2,3},{3,2},{4,5},{5,4},{6,7},{7,6},{8,9},{9,8},{10,11... | collective-permute-start | bytes 5898248 | tf_op jit(solution)/shard_map/ppermute | solution.py:255
  426.3 31.7 %collective-permute-start.45 = (bf16[640,1536]{1,0:T(8,128)(2,1)S(1)}, bf16[640,1536]{1,0:T(8,128)(2,1)S(1)}, u32[]{:S(2)}, u32[]{:S(2)}) collective-permute-start(bf16[640,1536]{1,0:T(8,128)(2,1)S(1)} %slice.503), channel_id=1, source_target_pairs={{0,1},{1,0},{2,3},{3,2},{4,5},{5,4},{6,7},{7,6},{8,9},{9,8},{10,11... | collective-permute-start | bytes 5898248 | tf_op jit(solution)/shard_map/ppermute | solution.py:255
  449.5 78.8 %collective-permute-start.88 = (bf16[3,2,96,768]{3,2,1,0:T(8,128)(2,1)S(1)}, bf16[3,2,96,768]{3,2,1,0:T(8,128)(2,1)}, u32[]{:S(2)}, u32[]{:S(2)}) collective-permute-start(bf16[3,2,96,768]{3,2,1,0:T(8,128)(2,1)S(1)} %fusion.30), channel_id=1, source_target_pairs={{0,4},{4,0},{8,12},{12,8},{16,20},{20,16},{24,28},{28,24},{1,5},{5... | collective-permute-start | bytes 2654216 | tf_op jit(solution)/shard_map/ppermute | solution.py:249
  453.6 86.5 %collective-permute-start.86 = (bf16[3,2,96,768]{3,2,1,0:T(8,128)(2,1)S(1)}, bf16[3,2,96,768]{3,2,1,0:T(8,128)(2,1)}, u32[]{:S(2)}, u32[]{:S(2)}) collective-permute-start(bf16[3,2,96,768]{3,2,1,0:T(8,128)(2,1)S(1)} %fusion.29), channel_id=1, source_target_pairs={{0,2},{2,0},{1,3},{3,1},{4,6},{6,4},{5,7},{7,5},{8,10},{10,8},{9,1... | collective-permute-start | bytes 2654216 | tf_op jit(solution)/shard_map/ppermute | solution.py:252
  457.8 16.0 %collective-permute-start.55 = (bf16[160,1536]{1,0:T(8,128)(2,1)S(1)}, bf16[160,1536]{1,0:T(8,128)(2,1)S(1)}, u32[]{:S(2)}, u32[]{:S(2)}) collective-permute-start(bf16[160,1536]{1,0:T(8,128)(2,1)S(1)} %slice.510), channel_id=1, source_target_pairs={{0,8},{4,12},{8,16},{12,20},{16,24},{20,28},{24,0},{28,4},{1,9},{5... | collective-permute-start | bytes 1474568 | tf_op jit(solution)/shard_map/ppermute | solution.py:244
  458.6 25.8 %collective-permute-start.46 = (bf16[160,1536]{1,0:T(8,128)(2,1)S(1)}, bf16[160,1536]{1,0:T(8,128)(2,1)S(1)}, u32[]{:S(2)}, u32[]{:S(2)}) collective-permute-start(bf16[160,1536]{1,0:T(8,128)(2,1)S(1)} %slice.511), channel_id=1, source_target_pairs={{0,8},{4,12},{8,16},{12,20},{16,24},{20,28},{24,0},{28,4},{1,9},{5... | collective-permute-start | bytes 1474568 | tf_op jit(solution)/shard_map/ppermute | solution.py:244
  474.0 21.0 %collective-permute-start.56 = (bf16[160,1536]{1,0:T(8,128)(2,1)S(1)}, bf16[160,1536]{1,0:T(8,128)(2,1)S(1)}, u32[]{:S(2)}, u32[]{:S(2)}) collective-permute-start(bf16[160,1536]{1,0:T(8,128)(2,1)S(1)} %fusion.24), channel_id=1, source_target_pairs={{0,8},{4,12},{8,16},{12,20},{16,24},{20,28},{24,0},{28,4},{1,9},{5... | collective-permute-start | bytes 1474568 | tf_op jit(solution)/shard_map/ppermute | solution.py:244
  484.5 21.0 %collective-permute-start.47 = (bf16[160,1536]{1,0:T(8,128)(2,1)S(1)}, bf16[160,1536]{1,0:T(8,128)(2,1)S(1)}, u32[]{:S(2)}, u32[]{:S(2)}) collective-permute-start(bf16[160,1536]{1,0:T(8,128)(2,1)S(1)} %fusion.27), channel_id=1, source_target_pairs={{0,8},{4,12},{8,16},{12,20},{16,24},{20,28},{24,0},{28,4},{1,9},{5... | collective-permute-start | bytes 1474568 | tf_op jit(solution)/shard_map/ppermute | solution.py:244
  495.0 21.0 %collective-permute-start.57 = (bf16[160,1536]{1,0:T(8,128)(2,1)S(1)}, bf16[160,1536]{1,0:T(8,128)(2,1)S(1)}, u32[]{:S(2)}, u32[]{:S(2)}) collective-permute-start(bf16[160,1536]{1,0:T(8,128)(2,1)S(1)} %fusion.23), channel_id=1, source_target_pairs={{0,8},{4,12},{8,16},{12,20},{16,24},{20,28},{24,0},{28,4},{1,9},{5... | collective-permute-start | bytes 1474568 | tf_op jit(solution)/shard_map/ppermute | solution.py:244
  505.6 19.1 %collective-permute-start.48 = (bf16[160,1536]{1,0:T(8,128)(2,1)S(1)}, bf16[160,1536]{1,0:T(8,128)(2,1)S(1)}, u32[]{:S(2)}, u32[]{:S(2)}) collective-permute-start(bf16[160,1536]{1,0:T(8,128)(2,1)S(1)} %fusion.26), channel_id=1, source_target_pairs={{0,8},{4,12},{8,16},{12,20},{16,24},{20,28},{24,0},{28,4},{1,9},{5... | collective-permute-start | bytes 1474568 | tf_op jit(solution)/shard_map/ppermute | solution.py:244
  540.0 96.1 %collective-permute-start.59 = (bf16[320,1536]{1,0:T(8,128)(2,1)}, bf16[320,1536]{1,0:T(8,128)(2,1)}, u32[]{:S(2)}, u32[]{:S(2)}) collective-permute-start(bf16[320,1536]{1,0:T(8,128)(2,1)} %pad_maximum_fusion.12), channel_id=1, source_target_pairs={{0,1},{1,0},{2,3},{3,2},{4,5},{5,4},{6,7},{7,6},{8,9},{9,8},{10,11... | collective-permute-start | bytes 2949128 | tf_op jit(solution)/shard_map/ppermute | solution.py:255
  543.2 26.9 %collective-permute-start.89 = (bf16[3,96,768]{2,1,0:T(8,128)(2,1)}, bf16[3,96,768]{2,1,0:T(8,128)(2,1)}, u32[]{:S(2)}, u32[]{:S(2)}) collective-permute-start(bf16[3,96,768]{2,1,0:T(8,128)(2,1)} %get-tuple-element.187), channel_id=1, source_target_pairs={{0,8},{4,12},{8,16},{12,20},{16,24},{20,28},{24,0},{28,4},{1,9},{5... | collective-permute-start | bytes 1327112 | tf_op jit(solution)/shard_map/ppermute | solution.py:244
  543.2 46.8 %collective-permute-start.90 = (bf16[3,96,768]{2,1,0:T(8,128)(2,1)}, bf16[3,96,768]{2,1,0:T(8,128)(2,1)}, u32[]{:S(2)}, u32[]{:S(2)}) collective-permute-start(bf16[3,96,768]{2,1,0:T(8,128)(2,1)} %get-tuple-element.188), channel_id=1, source_target_pairs={{0,16},{4,20},{8,24},{12,28},{16,0},{20,4},{24,8},{28,12},{1,17},{... | collective-permute-start | bytes 1327112 | tf_op jit(solution)/shard_map/ppermute | solution.py:244
  543.3 66.6 %collective-permute-start.91 = (bf16[3,96,768]{2,1,0:T(8,128)(2,1)}, bf16[3,96,768]{2,1,0:T(8,128)(2,1)}, u32[]{:S(2)}, u32[]{:S(2)}) collective-permute-start(bf16[3,96,768]{2,1,0:T(8,128)(2,1)} %get-tuple-element.185), channel_id=1, source_target_pairs={{0,24},{4,28},{8,0},{12,4},{16,8},{20,12},{24,16},{28,20},{1,25},{... | collective-permute-start | bytes 1327112 | tf_op jit(solution)/shard_map/ppermute | solution.py:244
  629.9 22.4 %collective-permute-start.49 = (f32[160,1536]{1,0:T(8,128)}, f32[160,1536]{1,0:T(8,128)}, u32[]{:S(2)}, u32[]{:S(2)}) collective-permute-start(f32[160,1536]{1,0:T(8,128)} %get-tuple-element.200), channel_id=1, source_target_pairs={{0,1},{1,0},{2,3},{3,2},{4,5},{5,4},{6,7},{7,6},{8,9},{9,8},{10,11... | collective-permute-start | bytes 2949128 | tf_op jit(solution)/shard_map/ppermute | solution.py:255
  656.8 26.5 %collective-permute-start.67 = (bf16[130,768]{1,0:T(8,128)(2,1)S(1)}, bf16[130,768]{1,0:T(8,128)(2,1)S(1)}, u32[]{:S(2)}, u32[]{:S(2)}) collective-permute-start(bf16[130,768]{1,0:T(8,128)(2,1)S(1)} %fusion.58), channel_id=1, source_target_pairs={{0,1},{1,0},{2,3},{3,2},{4,5},{5,4},{6,7},{7,6},{8,9},{9,8},{10,11... | collective-permute-start | bytes 599048 | tf_op jit(solution)/shard_map/ppermute | solution.py:255
  723.0 117.2 %collective-permute-start.75 = (bf16[3,1,192,384]{3,2,0,1:T(8,128)(2,1)}, bf16[3,1,192,384]{3,2,0,1:T(8,128)(2,1)}, u32[]{:S(2)}, u32[]{:S(2)}) collective-permute-start(bf16[3,1,192,384]{3,2,0,1:T(8,128)(2,1)} %get-tuple-element.175), channel_id=1, source_target_pairs={{0,4},{4,0},{8,12},{12,8},{16,20},{20,16},{24,28},{28,24},{1,5},{5... | collective-permute-start | bytes 1327112 | tf_op jit(solution)/shard_map/ppermute | solution.py:249
  723.5 86.0 %collective-permute-start.73 = (bf16[3,1,192,384]{3,2,0,1:T(8,128)(2,1)}, bf16[3,1,192,384]{3,2,0,1:T(8,128)(2,1)}, u32[]{:S(2)}, u32[]{:S(2)}) collective-permute-start(bf16[3,1,192,384]{3,2,0,1:T(8,128)(2,1)} %get-tuple-element.176), channel_id=1, source_target_pairs={{0,4},{4,0},{8,12},{12,8},{16,20},{20,16},{24,28},{28,24},{1,5},{5... | collective-permute-start | bytes 1327112 | tf_op jit(solution)/shard_map/ppermute | solution.py:249
  725.0 53.7 %collective-permute-start.71 = (bf16[3,1,192,384]{3,2,0,1:T(8,128)(2,1)S(1)}, bf16[3,1,192,384]{3,2,0,1:T(8,128)(2,1)S(1)}, u32[]{:S(2)}, u32[]{:S(2)}) collective-permute-start(bf16[3,1,192,384]{3,2,0,1:T(8,128)(2,1)S(1)} %get-tuple-element.177), channel_id=1, source_target_pairs={{0,4},{4,0},{8,12},{12,8},{16,20},{20,16},{24,28},{28,24},{1,5},{5... | collective-permute-start | bytes 1327112 | tf_op jit(solution)/shard_map/ppermute | solution.py:249
  729.3 45.9 %collective-permute-start.77 = (bf16[4,1,192,384]{3,2,0,1:T(8,128)(2,1)S(1)}, bf16[4,1,192,384]{3,2,0,1:T(8,128)(2,1)S(1)}, u32[]{:S(2)}, u32[]{:S(2)}) collective-permute-start(bf16[4,1,192,384]{3,2,0,1:T(8,128)(2,1)S(1)} %get-tuple-element.161), channel_id=1, source_target_pairs={{0,4},{4,0},{8,12},{12,8},{16,20},{20,16},{24,28},{28,24},{1,5},{5... | collective-permute-start | bytes 1769480 | tf_op jit(solution)/shard_map/ppermute | solution.py:249
  734.5 43.2 %collective-permute-start.65 = (bf16[160,1536]{1,0:T(8,128)(2,1)S(1)}, bf16[160,1536]{1,0:T(8,128)(2,1)S(1)}, u32[]{:S(2)}, u32[]{:S(2)}) collective-permute-start(bf16[160,1536]{1,0:T(8,128)(2,1)S(1)} %slice.508), channel_id=1, source_target_pairs={{0,2},{2,0},{1,3},{3,1},{4,6},{6,4},{5,7},{7,5},{8,10},{10,8},{9,1... | collective-permute-start | bytes 1474568 | tf_op jit(solution)/shard_map/ppermute | solution.py:252
  775.1 18.8 %collective-permute-start.79 = (bf16[4,1,192,384]{3,2,0,1:T(8,128)(2,1)}, bf16[4,1,192,384]{3,2,0,1:T(8,128)(2,1)}, u32[]{:S(2)}, u32[]{:S(2)}) collective-permute-start(bf16[4,1,192,384]{3,2,0,1:T(8,128)(2,1)} %get-tuple-element.164), channel_id=1, source_target_pairs={{0,4},{4,0},{8,12},{12,8},{16,20},{20,16},{24,28},{28,24},{1,5},{5... | collective-permute-start | bytes 1769480 | tf_op jit(solution)/shard_map/ppermute | solution.py:249
  777.6 14.9 %collective-permute-start.70 = (bf16[3,1,192,384]{3,2,0,1:T(8,128)(2,1)S(1)}, bf16[3,1,192,384]{3,2,0,1:T(8,128)(2,1)S(1)}, u32[]{:S(2)}, u32[]{:S(2)}) collective-permute-start(bf16[3,1,192,384]{3,2,0,1:T(8,128)(2,1)S(1)} %add_convert_fusion.5), channel_id=1, source_target_pairs={{0,8},{4,12},{8,16},{12,20},{16,24},{20,28},{24,0},{28,4},{1,9},{5... | collective-permute-start | bytes 1327112 | tf_op jit(solution)/shard_map/ppermute | solution.py:244
  778.8 26.5 %collective-permute-start.78 = (bf16[4,1,192,384]{3,2,0,1:T(8,128)(2,1)}, bf16[4,1,192,384]{3,2,0,1:T(8,128)(2,1)}, u32[]{:S(2)}, u32[]{:S(2)}) collective-permute-start(bf16[4,1,192,384]{3,2,0,1:T(8,128)(2,1)} %add_convert_fusion.2), channel_id=1, source_target_pairs={{0,8},{4,12},{8,16},{12,20},{16,24},{20,28},{24,0},{28,4},{1,9},{5... | collective-permute-start | bytes 1769480 | tf_op jit(solution)/shard_map/ppermute | solution.py:244
  793.7 21.0 %collective-permute-start.72 = (bf16[3,1,192,384]{3,2,0,1:T(8,128)(2,1)}, bf16[3,1,192,384]{3,2,0,1:T(8,128)(2,1)}, u32[]{:S(2)}, u32[]{:S(2)}) collective-permute-start(bf16[3,1,192,384]{3,2,0,1:T(8,128)(2,1)} %add_convert_fusion.4), channel_id=1, source_target_pairs={{0,8},{4,12},{8,16},{12,20},{16,24},{20,28},{24,0},{28,4},{1,9},{5... | collective-permute-start | bytes 1327112 | tf_op jit(solution)/shard_map/ppermute | solution.py:244
  793.9 66.8 %collective-permute-start.83 = (bf16[4,1,192,384]{3,2,0,1:T(8,128)(2,1)}, bf16[4,1,192,384]{3,2,0,1:T(8,128)(2,1)S(1)}, u32[]{:S(2)}, u32[]{:S(2)}) collective-permute-start(bf16[4,1,192,384]{3,2,0,1:T(8,128)(2,1)} %get-tuple-element.162), channel_id=1, source_target_pairs={{0,4},{4,0},{8,12},{12,8},{16,20},{20,16},{24,28},{28,24},{1,5},{5... | collective-permute-start | bytes 1769480 | tf_op jit(solution)/shard_map/ppermute | solution.py:249
  809.0 29.7 %collective-permute-start.81 = (bf16[4,1,192,384]{3,2,0,1:T(8,128)(2,1)}, bf16[4,1,192,384]{3,2,0,1:T(8,128)(2,1)S(1)}, u32[]{:S(2)}, u32[]{:S(2)}) collective-permute-start(bf16[4,1,192,384]{3,2,0,1:T(8,128)(2,1)} %get-tuple-element.163), channel_id=1, source_target_pairs={{0,4},{4,0},{8,12},{12,8},{16,20},{20,16},{24,28},{28,24},{1,5},{5... | collective-permute-start | bytes 1769480 | tf_op jit(solution)/shard_map/ppermute | solution.py:249
  809.5 29.3 %collective-permute-start.80 = (bf16[4,1,192,384]{3,2,0,1:T(8,128)(2,1)S(1)}, bf16[4,1,192,384]{3,2,0,1:T(8,128)(2,1)S(1)}, u32[]{:S(2)}, u32[]{:S(2)}) collective-permute-start(bf16[4,1,192,384]{3,2,0,1:T(8,128)(2,1)S(1)} %add_convert_fusion.1), channel_id=1, source_target_pairs={{0,8},{4,12},{8,16},{12,20},{16,24},{20,28},{24,0},{28,4},{1,9},{5... | collective-permute-start | bytes 1769480 | tf_op jit(solution)/shard_map/ppermute | solution.py:244
  838.7 24.7 %collective-permute-start.66 = (f32[160,1536]{1,0:T(8,128)S(1)}, f32[160,1536]{1,0:T(8,128)S(1)}, u32[]{:S(2)}, u32[]{:S(2)}) collective-permute-start(f32[160,1536]{1,0:T(8,128)S(1)} %fusion.20), channel_id=1, source_target_pairs={{0,1},{1,0},{2,3},{3,2},{4,5},{5,4},{6,7},{7,6},{8,9},{9,8},{10,11... | collective-permute-start | bytes 2949128 | tf_op jit(solution)/shard_map/ppermute | solution.py:255
  840.1 21.3 %collective-permute-start.82 = (bf16[4,1,192,384]{3,2,0,1:T(8,128)(2,1)S(1)}, bf16[4,1,192,384]{3,2,0,1:T(8,128)(2,1)S(1)}, u32[]{:S(2)}, u32[]{:S(2)}) collective-permute-start(bf16[4,1,192,384]{3,2,0,1:T(8,128)(2,1)S(1)} %add_convert_fusion), channel_id=1, source_target_pairs={{0,8},{4,12},{8,16},{12,20},{16,24},{20,28},{24,0},{28,4},{1,9},{5... | collective-permute-start | bytes 1769480 | tf_op jit(solution)/shard_map/ppermute | solution.py:244
  (126 other events, 1842.4 us)

commit v2 on v1

v2 whole, which is shorter than its diff:
```python
import functools
import math

import jax
import jax.numpy as jnp
from jax import lax
from jax.experimental import pallas as pl
from jax.experimental.pallas import tpu as pltpu
from jax.sharding import PartitionSpec as P

HDIM = 64
EPSILON = 1e-05
F32 = jnp.float32
BF16 = jnp.bfloat16
SCALE = HDIM ** (-0.5)
PAIR = 2 * HDIM
VMEM_LIMIT = 48 * 1024 * 1024


def mm(left, right):
    return lax.dot_general(left, right, (((1,), (0,)), ((), ())), preferred_element_type=F32)


def mm_tn(left, right):
    return lax.dot_general(left, right, (((0,), (0,)), ((), ())), preferred_element_type=F32)


def mm_nt(left, right):
    return lax.dot_general(left, right, (((1,), (1,)), ((), ())), preferred_element_type=F32)


def norm_stats(values):
    center = values - jnp.mean(values, axis=-1, keepdims=True)
    rate = lax.rsqrt(jnp.mean(center * center, axis=-1, keepdims=True) + EPSILON)
    return center * rate, rate


def params():
    return pltpu.CompilerParams(vmem_limit_bytes=VMEM_LIMIT)


def norm_forward_kernel(base_ref, near_ref, far_ref, gain_ref, x_ref, n_ref):
    values = base_ref[...].astype(F32) + near_ref[...] + far_ref[...].astype(F32)
    x_ref[...] = values
    n_ref[...] = (norm_stats(values)[0] * gain_ref[...]).astype(BF16)


def norm_forward(base, near, far, gain):
    rows, width = base.shape
    return pl.pallas_call(
        norm_forward_kernel,
        out_shape=(
            jax.ShapeDtypeStruct((rows, width), F32),
            jax.ShapeDtypeStruct((rows, width), BF16),
        ),
        compiler_params=params(),
    )(base, near, far, gain)


def norm_backward_kernel(
    x_ref, gain_ref, skip_ref, *refs
):
    *terms, dx_ref, low_ref, dg_ref = refs
    rows = x_ref.shape[0]
    upstream = terms[0][:rows, :].astype(F32)
    for term in terms[1:]:
        upstream = upstream + term[:rows, :].astype(F32)
    unit, rate = norm_stats(x_ref[...].astype(F32))
    scaled = upstream * gain_ref[...]
    back = rate * (
        scaled
        - jnp.mean(scaled, axis=-1, keepdims=True)
        - unit * jnp.mean(scaled * unit, axis=-1, keepdims=True)
    )
    total = skip_ref[...].astype(F32) + back
    dx_ref[...] = total
    low_ref[...] = total.astype(BF16)
    dg_ref[...] = jnp.sum(upstream * unit, axis=0, keepdims=True)


def norm_backward(values, gain, skip, *terms):
    rows, width = values.shape
    return pl.pallas_call(
        norm_backward_kernel,
        out_shape=(
            jax.ShapeDtypeStruct((rows, width), F32),
            jax.ShapeDtypeStruct((rows, width), BF16),
            jax.ShapeDtypeStruct((1, width), F32),
        ),
        compiler_params=params(),
    )(values, gain, skip, *terms)


def turned(values, cosine, upper, lower):
    width = values.shape[1]
    return (
        values * cosine
        + pltpu.roll(values, width - HDIM // 4, 1) * upper
        + pltpu.roll(values, HDIM // 4, 1) * lower
    )


def chunk_of(rows):
    return 128 if rows % 128 == 0 else rows


def low_half(shape):
    return lax.broadcasted_iota(jnp.int32, shape, len(shape) - 1) < HDIM


def of_head(values, head):
    first = low_half(values.shape)
    keep = first if head == 0 else jnp.logical_not(first)
    return jnp.where(keep, values, jnp.zeros((), values.dtype))


def forward_heads(q_ref, k_ref, v_ref, o_ref, lse_ref, valid):
    rows = q_ref.shape[0]
    step = chunk_of(rows)
    key, value = k_ref[...], v_ref[...]
    first_half = low_half(value.shape)
    ones = jnp.ones((), BF16)
    extended = jnp.where(first_half, value, ones), jnp.where(first_half, ones, value)
    for first in range(0, rows, step):
        part = slice(first, first + step)
        query = q_ref[part, :]
        results = []
        for head in range(2):
            scores = mm_nt(of_head(query, head), key)
            if valid < key.shape[0]:
                column = lax.broadcasted_iota(jnp.int32, scores.shape, 1)
                scores = jnp.where(column < valid, scores, -1e30)
            peak = jnp.max(scores, axis=-1, keepdims=True)
            mixed = mm(jnp.exp(scores - peak).astype(BF16), extended[head])
            total = pltpu.roll(mixed, HDIM, 1)
            results.append((mixed * (1.0 / total), peak + jnp.log(total)))
        lanes = low_half((step, PAIR))
        o_ref[part, :] = jnp.where(lanes, results[0][0], results[1][0]).astype(BF16)
        lse_ref[part, :] = jnp.where(lanes, results[0][1], results[1][1])


def thirds(ref):
    return ref.at[:, :PAIR], ref.at[:, PAIR : 2 * PAIR], ref.at[:, 2 * PAIR :]


def self_forward_kernel(qkv_ref, cos_ref, up_ref, low_ref, turned_ref, o_ref, lse_ref):
    tables = cos_ref[...], up_ref[...], low_ref[...]
    q_ref, k_ref, v_ref = thirds(turned_ref)
    q_ref[...] = turned(qkv_ref[:, :PAIR], *tables).astype(BF16) * jnp.asarray(SCALE, BF16)
    k_ref[...] = turned(qkv_ref[:, PAIR : 2 * PAIR], *tables).astype(BF16)
    v_ref[...] = qkv_ref[:, 2 * PAIR :].astype(BF16)
    forward_heads(q_ref, k_ref, v_ref, o_ref, lse_ref, k_ref.shape[0])


def cross_forward_kernel(valid, q_ref, k_ref, v_ref, o_ref, lse_ref):
    forward_heads(q_ref, k_ref, v_ref, o_ref, lse_ref, valid)


def backward_heads(q_ref, k_ref, v_ref, o_ref, do_ref, lse_ref, dq_ref, dk_ref, dv_ref, valid):
    rows = q_ref.shape[0]
    step = chunk_of(rows)
    key, value = k_ref[...], v_ref[...]
    for first in range(0, rows, step):
        part = slice(first, first + step)
        query, grad = q_ref[part, :], do_ref[part, :]
        lse = lse_ref[part, :].T
        delta = (grad.astype(F32) * o_ref[part, :].astype(F32)).T
        query_terms = []
        for head in range(2):
            query_head, grad_head = of_head(query, head), of_head(grad, head)
            lanes = slice(head * HDIM, (head + 1) * HDIM)
            mean_grad = jnp.sum(delta[lanes, :], axis=0, keepdims=True)
            probability = jnp.exp(mm_nt(key, query_head) - lse[head * HDIM : head * HDIM + 1, :])
            if valid < key.shape[0]:
                line = lax.broadcasted_iota(jnp.int32, probability.shape, 0)
                probability = jnp.where(line < valid, probability, 0.0)
            score_grad = (probability * (mm_nt(value, grad_head) - mean_grad)).astype(BF16)
            query_terms.append(mm_tn(score_grad, key))
            key_term = mm(score_grad, query_head)
            value_term = mm(probability.astype(BF16), grad_head)
            if first == 0 and head == 0:
                dk_ref[...] = key_term
                dv_ref[...] = value_term
            else:
                dk_ref[...] += key_term
                dv_ref[...] += value_term
        dq_ref[part, :] = jnp.where(low_half((step, PAIR)), *query_terms) * SCALE


def self_backward_kernel(
    turned_ref, o_ref, do_ref, lse_ref, cos_ref, up_ref, low_ref, out_ref, dq_acc, dk_acc, dv_acc
):
    q_ref, k_ref, v_ref = thirds(turned_ref)
    backward_heads(
        q_ref, k_ref, v_ref, o_ref, do_ref, lse_ref, dq_acc, dk_acc, dv_acc, k_ref.shape[0]
    )
    tables = cos_ref[...], -up_ref[...], -low_ref[...]
    dq_ref, dk_ref, dv_ref = thirds(out_ref)
    dq_ref[...] = turned(dq_acc[...], *tables).astype(BF16)
    dk_ref[...] = turned(dk_acc[...], *tables).astype(BF16)
    dv_ref[...] = dv_acc[...].astype(BF16)


def cross_backward_kernel(
    valid, q_ref, k_ref, v_ref, o_ref, do_ref, lse_ref, dq_ref, dk_ref, dv_ref, dq_acc, dk_acc, dv_acc
):
    some = -(-valid // 16) * 16
    backward_heads(
        q_ref, k_ref.at[:some, :], v_ref.at[:some, :], o_ref, do_ref, lse_ref,
        dq_acc, dk_acc.at[:some, :], dv_acc.at[:some, :], valid,
    )
    dq_ref[...] = dq_acc[...].astype(BF16)
    for ref, acc in ((dk_ref, dk_acc), (dv_ref, dv_acc)):
        ref[:some, :] = acc[:some, :].astype(BF16)
        if some < ref.shape[0]:
            ref[some:, :] = jnp.zeros((ref.shape[0] - some, PAIR), BF16)


def attention_call(kernel, pairs, ins, outs, scratch, flops):
    return pl.pallas_call(
        kernel,
        grid=(pairs,),
        in_specs=[
            pl.BlockSpec((rows, width), functools.partial(lambda place, pair: (0, place(pair)), place))
            for rows, width, place in ins
        ],
        out_specs=[pl.BlockSpec((rows, width), lambda pair: (0, pair)) for rows, width, _ in outs],
        out_shape=[
            jax.ShapeDtypeStruct((rows, width * pairs), kind) for rows, width, kind in outs
        ],
        scratch_shapes=[pltpu.VMEM((rows, PAIR), F32) for rows in scratch],
        compiler_params=params(),
        cost_estimate=pl.CostEstimate(
            flops=flops,
            bytes_accessed=4 * pairs * sum(rows * width for rows, width, _ in ins),
            transcendentals=flops // 256,
        ),
    )


def here(pair):
    return pair


def always(pair):
    return 0


def self_forward(qkv, tables):
    rows, pairs = qkv.shape[0], qkv.shape[1] // (3 * PAIR)
    return attention_call(
        self_forward_kernel,
        pairs,
        [(rows, 3 * PAIR, here)] + [(rows, PAIR, always)] * 3,
        [(rows, 3 * PAIR, BF16), (rows, PAIR, BF16), (rows, PAIR, F32)],
        (),
        4 * rows * rows * pairs * PAIR,
    )(qkv, *tables)


def self_backward(qkv, out, grad, lse, tables):
    rows, pairs = qkv.shape[0], qkv.shape[1] // (3 * PAIR)
    return attention_call(
        self_backward_kernel,
        pairs,
        [(rows, 3 * PAIR, here)] + [(rows, PAIR, here)] * 3 + [(rows, PAIR, always)] * 3,
        [(rows, 3 * PAIR, BF16)],
        (rows,) * 3,
        10 * rows * rows * pairs * PAIR,
    )(qkv, out, grad, lse, *tables)[0]


def cross_forward(query, context, valid):
    rows, pairs, keys = query.shape[0], query.shape[1] // PAIR, context.shape[0]
    return attention_call(
        functools.partial(cross_forward_kernel, valid),
        pairs,
        [(rows, PAIR, here), (keys, PAIR, here), (keys, PAIR, lambda pair: pairs + pair)],
        [(rows, PAIR, BF16), (rows, PAIR, F32)],
        (),
        4 * rows * keys * pairs * PAIR,
    )(query, context, context)


def cross_backward(query, context, out, grad, lse, valid):
    rows, pairs, keys = query.shape[0], query.shape[1] // PAIR, context.shape[0]
    return attention_call(
        functools.partial(cross_backward_kernel, valid),
        pairs,
        [(rows, PAIR, here), (keys, PAIR, here), (keys, PAIR, lambda pair: pairs + pair)]
        + [(rows, PAIR, here)] * 3,
        [(rows, PAIR, BF16), (keys, PAIR, BF16), (keys, PAIR, BF16)],
        (rows, keys, keys),
        10 * rows * keys * pairs * PAIR,
    )(query, context, context, out, grad, lse)


def rotary_tables(position):
    quarter = HDIM // 4
    lane = lax.broadcasted_iota(jnp.int32, (position.shape[0], PAIR), 1) & (HDIM - 1)
    turn = (lane & (quarter - 1)).astype(F32)
    frequency = jnp.exp(-(2.0 * turn / (2 * quarter)) * math.log(10000.0))
    angles = position.astype(F32)[:, None] * frequency
    cosine, sine = jnp.cos(angles), jnp.sin(angles)
    return (
        jnp.where(lane < 2 * quarter, cosine, 1.0),
        jnp.where(lane < quarter, -sine, 0.0),
        jnp.where((lane >= quarter) & (lane < 2 * quarter), sine, 0.0),
    )


def place_kernel(plan, n_pieces, place_ref, *refs):
    pieces, outs = refs[:n_pieces], refs[n_pieces:]
    for piece, spot, src_row, rows, src_col, cols, out, dst_col in plan:
        row = pl.multiple_of(place_ref[spot] * rows, rows)
        outs[out][pl.ds(row, rows), dst_col : dst_col + cols] = pieces[piece][
            src_row : src_row + rows, src_col : src_col + cols
        ]


def place_pieces(pieces, plan, place, outs):
    if any(entry[2] % 16 or entry[3] % 16 for entry in plan):
        whole = [jnp.zeros(out, BF16) for out in outs]
        for piece, spot, src_row, rows, src_col, cols, out, dst_col in plan:
            part = pieces[piece][src_row : src_row + rows, src_col : src_col + cols]
            whole[out] = lax.dynamic_update_slice(whole[out], part, (place[spot] * rows, dst_col))
        return whole
    vmem = pl.BlockSpec(memory_space=pltpu.VMEM)
    return pl.pallas_call(
        functools.partial(place_kernel, tuple(plan), len(pieces)),
        in_specs=[pl.BlockSpec(memory_space=pltpu.SMEM)] + [vmem] * len(pieces),
        out_specs=[vmem] * len(outs),
        out_shape=[jax.ShapeDtypeStruct(out, BF16) for out in outs],
        compiler_params=params(),
        cost_estimate=pl.CostEstimate(
            flops=0, transcendentals=0, bytes_accessed=4 * sum(math.prod(out) for out in outs)
        ),
    )(place, *pieces)


def early_kernel(shard, place_ref, *refs):
    *pieces, a_ref, b_ref, c_ref, d_ref, qkv_ref, output_ref, gain_ref, normed_ref = refs
    gains = pieces[0][2 * shard :, :].astype(F32)
    for piece in pieces[1:]:
        gains = gains + piece[2 * shard :, :].astype(F32)
    gain_ref[...] = gains
    first = 0
    for ref in (a_ref, b_ref, c_ref, d_ref):
        unit, _ = norm_stats(ref[...].astype(F32))
        normed_ref[first : first + ref.shape[0], :] = (unit * gains[:1]).astype(BF16)
        first += ref.shape[0]
    cols = qkv_ref.shape[1]
    for n, piece in enumerate(pieces):
        for there in (0, 1):
            row = pl.ds(pl.multiple_of(place_ref[2 * n + there] * shard, shard), shard)
            lines = slice(there * shard, (there + 1) * shard)
            qkv_ref[row, :] = piece[lines, :cols]
            output_ref[row, :] = piece[lines, cols:]


def early_full(pieces, place, tokens, shard):
    width, cols = tokens[0].shape[1], pieces[0].shape[1] // 4
    rows = sum(part.shape[0] for part in tokens)
    vmem = pl.BlockSpec(memory_space=pltpu.VMEM)
    return pl.pallas_call(
        functools.partial(early_kernel, shard),
        in_specs=[pl.BlockSpec(memory_space=pltpu.SMEM)] + [vmem] * (len(pieces) + 4),
        out_specs=[vmem] * 4,
        out_shape=[
            jax.ShapeDtypeStruct((width, 3 * cols), BF16),
            jax.ShapeDtypeStruct((width, cols), BF16),
            jax.ShapeDtypeStruct((pieces[0].shape[0] - 2 * shard, width), F32),
            jax.ShapeDtypeStruct((rows, width), BF16),
        ],
        compiler_params=params(),
    )(place, *pieces, *tokens)


def spread_kernel(place_ref, *refs):
    pieces, (down_out, gate_out, up_out) = refs[:RING], refs[RING:]
    cols = pieces[0].shape[1] // 3
    for n, piece in enumerate(pieces):
        spot = pl.ds(pl.multiple_of(place_ref[n] * cols, cols), cols)
        for m, out in enumerate((down_out, gate_out, up_out)):
            out[:, spot] = piece[:, m * cols : (m + 1) * cols].astype(F32)


def spread(pieces, place):
    rows, cols = pieces[0].shape
    vmem = pl.BlockSpec(memory_space=pltpu.VMEM)
    down, gate, up = pl.pallas_call(
        spread_kernel,
        in_specs=[pl.BlockSpec(memory_space=pltpu.SMEM)] + [vmem] * RING,
        out_specs=[vmem] * 3,
        out_shape=[jax.ShapeDtypeStruct((rows, cols // 3 * RING), F32)] * 3,
        compiler_params=params(),
    )(place, *pieces)
    return gate, up, down


def pack_early_kernel(half_ref, q_ref, k_ref, v_ref, o_ref, send_ref, keep_ref):
    cols = o_ref.shape[1] // 2
    for out, index in ((send_ref, 1 - half_ref[0]), (keep_ref, half_ref[0])):
        first = pl.multiple_of(index * cols, PAIR)
        for pair in range(cols // PAIR):
            for n, ref in enumerate((q_ref, k_ref, v_ref)):
                spot = (3 * pair + n) * PAIR
                out[:, spot : spot + PAIR] = ref[:, pl.ds(first + pair * PAIR, PAIR)]
        out[:, 3 * cols :] = o_ref[:, pl.ds(first, cols)]


def pack_early(query, key, value, output, half, cols):
    rows = query.shape[0]
    vmem = pl.BlockSpec(memory_space=pltpu.VMEM)
    return pl.pallas_call(
        pack_early_kernel,
        in_specs=[pl.BlockSpec(memory_space=pltpu.SMEM)] + [vmem] * 4,
        out_specs=[vmem] * 2,
        out_shape=[jax.ShapeDtypeStruct((rows, 4 * cols), BF16)] * 2,
        compiler_params=params(),
    )(half.reshape(1), query, key, value, output)


RING = 4


class Links:
    def __init__(self, mesh):
        self.fsdp = mesh.shape["fsdp"]
        self.width = self.fsdp // RING
        index = lax.axis_index("fsdp")
        self.at = lax.div(index, self.width)
        self.lane = index - self.at * self.width
        self.half = lax.axis_index("ctx")
        self.core = lax.axis_index("tp")
        self.step = jnp.zeros((8, 128), F32)

    def sync(self, *values):
        flat, tree = jax.tree.flatten(values)
        self.step, *flat = lax.optimization_barrier([self.step, *flat])
        return jax.tree.unflatten(tree, flat)

    def begun(self, value):
        return lax.optimization_barrier([value, self.step])[0]

    def ring(self, value, hops):
        z, r = RING, self.width
        pairs = [(a * r + b, (a + hops) % z * r + b) for a in range(z) for b in range(r)]
        return lax.ppermute(self.begun(value), "fsdp", pairs)

    def lanes(self, value):
        z, r = RING, self.width
        pairs = [(a * r + b, a * r + (b + 1) % r) for a in range(z) for b in range(r)]
        return lax.ppermute(self.begun(value), "fsdp", pairs)

    def over_half(self, value):
        return lax.ppermute(self.begun(value), "ctx", [(0, 1), (1, 0)])

    def over_core(self, value):
        return lax.ppermute(self.begun(value), "tp", [(0, 1), (1, 0)])

    def ring_at(self, back):
        return (self.at + (RING - back)) & (RING - 1)

    def lane_at(self, turn):
        return lax.rem(self.lane + (self.width - turn), self.width) if turn else self.lane

    def place(self, back, turn):
        return self.ring_at(back) * self.width + self.lane_at(turn)

    def block_places(self):
        n = lax.iota(jnp.int32, RING * self.width * 2)
        back = lax.div(n, 2 * self.width)
        turn = lax.rem(lax.div(n, 2), self.width)
        ring = (self.at + RING - back) & (RING - 1)
        lane = lax.rem(self.lane + self.width - turn, self.width)
        return (ring * self.width + lane) * 2 + (self.half ^ (n & 1))

    def all_lanes(self, value):
        values = [value]
        while len(values) < self.width:
            values.append(self.lanes(values[-1]))
        return values

    def sum_lanes(self, terms):
        total, *rest = terms
        for term in rest:
            total = (self.lanes(total).astype(F32) + term.astype(F32)).astype(BF16)
        return self.lanes(total)

    def both_cores(self, own):
        other = self.over_core(own)
        first = jnp.where(self.core == 0, own, other)
        second = jnp.where(self.core == 0, other, own)
        return jnp.concatenate([first, second], axis=0)

    def swap_halves(self, total):
        keep = lax.dynamic_index_in_dim(total, self.half, 0, keepdims=False)
        send = lax.dynamic_index_in_dim(total, 1 - self.half, 0, keepdims=False)
        return keep, self.over_half(send.astype(BF16)).astype(F32)

    def side_by_side(self, keep, recv):
        return jnp.concatenate(
            [jnp.where(self.half == 0, keep, recv), jnp.where(self.half == 0, recv, keep)], axis=-1
        )


def slot(values, count, index):
    size = values.shape[1] // count
    return lax.dynamic_slice_in_dim(values, index * size, size, 1)


def in_order(values, index):
    count = len(values)
    ahead = jnp.concatenate(values[::-1], axis=1)
    size = ahead.shape[1]
    first = lax.rem(2 * count - 1 - index, count)
    twice = jnp.concatenate([ahead, ahead], axis=1)
    return lax.dynamic_slice_in_dim(twice, first * (size // count), size, 1)


def on_device(
    mesh,
    inputs,
    conditioning,
    query_matrix,
    key_matrix,
    value_matrix,
    output_matrix,
    cross_query,
    cross_key,
    cross_value,
    cross_output,
    gate_matrix,
    up_matrix,
    down_matrix,
    first_gain,
    second_gain,
    third_gain,
    cotangent,
):
    links = Links(mesh)
    ring, lanes, all_lanes = links.ring, links.lanes, links.all_lanes
    over_half, over_core = links.over_half, links.over_core
    sync = links.sync
    core, half, lane_count = links.core, links.half, links.width
    rows = inputs.shape[1]
    own_rows = rows // 2
    width = inputs.shape[2]
    shard = query_matrix.shape[0]
    cols = query_matrix.shape[1] // 2
    pairs = cols // PAIR
    context_shard = cross_key.shape[0]
    context_width = conditioning.shape[2]
    context_count = conditioning.shape[1]
    hidden = gate_matrix.shape[1] // RING
    blocks = links.fsdp * 2
    places = links.block_places()

    def half_cols(values, index):
        return lax.dynamic_slice_in_dim(values, index * cols, cols, 1)

    def early_part(index):
        parts = [half_cols(w, index) for w in (query_matrix, key_matrix, value_matrix)]
        return jnp.concatenate(
            [p[:, n * PAIR : (n + 1) * PAIR] for n in range(pairs) for p in parts]
            + [half_cols(output_matrix.T, index)],
            axis=1,
        )

    def late_part(index):
        return jnp.concatenate(
            [
                half_cols(w, index)
                for w in (cross_query, cross_output.T, cross_key, cross_value)
            ],
            axis=0,
        )

    def feed_part(index):
        return jnp.concatenate(
            [
                lax.dynamic_slice_in_dim(w, index * hidden, hidden, 1)
                for w in (gate_matrix, up_matrix, down_matrix.T)
            ],
            axis=1,
        )

    def halves_of(left, weights):
        pair = 2 * own_rows
        return mm_nt(left[:pair], weights), mm_nt(left[pair:], weights).astype(BF16)

    def with_core(mine, recv):
        total = mine + recv.astype(F32)
        return total[:own_rows], total[own_rows:].astype(BF16)

    def spread_cores(own, over):
        pair = jnp.concatenate([own, over], axis=0)
        return jnp.concatenate([pair, over_core(pair)], axis=0)

    own = lax.dynamic_slice_in_dim(inputs[0], core * own_rows, own_rows, 0)
    other = lax.dynamic_slice_in_dim(inputs[0], (1 - core) * own_rows, own_rows, 0)
    upstream = lax.dynamic_slice_in_dim(cotangent[0], core * own_rows, own_rows, 0)
    row = lax.iota(jnp.int32, own_rows)
    position = jnp.concatenate(
        [
            row + (half ^ there) * rows + (core ^ beside) * own_rows
            for beside in (0, 1)
            for there in (0, 1)
        ]
    )
    mark = lax.broadcasted_iota(jnp.int32, (16, width), 1)
    place = (lax.axis_index("fsdp") * 2 + half) * shard
    gains = jnp.pad(jnp.stack([first_gain, second_gain, third_gain]), ((0, 13), (0, 0)))
    gains = jnp.where(
        (mark >= place) & (mark < place + shard), jnp.tile(gains, (1, blocks)), jnp.zeros((), BF16)
    )
    early_send, early_keep = pack_early(
        query_matrix, key_matrix, value_matrix, output_matrix.T, half, cols
    )

    early_recv, gains_over = over_half(early_send), over_half(gains)
    early_keep, early_recv, gains_over = sync(early_keep, early_recv, gains_over)

    early0 = jnp.concatenate([early_keep, early_recv, gains + gains_over], axis=0)
    early1, lanes0, own_over = ring(early0, 1), all_lanes(early0), over_half(own)
    early1, lanes0, own_over, late_send, late_keep = sync(
        early1, lanes0, own_over, late_part(1 - half), late_part(half)
    )

    early3, lanes1, late_recv = ring(lanes0[0], -1), all_lanes(early1), over_half(late_send)
    other_over = over_core(own_over)
    early3, lanes1, late_recv, other_over, tables, feed0, feed_send = sync(
        early3,
        lanes1,
        late_recv,
        other_over,
        rotary_tables(position),
        feed_part(links.at),
        feed_part(links.ring_at(RING - 1)),
    )

    early2, lanes3, feed0_over = ring(lanes1[0], 1), all_lanes(early3), over_half(feed0)
    late0 = jnp.concatenate([late_keep, late_recv], axis=0)
    early2, lanes3, feed0_over, late0 = sync(early2, lanes3, feed0_over, late0)

    feed1, lanes2 = ring(feed_send, 1), all_lanes(early2)
    context = jnp.pad(conditioning[0], ((0, -context_count % 128), (0, 0)))
    feed1, lanes2, context, feed_send = sync(
        feed1, lanes2, context, feed_part(links.ring_at(1))
    )

    late1, late_lanes0, feed1_over = ring(late0, 1), all_lanes(late0), over_half(feed1)
    qkv_full, output_full, gains, normed_one = early_full(
        lanes0 + lanes1 + lanes2 + lanes3, places, (own, own_over, other, other_over), shard
    )
    first_norm_gain, second_norm_gain, third_norm_gain = gains[0:1], gains[1:2], gains[2:3]
    qkv = mm(normed_one, qkv_full)
    qkv, late1, late_lanes0, feed1_over = sync(qkv, late1, late_lanes0, feed1_over)

    late3, late2 = ring(late0, -1), ring(late1, 1)
    late_lanes1, feed0_lanes = all_lanes(late1), all_lanes(feed0)
    qkv_low, self_low, self_logsum = self_forward(qkv, tables)
    partial, send = halves_of(self_low, output_full)
    partial, send, late3, late2, late_lanes1, feed0_lanes = sync(
        partial, send, late3, late2, late_lanes1, feed0_lanes
    )

    terms = with_core(partial, over_core(send))
    far_term, feed3, late_lanes3 = over_half(terms[1]), ring(feed_send, -1), all_lanes(late3)
    far_term, feed3, late_lanes3, feed_send = sync(
        far_term, feed3, late_lanes3, feed_part(links.ring_at(2))
    )

    hidden_one, normed = norm_forward(own, terms[0], far_term, second_norm_gain)
    normed_over, cotangent1, late_lanes2 = over_half(normed), ring(upstream, 1), all_lanes(late2)
    normed_over, cotangent1, late_lanes2 = sync(normed_over, cotangent1, late_lanes2)

    feed2, feed0_over_lanes, feed3_over = (
        ring(feed_send, 2),
        all_lanes(feed0_over),
        over_half(feed3),
    )
    plan = []
    for n in range(blocks):
        first = (n % 2) * 2 * (shard + context_shard)
        for out in range(2):
            plan.append((n // 2, n, first + out * shard, shard, 0, cols, out, 0))
        for out in range(2):
            start = first + 2 * shard + out * context_shard
            plan.append((n // 2, n, start, context_shard, 0, cols, 2, out * cols))
    cross_query_full, cross_output_full, context_full = place_pieces(
        late_lanes0 + late_lanes1 + late_lanes2 + late_lanes3,
        plan,
        places,
        [(width, cols)] * 2 + [(context_width, 2 * cols)],
    )
    context_low = mm(context, context_full).astype(BF16)
    normed_two = spread_cores(normed, normed_over)
    cross_query_low = mm(normed_two, cross_query_full).astype(BF16) * jnp.asarray(SCALE, BF16)
    cross_low, cross_logsum = cross_forward(cross_query_low, context_low, context_count)
    partial, send = halves_of(cross_low, cross_output_full)
    partial, send, feed2, feed0_over_lanes, feed3_over = sync(
        partial, send, feed2, feed0_over_lanes, feed3_over
    )

    terms = with_core(partial, over_core(send))
    far_term, cotangent3, feed1_lanes = over_half(terms[1]), ring(upstream, -1), all_lanes(feed1)
    far_term, cotangent3, feed1_lanes = sync(far_term, cotangent3, feed1_lanes)

    hidden_two, normed0 = norm_forward(hidden_one, terms[0], far_term, third_norm_gain)
    normed1, feed3_lanes, feed2_over = ring(normed0, 1), all_lanes(feed3), over_half(feed2)
    normed1, feed3_lanes, feed2_over = sync(normed1, feed3_lanes, feed2_over)

    normed2, feed2_lanes = ring(normed1, 1), all_lanes(feed2)
    feed3_lanes_over = [feed3_over] + [over_half(value) for value in feed3_lanes[1:]]
    normed2, feed2_lanes, feed3_lanes_over = sync(normed2, feed2_lanes, feed3_lanes_over)

    normed3, feed1_over_lanes = ring(normed2, 1), all_lanes(feed1_over)
    feed2_lanes_over = [feed2_over] + [over_half(value) for value in feed2_lanes[1:]]
    normed3, feed1_over_lanes, feed2_lanes_over = sync(normed3, feed1_over_lanes, feed2_lanes_over)

    normed_mine = jnp.concatenate([normed0, normed1, normed2, normed3], axis=0)
    normed_three = jnp.concatenate([normed_mine, over_core(normed_mine)], axis=0)
    cotangent2 = ring(cotangent1, 1)
    plan = []
    pieces = []
    for back, groups in (
        (0, (feed0_lanes, feed0_over_lanes)),
        (1, (feed1_lanes, feed1_over_lanes)),
        (2, (feed2_lanes, feed2_lanes_over)),
        (3, (feed3_lanes, feed3_lanes_over)),
    ):
        for there, group in enumerate(groups):
            for turn, piece in enumerate(group):
                spot = (back * lane_count + turn) * 2 + there
                for out in range(3):
                    plan.append((len(pieces), spot, 0, shard, out * hidden, hidden, out, 0))
                pieces.append(piece)
    gate_full, up_full, down_full = place_pieces(pieces, plan, places, [(width, hidden)] * 3)
    gate_value = mm(normed_three, gate_full)
    up_value = mm(normed_three, up_full)
    sigmoid_gate = jax.nn.sigmoid(gate_value)
    silu_gate = gate_value * sigmoid_gate
    feed_low = (silu_gate * up_value).astype(BF16)
    gate_value, up_value, feed_low, cotangent2 = sync(gate_value, up_value, feed_low, cotangent2)

    def ring_halves(left, weights):
        count = RING * own_rows
        return mm_nt(left[:count], weights), mm_nt(left[count:], weights).astype(BF16)

    def block_of(mine, recv, back):
        part = slice(back * own_rows, (back + 1) * own_rows)
        return mine[part] + recv[part].astype(F32)

    def lanes_block(grads, turn):
        place = links.lane_at(turn)
        return jnp.concatenate(
            [
                lax.dynamic_slice_in_dim(grads, (z * lane_count + place) * 2 * shard, 2 * shard, 0)
                for z in (0, 1)
            ],
            axis=0,
        )

    def halves_block(grads, index):
        return jnp.concatenate(
            [
                lax.dynamic_slice_in_dim(
                    grads, ((z * lane_count + n) * 2 + index) * shard, shard, 0
                )
                for z in (2, 3)
                for n in range(lane_count)
            ],
            axis=0,
        )

    def lanes_terms(grads):
        return [lanes_block(grads, turn) for turn in range(1, lane_count)]

    def lanes_second(grads, recv):
        total = (lanes_block(grads, 0).astype(F32) + recv.astype(F32)).reshape(2, 2, shard, hidden)
        keep = lax.dynamic_index_in_dim(total, half, 1, keepdims=False)
        send = lax.dynamic_index_in_dim(total, 1 - half, 1, keepdims=False)
        return keep, send.astype(BF16)

    def halves_second(grads, recv):
        total = (halves_block(grads, half).astype(F32) + recv.astype(F32)).reshape(
            2, lane_count, shard, hidden
        )
        keep, *send = [
            lax.dynamic_index_in_dim(total, links.lane_at(turn), 1, keepdims=False)
            for turn in range(lane_count)
        ]
        return keep, [term.astype(BF16) for term in send]

    def joined(*terms):
        keep, recv, keep_late, recv_late = terms
        return jnp.concatenate(
            [
                (keep + recv.astype(F32)).astype(BF16),
                (keep_late + recv_late.astype(F32)).astype(BF16),
            ],
            axis=0,
        )

    mine = jnp.concatenate([upstream, cotangent1, cotangent2, cotangent3], axis=0)
    upstream_all = jnp.concatenate([mine, over_core(mine)], axis=0)
    out_mine, out_send = ring_halves(feed_low, down_full)
    upstream_all, out_mine, out_send = sync(upstream_all, out_mine, out_send)

    out_recv = over_core(out_send)
    down_grad = mm_tn(upstream_all, feed_low).astype(BF16)
    down_grad, out_recv, down_lanes, down_halves = sync(
        down_grad, out_recv, lanes_terms(down_grad), halves_block(down_grad, 1 - half)
    )

    out_two = ring(block_of(out_mine, out_recv, 2).astype(BF16), -1)
    down_lanes, down_halves = links.sum_lanes(down_lanes), over_half(down_halves)
    feed_grad = mm(upstream_all, down_full).astype(BF16).astype(F32)
    gate_low = (
        feed_grad * up_value * sigmoid_gate * (1.0 + gate_value * (1.0 - sigmoid_gate))
    ).astype(BF16)
    up_low = (feed_grad * silu_gate).astype(BF16)
    gate_low, up_low, out_two, down_lanes, down_halves = sync(
        gate_low, up_low, out_two, down_lanes, down_halves
    )

    count = RING * own_rows
    send = (mm_nt(gate_low[count:], gate_full) + mm_nt(up_low[count:], up_full)).astype(BF16)
    (send,) = sync(send)
    recv = over_core(send)
    mine = mm_nt(gate_low[:count], gate_full) + mm_nt(up_low[:count], up_full)
    recv, mine = sync(recv, mine)

    two = ring(block_of(mine, recv, 2).astype(BF16), -1)
    gate_grad = mm_tn(normed_three, gate_low).astype(BF16)
    up_grad = mm_tn(normed_three, up_low).astype(BF16)
    two, gate_grad, up_grad, gate_lanes, up_halves = sync(
        two, gate_grad, up_grad, lanes_terms(gate_grad), halves_block(up_grad, 1 - half)
    )

    one = ring((block_of(mine, recv, 1) + two.astype(F32)).astype(BF16), -1)
    gate_lanes, up_halves = links.sum_lanes(gate_lanes), over_half(up_halves)
    lanes_keep, lanes_move = lanes_second(down_grad, down_lanes)
    halves_keep, halves_move = halves_second(down_grad, down_halves)
    three_send = block_of(mine, recv, 3).astype(BF16)
    one, gate_lanes, up_halves, gate_halves, up_lanes, lanes_move, halves_move, three_send = sync(
        one,
        gate_lanes,
        up_halves,
        halves_block(gate_grad, 1 - half),
        lanes_terms(up_grad),
        lanes_move,
        halves_move,
        three_send,
    )

    three = ring(three_send, 1)
    up_lanes, gate_halves = links.sum_lanes(up_lanes), over_half(gate_halves)
    gate_keep, gate_move = lanes_second(gate_grad, gate_lanes)
    up_late_keep, up_late_move = halves_second(up_grad, up_halves)
    three, up_lanes, gate_halves, gate_keep, gate_move, up_late_keep, up_late_move = sync(
        three, up_lanes, gate_halves, gate_keep, gate_move, up_late_keep, up_late_move
    )

    hidden_two_grad, low, third_gain_grad = norm_backward(
        hidden_two, third_norm_gain, upstream, mine, recv, one, three
    )
    low_over = over_half(low)
    out_one = ring((block_of(out_mine, out_recv, 1) + out_two.astype(F32)).astype(BF16), -1)
    up_late_move, halves_move = links.sum_lanes(up_late_move), links.sum_lanes(halves_move)
    out_send = block_of(out_mine, out_recv, 3).astype(BF16)
    low_over, out_one, up_late_move, halves_move, out_send = sync(
        low_over, out_one, up_late_move, halves_move, out_send
    )

    lanes_move, gate_move, out_three = over_half(lanes_move), over_half(gate_move), ring(out_send, 1)
    branch_two = spread_cores(low, low_over)
    cross_out_grad = mm(branch_two, cross_output_full).astype(BF16)
    cross_query_round, cross_key_back, cross_value_back = cross_backward(
        cross_query_low, context_low, cross_low, cross_out_grad, cross_logsum, context_count
    )
    partial, send = halves_of(cross_query_round, cross_query_full)
    partial, send, lanes_move, gate_move, out_three, branch_two = sync(
        partial, send, lanes_move, gate_move, out_three, branch_two
    )
    (recv,) = sync(over_core(send))

    def part_of(grads, place):
        count = grads.shape[0] // links.fsdp
        return lax.dynamic_slice_in_dim(grads, place * count, count, 0)

    def lanes_total(block, back, recv):
        return block(links.place(back, 0)).astype(F32) + recv.astype(F32)

    def lanes_send(block, back):
        return links.sum_lanes(lambda turn: block(links.place(back, turn)))

    def cross_block(place):
        return jnp.concatenate([part_of(g, place) for g in cross_grads], axis=0)

    def lanes_blocks(block, back):
        return [block(links.place(back, turn)) for turn in range(1, lane_count)]

    def out_of(values, back):
        return lax.dynamic_index_in_dim(values, links.ring_at(back), 0, keepdims=False)

    terms = with_core(partial, recv)
    far_term = over_half(terms[1])
    up_keep, up_move = lanes_second(up_grad, up_lanes)
    gate_late_keep, gate_late_move = halves_second(gate_grad, gate_halves)
    cross_grads = [
        mm_tn(branch_two, cross_low).astype(BF16),
        mm_tn(normed_two, cross_query_round).astype(BF16),
        mm_tn(context, cross_key_back).astype(BF16),
        mm_tn(context, cross_value_back).astype(BF16),
    ]
    far_term, cross_grads, up_move, gate_late_move, cross2 = sync(
        far_term, cross_grads, up_move, gate_late_move, lanes_blocks(cross_block, 2)
    )

    hidden_one_grad, low, second_gain_grad = norm_backward(
        hidden_one, second_norm_gain, hidden_two_grad, terms[0], far_term
    )
    low_over = over_half(low)
    up_move, gate_late_move = over_half(up_move), links.sum_lanes(gate_late_move)
    cross2 = links.sum_lanes(cross2)
    low_over, cross2, up_move, gate_late_move, cross3, cross1 = sync(
        low_over,
        cross2,
        up_move,
        gate_late_move,
        lanes_blocks(cross_block, 3),
        lanes_blocks(cross_block, 1),
    )

    feed_mine = jnp.concatenate(
        [
            joined(lanes_keep, lanes_move, halves_keep, halves_move),
            joined(gate_keep, gate_move, gate_late_keep, gate_late_move),
            joined(up_keep, up_move, up_late_keep, up_late_move),
        ],
        axis=2,
    )
    feed1_sum, feed3_sum = ring(out_of(feed_mine, 3), 1), ring(out_of(feed_mine, 1), -1)
    cross3, cross1 = links.sum_lanes(cross3), links.sum_lanes(cross1)
    branch_one = spread_cores(low, low_over)
    self_out_grad = mm(branch_one, output_full).astype(BF16)
    qkv_round = self_backward(qkv_low, self_low, self_out_grad, self_logsum, tables)
    partial, send = halves_of(qkv_round, qkv_full)
    feed_mine, branch_one, qkv_round, partial, send, feed1_sum, feed3_sum, cross3, cross1 = sync(
        feed_mine, branch_one, qkv_round, partial, send, feed1_sum, feed3_sum, cross3, cross1
    )
    (recv,) = sync(over_core(send))

    def self_block(place):
        return jnp.concatenate([part_of(output_grad, place), part_of(qkv_grad, place)], axis=1)

    terms = with_core(partial, recv)
    far_term = over_half(terms[1])
    cross_two = ring(lanes_total(cross_block, 2, cross2).astype(BF16), -1)
    cross0 = links.sum_lanes(lanes_blocks(cross_block, 0))
    output_grad = mm_tn(branch_one, self_low).astype(BF16)
    qkv_grad = mm_tn(normed_one, qkv_round).astype(BF16)
    context_term = (
        mm_nt(cross_key_back, context_full[:, :cols])
        + mm_nt(cross_value_back, context_full[:, cols:])
    )[:context_count]
    far_term, cross0, cross_two, output_grad, qkv_grad, self2, context_send = sync(
        far_term,
        cross0,
        cross_two,
        output_grad,
        qkv_grad,
        lanes_blocks(self_block, 2),
        context_term.astype(BF16),
    )

    self2 = links.sum_lanes(self2)
    feed2_sum = ring(out_of(feed_mine, 2), 2)
    context_recv = over_core(context_send)
    inputs_grad, _, first_gain_grad = norm_backward(
        own, first_norm_gain, hidden_one_grad, terms[0], far_term
    )
    context_low_sum = (context_term + context_recv.astype(F32)).astype(BF16)
    gain_grads = jnp.concatenate([first_gain_grad, second_gain_grad, third_gain_grad], axis=0)
    self2, feed2_sum, context_low_sum, gain_grads, inputs_grad, self3 = sync(
        self2, feed2_sum, context_low_sum, gain_grads, inputs_grad, lanes_blocks(self_block, 3)
    )

    self3 = links.sum_lanes(self3)
    self_two = ring(lanes_total(self_block, 2, self2).astype(BF16), -1)
    context_over = over_half(context_low_sum)
    gain_grads = gain_grads + over_core(gain_grads)
    gate_sum, up_sum, down_sum = spread(
        [out_of(feed_mine, 0), feed1_sum, feed2_sum, feed3_sum],
        jnp.stack([links.ring_at(back) for back in range(RING)]),
    )
    layer_result = links.both_cores(
        hidden_two + block_of(out_mine, out_recv, 0) + out_one.astype(F32) + out_three.astype(F32)
    )
    self3, self_two, context_over, gain_grads, layer_result, self1, cross_sends = sync(
        self3,
        self_two,
        context_over,
        gain_grads,
        layer_result,
        lanes_blocks(self_block, 1),
        [
            lanes_total(cross_block, 3, cross3).astype(BF16),
            (lanes_total(cross_block, 1, cross1) + cross_two.astype(F32)).astype(BF16),
        ],
    )

    self1 = links.sum_lanes(self1)
    cross_three, cross_one = ring(cross_sends[0], 1), ring(cross_sends[1], -1)
    context_grad = context_low_sum.astype(F32) + context_over.astype(F32)
    inputs_result = links.both_cores(inputs_grad)
    gain_over = over_half(gain_grads)
    self1, cross_three, cross_one, gain_over, inputs_result, self0 = sync(
        self1, cross_three, cross_one, gain_over, inputs_result, lanes_blocks(self_block, 0)
    )

    self0 = links.sum_lanes(self0)
    self_one = ring((lanes_total(self_block, 1, self1) + self_two.astype(F32)).astype(BF16), -1)
    self_three = ring(lanes_total(self_block, 3, self3).astype(BF16), 1)
    cross_total = (
        lanes_total(cross_block, 0, cross0) + cross_one.astype(F32) + cross_three.astype(F32)
    )
    sizes = (shard, shard, context_shard, context_shard)
    starts = [2 * sum(sizes[:n]) for n in range(4)]
    cross_total = jnp.concatenate(
        [
            cross_total[start : start + 2 * size].reshape(2, size, cols)
            for start, size in zip(starts, sizes)
        ],
        axis=1,
    )
    cross_keep, cross_recv = links.swap_halves(cross_total)
    gain_grads = gain_grads + gain_over
    gain_ring = [slot(gain_grads, RING, links.ring_at(back)) for back in range(RING)]
    gain_two, gain_three = ring(gain_ring[2], -1), ring(gain_ring[3], 1)
    self0, self_one, self_three, cross_recv, gain_two, gain_three = sync(
        self0, self_one, self_three, cross_recv, gain_two, gain_three
    )

    gain_one = ring(gain_ring[1] + gain_two, -1)
    cross_sums = links.side_by_side(cross_keep, cross_recv)
    self_total = (
        lanes_total(self_block, 0, self0) + self_one.astype(F32) + self_three.astype(F32)
    )
    keep, recv = links.swap_halves(self_total.reshape(2, shard, 4 * cols))
    gain_grads = gain_ring[0] + gain_one + gain_three
    gain_total = slot(gain_grads, lane_count, links.lane_at(1))
    for turn in list(range(2, lane_count)) + [0]:
        gain_total = links.lanes(gain_total) + slot(gain_grads, lane_count, links.lane_at(turn))
    gain_sums = slot(gain_total, 2, half)

    def of_self(values, n):
        if n == 3:
            return values[:, :cols]
        return jnp.concatenate(
            [
                values[:, cols + (3 * pair + n) * PAIR : cols + (3 * pair + n + 1) * PAIR]
                for pair in range(pairs)
            ],
            axis=1,
        )

    query_sum, key_sum, value_sum, output_sum = (
        links.side_by_side(of_self(keep, n), of_self(recv, n)) for n in range(4)
    )
    return (
        layer_result[None],
        inputs_result[None],
        context_grad[None],
        query_sum,
        key_sum,
        value_sum,
        output_sum.T,
        cross_sums[shard : 2 * shard],
        cross_sums[2 * shard : 2 * shard + context_shard],
        cross_sums[2 * shard + context_shard :],
        cross_sums[:shard].T,
        gate_sum,
        up_sum,
        down_sum.T,
        gain_sums[0],
        gain_sums[1],
        gain_sums[2],
    )


def solution(mesh):
    row = P(("fsdp", "ctx"), "tp")
    col = P("tp", ("fsdp", "ctx"))
    gain = P(("fsdp", "ctx"))
    token = P("fsdp", "ctx", None)
    context = P("fsdp", None, None)
    weights = (row, row, row, col, row, row, row, col, row, row, col, gain, gain, gain)
    return jax.shard_map(
        functools.partial(on_device, mesh),
        mesh=mesh,
        in_specs=(token, context) + weights + (token,),
        out_specs=(token, token, context) + weights,
        check_vma=False,
    )
```

time: 878 us -> 616 us (0.70)
  local copies, waits for them, and re-layouts: 192 us -> 55.9 us
  waiting for transfers between devices: 412 us -> 277 us
  Pallas kernels: 48.2 us -> 59.4 us
  other arithmetic: 52.9 us -> 41.9 us
    ppermute x98 -> x105, waiting for transfers between devices: 412 us -> 277 us  [the longest x33 124 us: ring(): return lax.ppermute(self.begun(value), 'fsdp', pairs)]
    dynamic_update_slice x43 -> x0, local copies, waits for them, and re-layouts: 95.8 us -> none  [the longest x4 70.2 us: scatter_feed(): lax.dynamic_update_slice(result, piece.astype(F32)[:, :, None], (0, 0, se...]
    broadcast_in_dim x10 -> x0, local copies, waits for them, and re-layouts: 14.5 us -> none  [the longest x3 7.14 us: scatter_feed(): piece.astype(F32)[:, :, None]]
    another operation x18 -> x2, local copies, waits for them, and re-layouts: 14.4 us -> 0.14 us  [on_device(): jnp.tile(gains, (1, blocks))]
    concatenate x8 -> x36, other arithmetic: 3.65 us -> 17 us  [the longest x4 3.56 us: feed_part(): jnp.concatenate([lax.dynamic_slice_in_dim(w, index * hidden, hidden, 1) f...]
    slice x19 -> x13, local copies, waits for them, and re-layouts: 12 us -> 0.6 us  [the longest x8 0.46 us: with_core(): return (total[:own_rows], total[own_rows:].astype(BF16))]
    pallas_call x4 -> x14, Pallas kernels: 48.2 us -> 59.4 us  [the longest x1 12.7 us: self_forward(): attention_call(self_forward_kernel, pairs, [(rows, 3 * PAIR, here)] + [(r...]
    dot_general x11 -> x8, matrix products: 22.8 us -> 30 us  [mm(): lax.dot_general(left, right, (((1,), (0,)), ((), ())), preferred_element_...]
  transfers between devices with their start and end apart: 98 -> 105, of which waited for: 44 -> 60; matrix products, arithmetic and copies ran while one was open for 31% -> 20% of each run, Pallas kernels for 4% -> 9%
where the time goes in v2:
time: 616 us; the launch traced here: 609 us
  waiting for transfers between devices  277 us (45%)
  starting transfers between devices  96.5 us (16%)
  matrix products  75.4 us (12%)
  Pallas kernels  59.4 us (10%)
  local copies, waits for them, and re-layouts  55.9 us (9%)
  other arithmetic  41.9 us (7%)
    ppermute x33, waiting for transfers between devices, ring(): return lax.ppermute(self.begun(value), 'fsdp', pairs)  124 us
    ppermute x29, waiting for transfers between devices, lanes(): return lax.ppermute(self.begun(value), 'fsdp', pairs)  88.5 us
    ppermute x27, waiting for transfers between devices, over_half(): return lax.ppermute(self.begun(value), 'ctx', [(0, 1), (1, 0)])  62.2 us
    ppermute x33, starting transfers between devices, ring(): return lax.ppermute(self.begun(value), 'fsdp', pairs)  38.2 us
    unnamed x289, local copies, waits for them, and re-layouts  33.7 us
    dot_general x8, matrix products, mm(): lax.dot_general(left, right, (((1,), (0,)), ((), ())), preferred_element_...  30 us
    ppermute x27, starting transfers between devices, over_half(): return lax.ppermute(self.begun(value), 'ctx', [(0, 1), (1, 0)])  28.7 us
    ppermute x29, starting transfers between devices, lanes(): return lax.ppermute(self.begun(value), 'fsdp', pairs)  27.2 us
  transfers between devices with their start and end apart: 105, of which 60 were waited for; matrix products, arithmetic and copies ran while one was open for 20% of the time, Pallas kernels for 9%

profile of v2, /device:TPU:0, one launch (start us, length us, event | category | flops | bytes accessed | tf_op | source)
XLA Modules:
  0.0 609.1 jit_solution(13677316434631373388)
XLA Ops:
  2.2 3.0 collective-permute-start.1
  14.8 2.6 collective-permute-done
  27.1 7.9 %collective-permute-done.4.refs_9_ = bf16[160,1536]{1,0:T(8,128)(2,1)S(1)} collective-permute-done((bf16[160,1536]{1,0:T(8,128)(2,1)S(1)}, bf16[160,1536]{1,0:T(8,128)(2,1)S(1)}, u32[]{:S(2)}, u32[]{:S(2)}) %collective-permute-start.4) | collective-permute-done | bytes 491552 | tf_op jit(solution)/shard_map/ppermute | solution.py:457
  35.1 3.1 collective-permute-done.2.refs_2_
  43.1 5.3 collective-permute-done.7
  49.1 3.5 collective-permute-done.6.refs_3_
  54.8 7.8 %collective-permute-done.11.refs_2_ = bf16[96,2304]{1,0:T(8,128)(2,1)S(1)} collective-permute-done((bf16[96,2304]{1,0:T(8,128)(2,1)S(1)}, bf16[96,2304]{1,0:T(8,128)(2,1)S(1)}, u32[]{:S(2)}, u32[]{:S(2)}) %collective-permute-start.11) | collective-permute-done | bytes 442400 | tf_op jit(solution)/shard_map/ppermute | solution.py:457
  62.6 3.2 collective-permute-done.10.refs_7_
  65.8 2.8 collective-permute-done.9.refs_4_
  72.2 9.6 %collective-permute-done.12.refs_4_ = bf16[96,2304]{1,0:T(8,128)(2,1)S(1)} collective-permute-done((bf16[96,2304]{1,0:T(8,128)(2,1)}, bf16[96,2304]{1,0:T(8,128)(2,1)S(1)}, u32[]{:S(2)}, u32[]{:S(2)}) %collective-permute-start.12) | collective-permute-done | bytes 442400 | tf_op jit(solution)/shard_map/ppermute | solution.py:449
  87.6 6.2 %shard_map.297 = (bf16[1536,1152]{1,0:T(8,128)(2,1)}, bf16[1536,384]{1,0:T(8,128)(2,1)}, f32[16,1536]{1,0:T(8,128)S(1)}, bf16[640,1536]{1,0:T(8,128)(2,1)}) custom-call(s32[16]{0:T(128)S(1)} %xor_add_fusion.place_ref, bf16[208,1536]{1,0:T(8,128)(2,1)S(1)} %pad_maximum_fusion.8.refs_0_, bf16[208,1536]{1,0:T(8,128)(2,1)S(1)} %collective-permute-done.3.refs_1_, ...), custom_call_target="tpu_custom_call" | custom-call | tf_op jit(solution)/shard_map/pallas_call | solution.py:365
  93.8 7.0 %fusion.83.qkv_ref = f32[640,1152]{1,0:T(8,128)} fusion(bf16[640,1536]{1,0:T(8,128)(2,1)} %get-tuple-element.413, bf16[1536,1152]{1,0:T(8,128)(2,1)} %get-tuple-element.414), kind=kOutput, calls=%fused_computation.372 | convolution fusion | flops 2264924160 | bytes 8454144 | tf_op jit(solution)/shard_map/dot_general | solution.py:21
  102.8 2.6 collective-permute-start.17
  106.9 12.7 %shard_map.298 = (bf16[640,1152]{1,0:T(8,128)(2,1)S(1)}, bf16[640,384]{1,0:T(8,128)(2,1)S(1)}, f32[640,384]{1,0:T(8,128)S(1)}) custom-call(f32[640,1152]{1,0:T(8,128)} %fusion.83.qkv_ref, f32[640,128]{1,0:T(8,128)S(1)} %copy-done.26, f32[640,128]{1,0:T(8,128)S(1)} %copy-done.24, f32[640,128]{1,0:T(8,128)S(1)} %get-tuple-element.423.low_ref), custom_call_target="tpu_custom_call" | custom-call | flops 629145600 | bytes 5898240 | tf_op jit(solution)/shard_map/pallas_call | solution.py:251
  130.0 9.2 %collective-permute-done.23.refs_12_ = bf16[96,2304]{1,0:T(8,128)(2,1)S(1)} collective-permute-done((bf16[96,2304]{1,0:T(8,128)(2,1)S(1)}, bf16[96,2304]{1,0:T(8,128)(2,1)S(1)}, u32[]{:S(2)}, u32[]{:S(2)}) %collective-permute-start.23) | collective-permute-done | bytes 442400 | tf_op jit(solution)/shard_map/ppermute | solution.py:449
  142.6 9.9 %collective-permute-done.27.refs_5_ = bf16[576,384]{1,0:T(8,128)(2,1)S(1)} collective-permute-done((bf16[576,384]{1,0:T(8,128)(2,1)S(1)}, bf16[576,384]{1,0:T(8,128)(2,1)S(1)}, u32[]{:S(2)}, u32[]{:S(2)}) %collective-permute-start.27) | collective-permute-done | bytes 442400 | tf_op jit(solution)/shard_map/ppermute | solution.py:454
  165.6 3.5 shard_map.301
  170.5 6.9 %collective-permute-done.29.refs_8_ = bf16[96,2304]{1,0:T(8,128)(2,1)S(1)} collective-permute-done((bf16[96,2304]{1,0:T(8,128)(2,1)}, bf16[96,2304]{1,0:T(8,128)(2,1)S(1)}, u32[]{:S(2)}, u32[]{:S(2)}) %collective-permute-start.29) | collective-permute-done | bytes 442400 | tf_op jit(solution)/shard_map/ppermute | solution.py:449
  177.6 2.6 collective-permute-start.34
  182.8 11.0 %collective-permute-done.35.refs_5_ = bf16[96,2304]{1,0:T(8,128)(2,1)S(1)} collective-permute-done((bf16[96,2304]{1,0:T(8,128)(2,1)S(1)}, bf16[96,2304]{1,0:T(8,128)(2,1)S(1)}, u32[]{:S(2)}, u32[]{:S(2)}) %collective-permute-start.35) | collective-permute-done | bytes 442400 | tf_op jit(solution)/shard_map/ppermute | solution.py:454
  196.5 9.3 %collective-permute-done.37.refs_13_ = bf16[96,2304]{1,0:T(8,128)(2,1)S(1)} collective-permute-done((bf16[96,2304]{1,0:T(8,128)(2,1)S(1)}, bf16[96,2304]{1,0:T(8,128)(2,1)S(1)}, u32[]{:S(2)}, u32[]{:S(2)}) %collective-permute-start.37) | collective-permute-done | bytes 442400 | tf_op jit(solution)/shard_map/ppermute | solution.py:454
  206.1 2.5 collective-permute-done.36
  210.7 8.3 %collective-permute-done.40.refs_9_ = bf16[96,2304]{1,0:T(8,128)(2,1)S(1)} collective-permute-done((bf16[96,2304]{1,0:T(8,128)(2,1)S(1)}, bf16[96,2304]{1,0:T(8,128)(2,1)S(1)}, u32[]{:S(2)}, u32[]{:S(2)}) %collective-permute-start.40) | collective-permute-done | bytes 442400 | tf_op jit(solution)/shard_map/ppermute | solution.py:454
  224.1 7.4 %collective-permute-done.43.refs_7_ = bf16[96,2304]{1,0:T(8,128)(2,1)S(1)} collective-permute-done((bf16[96,2304]{1,0:T(8,128)(2,1)S(1)}, bf16[96,2304]{1,0:T(8,128)(2,1)S(1)}, u32[]{:S(2)}, u32[]{:S(2)}) %collective-permute-start.43) | collective-permute-done | bytes 442400 | tf_op jit(solution)/shard_map/ppermute | solution.py:454
  231.6 2.7 collective-permute-done.42
  238.2 4.5 shard_map.303
  245.8 5.5 fusion.84
  251.3 5.6 multiply_convert_fusion
  260.5 3.0 convolution_convert_fusion.5
  263.5 3.7 fusion.13
  269.7 6.4 %convolution_convert_fusion.4 = bf16[1536,768]{1,0:T(8,128)(2,1)S(1)} fusion(bf16[1280,1536]{1,0:T(8,128)(2,1)} %copy-done.127, bf16[1280,768]{1,0:T(8,128)(2,1)} %copy-done.135), kind=kOutput, calls=%fused_computation.14 | convolution fusion | flops 3021078528 | bytes 8257536 | tf_op jit(solution)/shard_map/dot_general | solution.py:25
  279.3 3.6 collective-permute-start.49
  285.1 6.5 %fusion.3 = (bf16[1280,768]{1,0:T(8,128)(2,1)S(1)}, bf16[1280,768]{1,0:T(8,128)(2,1)S(1)}) fusion(f32[1280,768]{1,0:T(8,128)} %copy-done.136, f32[1280,768]{1,0:T(8,128)} %get-tuple-element.531, bf16[1280,1536]{1,0:T(8,128)(2,1)S(1)} %copy-done.128, bf16[1536,768]{1,0:T(8,128)(2,1)S(1)} %copy-done.133), kind=kOutput, calls=%fused_computation.6 | convolution fusion | flops 3034644480 | bytes 18087936 | tf_op jit(solution)/shard_map/dot_general | solution.py:21
  293.8 4.3 collective-permute-done.51
  299.2 3.6 convolution_convert_fusion.1
  309.2 3.6 convolution_convert_fusion.2
  317.4 2.9 add_convert_fusion.4
  320.3 10.4 %collective-permute-done.53 = bf16[160,1536]{1,0:T(8,128)(2,1)S(1)} collective-permute-done((bf16[160,1536]{1,0:T(8,128)(2,1)S(1)}, bf16[160,1536]{1,0:T(8,128)(2,1)S(1)}, u32[]{:S(2)}, u32[]{:S(2)}) %collective-permute-start.53) | collective-permute-done | bytes 491552 | tf_op jit(solution)/shard_map/ppermute | solution.py:449
  334.9 9.0 %collective-permute-done.54.refs_2_ = bf16[160,1536]{1,0:T(8,128)(2,1)S(1)} collective-permute-done((bf16[160,1536]{1,0:T(8,128)(2,1)S(1)}, bf16[160,1536]{1,0:T(8,128)(2,1)S(1)}, u32[]{:S(2)}, u32[]{:S(2)}) %collective-permute-start.54) | collective-permute-done | bytes 491552 | tf_op jit(solution)/shard_map/ppermute | solution.py:449
  343.9 4.1 collective-permute-done.56
  351.9 9.8 %collective-permute-done.57.refs_3_ = bf16[160,1536]{1,0:T(8,128)(2,1)S(1)} collective-permute-done((bf16[160,1536]{1,0:T(8,128)(2,1)S(1)}, bf16[160,1536]{1,0:T(8,128)(2,1)S(1)}, u32[]{:S(2)}, u32[]{:S(2)}) %collective-permute-start.57) | collective-permute-done | bytes 491552 | tf_op jit(solution)/shard_map/ppermute | solution.py:449
  363.0 3.1 shard_map.304
  368.2 3.5 collective-permute-start.61
  375.3 3.2 collective-permute-done.62
  386.4 9.7 %shard_map.305 = (bf16[640,384]{1,0:T(8,128)(2,1)S(1)}, bf16[256,384]{1,0:T(8,128)(2,1)S(1)}, bf16[256,384]{1,0:T(8,128)(2,1)S(1)}) custom-call(bf16[640,384]{1,0:T(8,128)(2,1)S(1)} %copy-done.39, bf16[256,768]{1,0:T(8,128)(2,1)S(1)} %copy-done.21, bf16[256,768]{1,0:T(8,128)(2,1)S(1)} %copy-done.21, bf16[640,384]{1,0:T(8,128)(2,1)S(1)} %copy-done.17, ...), custom_call_target="tpu_custom_call" | custom-call | flops 629145600 | bytes 4718592 | tf_op jit(solution)/shard_map/pallas_call | solution.py:287
  409.5 11.1 %collective-permute-done.69.refs_1_ = bf16[160,1536]{1,0:T(8,128)(2,1)S(1)} collective-permute-done((bf16[160,1536]{1,0:T(8,128)(2,1)S(1)}, bf16[160,1536]{1,0:T(8,128)(2,1)S(1)}, u32[]{:S(2)}, u32[]{:S(2)}) %collective-permute-start.69) | collective-permute-done | bytes 491552 | tf_op jit(solution)/shard_map/ppermute | solution.py:457
  428.7 2.6 collective-permute-done.73
  432.2 7.3 %collective-permute-done.71 = bf16[576,384]{1,0:T(8,128)(2,1)S(1)} collective-permute-done((bf16[576,384]{1,0:T(8,128)(2,1)S(1)}, bf16[576,384]{1,0:T(8,128)(2,1)S(1)}, u32[]{:S(2)}, u32[]{:S(2)}) %collective-permute-start.71) | collective-permute-done | bytes 442400 | tf_op jit(solution)/shard_map/ppermute | solution.py:454
  444.7 4.0 collective-permute-start.76
  452.5 12.3 %shard_map.307 = bf16[640,1152]{1,0:T(8,128)(2,1)S(1)} custom-call(bf16[640,1152]{1,0:T(8,128)(2,1)S(1)} %copy-done.35, bf16[640,384]{1,0:T(8,128)(2,1)S(1)} %copy-done.15, bf16[640,384]{1,0:T(8,128)(2,1)S(1)} %convolution_convert_fusion.15.do_ref, f32[640,384]{1,0:T(8,128)S(1)} %copy-done.37, f32[640,128]{1,0:T(8,128)S(1)} %copy-done.27, ...), custom_call_target="tpu_custom_call" | custom-call | flops 1572864000 | bytes 8847360 | tf_op jit(solution)/shard_map/pallas_call | solution.py:263
  464.8 3.6 convolution_convert_fusion.9
  471.6 3.4 convolution_convert_fusion
  482.6 6.9 %collective-permute-done.81 = bf16[576,384]{1,0:T(8,128)(2,1)S(1)} collective-permute-done((bf16[576,384]{1,0:T(8,128)(2,1)S(1)}, bf16[576,384]{1,0:T(8,128)(2,1)S(1)}, u32[]{:S(2)}, u32[]{:S(2)}) %collective-permute-start.81) | collective-permute-done | bytes 442400 | tf_op jit(solution)/shard_map/ppermute | solution.py:454
  490.6 3.2 collective-permute-done.80.refs_1_
  498.7 17.5 %collective-permute-done.84.refs_2_ = bf16[96,2304]{1,0:T(8,128)(2,1)S(1)} collective-permute-done((bf16[96,2304]{1,0:T(8,128)(2,1)S(1)}, bf16[96,2304]{1,0:T(8,128)(2,1)S(1)}, u32[]{:S(2)}, u32[]{:S(2)}) %collective-permute-start.84) | collective-permute-done | bytes 442400 | tf_op jit(solution)/shard_map/ppermute | solution.py:449
  523.2 2.6 collective-permute-done.88
  525.9 8.6 %collective-permute-done.86 = bf16[192,1536]{1,0:T(8,128)(2,1)S(1)} collective-permute-done((bf16[192,1536]{1,0:T(8,128)(2,1)S(1)}, bf16[192,1536]{1,0:T(8,128)(2,1)S(1)}, u32[]{:S(2)}, u32[]{:S(2)}) %collective-permute-start.86) | collective-permute-done | bytes 589856 | tf_op jit(solution)/shard_map/ppermute | solution.py:454
  538.6 2.8 collective-permute-start.93
  546.7 5.5 collective-permute-done.93
  552.2 9.4 %collective-permute-done.92 = bf16[576,384]{1,0:T(8,128)(2,1)S(1)} collective-permute-done((bf16[576,384]{1,0:T(8,128)(2,1)}, bf16[576,384]{1,0:T(8,128)(2,1)S(1)}, u32[]{:S(2)}, u32[]{:S(2)}) %collective-permute-start.92) | collective-permute-done | bytes 442400 | tf_op jit(solution)/shard_map/ppermute | solution.py:449
  569.1 2.5 shard_map.309
  571.8 2.8 collective-permute-done.99
  575.8 16.4 %collective-permute-done.100 = f32[3,384]{1,0:T(4,128)S(1)} collective-permute-done((f32[3,384]{1,0:T(4,128)S(1)}, f32[3,384]{1,0:T(4,128)S(1)}, u32[]{:S(2)}, u32[]{:S(2)}) %collective-permute-start.100) | collective-permute-done | bytes 4640 | tf_op jit(solution)/shard_map/ppermute | solution.py:449
  601.3 4.4 collective-permute-done.102
  (644 shorter events, 222.7 us)
Async XLA Ops:
  2.2 12.6 %collective-permute-start.1 = (bf16[16,1536]{1,0:T(8,128)(2,1)}, bf16[16,1536]{1,0:T(8,128)(2,1)}, u32[]{:S(2)}, u32[]{:S(2)}) collective-permute-start(bf16[16,1536]{1,0:T(8,128)(2,1)} %broadcast_select_fusion.4), channel_id=1, source_target_pairs={{0,2},{2,0},{1,3},{3,1},{4,6},{6,4},{5,7},{7,5},{8,10},{10,8},{9,1... | collective-permute-start | bytes 147464 | tf_op jit(solution)/shard_map/ppermute | solution.py:457
  19.9 15.1 %collective-permute-start.3 = (bf16[208,1536]{1,0:T(8,128)(2,1)S(1)}, bf16[208,1536]{1,0:T(8,128)(2,1)S(1)}, u32[]{:S(2)}, u32[]{:S(2)}) collective-permute-start(bf16[208,1536]{1,0:T(8,128)(2,1)S(1)} %pad_maximum_fusion.8.refs_0_), channel_id=1, source_target_pairs={{0,4},{4,0},{8,12},{12,8},{16,20},{20,16},{24,28},{28,24},{1,5},{5... | collective-permute-start | bytes 1916936 | tf_op jit(solution)/shard_map/ppermute | solution.py:454
  21.5 16.7 %collective-permute-start.2 = (bf16[208,1536]{1,0:T(8,128)(2,1)S(1)}, bf16[208,1536]{1,0:T(8,128)(2,1)}, u32[]{:S(2)}, u32[]{:S(2)}) collective-permute-start(bf16[208,1536]{1,0:T(8,128)(2,1)S(1)} %pad_maximum_fusion.8.refs_0_), channel_id=1, source_target_pairs={{0,8},{4,12},{8,16},{12,20},{16,24},{20,28},{24,0},{28,4},{1,9},{5... | collective-permute-start | bytes 1916936 | tf_op jit(solution)/shard_map/ppermute | solution.py:449
  38.1 14.5 %collective-permute-start.6 = (bf16[208,1536]{1,0:T(8,128)(2,1)}, bf16[208,1536]{1,0:T(8,128)(2,1)S(1)}, u32[]{:S(2)}, u32[]{:S(2)}) collective-permute-start(bf16[208,1536]{1,0:T(8,128)(2,1)} %collective-permute-done.2.refs_2_), channel_id=1, source_target_pairs={{0,4},{4,0},{8,12},{12,8},{16,20},{20,16},{24,28},{28,24},{1,5},{5... | collective-permute-start | bytes 1916936 | tf_op jit(solution)/shard_map/ppermute | solution.py:454
  38.6 14.0 %collective-permute-start.5 = (bf16[208,1536]{1,0:T(8,128)(2,1)S(1)}, bf16[208,1536]{1,0:T(8,128)(2,1)S(1)}, u32[]{:S(2)}, u32[]{:S(2)}) collective-permute-start(bf16[208,1536]{1,0:T(8,128)(2,1)S(1)} %pad_maximum_fusion.8.refs_0_), channel_id=1, source_target_pairs={{0,24},{4,28},{8,0},{12,4},{16,8},{20,12},{24,16},{28,20},{1,25},{... | collective-permute-start | bytes 1916936 | tf_op jit(solution)/shard_map/ppermute | solution.py:449
  52.6 13.2 %collective-permute-start.10 = (bf16[208,1536]{1,0:T(8,128)(2,1)S(1)}, bf16[208,1536]{1,0:T(8,128)(2,1)S(1)}, u32[]{:S(2)}, u32[]{:S(2)}) collective-permute-start(bf16[208,1536]{1,0:T(8,128)(2,1)S(1)} %collective-permute-done.5.refs_6_), channel_id=1, source_target_pairs={{0,4},{4,0},{8,12},{12,8},{16,20},{20,16},{24,28},{28,24},{1,5},{5... | collective-permute-start | bytes 1916936 | tf_op jit(solution)/shard_map/ppermute | solution.py:454
  54.3 14.2 %collective-permute-start.9 = (bf16[208,1536]{1,0:T(8,128)(2,1)}, bf16[208,1536]{1,0:T(8,128)(2,1)}, u32[]{:S(2)}, u32[]{:S(2)}) collective-permute-start(bf16[208,1536]{1,0:T(8,128)(2,1)} %collective-permute-done.2.refs_2_), channel_id=1, source_target_pairs={{0,8},{4,12},{8,16},{12,20},{16,24},{20,28},{24,0},{28,4},{1,9},{5... | collective-permute-start | bytes 1916936 | tf_op jit(solution)/shard_map/ppermute | solution.py:449
  68.6 14.0 %collective-permute-start.13 = (bf16[208,1536]{1,0:T(8,128)(2,1)}, bf16[208,1536]{1,0:T(8,128)(2,1)}, u32[]{:S(2)}, u32[]{:S(2)}) collective-permute-start(bf16[208,1536]{1,0:T(8,128)(2,1)} %collective-permute-done.9.refs_4_), channel_id=1, source_target_pairs={{0,4},{4,0},{8,12},{12,8},{16,20},{20,16},{24,28},{28,24},{1,5},{5... | collective-permute-start | bytes 1916936 | tf_op jit(solution)/shard_map/ppermute | solution.py:454
  82.6 18.2 %collective-permute-start.15 = (bf16[576,384]{1,0:T(8,128)(2,1)S(1)}, bf16[576,384]{1,0:T(8,128)(2,1)S(1)}, u32[]{:S(2)}, u32[]{:S(2)}) collective-permute-start(bf16[576,384]{1,0:T(8,128)(2,1)S(1)} %pad_maximum_fusion.21.refs_0_), channel_id=1, source_target_pairs={{0,4},{4,0},{8,12},{12,8},{16,20},{20,16},{24,28},{28,24},{1,5},{5... | collective-permute-start | bytes 1327112 | tf_op jit(solution)/shard_map/ppermute | solution.py:454
  83.7 17.0 %collective-permute-start.14 = (bf16[576,384]{1,0:T(8,128)(2,1)S(1)}, bf16[576,384]{1,0:T(8,128)(2,1)S(1)}, u32[]{:S(2)}, u32[]{:S(2)}) collective-permute-start(bf16[576,384]{1,0:T(8,128)(2,1)S(1)} %pad_maximum_fusion.21.refs_0_), channel_id=1, source_target_pairs={{0,8},{4,12},{8,16},{12,20},{16,24},{20,28},{24,0},{28,4},{1,9},{5... | collective-permute-start | bytes 1327112 | tf_op jit(solution)/shard_map/ppermute | solution.py:449
  84.0 16.8 %collective-permute-start.16 = (bf16[96,2304]{1,0:T(8,128)(2,1)S(1)}, bf16[96,2304]{1,0:T(8,128)(2,1)S(1)}, u32[]{:S(2)}, u32[]{:S(2)}) collective-permute-start(bf16[96,2304]{1,0:T(8,128)(2,1)S(1)} %collective-permute-done.12.refs_4_), channel_id=1, source_target_pairs={{0,2},{2,0},{1,3},{3,1},{4,6},{6,4},{5,7},{7,5},{8,10},{10,8},{9,1... | collective-permute-start | bytes 1327112 | tf_op jit(solution)/shard_map/ppermute | solution.py:457
  100.8 21.1 %collective-permute-start.19 = (bf16[576,384]{1,0:T(8,128)(2,1)S(1)}, bf16[576,384]{1,0:T(8,128)(2,1)S(1)}, u32[]{:S(2)}, u32[]{:S(2)}) collective-permute-start(bf16[576,384]{1,0:T(8,128)(2,1)S(1)} %collective-permute-done.14.refs_2_), channel_id=1, source_target_pairs={{0,4},{4,0},{8,12},{12,8},{16,20},{20,16},{24,28},{28,24},{1,5},{5... | collective-permute-start | bytes 1327112 | tf_op jit(solution)/shard_map/ppermute | solution.py:454
  101.4 20.5 %collective-permute-start.18 = (bf16[576,384]{1,0:T(8,128)(2,1)S(1)}, bf16[576,384]{1,0:T(8,128)(2,1)S(1)}, u32[]{:S(2)}, u32[]{:S(2)}) collective-permute-start(bf16[576,384]{1,0:T(8,128)(2,1)S(1)} %collective-permute-done.14.refs_2_), channel_id=1, source_target_pairs={{0,8},{4,12},{8,16},{12,20},{16,24},{20,28},{24,0},{28,4},{1,9},{5... | collective-permute-start | bytes 1327112 | tf_op jit(solution)/shard_map/ppermute | solution.py:449
  102.8 19.1 %collective-permute-start.17 = (bf16[576,384]{1,0:T(8,128)(2,1)S(1)}, bf16[576,384]{1,0:T(8,128)(2,1)S(1)}, u32[]{:S(2)}, u32[]{:S(2)}) collective-permute-start(bf16[576,384]{1,0:T(8,128)(2,1)S(1)} %pad_maximum_fusion.21.refs_0_), channel_id=1, source_target_pairs={{0,24},{4,28},{8,0},{12,4},{16,8},{20,12},{24,16},{28,20},{1,25},{... | collective-permute-start | bytes 1327112 | tf_op jit(solution)/shard_map/ppermute | solution.py:449
  105.4 16.5 %collective-permute-start.20 = (bf16[96,2304]{1,0:T(8,128)(2,1)S(1)}, bf16[96,2304]{1,0:T(8,128)(2,1)S(1)}, u32[]{:S(2)}, u32[]{:S(2)}) collective-permute-start(bf16[96,2304]{1,0:T(8,128)(2,1)S(1)} %pad_maximum_fusion.19.refs_0_), channel_id=1, source_target_pairs={{0,4},{4,0},{8,12},{12,8},{16,20},{20,16},{24,28},{28,24},{1,5},{5... | collective-permute-start | bytes 1327112 | tf_op jit(solution)/shard_map/ppermute | solution.py:454
  124.9 15.9 %collective-permute-start.22 = (bf16[160,1536]{1,0:T(8,128)(2,1)S(1)}, bf16[160,1536]{1,0:T(8,128)(2,1)S(1)}, u32[]{:S(2)}, u32[]{:S(2)}) collective-permute-start(bf16[160,1536]{1,0:T(8,128)(2,1)S(1)} %slice.426), channel_id=1, source_target_pairs={{0,2},{2,0},{1,3},{3,1},{4,6},{6,4},{5,7},{7,5},{8,10},{10,8},{9,1... | collective-permute-start | bytes 1474568 | tf_op jit(solution)/shard_map/ppermute | solution.py:457
  127.3 11.9 %collective-permute-start.23 = (bf16[96,2304]{1,0:T(8,128)(2,1)S(1)}, bf16[96,2304]{1,0:T(8,128)(2,1)S(1)}, u32[]{:S(2)}, u32[]{:S(2)}) collective-permute-start(bf16[96,2304]{1,0:T(8,128)(2,1)S(1)} %copy-done.94), channel_id=1, source_target_pairs={{0,24},{4,28},{8,0},{12,4},{16,8},{20,12},{24,16},{28,20},{1,25},{... | collective-permute-start | bytes 1327112 | tf_op jit(solution)/shard_map/ppermute | solution.py:449
  141.2 11.9 %collective-permute-start.25 = (bf16[160,1536]{1,0:T(8,128)(2,1)S(1)}, bf16[160,1536]{1,0:T(8,128)(2,1)S(1)}, u32[]{:S(2)}, u32[]{:S(2)}) collective-permute-start(bf16[160,1536]{1,0:T(8,128)(2,1)S(1)} %get-tuple-element.443), channel_id=1, source_target_pairs={{0,2},{2,0},{1,3},{3,1},{4,6},{6,4},{5,7},{7,5},{8,10},{10,8},{9,1... | collective-permute-start | bytes 1474568 | tf_op jit(solution)/shard_map/ppermute | solution.py:457
  142.0 13.3 %collective-permute-start.26 = (bf16[160,1536]{1,0:T(8,128)(2,1)S(1)}, bf16[160,1536]{1,0:T(8,128)(2,1)S(1)}, u32[]{:S(2)}, u32[]{:S(2)}) collective-permute-start(bf16[160,1536]{1,0:T(8,128)(2,1)S(1)} %get-tuple-element.474.skip_ref), channel_id=1, source_target_pairs={{0,8},{4,12},{8,16},{12,20},{16,24},{20,28},{24,0},{28,4},{1,9},{5... | collective-permute-start | bytes 1474568 | tf_op jit(solution)/shard_map/ppermute | solution.py:449
  156.2 21.2 %collective-permute-start.29 = (bf16[96,2304]{1,0:T(8,128)(2,1)}, bf16[96,2304]{1,0:T(8,128)(2,1)S(1)}, u32[]{:S(2)}, u32[]{:S(2)}) collective-permute-start(bf16[96,2304]{1,0:T(8,128)(2,1)} %pad_maximum_fusion.23), channel_id=1, source_target_pairs={{0,16},{4,20},{8,24},{12,28},{16,0},{20,4},{24,8},{28,12},{1,17},{... | collective-permute-start | bytes 1327112 | tf_op jit(solution)/shard_map/ppermute | solution.py:449
  156.2 21.2 %collective-permute-start.30 = (bf16[96,2304]{1,0:T(8,128)(2,1)S(1)}, bf16[96,2304]{1,0:T(8,128)(2,1)S(1)}, u32[]{:S(2)}, u32[]{:S(2)}) collective-permute-start(bf16[96,2304]{1,0:T(8,128)(2,1)S(1)} %copy-done.19), channel_id=1, source_target_pairs={{0,4},{4,0},{8,12},{12,8},{16,20},{20,16},{24,28},{28,24},{1,5},{5... | collective-permute-start | bytes 1327112 | tf_op jit(solution)/shard_map/ppermute | solution.py:454
  156.8 20.6 %collective-permute-start.31 = (bf16[96,2304]{1,0:T(8,128)(2,1)S(1)}, bf16[96,2304]{1,0:T(8,128)(2,1)S(1)}, u32[]{:S(2)}, u32[]{:S(2)}) collective-permute-start(bf16[96,2304]{1,0:T(8,128)(2,1)S(1)} %collective-permute-done.23.refs_12_), channel_id=1, source_target_pairs={{0,2},{2,0},{1,3},{3,1},{4,6},{6,4},{5,7},{7,5},{8,10},{10,8},{9,1... | collective-permute-start | bytes 1327112 | tf_op jit(solution)/shard_map/ppermute | solution.py:457
  177.6 16.3 %collective-permute-start.34 = (bf16[160,1536]{1,0:T(8,128)(2,1)S(1)}, bf16[160,1536]{1,0:T(8,128)(2,1)S(1)}, u32[]{:S(2)}, u32[]{:S(2)}) collective-permute-start(bf16[160,1536]{1,0:T(8,128)(2,1)S(1)} %get-tuple-element.474.skip_ref), channel_id=1, source_target_pairs={{0,24},{4,28},{8,0},{12,4},{16,8},{20,12},{24,16},{28,20},{1,25},{... | collective-permute-start | bytes 1474568 | tf_op jit(solution)/shard_map/ppermute | solution.py:449
  180.5 13.4 %collective-permute-start.33 = (bf16[160,1536]{1,0:T(8,128)(2,1)S(1)}, bf16[160,1536]{1,0:T(8,128)(2,1)S(1)}, u32[]{:S(2)}, u32[]{:S(2)}) collective-permute-start(bf16[160,1536]{1,0:T(8,128)(2,1)S(1)} %slice.425), channel_id=1, source_target_pairs={{0,2},{2,0},{1,3},{3,1},{4,6},{6,4},{5,7},{7,5},{8,10},{10,8},{9,1... | collective-permute-start | bytes 1474568 | tf_op jit(solution)/shard_map/ppermute | solution.py:457
  181.9 12.0 %collective-permute-start.35 = (bf16[96,2304]{1,0:T(8,128)(2,1)S(1)}, bf16[96,2304]{1,0:T(8,128)(2,1)S(1)}, u32[]{:S(2)}, u32[]{:S(2)}) collective-permute-start(bf16[96,2304]{1,0:T(8,128)(2,1)S(1)} %collective-permute-done.12.refs_4_), channel_id=1, source_target_pairs={{0,4},{4,0},{8,12},{12,8},{16,20},{20,16},{24,28},{28,24},{1,5},{5... | collective-permute-start | bytes 1327112 | tf_op jit(solution)/shard_map/ppermute | solution.py:454
  194.3 14.3 %collective-permute-start.36 = (bf16[160,1536]{1,0:T(8,128)(2,1)S(1)}, bf16[160,1536]{1,0:T(8,128)(2,1)S(1)}, u32[]{:S(2)}, u32[]{:S(2)}) collective-permute-start(bf16[160,1536]{1,0:T(8,128)(2,1)S(1)} %get-tuple-element.480), channel_id=1, source_target_pairs={{0,8},{4,12},{8,16},{12,20},{16,24},{20,28},{24,0},{28,4},{1,9},{5... | collective-permute-start | bytes 1474568 | tf_op jit(solution)/shard_map/ppermute | solution.py:449
  208.6 13.3 %collective-permute-start.39 = (bf16[160,1536]{1,0:T(8,128)(2,1)S(1)}, bf16[160,1536]{1,0:T(8,128)(2,1)S(1)}, u32[]{:S(2)}, u32[]{:S(2)}) collective-permute-start(bf16[160,1536]{1,0:T(8,128)(2,1)S(1)} %collective-permute-done.36), channel_id=1, source_target_pairs={{0,8},{4,12},{8,16},{12,20},{16,24},{20,28},{24,0},{28,4},{1,9},{5... | collective-permute-start | bytes 1474568 | tf_op jit(solution)/shard_map/ppermute | solution.py:449
  221.9 12.4 %collective-permute-start.42 = (bf16[160,1536]{1,0:T(8,128)(2,1)S(1)}, bf16[160,1536]{1,0:T(8,128)(2,1)S(1)}, u32[]{:S(2)}, u32[]{:S(2)}) collective-permute-start(bf16[160,1536]{1,0:T(8,128)(2,1)S(1)} %collective-permute-done.39), channel_id=1, source_target_pairs={{0,8},{4,12},{8,16},{12,20},{16,24},{20,28},{24,0},{28,4},{1,9},{5... | collective-permute-start | bytes 1474568 | tf_op jit(solution)/shard_map/ppermute | solution.py:449
  237.7 19.2 %collective-permute-start.46 = (bf16[160,1536]{1,0:T(8,128)(2,1)S(1)}, bf16[160,1536]{1,0:T(8,128)(2,1)S(1)}, u32[]{:S(2)}, u32[]{:S(2)}) collective-permute-start(bf16[160,1536]{1,0:T(8,128)(2,1)S(1)} %collective-permute-done.26), channel_id=1, source_target_pairs={{0,8},{4,12},{8,16},{12,20},{16,24},{20,28},{24,0},{28,4},{1,9},{5... | collective-permute-start | bytes 1474568 | tf_op jit(solution)/shard_map/ppermute | solution.py:449
  279.3 14.5 %collective-permute-start.49 = (bf16[160,1536]{1,0:T(8,128)(2,1)S(1)}, bf16[160,1536]{1,0:T(8,128)(2,1)S(1)}, u32[]{:S(2)}, u32[]{:S(2)}) collective-permute-start(bf16[160,1536]{1,0:T(8,128)(2,1)S(1)} %add_convert_fusion.9), channel_id=1, source_target_pairs={{0,24},{4,28},{8,0},{12,4},{16,8},{20,12},{24,16},{28,20},{1,25},{... | collective-permute-start | bytes 1474568 | tf_op jit(solution)/shard_map/ppermute | solution.py:449
  282.9 15.2 %collective-permute-start.51 = (bf16[384,768]{1,0:T(8,128)(2,1)S(1)}, bf16[384,768]{1,0:T(8,128)(2,1)S(1)}, u32[]{:S(2)}, u32[]{:S(2)}) collective-permute-start(bf16[384,768]{1,0:T(8,128)(2,1)S(1)} %pad_maximum_fusion.10), channel_id=1, source_target_pairs={{0,2},{2,0},{1,3},{3,1},{4,6},{6,4},{5,7},{7,5},{8,10},{10,8},{9,1... | collective-permute-start | bytes 1769480 | tf_op jit(solution)/shard_map/ppermute | solution.py:457
  284.2 15.0 %collective-permute-start.50 = (bf16[384,768]{1,0:T(8,128)(2,1)S(1)}, bf16[384,768]{1,0:T(8,128)(2,1)S(1)}, u32[]{:S(2)}, u32[]{:S(2)}) collective-permute-start(bf16[384,768]{1,0:T(8,128)(2,1)S(1)} %pad_maximum_fusion.9), channel_id=1, source_target_pairs={{0,4},{4,0},{8,12},{12,8},{16,20},{20,16},{24,28},{28,24},{1,5},{5... | collective-permute-start | bytes 1769480 | tf_op jit(solution)/shard_map/ppermute | solution.py:454
  316.6 14.1 %collective-permute-start.53 = (bf16[160,1536]{1,0:T(8,128)(2,1)S(1)}, bf16[160,1536]{1,0:T(8,128)(2,1)S(1)}, u32[]{:S(2)}, u32[]{:S(2)}) collective-permute-start(bf16[160,1536]{1,0:T(8,128)(2,1)S(1)} %add_convert_fusion.8), channel_id=1, source_target_pairs={{0,24},{4,28},{8,0},{12,4},{16,8},{20,12},{24,16},{28,20},{1,25},{... | collective-permute-start | bytes 1474568 | tf_op jit(solution)/shard_map/ppermute | solution.py:449
  331.0 12.9 %collective-permute-start.54 = (bf16[160,1536]{1,0:T(8,128)(2,1)S(1)}, bf16[160,1536]{1,0:T(8,128)(2,1)S(1)}, u32[]{:S(2)}, u32[]{:S(2)}) collective-permute-start(bf16[160,1536]{1,0:T(8,128)(2,1)S(1)} %get-tuple-element.552), channel_id=1, source_target_pairs={{0,24},{4,28},{8,0},{12,4},{16,8},{20,12},{24,16},{28,20},{1,25},{... | collective-permute-start | bytes 1474568 | tf_op jit(solution)/shard_map/ppermute | solution.py:449
  333.3 14.7 %collective-permute-start.56 = (bf16[384,768]{1,0:T(8,128)(2,1)S(1)}, bf16[384,768]{1,0:T(8,128)(2,1)S(1)}, u32[]{:S(2)}, u32[]{:S(2)}) collective-permute-start(bf16[384,768]{1,0:T(8,128)(2,1)S(1)} %pad_maximum_fusion.12), channel_id=1, source_target_pairs={{0,2},{2,0},{1,3},{3,1},{4,6},{6,4},{5,7},{7,5},{8,10},{10,8},{9,1... | collective-permute-start | bytes 1769480 | tf_op jit(solution)/shard_map/ppermute | solution.py:457
  334.1 14.4 %collective-permute-start.55 = (bf16[384,768]{1,0:T(8,128)(2,1)S(1)}, bf16[384,768]{1,0:T(8,128)(2,1)S(1)}, u32[]{:S(2)}, u32[]{:S(2)}) collective-permute-start(bf16[384,768]{1,0:T(8,128)(2,1)S(1)} %pad_maximum_fusion.11), channel_id=1, source_target_pairs={{0,4},{4,0},{8,12},{12,8},{16,20},{20,16},{24,28},{28,24},{1,5},{5... | collective-permute-start | bytes 1769480 | tf_op jit(solution)/shard_map/ppermute | solution.py:454
  348.5 13.2 %collective-permute-start.57 = (bf16[160,1536]{1,0:T(8,128)(2,1)S(1)}, bf16[160,1536]{1,0:T(8,128)(2,1)S(1)}, u32[]{:S(2)}, u32[]{:S(2)}) collective-permute-start(bf16[160,1536]{1,0:T(8,128)(2,1)S(1)} %get-tuple-element.564), channel_id=1, source_target_pairs={{0,8},{4,12},{8,16},{12,20},{16,24},{20,28},{24,0},{28,4},{1,9},{5... | collective-permute-start | bytes 1474568 | tf_op jit(solution)/shard_map/ppermute | solution.py:449
  348.5 13.5 %collective-permute-start.59 = (bf16[384,768]{1,0:T(8,128)(2,1)S(1)}, bf16[384,768]{1,0:T(8,128)(2,1)S(1)}, u32[]{:S(2)}, u32[]{:S(2)}) collective-permute-start(bf16[384,768]{1,0:T(8,128)(2,1)S(1)} %pad_maximum_fusion.13), channel_id=1, source_target_pairs={{0,2},{2,0},{1,3},{3,1},{4,6},{6,4},{5,7},{7,5},{8,10},{10,8},{9,1... | collective-permute-start | bytes 1769480 | tf_op jit(solution)/shard_map/ppermute | solution.py:457
  349.8 13.2 %collective-permute-start.58 = (bf16[384,768]{1,0:T(8,128)(2,1)S(1)}, bf16[384,768]{1,0:T(8,128)(2,1)S(1)}, u32[]{:S(2)}, u32[]{:S(2)}) collective-permute-start(bf16[384,768]{1,0:T(8,128)(2,1)S(1)} %pad_maximum_fusion.14), channel_id=1, source_target_pairs={{0,4},{4,0},{8,12},{12,8},{16,20},{20,16},{24,28},{28,24},{1,5},{5... | collective-permute-start | bytes 1769480 | tf_op jit(solution)/shard_map/ppermute | solution.py:454
  381.8 19.4 %collective-permute-start.65 = (bf16[2,96,768]{2,1,0:T(8,128)(2,1)S(1)}, bf16[2,96,768]{2,1,0:T(8,128)(2,1)}, u32[]{:S(2)}, u32[]{:S(2)}) collective-permute-start(bf16[2,96,768]{2,1,0:T(8,128)(2,1)S(1)} %copy-done.104), channel_id=1, source_target_pairs={{0,2},{2,0},{1,3},{3,1},{4,6},{6,4},{5,7},{7,5},{8,10},{10,8},{9,1... | collective-permute-start | bytes 884744 | tf_op jit(solution)/shard_map/ppermute | solution.py:457
  382.6 18.6 %collective-permute-start.66 = (bf16[2,96,768]{2,1,0:T(8,128)(2,1)}, bf16[2,96,768]{2,1,0:T(8,128)(2,1)}, u32[]{:S(2)}, u32[]{:S(2)}) collective-permute-start(bf16[2,96,768]{2,1,0:T(8,128)(2,1)} %fusion.33), channel_id=1, source_target_pairs={{0,2},{2,0},{1,3},{3,1},{4,6},{6,4},{5,7},{7,5},{8,10},{10,8},{9,1... | collective-permute-start | bytes 884744 | tf_op jit(solution)/shard_map/ppermute | solution.py:457
  383.9 17.3 %collective-permute-start.67 = (bf16[160,1536]{1,0:T(8,128)(2,1)S(1)}, bf16[160,1536]{1,0:T(8,128)(2,1)}, u32[]{:S(2)}, u32[]{:S(2)}) collective-permute-start(bf16[160,1536]{1,0:T(8,128)(2,1)S(1)} %copy-done.86), channel_id=1, source_target_pairs={{0,8},{4,12},{8,16},{12,20},{16,24},{20,28},{24,0},{28,4},{1,9},{5... | collective-permute-start | bytes 1474568 | tf_op jit(solution)/shard_map/ppermute | solution.py:449
  406.9 13.7 %collective-permute-start.69 = (bf16[160,1536]{1,0:T(8,128)(2,1)S(1)}, bf16[160,1536]{1,0:T(8,128)(2,1)S(1)}, u32[]{:S(2)}, u32[]{:S(2)}) collective-permute-start(bf16[160,1536]{1,0:T(8,128)(2,1)S(1)} %slice.424), channel_id=1, source_target_pairs={{0,2},{2,0},{1,3},{3,1},{4,6},{6,4},{5,7},{7,5},{8,10},{10,8},{9,1... | collective-permute-start | bytes 1474568 | tf_op jit(solution)/shard_map/ppermute | solution.py:457
  423.0 16.5 %collective-permute-start.71 = (bf16[576,384]{1,0:T(8,128)(2,1)S(1)}, bf16[576,384]{1,0:T(8,128)(2,1)S(1)}, u32[]{:S(2)}, u32[]{:S(2)}) collective-permute-start(bf16[576,384]{1,0:T(8,128)(2,1)S(1)} %pad_maximum_fusion.24), channel_id=1, source_target_pairs={{0,4},{4,0},{8,12},{12,8},{16,20},{20,16},{24,28},{28,24},{1,5},{5... | collective-permute-start | bytes 1327112 | tf_op jit(solution)/shard_map/ppermute | solution.py:454
  424.2 17.0 %collective-permute-start.70 = (bf16[160,1536]{1,0:T(8,128)(2,1)S(1)}, bf16[160,1536]{1,0:T(8,128)(2,1)S(1)}, u32[]{:S(2)}, u32[]{:S(2)}) collective-permute-start(bf16[160,1536]{1,0:T(8,128)(2,1)S(1)} %get-tuple-element.610), channel_id=1, source_target_pairs={{0,2},{2,0},{1,3},{3,1},{4,6},{6,4},{5,7},{7,5},{8,10},{10,8},{9,1... | collective-permute-start | bytes 1474568 | tf_op jit(solution)/shard_map/ppermute | solution.py:457
  441.3 28.6 %collective-permute-start.78 = (bf16[576,384]{1,0:T(8,128)(2,1)S(1)}, bf16[576,384]{1,0:T(8,128)(2,1)S(1)}, u32[]{:S(2)}, u32[]{:S(2)}) collective-permute-start(bf16[576,384]{1,0:T(8,128)(2,1)S(1)} %pad_maximum_fusion.26), channel_id=1, source_target_pairs={{0,4},{4,0},{8,12},{12,8},{16,20},{20,16},{24,28},{28,24},{1,5},{5... | collective-permute-start | bytes 1327112 | tf_op jit(solution)/shard_map/ppermute | solution.py:454
  442.5 27.4 %collective-permute-start.77 = (bf16[576,384]{1,0:T(8,128)(2,1)S(1)}, bf16[576,384]{1,0:T(8,128)(2,1)}, u32[]{:S(2)}, u32[]{:S(2)}) collective-permute-start(bf16[576,384]{1,0:T(8,128)(2,1)S(1)} %pad_maximum_fusion.25), channel_id=1, source_target_pairs={{0,4},{4,0},{8,12},{12,8},{16,20},{20,16},{24,28},{28,24},{1,5},{5... | collective-permute-start | bytes 1327112 | tf_op jit(solution)/shard_map/ppermute | solution.py:454
  444.7 25.3 %collective-permute-start.75 = (bf16[96,2304]{1,0:T(8,128)(2,1)}, bf16[96,2304]{1,0:T(8,128)(2,1)S(1)}, u32[]{:S(2)}, u32[]{:S(2)}) collective-permute-start(bf16[96,2304]{1,0:T(8,128)(2,1)} %get-tuple-element.634), channel_id=1, source_target_pairs={{0,8},{4,12},{8,16},{12,20},{16,24},{20,28},{24,0},{28,4},{1,9},{5... | collective-permute-start | bytes 1327112 | tf_op jit(solution)/shard_map/ppermute | solution.py:449
  444.7 25.3 %collective-permute-start.76 = (bf16[96,2304]{1,0:T(8,128)(2,1)}, bf16[96,2304]{1,0:T(8,128)(2,1)S(1)}, u32[]{:S(2)}, u32[]{:S(2)}) collective-permute-start(bf16[96,2304]{1,0:T(8,128)(2,1)} %get-tuple-element.635), channel_id=1, source_target_pairs={{0,24},{4,28},{8,0},{12,4},{16,8},{20,12},{24,16},{28,20},{1,25},{... | collective-permute-start | bytes 1327112 | tf_op jit(solution)/shard_map/ppermute | solution.py:449
  477.1 12.4 %collective-permute-start.81 = (bf16[576,384]{1,0:T(8,128)(2,1)S(1)}, bf16[576,384]{1,0:T(8,128)(2,1)S(1)}, u32[]{:S(2)}, u32[]{:S(2)}) collective-permute-start(bf16[576,384]{1,0:T(8,128)(2,1)S(1)} %pad_maximum_fusion.27), channel_id=1, source_target_pairs={{0,4},{4,0},{8,12},{12,8},{16,20},{20,16},{24,28},{28,24},{1,5},{5... | collective-permute-start | bytes 1327112 | tf_op jit(solution)/shard_map/ppermute | solution.py:454
  478.3 12.3 %collective-permute-start.82 = (bf16[576,384]{1,0:T(8,128)(2,1)S(1)}, bf16[576,384]{1,0:T(8,128)(2,1)S(1)}, u32[]{:S(2)}, u32[]{:S(2)}) collective-permute-start(bf16[576,384]{1,0:T(8,128)(2,1)S(1)} %copy-done.95), channel_id=1, source_target_pairs={{0,24},{4,28},{8,0},{12,4},{16,8},{20,12},{24,16},{28,20},{1,25},{... | collective-permute-start | bytes 1327112 | tf_op jit(solution)/shard_map/ppermute | solution.py:449
  480.8 13.0 %collective-permute-start.80 = (bf16[160,1536]{1,0:T(8,128)(2,1)S(1)}, bf16[160,1536]{1,0:T(8,128)(2,1)S(1)}, u32[]{:S(2)}, u32[]{:S(2)}) collective-permute-start(bf16[160,1536]{1,0:T(8,128)(2,1)S(1)} %slice.423), channel_id=1, source_target_pairs={{0,2},{2,0},{1,3},{3,1},{4,6},{6,4},{5,7},{7,5},{8,10},{10,8},{9,1... | collective-permute-start | bytes 1474568 | tf_op jit(solution)/shard_map/ppermute | solution.py:457
  493.8 22.4 %collective-permute-start.84 = (bf16[96,2304]{1,0:T(8,128)(2,1)S(1)}, bf16[96,2304]{1,0:T(8,128)(2,1)S(1)}, u32[]{:S(2)}, u32[]{:S(2)}) collective-permute-start(bf16[96,2304]{1,0:T(8,128)(2,1)S(1)} %get-tuple-element.656), channel_id=1, source_target_pairs={{0,16},{4,20},{8,24},{12,28},{16,0},{20,4},{24,8},{28,12},{1,17},{... | collective-permute-start | bytes 1327112 | tf_op jit(solution)/shard_map/ppermute | solution.py:449
  493.8 22.4 %collective-permute-start.83 = (bf16[192,1536]{1,0:T(8,128)(2,1)}, bf16[192,1536]{1,0:T(8,128)(2,1)S(1)}, u32[]{:S(2)}, u32[]{:S(2)}) collective-permute-start(bf16[192,1536]{1,0:T(8,128)(2,1)} %pad_maximum_fusion.15), channel_id=1, source_target_pairs={{0,4},{4,0},{8,12},{12,8},{16,20},{20,16},{24,28},{28,24},{1,5},{5... | collective-permute-start | bytes 1769480 | tf_op jit(solution)/shard_map/ppermute | solution.py:454
  519.5 15.0 %collective-permute-start.86 = (bf16[192,1536]{1,0:T(8,128)(2,1)S(1)}, bf16[192,1536]{1,0:T(8,128)(2,1)S(1)}, u32[]{:S(2)}, u32[]{:S(2)}) collective-permute-start(bf16[192,1536]{1,0:T(8,128)(2,1)S(1)} %pad_maximum_fusion.16), channel_id=1, source_target_pairs={{0,4},{4,0},{8,12},{12,8},{16,20},{20,16},{24,28},{28,24},{1,5},{5... | collective-permute-start | bytes 1769480 | tf_op jit(solution)/shard_map/ppermute | solution.py:454
  520.3 15.0 %collective-permute-start.87 = (bf16[192,1536]{1,0:T(8,128)(2,1)S(1)}, bf16[192,1536]{1,0:T(8,128)(2,1)S(1)}, u32[]{:S(2)}, u32[]{:S(2)}) collective-permute-start(bf16[192,1536]{1,0:T(8,128)(2,1)S(1)} %add_convert_fusion.3), channel_id=1, source_target_pairs={{0,24},{4,28},{8,0},{12,4},{16,8},{20,12},{24,16},{28,20},{1,25},{... | collective-permute-start | bytes 1769480 | tf_op jit(solution)/shard_map/ppermute | solution.py:449
  538.6 13.6 %collective-permute-start.93 = (bf16[576,384]{1,0:T(8,128)(2,1)}, bf16[576,384]{1,0:T(8,128)(2,1)S(1)}, u32[]{:S(2)}, u32[]{:S(2)}) collective-permute-start(bf16[576,384]{1,0:T(8,128)(2,1)} %add_convert_fusion.10), channel_id=1, source_target_pairs={{0,24},{4,28},{8,0},{12,4},{16,8},{20,12},{24,16},{28,20},{1,25},{... | collective-permute-start | bytes 1327112 | tf_op jit(solution)/shard_map/ppermute | solution.py:449
  541.3 20.2 %collective-permute-start.92 = (bf16[576,384]{1,0:T(8,128)(2,1)}, bf16[576,384]{1,0:T(8,128)(2,1)S(1)}, u32[]{:S(2)}, u32[]{:S(2)}) collective-permute-start(bf16[576,384]{1,0:T(8,128)(2,1)} %add_convert_fusion.11), channel_id=1, source_target_pairs={{0,8},{4,12},{8,16},{12,20},{16,24},{20,28},{24,0},{28,4},{1,9},{5... | collective-permute-start | bytes 1327112 | tf_op jit(solution)/shard_map/ppermute | solution.py:449
  541.3 20.2 %collective-permute-start.91 = (bf16[192,1536]{1,0:T(8,128)(2,1)}, bf16[192,1536]{1,0:T(8,128)(2,1)S(1)}, u32[]{:S(2)}, u32[]{:S(2)}) collective-permute-start(bf16[192,1536]{1,0:T(8,128)(2,1)} %pad_maximum_fusion.17), channel_id=1, source_target_pairs={{0,4},{4,0},{8,12},{12,8},{16,20},{20,16},{24,28},{28,24},{1,5},{5... | collective-permute-start | bytes 1769480 | tf_op jit(solution)/shard_map/ppermute | solution.py:454
  563.1 29.8 %collective-permute-start.98 = (bf16[192,1536]{1,0:T(8,128)(2,1)S(1)}, bf16[192,1536]{1,0:T(8,128)(2,1)S(1)}, u32[]{:S(2)}, u32[]{:S(2)}) collective-permute-start(bf16[192,1536]{1,0:T(8,128)(2,1)S(1)} %add_convert_fusion.1), channel_id=1, source_target_pairs={{0,8},{4,12},{8,16},{12,20},{16,24},{20,28},{24,0},{28,4},{1,9},{5... | collective-permute-start | bytes 1769480 | tf_op jit(solution)/shard_map/ppermute | solution.py:449
  565.0 27.9 %collective-permute-start.97 = (bf16[192,1536]{1,0:T(8,128)(2,1)S(1)}, bf16[192,1536]{1,0:T(8,128)(2,1)S(1)}, u32[]{:S(2)}, u32[]{:S(2)}) collective-permute-start(bf16[192,1536]{1,0:T(8,128)(2,1)S(1)} %add_convert_fusion.2), channel_id=1, source_target_pairs={{0,24},{4,28},{8,0},{12,4},{16,8},{20,12},{24,16},{28,20},{1,25},{... | collective-permute-start | bytes 1769480 | tf_op jit(solution)/shard_map/ppermute | solution.py:449
  567.0 25.9 %collective-permute-start.96 = (bf16[192,1536]{1,0:T(8,128)(2,1)S(1)}, bf16[192,1536]{1,0:T(8,128)(2,1)S(1)}, u32[]{:S(2)}, u32[]{:S(2)}) collective-permute-start(bf16[192,1536]{1,0:T(8,128)(2,1)S(1)} %pad_maximum_fusion.18), channel_id=1, source_target_pairs={{0,4},{4,0},{8,12},{12,8},{16,20},{20,16},{24,28},{28,24},{1,5},{5... | collective-permute-start | bytes 1769480 | tf_op jit(solution)/shard_map/ppermute | solution.py:454
  571.7 20.4 %collective-permute-start.100 = (f32[3,384]{1,0:T(4,128)S(1)}, f32[3,384]{1,0:T(4,128)S(1)}, u32[]{:S(2)}, u32[]{:S(2)}) collective-permute-start(f32[3,384]{1,0:T(4,128)S(1)} %get-tuple-element.709), channel_id=1, source_target_pairs={{0,24},{4,28},{8,0},{12,4},{16,8},{20,12},{24,16},{28,20},{1,25},{... | collective-permute-start | bytes 13832 | tf_op jit(solution)/shard_map/ppermute | solution.py:449
  574.6 18.3 %collective-permute-start.101 = (f32[3,384]{1,0:T(4,128)S(1)}, f32[3,384]{1,0:T(4,128)S(1)}, u32[]{:S(2)}, u32[]{:S(2)}) collective-permute-start(f32[3,384]{1,0:T(4,128)S(1)} %get-tuple-element.710), channel_id=1, source_target_pairs={{0,8},{4,12},{8,16},{12,20},{16,24},{20,28},{24,0},{28,4},{1,9},{5... | collective-permute-start | bytes 13832 | tf_op jit(solution)/shard_map/ppermute | solution.py:449
  (178 other events, 1509.4 us)

commit v3 on v2

--- a/solution.py
+++ b/solution.py
@@ -15,6 +15,7 @@
 SCALE = HDIM ** (-0.5)
 PAIR = 2 * HDIM
 VMEM_LIMIT = 48 * 1024 * 1024
+VMEM_MOST = 60 * 1024 * 1024
 
 
 def mm(left, right):
@@ -35,36 +36,100 @@
     return center * rate, rate
 
 
-def params():
-    return pltpu.CompilerParams(vmem_limit_bytes=VMEM_LIMIT)
-
-
-def norm_forward_kernel(base_ref, near_ref, far_ref, gain_ref, x_ref, n_ref):
-    values = base_ref[...].astype(F32) + near_ref[...] + far_ref[...].astype(F32)
+def params(limit=VMEM_LIMIT):
+    return pltpu.CompilerParams(vmem_limit_bytes=limit)
+
+
+def norm_call(kernel, rows, outs, *operands):
+    width = operands[0].shape[1]
+
+    def block(count):
+        return pl.BlockSpec((count, width), lambda step: (0, 0))
+
+    return pl.pallas_call(
+        kernel,
+        grid=(1,),
+        in_specs=[block(min(rows, operand.shape[0])) for operand in operands],
+        out_specs=[block(count) for count, _ in outs],
+        out_shape=[jax.ShapeDtypeStruct((count, width), kind) for count, kind in outs],
+        compiler_params=params(),
+    )(*operands)
+
+
+def norm_forward_kernel(gain_ref, base_ref, *refs):
+    *terms, x_ref, n_ref = refs
+    values = base_ref[...].astype(F32)
+    for term in terms:
+        values = values + term[...].astype(F32)
     x_ref[...] = values
     n_ref[...] = (norm_stats(values)[0] * gain_ref[...]).astype(BF16)
 
 
-def norm_forward(base, near, far, gain):
-    rows, width = base.shape
+def norm_forward(rows, base, gain, *terms):
+    return norm_call(norm_forward_kernel, rows, ((rows, F32), (rows, BF16)), gain, base, *terms)
+
+
+def pair_forward_kernel(gain_ref, own_ref, over_ref, near_ref, core_ref, far_ref, x_ref, n_ref):
+    rows = own_ref.shape[0]
+    for base, first in ((own_ref, 0), (over_ref, rows)):
+        part, other = slice(first, first + rows), slice(rows - first, 2 * rows - first)
+        values = base[...].astype(F32) + near_ref[part, :]
+        values = values + core_ref[part, :].astype(F32) + far_ref[other, :].astype(F32)
+        x_ref[part, :] = values
+        n_ref[part, :] = (norm_stats(values)[0] * gain_ref[...]).astype(BF16)
+
+
+def pair_forward(gain, own, over, near, core, far):
+    rows, width = near.shape
     return pl.pallas_call(
-        norm_forward_kernel,
+        pair_forward_kernel,
         out_shape=(
             jax.ShapeDtypeStruct((rows, width), F32),
             jax.ShapeDtypeStruct((rows, width), BF16),
         ),
         compiler_params=params(),
-    )(base, near, far, gain)
-
-
-def norm_backward_kernel(
-    x_ref, gain_ref, skip_ref, *refs
+    )(gain, own, over, near, core, far)
+
+
+def pair_backward_kernel(
+    gain_ref, x_ref, skip_ref, over_ref, near_ref, core_ref, far_ref, dx_ref, low_ref, dg_ref
 ):
+    rows = skip_ref.shape[0]
+    for skip, first in ((skip_ref, 0), (over_ref, rows)):
+        part, other = slice(first, first + rows), slice(rows - first, 2 * rows - first)
+        upstream = near_ref[part, :] + core_ref[part, :].astype(F32) + far_ref[other, :].astype(F32)
+        unit, rate = norm_stats(x_ref[part, :])
+        scaled = upstream * gain_ref[...]
+        back = rate * (
+            scaled
+            - jnp.mean(scaled, axis=-1, keepdims=True)
+            - unit * jnp.mean(scaled * unit, axis=-1, keepdims=True)
+        )
+        total = skip[...].astype(F32) + back
+        low_ref[part, :] = total.astype(BF16)
+        if first == 0:
+            dx_ref[...] = total
+            dg_ref[...] = jnp.sum(upstream * unit, axis=0, keepdims=True)
+
+
+def pair_backward(gain, values, skip, over, near, core, far):
+    rows, width = values.shape
+    return pl.pallas_call(
+        pair_backward_kernel,
+        out_shape=(
+            jax.ShapeDtypeStruct((rows // 2, width), F32),
+            jax.ShapeDtypeStruct((rows, width), BF16),
+            jax.ShapeDtypeStruct((1, width), F32),
+        ),
+        compiler_params=params(),
+    )(gain, values, skip, over, near, core, far)
+
+
+def norm_backward_kernel(gain_ref, x_ref, skip_ref, *refs):
     *terms, dx_ref, low_ref, dg_ref = refs
-    rows = x_ref.shape[0]
-    upstream = terms[0][:rows, :].astype(F32)
+    upstream = terms[0][...].astype(F32)
     for term in terms[1:]:
-        upstream = upstream + term[:rows, :].astype(F32)
+        upstream = upstream + term[...].astype(F32)
     unit, rate = norm_stats(x_ref[...].astype(F32))
     scaled = upstream * gain_ref[...]
     back = rate * (
@@ -79,16 +144,9 @@
 
 
 def norm_backward(values, gain, skip, *terms):
-    rows, width = values.shape
-    return pl.pallas_call(
-        norm_backward_kernel,
-        out_shape=(
-            jax.ShapeDtypeStruct((rows, width), F32),
-            jax.ShapeDtypeStruct((rows, width), BF16),
-            jax.ShapeDtypeStruct((1, width), F32),
-        ),
-        compiler_params=params(),
-    )(values, gain, skip, *terms)
+    rows = values.shape[0]
+    outs = (rows, F32), (rows, BF16), (1, F32)
+    return norm_call(norm_backward_kernel, rows, outs, gain, values, skip, *terms)
 
 
 def turned(values, cosine, upper, lower):
@@ -143,13 +201,131 @@
     return ref.at[:, :PAIR], ref.at[:, PAIR : 2 * PAIR], ref.at[:, 2 * PAIR :]
 
 
-def self_forward_kernel(qkv_ref, cos_ref, up_ref, low_ref, turned_ref, o_ref, lse_ref):
+def self_forward_kernel(shard, place_ref, *refs):
+    n_pieces = len(refs) - 23
+    pieces, refs = refs[:n_pieces], refs[n_pieces:]
+    parts, refs = refs[:4], refs[4:]
+    cos_ref, up_ref, low_ref, *refs = refs
+    turned_ref, o_ref, lse_ref, mine_ref, send_ref, gain_ref, *refs = refs
+    qkv_out, output_out, normed_out, *refs = refs
+    qkv_all, output_all, normed_all, gain_all, o_all = refs[:-2]
+    sems, out_sems = refs[-2:]
+    pair, cols = pl.program_id(0), qkv_all.shape[1]
+    gain_rows = gain_all.shape[0] // n_pieces
+
+    @pl.when(pair == 0)
+    def _():
+        copies = []
+        for n, piece in enumerate(pieces):
+            mark = pl.ds(n * gain_rows, gain_rows)
+            copies.append((piece.at[pl.ds(2 * shard, gain_rows), pl.ds(0, gain_all.shape[1])], gain_all.at[mark, :]))
+        for n, piece in enumerate(pieces):
+            for there in (0, 1):
+                row = pl.ds(pl.multiple_of(place_ref[2 * n + there] * shard, shard), shard)
+                lines = pl.ds(there * shard, shard)
+                copies.append((piece.at[lines, pl.ds(0, cols)], qkv_all.at[row, :]))
+                copies.append((piece.at[lines, pl.ds(cols, output_all.shape[1])], output_all.at[row, :]))
+        copies = [
+            pltpu.make_async_copy(source, target, sems.at[n])
+            for n, (source, target) in enumerate(copies)
+        ]
+        for copy in copies:
+            copy.start()
+        for copy in copies[:n_pieces]:
+            copy.wait()
+        gains = jnp.zeros((gain_rows, gain_all.shape[1]), F32)
+        for n in range(n_pieces):
+            gains = gains + gain_all[n * gain_rows : (n + 1) * gain_rows, :].astype(F32)
+        gain_ref[...] = gains
+        first = 0
+        for part in parts:
+            unit, _ = norm_stats(part[...].astype(F32))
+            normed_all[first : first + part.shape[0], :] = (unit * gains[:1]).astype(BF16)
+            first += part.shape[0]
+        for copy in copies[n_pieces:]:
+            copy.wait()
+
+    exports = [
+        pltpu.make_async_copy(source, target, out_sems.at[n])
+        for n, (source, target) in enumerate(
+            ((qkv_all, qkv_out), (output_all, output_out), (normed_all, normed_out))
+        )
+    ]
+
+    @pl.when(pair == 0)
+    def _():
+        for export in exports:
+            export.start()
+
     tables = cos_ref[...], up_ref[...], low_ref[...]
     q_ref, k_ref, v_ref = thirds(turned_ref)
-    q_ref[...] = turned(qkv_ref[:, :PAIR], *tables).astype(BF16) * jnp.asarray(SCALE, BF16)
-    k_ref[...] = turned(qkv_ref[:, PAIR : 2 * PAIR], *tables).astype(BF16)
-    v_ref[...] = qkv_ref[:, 2 * PAIR :].astype(BF16)
+    first = pl.multiple_of(pair * 3 * PAIR, PAIR)
+    qkv = mm(normed_all[...], qkv_all[:, pl.ds(first, 3 * PAIR)])
+    q_ref[...] = turned(qkv[:, :PAIR], *tables).astype(BF16) * jnp.asarray(SCALE, BF16)
+    k_ref[...] = turned(qkv[:, PAIR : 2 * PAIR], *tables).astype(BF16)
+    v_ref[...] = qkv[:, 2 * PAIR :].astype(BF16)
     forward_heads(q_ref, k_ref, v_ref, o_ref, lse_ref, k_ref.shape[0])
+    o_all[:, pl.ds(pl.multiple_of(pair * PAIR, PAIR), PAIR)] = o_ref[...]
+
+    @pl.when(pair == pl.num_programs(0) - 1)
+    def _():
+        half = o_all.shape[0] // 2
+        mine_ref[...] = mm_nt(o_all[:half, :], output_all[...])
+        send_ref[...] = mm_nt(o_all[half:, :], output_all[...]).astype(BF16)
+        for export in exports:
+            export.wait()
+
+
+def self_forward(pieces, place, parts, tables, shard):
+    width, cols = parts[0].shape[1], pieces[0].shape[1] // 4
+    rows, pairs = sum(part.shape[0] for part in parts), cols // PAIR
+    gain_rows = pieces[0].shape[0] - 2 * shard
+    vmem, anywhere = pl.BlockSpec(memory_space=pltpu.VMEM), pl.BlockSpec(memory_space=pl.ANY)
+
+    def paired(width):
+        return pl.BlockSpec((rows, width), lambda pair: (0, pair))
+
+    def whole(shape):
+        return pl.BlockSpec(shape, lambda pair: (0, 0))
+
+    return pl.pallas_call(
+        functools.partial(self_forward_kernel, shard),
+        grid=(pairs,),
+        in_specs=[pl.BlockSpec(memory_space=pltpu.SMEM)]
+        + [anywhere] * len(pieces)
+        + [whole(part.shape) for part in parts]
+        + [whole((rows, PAIR))] * 3,
+        out_specs=[paired(3 * PAIR), paired(PAIR), paired(PAIR)]
+        + [whole((rows // 2, width))] * 2
+        + [whole((gain_rows, width))]
+        + [anywhere] * 3,
+        out_shape=[
+            jax.ShapeDtypeStruct((rows, 3 * cols), BF16),
+            jax.ShapeDtypeStruct((rows, cols), BF16),
+            jax.ShapeDtypeStruct((rows, cols), F32),
+            jax.ShapeDtypeStruct((rows // 2, width), F32),
+            jax.ShapeDtypeStruct((rows // 2, width), BF16),
+            jax.ShapeDtypeStruct((gain_rows, width), F32),
+            jax.ShapeDtypeStruct((width, 3 * cols), BF16),
+            jax.ShapeDtypeStruct((width, cols), BF16),
+            jax.ShapeDtypeStruct((rows, width), BF16),
+        ],
+        scratch_shapes=[
+            pltpu.VMEM((width, 3 * cols), BF16),
+            pltpu.VMEM((width, cols), BF16),
+            pltpu.VMEM((rows, width), BF16),
+            pltpu.VMEM((len(pieces) * gain_rows, width), BF16),
+            pltpu.VMEM((rows, cols), BF16),
+            pltpu.SemaphoreType.DMA((5 * len(pieces),)),
+            pltpu.SemaphoreType.DMA((3,)),
+        ],
+        compiler_params=params(VMEM_MOST),
+        cost_estimate=pl.CostEstimate(
+            flops=4 * rows * rows * cols + 2 * rows * width * 4 * cols,
+            bytes_accessed=8 * width * cols + 2 * rows * width,
+            transcendentals=rows * rows * cols // HDIM,
+        ),
+    )(place, *pieces, *parts, *tables)
 
 
 def cross_forward_kernel(valid, q_ref, k_ref, v_ref, o_ref, lse_ref):
@@ -246,18 +422,6 @@
     return 0
 
 
-def self_forward(qkv, tables):
-    rows, pairs = qkv.shape[0], qkv.shape[1] // (3 * PAIR)
-    return attention_call(
-        self_forward_kernel,
-        pairs,
-        [(rows, 3 * PAIR, here)] + [(rows, PAIR, always)] * 3,
-        [(rows, 3 * PAIR, BF16), (rows, PAIR, BF16), (rows, PAIR, F32)],
-        (),
-        4 * rows * rows * pairs * PAIR,
-    )(qkv, *tables)
-
-
 def self_backward(qkv, out, grad, lse, tables):
     rows, pairs = qkv.shape[0], qkv.shape[1] // (3 * PAIR)
     return attention_call(
@@ -338,42 +502,158 @@
     )(place, *pieces)
 
 
-def early_kernel(shard, place_ref, *refs):
-    *pieces, a_ref, b_ref, c_ref, d_ref, qkv_ref, output_ref, gain_ref, normed_ref = refs
-    gains = pieces[0][2 * shard :, :].astype(F32)
-    for piece in pieces[1:]:
-        gains = gains + piece[2 * shard :, :].astype(F32)
-    gain_ref[...] = gains
-    first = 0
-    for ref in (a_ref, b_ref, c_ref, d_ref):
-        unit, _ = norm_stats(ref[...].astype(F32))
-        normed_ref[first : first + ref.shape[0], :] = (unit * gains[:1]).astype(BF16)
-        first += ref.shape[0]
-    cols = qkv_ref.shape[1]
-    for n, piece in enumerate(pieces):
-        for there in (0, 1):
-            row = pl.ds(pl.multiple_of(place_ref[2 * n + there] * shard, shard), shard)
-            lines = slice(there * shard, (there + 1) * shard)
-            qkv_ref[row, :] = piece[lines, :cols]
-            output_ref[row, :] = piece[lines, cols:]
-
-
-def early_full(pieces, place, tokens, shard):
-    width, cols = tokens[0].shape[1], pieces[0].shape[1] // 4
-    rows = sum(part.shape[0] for part in tokens)
-    vmem = pl.BlockSpec(memory_space=pltpu.VMEM)
+def feed_kernel(shard, own, n_held, plan, place_ref, *refs):
+    n_pieces = len(refs) - 13 - n_held
+    pieces, held, refs = refs[:n_pieces], refs[n_pieces : n_pieces + n_held], refs[n_pieces + n_held :]
+    tokens, cotangents = [
+        [held[n].at[pl.ds(part * own, own), :] for n, part in parts] for parts in plan
+    ]
+    hid_ref, low_ref, send_ref, mine_ref, n_out, ct_out, down_out, *refs = refs
+    gate_up, down, n_all, ct_all, sems, out_sems = refs
+    step, steps = pl.program_id(0), pl.num_programs(0)
+    hidden = down.shape[1]
+    block = n_all.shape[0] // steps
+    each = 8 // steps
+
+    def row(n):
+        return pl.ds(pl.multiple_of(place_ref[n] * shard, shard), shard)
+
+    def copies_of(sources, target, first):
+        return [
+            pltpu.make_async_copy(source, target.at[pl.ds(n * own, own), :], sems.at[first + n])
+            for n, source in enumerate(sources)
+        ]
+
+    inward = copies_of(tokens, n_all, 0), copies_of(cotangents, ct_all, 8)
+    weights = [
+        pltpu.make_async_copy(piece.at[:, pl.ds(0, 2 * hidden)], gate_up.at[row(n), :], sems.at[16 + n])
+        for n, piece in enumerate(pieces)
+    ]
+    downs = [
+        pltpu.make_async_copy(
+            piece.at[:, pl.ds(2 * hidden, hidden)], down.at[row(n), :], sems.at[16 + n_pieces + n]
+        )
+        for n, piece in enumerate(pieces)
+    ]
+
+    @pl.when(step == 0)
+    def _():
+        for copy in inward[0][:each] + weights + inward[1][:each] + downs:
+            copy.start()
+        for copy in inward[0][each:] + inward[1][each:]:
+            copy.start()
+        for copy in weights:
+            copy.wait()
+
+    @pl.when(step == 0)
+    def _():
+        for copy in inward[0][:each]:
+            copy.wait()
+
+    @pl.when(step == 1)
+    def _():
+        for copy in inward[0][each:]:
+            copy.wait()
+
+    part = pl.ds(pl.multiple_of(step * block, block), block)
+    both = mm(n_all[part, :], gate_up[...])
+    gate, up = both[:, :hidden], both[:, hidden:]
+    sigmoid = 1.0 / (1.0 + jnp.exp(-gate))
+    silu = gate * sigmoid
+    hid_ref[...] = (silu * up).astype(BF16)
+    slope = up * sigmoid * (1.0 + gate * (1.0 - sigmoid))
+
+    @pl.when(step == 0)
+    def _():
+        for copy in downs:
+            copy.wait()
+
+    @pl.when(step == 0)
+    def _():
+        for copy in inward[1][:each]:
+            copy.wait()
+
+    exports = [
+        pltpu.make_async_copy(source, target, out_sems.at[n])
+        for n, (source, target) in enumerate(((n_all, n_out), (ct_all, ct_out), (down, down_out)))
+    ]
+
+    @pl.when(step == 1)
+    def _():
+        for copy in inward[1][each:]:
+            copy.wait()
+        for export in exports:
+            export.start()
+
+    back = mm(ct_all[part, :], down[...]).astype(BF16).astype(F32)
+    gate_low = (back * slope).astype(BF16)
+    up_low = (back * silu).astype(BF16)
+    low_ref[:, :hidden] = gate_low
+    low_ref[:, hidden:] = up_low
+    result = mm_nt(low_ref[...], gate_up[...])
+
+    @pl.when(step < steps // 2)
+    def _():
+        send_ref[...] = result.astype(BF16)
+
+    @pl.when(step >= steps // 2)
+    def _():
+        mine_ref[...] = result
+
+    @pl.when(step == steps - 1)
+    def _():
+        for export in exports:
+            export.wait()
+
+
+def feed_forward(pieces, place, held, tokens, cotangents, shard, own):
+    width = held[0].shape[1]
+    hidden = pieces[0].shape[1] // 3
+    rows = 8 * own
+    steps = 4
+    block = rows // steps
+    vmem, anywhere = pl.BlockSpec(memory_space=pltpu.VMEM), pl.BlockSpec(memory_space=pl.ANY)
+    half = steps // 2
+
+    def blocks(cols):
+        return pl.BlockSpec((block, cols), lambda step: (step, 0))
+
     return pl.pallas_call(
-        functools.partial(early_kernel, shard),
-        in_specs=[pl.BlockSpec(memory_space=pltpu.SMEM)] + [vmem] * (len(pieces) + 4),
-        out_specs=[vmem] * 4,
+        functools.partial(
+            feed_kernel, shard, own, len(held), (tuple(tokens), tuple(cotangents))
+        ),
+        grid=(steps,),
+        in_specs=[pl.BlockSpec(memory_space=pltpu.SMEM)] + [anywhere] * (len(pieces) + len(held)),
+        out_specs=[blocks(hidden), blocks(2 * hidden)]
+        + [
+            pl.BlockSpec((block, width), lambda step: (jnp.minimum(step, half - 1), 0)),
+            pl.BlockSpec((block, width), lambda step: (jnp.maximum(step - half, 0), 0)),
+        ]
+        + [anywhere] * 3,
         out_shape=[
-            jax.ShapeDtypeStruct((width, 3 * cols), BF16),
-            jax.ShapeDtypeStruct((width, cols), BF16),
-            jax.ShapeDtypeStruct((pieces[0].shape[0] - 2 * shard, width), F32),
+            jax.ShapeDtypeStruct((rows, hidden), BF16),
+            jax.ShapeDtypeStruct((rows, 2 * hidden), BF16),
+            jax.ShapeDtypeStruct((rows // 2, width), BF16),
+            jax.ShapeDtypeStruct((rows // 2, width), F32),
             jax.ShapeDtypeStruct((rows, width), BF16),
+            jax.ShapeDtypeStruct((rows, width), BF16),
+            jax.ShapeDtypeStruct((width, hidden), BF16),
         ],
-        compiler_params=params(),
-    )(place, *pieces, *tokens)
+        scratch_shapes=[
+            pltpu.VMEM((width, 2 * hidden), BF16),
+            pltpu.VMEM((width, hidden), BF16),
+            pltpu.VMEM((rows, width), BF16),
+            pltpu.VMEM((rows, width), BF16),
+            pltpu.SemaphoreType.DMA((16 + 2 * len(pieces),)),
+            pltpu.SemaphoreType.DMA((3,)),
+        ],
+        compiler_params=params(VMEM_MOST),
+        cost_estimate=pl.CostEstimate(
+            flops=10 * rows * width * hidden,
+            bytes_accessed=6 * width * hidden + 8 * rows * width,
+            transcendentals=rows * hidden,
+        ),
+    )(place, *pieces, *held)
 
 
 def spread_kernel(place_ref, *refs):
@@ -398,27 +678,72 @@
     return gate, up, down
 
 
-def pack_early_kernel(half_ref, q_ref, k_ref, v_ref, o_ref, send_ref, keep_ref):
-    cols = o_ref.shape[1] // 2
+def split_kernel(down, place_ref, *refs):
+    grads, outs = refs[: len(down)], refs[len(down) :]
+    for n, out in enumerate(outs):
+        row = col = 0
+        for grad, below in zip(grads, down):
+            count, cols = grad.shape[0] // len(outs), grad.shape[1]
+            line = pl.ds(pl.multiple_of(place_ref[n] * count, count), count)
+            out[row : row + count, col : col + cols] = grad[line, :]
+            if below:
+                row += count
+            else:
+                col += cols
+
+
+def split_blocks(grads, place, below):
+    count = place.shape[0]
+    rows = [grad.shape[0] // count for grad in grads]
+    cols = [grad.shape[1] for grad in grads]
+    shape = (sum(rows), cols[0]) if below else (rows[0], sum(cols))
+    vmem = pl.BlockSpec(memory_space=pltpu.VMEM)
+    return pl.pallas_call(
+        functools.partial(split_kernel, (below,) * len(grads)),
+        in_specs=[pl.BlockSpec(memory_space=pltpu.SMEM)] + [vmem] * len(grads),
+        out_specs=[vmem] * count,
+        out_shape=[jax.ShapeDtypeStruct(shape, BF16)] * count,
+        compiler_params=params(),
+    )(place, *grads)
+
+
+def pack_early_kernel(half_ref, q_any, k_any, v_any, o_any, gain_ref, send_ref, keep_ref, *scratch):
+    *held, sems = scratch
+    copies = [
+        pltpu.make_async_copy(source, target, sems.at[n])
+        for n, (source, target) in enumerate(zip((q_any, k_any, v_any, o_any), held))
+    ]
+    for copy in copies:
+        copy.start()
+    for copy in copies:
+        copy.wait()
+    q_ref, k_ref, v_ref, o_ref = held
+    rows, cols = o_ref.shape[0], o_ref.shape[1] // 2
     for out, index in ((send_ref, 1 - half_ref[0]), (keep_ref, half_ref[0])):
         first = pl.multiple_of(index * cols, PAIR)
         for pair in range(cols // PAIR):
             for n, ref in enumerate((q_ref, k_ref, v_ref)):
                 spot = (3 * pair + n) * PAIR
-                out[:, spot : spot + PAIR] = ref[:, pl.ds(first + pair * PAIR, PAIR)]
-        out[:, 3 * cols :] = o_ref[:, pl.ds(first, cols)]
-
-
-def pack_early(query, key, value, output, half, cols):
-    rows = query.shape[0]
+                out[:rows, spot : spot + PAIR] = ref[:, pl.ds(first + pair * PAIR, PAIR)]
+        out[:rows, 3 * cols :] = o_ref[:, pl.ds(first, cols)]
+    send_ref[rows:, :] = gain_ref[...]
+
+
+def pack_early(query, key, value, output, gains, half, cols):
+    rows, full = query.shape
     vmem = pl.BlockSpec(memory_space=pltpu.VMEM)
+    anywhere = pl.BlockSpec(memory_space=pl.ANY)
     return pl.pallas_call(
         pack_early_kernel,
-        in_specs=[pl.BlockSpec(memory_space=pltpu.SMEM)] + [vmem] * 4,
+        in_specs=[pl.BlockSpec(memory_space=pltpu.SMEM)] + [anywhere] * 4 + [vmem],
         out_specs=[vmem] * 2,
-        out_shape=[jax.ShapeDtypeStruct((rows, 4 * cols), BF16)] * 2,
-        compiler_params=params(),
-    )(half.reshape(1), query, key, value, output)
+        out_shape=[
+            jax.ShapeDtypeStruct((rows + gains.shape[0], 4 * cols), BF16),
+            jax.ShapeDtypeStruct((rows, 4 * cols), BF16),
+        ],
+        scratch_shapes=[pltpu.VMEM((rows, full), BF16)] * 4 + [pltpu.SemaphoreType.DMA((4,))],
+        compiler_params=params(VMEM_MOST),
+    )(half.reshape(1), query, key, value, output, gains)
 
 
 RING = 4
@@ -590,9 +915,8 @@
         pair = 2 * own_rows
         return mm_nt(left[:pair], weights), mm_nt(left[pair:], weights).astype(BF16)
 
-    def with_core(mine, recv):
-        total = mine + recv.astype(F32)
-        return total[:own_rows], total[own_rows:].astype(BF16)
+    def for_half(mine, recv):
+        return (mine[own_rows:] + recv[own_rows:].astype(F32)).astype(BF16)
 
     def spread_cores(own, over):
         pair = jnp.concatenate([own, over], axis=0)
@@ -616,16 +940,15 @@
         (mark >= place) & (mark < place + shard), jnp.tile(gains, (1, blocks)), jnp.zeros((), BF16)
     )
     early_send, early_keep = pack_early(
-        query_matrix, key_matrix, value_matrix, output_matrix.T, half, cols
-    )
-
-    early_recv, gains_over = over_half(early_send), over_half(gains)
-    early_keep, early_recv, gains_over = sync(early_keep, early_recv, gains_over)
-
-    early0 = jnp.concatenate([early_keep, early_recv, gains + gains_over], axis=0)
+        query_matrix, key_matrix, value_matrix, output_matrix.T, gains, half, cols
+    )
+    early_recv, cotangent1 = over_half(early_send), ring(upstream, 1)
+    early_keep, early_recv, gains = sync(early_keep, early_recv, gains)
+
+    early0 = jnp.concatenate([early_keep, early_recv[:shard], gains + early_recv[shard:]], axis=0)
     early1, lanes0, own_over = ring(early0, 1), all_lanes(early0), over_half(own)
-    early1, lanes0, own_over, late_send, late_keep = sync(
-        early1, lanes0, own_over, late_part(1 - half), late_part(half)
+    early1, lanes0, own_over, late_send, late_keep, cotangent1 = sync(
+        early1, lanes0, own_over, late_part(1 - half), late_part(half), cotangent1
     )
 
     early3, lanes1, late_recv = ring(lanes0[0], -1), all_lanes(early1), over_half(late_send)
@@ -642,45 +965,52 @@
 
     early2, lanes3, feed0_over = ring(lanes1[0], 1), all_lanes(early3), over_half(feed0)
     late0 = jnp.concatenate([late_keep, late_recv], axis=0)
-    early2, lanes3, feed0_over, late0 = sync(early2, lanes3, feed0_over, late0)
-
-    feed1, lanes2 = ring(feed_send, 1), all_lanes(early2)
+    early2, lanes3, feed0_over, late0, feed0, feed_sends = sync(
+        early2,
+        lanes3,
+        feed0_over,
+        late0,
+        feed0,
+        [feed_part(links.ring_at(back)) for back in (1, 2)],
+    )
+
+    late1, lanes2 = ring(late0, 1), all_lanes(early2)
     context = jnp.pad(conditioning[0], ((0, -context_count % 128), (0, 0)))
-    feed1, lanes2, context, feed_send = sync(
-        feed1, lanes2, context, feed_part(links.ring_at(1))
-    )
-
-    late1, late_lanes0, feed1_over = ring(late0, 1), all_lanes(late0), over_half(feed1)
-    qkv_full, output_full, gains, normed_one = early_full(
-        lanes0 + lanes1 + lanes2 + lanes3, places, (own, own_over, other, other_over), shard
+    late1, lanes2, context, late_both = sync(
+        late1, lanes2, context, jnp.concatenate([late0, late1], axis=0)
+    )
+
+    feed1, late2, late3 = ring(feed_send, 1), ring(late1, 1), ring(late0, -1)
+    late_lanes01, feed0_lanes = all_lanes(late_both), all_lanes(feed0)
+    (
+        qkv_low, self_low, self_logsum, partial, send, gains, qkv_full, output_full, normed_one,
+    ) = self_forward(
+        lanes0 + lanes1 + lanes2 + lanes3, places, (own, own_over, other, other_over), tables, shard
     )
     first_norm_gain, second_norm_gain, third_norm_gain = gains[0:1], gains[1:2], gains[2:3]
-    qkv = mm(normed_one, qkv_full)
-    qkv, late1, late_lanes0, feed1_over = sync(qkv, late1, late_lanes0, feed1_over)
-
-    late3, late2 = ring(late0, -1), ring(late1, 1)
-    late_lanes1, feed0_lanes = all_lanes(late1), all_lanes(feed0)
-    qkv_low, self_low, self_logsum = self_forward(qkv, tables)
-    partial, send = halves_of(self_low, output_full)
-    partial, send, late3, late2, late_lanes1, feed0_lanes = sync(
-        partial, send, late3, late2, late_lanes1, feed0_lanes
-    )
-
-    terms = with_core(partial, over_core(send))
-    far_term, feed3, late_lanes3 = over_half(terms[1]), ring(feed_send, -1), all_lanes(late3)
-    far_term, feed3, late_lanes3, feed_send = sync(
-        far_term, feed3, late_lanes3, feed_part(links.ring_at(2))
-    )
-
-    hidden_one, normed = norm_forward(own, terms[0], far_term, second_norm_gain)
-    normed_over, cotangent1, late_lanes2 = over_half(normed), ring(upstream, 1), all_lanes(late2)
-    normed_over, cotangent1, late_lanes2 = sync(normed_over, cotangent1, late_lanes2)
-
-    feed2, feed0_over_lanes, feed3_over = (
-        ring(feed_send, 2),
-        all_lanes(feed0_over),
-        over_half(feed3),
-    )
+    partial, send, feed1, late_lanes01, feed0_lanes, late_both = sync(
+        partial, send, feed1, late_lanes01, feed0_lanes, jnp.concatenate([late2, late3], axis=0)
+    )
+
+    recv = over_core(send)
+    far_term = over_half((partial + recv.astype(F32)).astype(BF16))
+    feed2, feed3, late_lanes23 = (
+        ring(feed_sends[1], 2),
+        ring(feed_sends[0], -1),
+        all_lanes(late_both),
+    )
+    far_term, late_lanes23, feed2, cotangents, x_send, y_send = sync(
+        far_term,
+        late_lanes23,
+        feed2,
+        jnp.concatenate([upstream, cotangent1], axis=0),
+        jnp.concatenate([feed0_over, feed1], axis=0),
+        jnp.concatenate([feed1, feed3], axis=0),
+    )
+    hidden_one, normed = pair_forward(second_norm_gain, own, own_over, partial, recv, far_term)
+
+    cotangent3, x_recv, y_recv = ring(upstream, -1), all_lanes(x_send), over_half(y_send)
+    late_rows = 2 * (shard + context_shard)
     plan = []
     for n in range(blocks):
         first = (n % 2) * 2 * (shard + context_shard)
@@ -690,67 +1020,91 @@
             start = first + 2 * shard + out * context_shard
             plan.append((n // 2, n, start, context_shard, 0, cols, 2, out * cols))
     cross_query_full, cross_output_full, context_full = place_pieces(
-        late_lanes0 + late_lanes1 + late_lanes2 + late_lanes3,
+        [part[: 2 * late_rows] for part in late_lanes01]
+        + [part[2 * late_rows :] for part in late_lanes01]
+        + [part[: 2 * late_rows] for part in late_lanes23]
+        + [part[2 * late_rows :] for part in late_lanes23],
         plan,
         places,
         [(width, cols)] * 2 + [(context_width, 2 * cols)],
     )
     context_low = mm(context, context_full).astype(BF16)
-    normed_two = spread_cores(normed, normed_over)
+    normed_two = jnp.concatenate([normed, over_core(normed)], axis=0)
     cross_query_low = mm(normed_two, cross_query_full).astype(BF16) * jnp.asarray(SCALE, BF16)
     cross_low, cross_logsum = cross_forward(cross_query_low, context_low, context_count)
     partial, send = halves_of(cross_low, cross_output_full)
-    partial, send, feed2, feed0_over_lanes, feed3_over = sync(
-        partial, send, feed2, feed0_over_lanes, feed3_over
-    )
-
-    terms = with_core(partial, over_core(send))
-    far_term, cotangent3, feed1_lanes = over_half(terms[1]), ring(upstream, -1), all_lanes(feed1)
-    far_term, cotangent3, feed1_lanes = sync(far_term, cotangent3, feed1_lanes)
-
-    hidden_two, normed0 = norm_forward(hidden_one, terms[0], far_term, third_norm_gain)
-    normed1, feed3_lanes, feed2_over = ring(normed0, 1), all_lanes(feed3), over_half(feed2)
-    normed1, feed3_lanes, feed2_over = sync(normed1, feed3_lanes, feed2_over)
-
-    normed2, feed2_lanes = ring(normed1, 1), all_lanes(feed2)
-    feed3_lanes_over = [feed3_over] + [over_half(value) for value in feed3_lanes[1:]]
-    normed2, feed2_lanes, feed3_lanes_over = sync(normed2, feed2_lanes, feed3_lanes_over)
-
-    normed3, feed1_over_lanes = ring(normed2, 1), all_lanes(feed1_over)
+    cotangents_core = over_core(cotangents)
+    partial, send, cotangent3, x_recv, y_recv, cotangents_core = sync(
+        partial, send, cotangent3, x_recv, y_recv, cotangents_core
+    )
+    feed0_over_lanes = [part[:shard] for part in x_recv]
+    feed1_lanes = [part[shard:] for part in x_recv]
+    feed1_over, feed3_over, feed3 = y_recv[:shard], y_recv[shard:], y_send[shard:]
+
+    recv = over_core(send)
+    far_term, cotangent2, feed3_lanes = over_half(for_half(partial, recv)), ring(cotangent1, 1), all_lanes(feed3)
+    far_term, cotangent2, feed3_lanes, x_send, y_send = sync(
+        far_term,
+        cotangent2,
+        feed3_lanes,
+        jnp.concatenate([feed1_over, feed2], axis=0),
+        jnp.concatenate([feed2, *feed3_lanes[1:]], axis=0),
+    )
+
+    hidden_two, normed0 = norm_forward(
+        own_rows, hidden_one, third_norm_gain, partial, recv, far_term
+    )
+    normed1, normed3 = ring(normed0, 1), ring(normed0, -1)
+    x_recv, y_recv = all_lanes(x_send), over_half(y_send)
+    core0 = over_core(jnp.concatenate([cotangent3, cotangent2, normed0], axis=0))
+    normed1, normed3, x_recv, y_recv, core0 = sync(normed1, normed3, x_recv, y_recv, core0)
+    feed1_over_lanes = [part[:shard] for part in x_recv]
+    feed2_lanes = [part[shard:] for part in x_recv]
+    feed2_over = y_recv[:shard]
+    feed3_lanes_over = [feed3_over] + [
+        y_recv[shard * n : shard * (n + 1)] for n in range(1, lane_count)
+    ]
+
+    normed2 = ring(normed1, 1)
     feed2_lanes_over = [feed2_over] + [over_half(value) for value in feed2_lanes[1:]]
-    normed3, feed1_over_lanes, feed2_lanes_over = sync(normed3, feed1_over_lanes, feed2_lanes_over)
-
-    normed_mine = jnp.concatenate([normed0, normed1, normed2, normed3], axis=0)
-    normed_three = jnp.concatenate([normed_mine, over_core(normed_mine)], axis=0)
-    cotangent2 = ring(cotangent1, 1)
-    plan = []
-    pieces = []
-    for back, groups in (
-        (0, (feed0_lanes, feed0_over_lanes)),
-        (1, (feed1_lanes, feed1_over_lanes)),
-        (2, (feed2_lanes, feed2_lanes_over)),
-        (3, (feed3_lanes, feed3_lanes_over)),
-    ):
-        for there, group in enumerate(groups):
-            for turn, piece in enumerate(group):
-                spot = (back * lane_count + turn) * 2 + there
-                for out in range(3):
-                    plan.append((len(pieces), spot, 0, shard, out * hidden, hidden, out, 0))
-                pieces.append(piece)
-    gate_full, up_full, down_full = place_pieces(pieces, plan, places, [(width, hidden)] * 3)
-    gate_value = mm(normed_three, gate_full)
-    up_value = mm(normed_three, up_full)
-    sigmoid_gate = jax.nn.sigmoid(gate_value)
-    silu_gate = gate_value * sigmoid_gate
-    feed_low = (silu_gate * up_value).astype(BF16)
-    gate_value, up_value, feed_low, cotangent2 = sync(gate_value, up_value, feed_low, cotangent2)
+    core1 = over_core(jnp.concatenate([normed1, normed3], axis=0))
+    normed2, feed2_lanes_over, core1 = sync(normed2, feed2_lanes_over, core1)
+
+    core2 = over_core(normed2)
+    pieces = [
+        piece
+        for lanes_pieces, over_pieces in (
+            (feed0_lanes, feed0_over_lanes),
+            (feed1_lanes, feed1_over_lanes),
+            (feed2_lanes, feed2_lanes_over),
+            (feed3_lanes, feed3_lanes_over),
+        )
+        for piece in [part for both in zip(lanes_pieces, over_pieces) for part in both]
+    ]
+    held = [
+        core0, core1, core2, normed0, normed1, normed3, normed2,
+        cotangents_core, cotangents, cotangent3, cotangent2,
+    ]
+    feed_low, both_low, send, mine, normed_three, upstream_all, down_full = feed_forward(
+        pieces,
+        places,
+        held,
+        [(0, 2), (1, 0), (1, 1), (2, 0), (3, 0), (4, 0), (5, 0), (6, 0)],
+        [(7, 0), (7, 1), (0, 0), (0, 1), (8, 0), (8, 1), (9, 0), (10, 0)],
+        shard,
+        own_rows,
+    )
+    feed_low, both_low, send, mine, normed_three, upstream_all, down_full = sync(
+        feed_low, both_low, send, mine, normed_three, upstream_all, down_full
+    )
 
     def ring_halves(left, weights):
         count = RING * own_rows
-        return mm_nt(left[:count], weights), mm_nt(left[count:], weights).astype(BF16)
+        return mm_nt(left[count:], weights), mm_nt(left[:count], weights).astype(BF16)
 
     def block_of(mine, recv, back):
-        part = slice(back * own_rows, (back + 1) * own_rows)
+        spot = (0, 1, 3, 2)[back]
+        part = slice(spot * own_rows, (spot + 1) * own_rows)
         return mine[part] + recv[part].astype(F32)
 
     def lanes_block(grads, turn):
@@ -779,14 +1133,14 @@
         return [lanes_block(grads, turn) for turn in range(1, lane_count)]
 
     def lanes_second(grads, recv):
-        total = (lanes_block(grads, 0).astype(F32) + recv.astype(F32)).reshape(2, 2, shard, hidden)
+        total = (lanes_block(grads, 0).astype(F32) + recv.astype(F32)).reshape(2, 2, shard, -1)
         keep = lax.dynamic_index_in_dim(total, half, 1, keepdims=False)
         send = lax.dynamic_index_in_dim(total, 1 - half, 1, keepdims=False)
         return keep, send.astype(BF16)
 
     def halves_second(grads, recv):
         total = (halves_block(grads, half).astype(F32) + recv.astype(F32)).reshape(
-            2, lane_count, shard, hidden
+            2, lane_count, shard, -1
         )
         keep, *send = [
             lax.dynamic_index_in_dim(total, links.lane_at(turn), 1, keepdims=False)
@@ -804,230 +1158,204 @@
             axis=0,
         )
 
-    mine = jnp.concatenate([upstream, cotangent1, cotangent2, cotangent3], axis=0)
-    upstream_all = jnp.concatenate([mine, over_core(mine)], axis=0)
+    recv = over_core(send)
+    down_grad = mm_tn(upstream_all, feed_low).astype(BF16)
+    recv, mine, both_low, normed_three, feed_low, down_grad = sync(
+        recv, mine, both_low, normed_three, feed_low, down_grad
+    )
+    mine, recv, both_low, normed_three, down_grad, down_lanes, down_halves, ring_low = sync(
+        mine,
+        recv,
+        both_low,
+        normed_three,
+        down_grad,
+        lanes_terms(down_grad),
+        halves_block(down_grad, 1 - half),
+        block_of(mine, recv, 2).astype(BF16),
+    )
+
+    two = ring(ring_low, -1)
+    down_lanes, down_halves = links.sum_lanes(down_lanes), over_half(down_halves)
+    both_grad = mm_tn(normed_three, both_low).astype(BF16)
     out_mine, out_send = ring_halves(feed_low, down_full)
-    upstream_all, out_mine, out_send = sync(upstream_all, out_mine, out_send)
-
+    two, both_grad, down_lanes, down_halves, out_mine, out_send, three = sync(
+        two,
+        both_grad,
+        down_lanes,
+        down_halves,
+        out_mine,
+        out_send,
+        block_of(mine, recv, 3).astype(BF16),
+    )
+
+    three = ring(three, 1)
+    one = ring((block_of(mine, recv, 1) + two.astype(F32)).astype(BF16), -1)
+    both_lanes = links.sum_lanes(lanes_terms(both_grad))
+    both_halves = over_half(halves_block(both_grad, 1 - half))
     out_recv = over_core(out_send)
-    down_grad = mm_tn(upstream_all, feed_low).astype(BF16)
-    down_grad, out_recv, down_lanes, down_halves = sync(
-        down_grad, out_recv, lanes_terms(down_grad), halves_block(down_grad, 1 - half)
-    )
-
-    out_two = ring(block_of(out_mine, out_recv, 2).astype(BF16), -1)
-    down_lanes, down_halves = links.sum_lanes(down_lanes), over_half(down_halves)
-    feed_grad = mm(upstream_all, down_full).astype(BF16).astype(F32)
-    gate_low = (
-        feed_grad * up_value * sigmoid_gate * (1.0 + gate_value * (1.0 - sigmoid_gate))
-    ).astype(BF16)
-    up_low = (feed_grad * silu_gate).astype(BF16)
-    gate_low, up_low, out_two, down_lanes, down_halves = sync(
-        gate_low, up_low, out_two, down_lanes, down_halves
-    )
-
-    count = RING * own_rows
-    send = (mm_nt(gate_low[count:], gate_full) + mm_nt(up_low[count:], up_full)).astype(BF16)
-    (send,) = sync(send)
-    recv = over_core(send)
-    mine = mm_nt(gate_low[:count], gate_full) + mm_nt(up_low[:count], up_full)
-    recv, mine = sync(recv, mine)
-
-    two = ring(block_of(mine, recv, 2).astype(BF16), -1)
-    gate_grad = mm_tn(normed_three, gate_low).astype(BF16)
-    up_grad = mm_tn(normed_three, up_low).astype(BF16)
-    two, gate_grad, up_grad, gate_lanes, up_halves = sync(
-        two, gate_grad, up_grad, lanes_terms(gate_grad), halves_block(up_grad, 1 - half)
-    )
-
-    one = ring((block_of(mine, recv, 1) + two.astype(F32)).astype(BF16), -1)
-    gate_lanes, up_halves = links.sum_lanes(gate_lanes), over_half(up_halves)
-    lanes_keep, lanes_move = lanes_second(down_grad, down_lanes)
-    halves_keep, halves_move = halves_second(down_grad, down_halves)
-    three_send = block_of(mine, recv, 3).astype(BF16)
-    one, gate_lanes, up_halves, gate_halves, up_lanes, lanes_move, halves_move, three_send = sync(
+    down_keep, down_move = lanes_second(down_grad, down_lanes)
+    down_late_keep, down_late_move = halves_second(down_grad, down_halves)
+    one, three, both_lanes, both_halves, out_recv, out_low, downs = sync(
         one,
-        gate_lanes,
-        up_halves,
-        halves_block(gate_grad, 1 - half),
-        lanes_terms(up_grad),
-        lanes_move,
-        halves_move,
-        three_send,
-    )
-
-    three = ring(three_send, 1)
-    up_lanes, gate_halves = links.sum_lanes(up_lanes), over_half(gate_halves)
-    gate_keep, gate_move = lanes_second(gate_grad, gate_lanes)
-    up_late_keep, up_late_move = halves_second(up_grad, up_halves)
-    three, up_lanes, gate_halves, gate_keep, gate_move, up_late_keep, up_late_move = sync(
-        three, up_lanes, gate_halves, gate_keep, gate_move, up_late_keep, up_late_move
-    )
+        three,
+        both_lanes,
+        both_halves,
+        out_recv,
+        [block_of(out_mine, out_recv, back).astype(BF16) for back in (2, 3)],
+        (down_keep, down_move, down_late_keep, down_late_move),
+    )
+    down_keep, down_move, down_late_keep, down_late_move = downs
 
     hidden_two_grad, low, third_gain_grad = norm_backward(
         hidden_two, third_norm_gain, upstream, mine, recv, one, three
     )
     low_over = over_half(low)
-    out_one = ring((block_of(out_mine, out_recv, 1) + out_two.astype(F32)).astype(BF16), -1)
-    up_late_move, halves_move = links.sum_lanes(up_late_move), links.sum_lanes(halves_move)
-    out_send = block_of(out_mine, out_recv, 3).astype(BF16)
-    low_over, out_one, up_late_move, halves_move, out_send = sync(
-        low_over, out_one, up_late_move, halves_move, out_send
-    )
-
-    lanes_move, gate_move, out_three = over_half(lanes_move), over_half(gate_move), ring(out_send, 1)
+    out_two = ring(out_low[0], -1)
+    both_keep, both_move = lanes_second(both_grad, both_lanes)
+    both_late_keep, both_late_move = halves_second(both_grad, both_halves)
+    low_over, low, out_two, both_keep, both_late_keep, x_send, y_send, out_one = sync(
+        low_over,
+        low,
+        out_two,
+        both_keep,
+        both_late_keep,
+        [jnp.concatenate(pair, axis=-1) for pair in zip(down_late_move, both_late_move)],
+        jnp.concatenate([down_move, both_move], axis=-1),
+        (block_of(out_mine, out_recv, 1) + out_two.astype(F32)).astype(BF16),
+    )
+
+    moved, late_sum, out_three, out_one = (
+        over_half(y_send),
+        links.sum_lanes(x_send),
+        ring(out_low[1], 1),
+        ring(out_one, -1),
+    )
     branch_two = spread_cores(low, low_over)
     cross_out_grad = mm(branch_two, cross_output_full).astype(BF16)
     cross_query_round, cross_key_back, cross_value_back = cross_backward(
         cross_query_low, context_low, cross_low, cross_out_grad, cross_logsum, context_count
     )
     partial, send = halves_of(cross_query_round, cross_query_full)
-    partial, send, lanes_move, gate_move, out_three, branch_two = sync(
-        partial, send, lanes_move, gate_move, out_three, branch_two
-    )
-    (recv,) = sync(over_core(send))
-
-    def part_of(grads, place):
-        count = grads.shape[0] // links.fsdp
-        return lax.dynamic_slice_in_dim(grads, place * count, count, 0)
-
-    def lanes_total(block, back, recv):
-        return block(links.place(back, 0)).astype(F32) + recv.astype(F32)
-
-    def lanes_send(block, back):
-        return links.sum_lanes(lambda turn: block(links.place(back, turn)))
-
-    def cross_block(place):
-        return jnp.concatenate([part_of(g, place) for g in cross_grads], axis=0)
-
-    def lanes_blocks(block, back):
-        return [block(links.place(back, turn)) for turn in range(1, lane_count)]
-
-    def out_of(values, back):
-        return lax.dynamic_index_in_dim(values, links.ring_at(back), 0, keepdims=False)
-
-    terms = with_core(partial, recv)
-    far_term = over_half(terms[1])
-    up_keep, up_move = lanes_second(up_grad, up_lanes)
-    gate_late_keep, gate_late_move = halves_second(gate_grad, gate_halves)
+    partial, send, moved, late_sum, out_three, out_one, branch_two = sync(
+        partial, send, moved, late_sum, out_three, out_one, branch_two
+    )
+    recv = over_core(send)
+    feed_mine = jnp.concatenate(
+        [
+            joined(down_keep, moved[..., :hidden], down_late_keep, late_sum[..., :hidden]),
+            joined(both_keep, moved[..., hidden:], both_late_keep, late_sum[..., hidden:]),
+        ],
+        axis=2,
+    )
+    ring_places = jnp.stack(
+        [links.place(back, turn) for back in range(RING) for turn in range(lane_count)]
+    )
+
+    def by_back(blocks):
+        rows = [blocks[back * lane_count : (back + 1) * lane_count] for back in range(RING)]
+        return [row[0] for row in rows], [row[1:] for row in rows]
+
+    def below(others, backs):
+        return [jnp.concatenate(parts, axis=0) for parts in zip(*[others[back] for back in backs])]
+
     cross_grads = [
         mm_tn(branch_two, cross_low).astype(BF16),
         mm_tn(normed_two, cross_query_round).astype(BF16),
         mm_tn(context, cross_key_back).astype(BF16),
         mm_tn(context, cross_value_back).astype(BF16),
     ]
-    far_term, cross_grads, up_move, gate_late_move, cross2 = sync(
-        far_term, cross_grads, up_move, gate_late_move, lanes_blocks(cross_block, 2)
-    )
-
-    hidden_one_grad, low, second_gain_grad = norm_backward(
-        hidden_one, second_norm_gain, hidden_two_grad, terms[0], far_term
-    )
-    low_over = over_half(low)
-    up_move, gate_late_move = over_half(up_move), links.sum_lanes(gate_late_move)
-    cross2 = links.sum_lanes(cross2)
-    low_over, cross2, up_move, gate_late_move, cross3, cross1 = sync(
-        low_over,
-        cross2,
-        up_move,
-        gate_late_move,
-        lanes_blocks(cross_block, 3),
-        lanes_blocks(cross_block, 1),
-    )
-
-    feed_mine = jnp.concatenate(
+    cross_own, cross_other = by_back(split_blocks(cross_grads, ring_places, True))
+    recv, feed_mine, feed_send, cross_own, cross_late, cross_most, backs = sync(
+        recv,
+        feed_mine,
         [
-            joined(lanes_keep, lanes_move, halves_keep, halves_move),
-            joined(gate_keep, gate_move, gate_late_keep, gate_late_move),
-            joined(up_keep, up_move, up_late_keep, up_late_move),
+            lax.dynamic_index_in_dim(feed_mine, links.ring_at(back), 0, keepdims=False)
+            for back in (1, 2, 3)
         ],
-        axis=2,
-    )
-    feed1_sum, feed3_sum = ring(out_of(feed_mine, 3), 1), ring(out_of(feed_mine, 1), -1)
-    cross3, cross1 = links.sum_lanes(cross3), links.sum_lanes(cross1)
-    branch_one = spread_cores(low, low_over)
+        cross_own,
+        below(cross_other, (0, 1)),
+        below(cross_other, (2, 3)),
+        (cross_key_back, cross_value_back),
+    )
+    cross_key_back, cross_value_back = backs
+
+    def out_of(values, back):
+        return lax.dynamic_index_in_dim(values, links.ring_at(back), 0, keepdims=False)
+
+    far_term = over_half((partial + recv.astype(F32)).astype(BF16))
+    feed1_sum, feed3_sum = ring(feed_send[2], 1), ring(feed_send[0], -1)
+    cross_most = links.sum_lanes(cross_most)
+    block_rows = cross_most.shape[0] // 2
+    far_term, feed1_sum, feed3_sum, cross_two, cross_three, cross_late = sync(
+        far_term,
+        feed1_sum,
+        feed3_sum,
+        (cross_own[2].astype(F32) + cross_most[:block_rows].astype(F32)).astype(BF16),
+        (cross_own[3].astype(F32) + cross_most[block_rows:].astype(F32)).astype(BF16),
+        cross_late,
+    )
+    hidden_one_grad, low, second_gain_grad = pair_backward(
+        second_norm_gain, hidden_one, hidden_two_grad, low_over, partial, recv, far_term
+    )
+
+    feed2_sum, cross_two = ring(feed_send[1], 2), ring(cross_two, -1)
+    cross_late = links.sum_lanes(cross_late)
+    branch_one = jnp.concatenate([low, over_core(low)], axis=0)
     self_out_grad = mm(branch_one, output_full).astype(BF16)
     qkv_round = self_backward(qkv_low, self_low, self_out_grad, self_logsum, tables)
     partial, send = halves_of(qkv_round, qkv_full)
-    feed_mine, branch_one, qkv_round, partial, send, feed1_sum, feed3_sum, cross3, cross1 = sync(
-        feed_mine, branch_one, qkv_round, partial, send, feed1_sum, feed3_sum, cross3, cross1
-    )
-    (recv,) = sync(over_core(send))
-
-    def self_block(place):
-        return jnp.concatenate([part_of(output_grad, place), part_of(qkv_grad, place)], axis=1)
-
-    terms = with_core(partial, recv)
-    far_term = over_half(terms[1])
-    cross_two = ring(lanes_total(cross_block, 2, cross2).astype(BF16), -1)
-    cross0 = links.sum_lanes(lanes_blocks(cross_block, 0))
+    partial, send, feed2_sum, cross_late, cross_two, qkv_round, branch_one = sync(
+        partial, send, feed2_sum, cross_late, cross_two, qkv_round, branch_one
+    )
     output_grad = mm_tn(branch_one, self_low).astype(BF16)
     qkv_grad = mm_tn(normed_one, qkv_round).astype(BF16)
+    self_own, self_other = by_back(split_blocks([output_grad, qkv_grad], ring_places, False))
+    cross_zero = cross_own[0].astype(F32) + cross_late[:block_rows].astype(F32)
+    cross_one = cross_own[1].astype(F32) + cross_late[block_rows:].astype(F32)
+    recv, self_own, self_other, cross_zero, cross_one, backs = sync(
+        over_core(send),
+        self_own,
+        self_other,
+        cross_zero,
+        (cross_one + cross_two.astype(F32)).astype(BF16),
+        (cross_key_back, cross_value_back),
+    )
+    cross_key_back, cross_value_back = backs
+
+    far_term = over_half(for_half(partial, recv))
+    cross_one, cross_three = ring(cross_one, -1), ring(cross_three, 1)
+    self2 = links.sum_lanes(self_other[2])
     context_term = (
         mm_nt(cross_key_back, context_full[:, :cols])
         + mm_nt(cross_value_back, context_full[:, cols:])
     )[:context_count]
-    far_term, cross0, cross_two, output_grad, qkv_grad, self2, context_send = sync(
+    context_recv = over_core(context_term.astype(BF16))
+    far_term, cross_one, cross_three, self2, context_term, context_recv, self_two = sync(
         far_term,
-        cross0,
-        cross_two,
-        output_grad,
-        qkv_grad,
-        lanes_blocks(self_block, 2),
-        context_term.astype(BF16),
-    )
-
-    self2 = links.sum_lanes(self2)
-    feed2_sum = ring(out_of(feed_mine, 2), 2)
-    context_recv = over_core(context_send)
+        cross_one,
+        cross_three,
+        self2,
+        context_term,
+        context_recv,
+        (self_own[2].astype(F32) + self2.astype(F32)).astype(BF16),
+    )
+
+    self3 = links.sum_lanes(self_other[3])
+    self_two = ring(self_two, -1)
+    context_low_sum = (context_term + context_recv.astype(F32)).astype(BF16)
+    context_over = over_half(context_low_sum)
     inputs_grad, _, first_gain_grad = norm_backward(
-        own, first_norm_gain, hidden_one_grad, terms[0], far_term
-    )
-    context_low_sum = (context_term + context_recv.astype(F32)).astype(BF16)
+        own, first_norm_gain, hidden_one_grad, partial, recv, far_term
+    )
+    layer_result = links.both_cores(
+        hidden_two + block_of(out_mine, out_recv, 0) + out_one.astype(F32) + out_three.astype(F32)
+    )
     gain_grads = jnp.concatenate([first_gain_grad, second_gain_grad, third_gain_grad], axis=0)
-    self2, feed2_sum, context_low_sum, gain_grads, inputs_grad, self3 = sync(
-        self2, feed2_sum, context_low_sum, gain_grads, inputs_grad, lanes_blocks(self_block, 3)
-    )
-
-    self3 = links.sum_lanes(self3)
-    self_two = ring(lanes_total(self_block, 2, self2).astype(BF16), -1)
-    context_over = over_half(context_low_sum)
-    gain_grads = gain_grads + over_core(gain_grads)
     gate_sum, up_sum, down_sum = spread(
         [out_of(feed_mine, 0), feed1_sum, feed2_sum, feed3_sum],
         jnp.stack([links.ring_at(back) for back in range(RING)]),
     )
-    layer_result = links.both_cores(
-        hidden_two + block_of(out_mine, out_recv, 0) + out_one.astype(F32) + out_three.astype(F32)
-    )
-    self3, self_two, context_over, gain_grads, layer_result, self1, cross_sends = sync(
-        self3,
-        self_two,
-        context_over,
-        gain_grads,
-        layer_result,
-        lanes_blocks(self_block, 1),
-        [
-            lanes_total(cross_block, 3, cross3).astype(BF16),
-            (lanes_total(cross_block, 1, cross1) + cross_two.astype(F32)).astype(BF16),
-        ],
-    )
-
-    self1 = links.sum_lanes(self1)
-    cross_three, cross_one = ring(cross_sends[0], 1), ring(cross_sends[1], -1)
-    context_grad = context_low_sum.astype(F32) + context_over.astype(F32)
-    inputs_result = links.both_cores(inputs_grad)
-    gain_over = over_half(gain_grads)
-    self1, cross_three, cross_one, gain_over, inputs_result, self0 = sync(
-        self1, cross_three, cross_one, gain_over, inputs_result, lanes_blocks(self_block, 0)
-    )
-
-    self0 = links.sum_lanes(self0)
-    self_one = ring((lanes_total(self_block, 1, self1) + self_two.astype(F32)).astype(BF16), -1)
-    self_three = ring(lanes_total(self_block, 3, self3).astype(BF16), 1)
-    cross_total = (
-        lanes_total(cross_block, 0, cross0) + cross_one.astype(F32) + cross_three.astype(F32)
-    )
+    cross_total = cross_zero + cross_one.astype(F32) + cross_three.astype(F32)
     sizes = (shard, shard, context_shard, context_shard)
     starts = [2 * sum(sizes[:n]) for n in range(4)]
     cross_total = jnp.concatenate(
@@ -1037,18 +1365,46 @@
         ],
         axis=1,
     )
+    context_grad = context_low_sum.astype(F32) + context_over.astype(F32)
+    self3, self_two, context_grad, layer_result, gain_grads, inputs_grad, feed_sums, cross_total, self_three = sync(
+        self3,
+        self_two,
+        context_grad,
+        layer_result,
+        gain_grads,
+        inputs_grad,
+        (gate_sum, up_sum, down_sum),
+        cross_total,
+        (self_own[3].astype(F32) + self3.astype(F32)).astype(BF16),
+    )
+    gate_sum, up_sum, down_sum = feed_sums
+
+    self1 = links.sum_lanes(self_other[1])
+    self_three = ring(self_three, 1)
+    gain_grads = gain_grads + over_core(gain_grads)
+    gain_grads = gain_grads + over_half(gain_grads)
     cross_keep, cross_recv = links.swap_halves(cross_total)
-    gain_grads = gain_grads + gain_over
+    self1, self_three, gain_grads, cross_recv, self_one = sync(
+        self1,
+        self_three,
+        gain_grads,
+        cross_recv,
+        (self_own[1].astype(F32) + self1.astype(F32) + self_two.astype(F32)).astype(BF16),
+    )
+
+    self0 = links.sum_lanes(self_other[0])
+    self_one = ring(self_one, -1)
     gain_ring = [slot(gain_grads, RING, links.ring_at(back)) for back in range(RING)]
     gain_two, gain_three = ring(gain_ring[2], -1), ring(gain_ring[3], 1)
-    self0, self_one, self_three, cross_recv, gain_two, gain_three = sync(
-        self0, self_one, self_three, cross_recv, gain_two, gain_three
-    )
-
+    inputs_result = links.both_cores(inputs_grad)
+    cross_sums = links.side_by_side(cross_keep, cross_recv)
+    self0, self_one, gain_two, gain_three, inputs_result, cross_sums = sync(
+        self0, self_one, gain_two, gain_three, inputs_result, cross_sums
+    )
     gain_one = ring(gain_ring[1] + gain_two, -1)
-    cross_sums = links.side_by_side(cross_keep, cross_recv)
+
     self_total = (
-        lanes_total(self_block, 0, self0) + self_one.astype(F32) + self_three.astype(F32)
+        self_own[0].astype(F32) + self0.astype(F32) + self_one.astype(F32) + self_three.astype(F32)
     )
     keep, recv = links.swap_halves(self_total.reshape(2, shard, 4 * cols))
     gain_grads = gain_ring[0] + gain_one + gain_three

time: 616 us -> 567 us (0.920)
  waiting for transfers between devices: 277 us -> 237 us
  Pallas kernels: 59.4 us -> 98.5 us
  matrix products: 75.4 us -> 40.4 us
  local copies, waits for them, and re-layouts: 55.9 us -> 39.6 us
    pallas_call x7 -> x9, Pallas kernels: 25 us -> 65.1 us  [the longest x1 25.5 us: feed_forward(): pl.pallas_call(functools.partial(feed_kernel, shard, own, len(held), (tup...]
    ppermute x29 -> x20, waiting for transfers between devices: 88.5 us -> 58.5 us  [lanes(): return lax.ppermute(self.begun(value), 'fsdp', pairs)]
    dot_general x8 -> x4, matrix products: 30 us -> 4.02 us  [mm(): lax.dot_general(left, right, (((1,), (0,)), ((), ())), preferred_element_...]
    unnamed x289 -> x241, local copies, waits for them, and re-layouts: 33.7 us -> 14.6 us
    ppermute x27 -> x19, waiting for transfers between devices: 62.2 us -> 48.3 us  [over_half(): return lax.ppermute(self.begun(value), 'ctx', [(0, 1), (1, 0)])]
    ppermute x33, starting transfers between devices: 38.2 us -> 50.6 us  [ring(): return lax.ppermute(self.begun(value), 'fsdp', pairs)]
    dot_general x16 -> x10, matrix products: 23.6 us -> 13 us  [mm_nt(): lax.dot_general(left, right, (((1,), (1,)), ((), ())), preferred_element_...]
    slice x8 -> x13, local copies, waits for them, and re-layouts: 0.46 us -> 10.4 us  [the longest x4 2.65 us: on_device(): part[2 * late_rows:]]
  transfers between devices with their start and end apart: 105 -> 90, of which waited for: 60 -> 52; matrix products, arithmetic and copies ran while one was open for 20% -> 18% of each run, Pallas kernels for 9% -> 12%
where the time goes in v3:
time: 567 us; the launch traced here: 558 us
  waiting for transfers between devices  237 us (42%)
  Pallas kernels  98.5 us (17%)
  starting transfers between devices  95.8 us (17%)
  other arithmetic  44.6 us (8%)
  matrix products  40.4 us (7%)
  local copies, waits for them, and re-layouts  39.6 us (7%)
    ppermute x33, waiting for transfers between devices, ring(): return lax.ppermute(self.begun(value), 'fsdp', pairs)  126 us
    ppermute x20, waiting for transfers between devices, lanes(): return lax.ppermute(self.begun(value), 'fsdp', pairs)  58.5 us
    ppermute x33, starting transfers between devices, ring(): return lax.ppermute(self.begun(value), 'fsdp', pairs)  50.6 us
    ppermute x19, waiting for transfers between devices, over_half(): return lax.ppermute(self.begun(value), 'ctx', [(0, 1), (1, 0)])  48.3 us
    pallas_call x1, Pallas kernels, feed_forward(): pl.pallas_call(functools.partial(feed_kernel, shard, own, len(held), (tup...  25.5 us
    dot_general x8, matrix products, mm_tn(): lax.dot_general(left, right, (((0,), (0,)), ((), ())), preferred_element_...  23.3 us
    ppermute x20, starting transfers between devices, lanes(): return lax.ppermute(self.begun(value), 'fsdp', pairs)  23.1 us
    pallas_call x1, Pallas kernels, self_forward(): pl.pallas_call(functools.partial(self_forward_kernel, shard), grid=(pairs...  22.4 us
  transfers between devices with their start and end apart: 90, of which 52 were waited for; matrix products, arithmetic and copies ran while one was open for 18% of the time, Pallas kernels for 12%

profile of v3, /device:TPU:0, one launch (start us, length us, event | category | flops | bytes accessed | tf_op | source)
XLA Modules:
  0.0 558.2 jit_solution(16122342778033758958)
XLA Ops:
  2.4 2.9 shard_map.296
  5.3 3.0 collective-permute-start
  12.6 4.1 collective-permute-done
  25.3 8.3 %collective-permute-done.3.refs_9_.over_ref = bf16[160,1536]{1,0:T(8,128)(2,1)S(1)} collective-permute-done((bf16[160,1536]{1,0:T(8,128)(2,1)S(1)}, bf16[160,1536]{1,0:T(8,128)(2,1)S(1)}, u32[]{:S(2)}, u32[]{:S(2)}) %collective-permute-start.3) | collective-permute-done | bytes 491552 | tf_op jit(solution)/shard_map/ppermute | solution.py:782
  33.6 4.1 collective-permute-done.1.refs_2_
  44.4 5.2 collective-permute-done.7
  49.6 3.3 collective-permute-done.6.refs_3_
  56.7 8.2 %collective-permute-done.11 = bf16[96,2304]{1,0:T(8,128)(2,1)S(1)} collective-permute-done((bf16[96,2304]{1,0:T(8,128)(2,1)S(1)}, bf16[96,2304]{1,0:T(8,128)(2,1)S(1)}, u32[]{:S(2)}, u32[]{:S(2)}) %collective-permute-start.11) | collective-permute-done | bytes 442400 | tf_op jit(solution)/shard_map/ppermute | solution.py:782
  64.9 2.8 collective-permute-done.10.refs_7_
  72.2 8.5 %collective-permute-done.12 = bf16[576,384]{1,0:T(8,128)(2,1)S(1)} collective-permute-done((bf16[576,384]{1,0:T(8,128)(2,1)S(1)}, bf16[576,384]{1,0:T(8,128)(2,1)S(1)}, u32[]{:S(2)}, u32[]{:S(2)}) %collective-permute-start.12) | collective-permute-done | bytes 442400 | tf_op jit(solution)/shard_map/ppermute | solution.py:774
  80.8 4.0 collective-permute-done.13.refs_5_
  86.0 3.8 collective-permute-start.18
  91.2 22.4 %shard_map.297 = (bf16[640,1152]{1,0:T(8,128)(2,1)}, bf16[640,384]{1,0:T(8,128)(2,1)}, f32[640,384]{1,0:T(8,128)}, f32[320,1536]{1,0:T(8,128)}, bf16[320,1536]{1...) custom-call(s32[16]{0:T(128)} %xor_add_fusion.place_ref, ...), custom_call_target="tpu_custom_call" | custom-call | flops 3649044480 | bytes 6684672 | tf_op jit(solution)/shard_map/pallas_call | solution.py:291
  120.2 4.1 collective-permute-start.23
  126.8 8.0 %collective-permute-done.23 = bf16[96,2304]{1,0:T(8,128)(2,1)S(1)} collective-permute-done((bf16[96,2304]{1,0:T(8,128)(2,1)S(1)}, bf16[96,2304]{1,0:T(8,128)(2,1)S(1)}, u32[]{:S(2)}, u32[]{:S(2)}) %collective-permute-start.23) | collective-permute-done | bytes 442400 | tf_op jit(solution)/shard_map/ppermute | solution.py:774
  136.1 16.1 %collective-permute-done.22 = bf16[96,2304]{1,0:T(8,128)(2,1)S(1)} collective-permute-done((bf16[96,2304]{1,0:T(8,128)(2,1)S(1)}, bf16[96,2304]{1,0:T(8,128)(2,1)S(1)}, u32[]{:S(2)}, u32[]{:S(2)}) %collective-permute-start.22) | collective-permute-done | bytes 442400 | tf_op jit(solution)/shard_map/ppermute | solution.py:774
  155.5 2.5 shard_map.298
  158.0 3.5 collective-permute-start.25
  169.6 3.5 shard_map.300
  179.7 8.5 %collective-permute-done.32.refs_14_ = bf16[96,2304]{1,0:T(8,128)(2,1)S(1)} collective-permute-done((bf16[96,2304]{1,0:T(8,128)(2,1)S(1)}, bf16[96,2304]{1,0:T(8,128)(2,1)S(1)}, u32[]{:S(2)}, u32[]{:S(2)}) %collective-permute-start.32) | collective-permute-done | bytes 442400 | tf_op jit(solution)/shard_map/ppermute | solution.py:779
  188.4 4.0 collective-permute-done.31.refs_26_
  198.7 3.4 collective-permute-start.34
  203.1 11.1 %collective-permute-done.33.refs_20_ = bf16[160,1536]{1,0:T(8,128)(2,1)S(1)} collective-permute-done((bf16[160,1536]{1,0:T(8,128)(2,1)S(1)}, bf16[160,1536]{1,0:T(8,128)(2,1)S(1)}, u32[]{:S(2)}, u32[]{:S(2)}) %collective-permute-start.33) | collective-permute-done | bytes 491552 | tf_op jit(solution)/shard_map/ppermute | solution.py:774
  214.2 8.2 %collective-permute-done.34.refs_21_ = bf16[160,1536]{1,0:T(8,128)(2,1)S(1)} collective-permute-done((bf16[160,1536]{1,0:T(8,128)(2,1)S(1)}, bf16[160,1536]{1,0:T(8,128)(2,1)S(1)}, u32[]{:S(2)}, u32[]{:S(2)}) %collective-permute-start.34) | collective-permute-done | bytes 491552 | tf_op jit(solution)/shard_map/ppermute | solution.py:774
  225.1 2.3 collective-permute-start.38
  228.4 7.5 %collective-permute-done.39.refs_11_ = bf16[96,2304]{1,0:T(8,128)(2,1)S(1)} collective-permute-done((bf16[96,2304]{1,0:T(8,128)(2,1)S(1)}, bf16[96,2304]{1,0:T(8,128)(2,1)S(1)}, u32[]{:S(2)}, u32[]{:S(2)}) %collective-permute-start.39) | collective-permute-done | bytes 442400 | tf_op jit(solution)/shard_map/ppermute | solution.py:782
  235.9 4.5 collective-permute-done.38.refs_22_
  243.2 25.5 %shard_map.302 = (bf16[1280,768]{1,0:T(8,128)(2,1)}, bf16[1280,1536]{1,0:T(8,128)(2,1)}, bf16[640,1536]{1,0:T(8,128)(2,1)}, f32[640,1536]{1,0:T(8,128)}, bf16[12...) custom-call(s32[16]{0:T(128)} %xor_add_fusion.place_ref, bf16[96,2304]{1,0:T(8,128)(2,1)} %copy-done.77, ...), custom_call_target="tpu_custom_call" | custom-call | flops 15099494400 | bytes 22806528 | tf_op jit(solution)/shard_map/pallas_call | solution.py:621
  269.0 6.2 %convolution_convert_fusion.2 = bf16[1536,768]{1,0:T(8,128)(2,1)S(1)} fusion(bf16[1280,1536]{1,0:T(8,128)(2,1)} %get-tuple-element.525, bf16[1280,768]{1,0:T(8,128)(2,1)} %get-tuple-element.541), kind=kOutput, calls=%fused_computation.2 | convolution fusion | flops 3021078528 | bytes 8257536 | tf_op jit(solution)/shard_map/dot_general | solution.py:26
  282.9 6.6 %convolution_convert_fusion.1 = bf16[1536,1536]{1,0:T(8,128)(2,1)S(1)} fusion(bf16[1280,1536]{1,0:T(8,128)(2,1)S(1)} %copy-done.117, bf16[1280,1536]{1,0:T(8,128)(2,1)S(1)} %copy-done.116), kind=kOutput, calls=%fused_computation.1 | convolution fusion | flops 6042157056 | bytes 12582912 | tf_op jit(solution)/shard_map/dot_general | solution.py:26
  289.7 4.5 collective-permute-done.43
  298.9 3.9 collective-permute-start.46
  306.2 8.4 %collective-permute-done.47.refs_3_ = bf16[160,1536]{1,0:T(8,128)(2,1)S(1)} collective-permute-done((bf16[160,1536]{1,0:T(8,128)(2,1)S(1)}, bf16[160,1536]{1,0:T(8,128)(2,1)S(1)}, u32[]{:S(2)}, u32[]{:S(2)}) %collective-permute-start.47) | collective-permute-done | bytes 491552 | tf_op jit(solution)/shard_map/ppermute | solution.py:774
  314.6 7.9 %collective-permute-done.46.refs_2_ = bf16[160,1536]{1,0:T(8,128)(2,1)S(1)} collective-permute-done((bf16[160,1536]{1,0:T(8,128)(2,1)S(1)}, bf16[160,1536]{1,0:T(8,128)(2,1)S(1)}, u32[]{:S(2)}, u32[]{:S(2)}) %collective-permute-start.46) | collective-permute-done | bytes 491552 | tf_op jit(solution)/shard_map/ppermute | solution.py:774
  330.4 2.3 shard_map.303
  335.3 4.3 collective-permute-done.52
  339.6 2.2 add_convert_fusion.8
  341.8 3.2 collective-permute-done.51.over_ref
  353.5 9.7 %shard_map.304 = (bf16[640,384]{1,0:T(8,128)(2,1)S(1)}, bf16[256,384]{1,0:T(8,128)(2,1)S(1)}, bf16[256,384]{1,0:T(8,128)(2,1)S(1)}) custom-call(bf16[640,384]{1,0:T(8,128)(2,1)S(1)} %copy-done.39, bf16[256,768]{1,0:T(8,128)(2,1)S(1)} %convolution_convert_fusion.15.k_ref.v_ref, bf16[256,768]{1,0:T(8,128)(2,1)S(1)} %convolution_convert_fusion.15.k_ref.v_ref, ...), custom_call_target="tpu_custom_call" | custom-call | flops 629145600 | bytes 4718592 | tf_op jit(solution)/shard_map/pallas_call | solution.py:451
  366.3 2.4 convolution_convert_fusion.5.refs_1_
  384.5 17.5 %collective-permute-done.62 = bf16[1152,384]{1,0:T(8,128)(2,1)} collective-permute-done((bf16[1152,384]{1,0:T(8,128)(2,1)}, bf16[1152,384]{1,0:T(8,128)(2,1)}, u32[]{:S(2)}, u32[]{:S(2)}) %collective-permute-start.62) | collective-permute-done | bytes 884768 | tf_op jit(solution)/shard_map/ppermute | solution.py:779
  402.0 2.5 add_convert_fusion.16
  405.8 3.8 shard_map.306
  412.5 2.7 collective-permute-start.66
  418.7 12.2 %shard_map.307 = bf16[640,1152]{1,0:T(8,128)(2,1)S(1)} custom-call(bf16[640,1152]{1,0:T(8,128)(2,1)S(1)} %copy-done.41, bf16[640,384]{1,0:T(8,128)(2,1)S(1)} %copy-done.40, bf16[640,384]{1,0:T(8,128)(2,1)S(1)} %convolution_convert_fusion.12.do_ref, f32[640,384]{1,0:T(8,128)S(1)} %copy-done.42, f32[640,128]{1,0:T(8,128)S(1)} %copy-done.31, ...), custom_call_target="tpu_custom_call" | custom-call | flops 1572864000 | bytes 8847360 | tf_op jit(solution)/shard_map/pallas_call | solution.py:427
  431.0 4.6 convolution_convert_fusion.7
  437.0 7.8 %collective-permute-done.64.refs_2_ = bf16[96,2304]{1,0:T(8,128)(2,1)S(1)} collective-permute-done((bf16[96,2304]{1,0:T(8,128)(2,1)S(1)}, bf16[96,2304]{1,0:T(8,128)(2,1)S(1)}, u32[]{:S(2)}, u32[]{:S(2)}) %collective-permute-start.64) | collective-permute-done | bytes 442400 | tf_op jit(solution)/shard_map/ppermute | solution.py:774
  446.2 4.7 convolution_convert_fusion.refs_1_
  450.8 2.4 shard_map.308
  453.2 3.2 shard_map.310
  460.2 2.9 collective-permute-start.69
  464.5 8.1 %collective-permute-done.71 = bf16[192,1536]{1,0:T(8,128)(2,1)S(1)} collective-permute-done((bf16[192,1536]{1,0:T(8,128)(2,1)S(1)}, bf16[192,1536]{1,0:T(8,128)(2,1)S(1)}, u32[]{:S(2)}, u32[]{:S(2)}) %collective-permute-start.71) | collective-permute-done | bytes 589856 | tf_op jit(solution)/shard_map/ppermute | solution.py:779
  474.2 7.4 %collective-permute-done.69 = bf16[576,384]{1,0:T(8,128)(2,1)S(1)} collective-permute-done((bf16[576,384]{1,0:T(8,128)(2,1)S(1)}, bf16[576,384]{1,0:T(8,128)(2,1)S(1)}, u32[]{:S(2)}, u32[]{:S(2)}) %collective-permute-start.69) | collective-permute-done | bytes 442400 | tf_op jit(solution)/shard_map/ppermute | solution.py:774
  483.9 2.9 collective-permute-start.74
  486.9 2.9 shard_map.309
  491.3 4.7 collective-permute-done.73
  506.5 2.4 collective-permute-done.80
  508.9 5.6 collective-permute-done.77
  516.6 2.6 collective-permute-done.78
  519.2 2.2 copy.38
  521.4 3.8 collective-permute-start.84
  529.1 11.5 %collective-permute-done.83 = bf16[192,1536]{1,0:T(8,128)(2,1)S(1)} collective-permute-done((bf16[192,1536]{1,0:T(8,128)(2,1)}, bf16[192,1536]{1,0:T(8,128)(2,1)S(1)}, u32[]{:S(2)}, u32[]{:S(2)}) %collective-permute-start.83) | collective-permute-done | bytes 589856 | tf_op jit(solution)/shard_map/ppermute | solution.py:774
  540.6 2.2 collective-permute-start.88
  550.2 4.7 collective-permute-done.87
  (538 shorter events, 175.3 us)
Async XLA Ops:
  9.1 16.1 %collective-permute-start.4 = (bf16[160,1536]{1,0:T(8,128)(2,1)}, bf16[160,1536]{1,0:T(8,128)(2,1)S(1)}, u32[]{:S(2)}, u32[]{:S(2)}) collective-permute-start(bf16[160,1536]{1,0:T(8,128)(2,1)} %dynamic-slice_bitcast_fusion.6.skip_ref), channel_id=1, source_target_pairs={{0,8},{4,12},{8,16},{12,20},{16,24},{20,28},{24,0},{28,4},{1,9},{5... | collective-permute-start | bytes 1474568 | tf_op jit(solution)/shard_map/ppermute | solution.py:774
  18.5 19.1 %collective-permute-start.1 = (bf16[208,1536]{1,0:T(8,128)(2,1)S(1)}, bf16[208,1536]{1,0:T(8,128)(2,1)}, u32[]{:S(2)}, u32[]{:S(2)}) collective-permute-start(bf16[208,1536]{1,0:T(8,128)(2,1)S(1)} %pad_maximum_fusion.20.refs_0_), channel_id=1, source_target_pairs={{0,8},{4,12},{8,16},{12,20},{16,24},{20,28},{24,0},{28,4},{1,9},{5... | collective-permute-start | bytes 1916936 | tf_op jit(solution)/shard_map/ppermute | solution.py:774
  20.4 17.3 %collective-permute-start.2 = (bf16[208,1536]{1,0:T(8,128)(2,1)S(1)}, bf16[208,1536]{1,0:T(8,128)(2,1)}, u32[]{:S(2)}, u32[]{:S(2)}) collective-permute-start(bf16[208,1536]{1,0:T(8,128)(2,1)S(1)} %pad_maximum_fusion.20.refs_0_), channel_id=1, source_target_pairs={{0,4},{4,0},{8,12},{12,8},{16,20},{20,16},{24,28},{28,24},{1,5},{5... | collective-permute-start | bytes 1916936 | tf_op jit(solution)/shard_map/ppermute | solution.py:779
  37.7 15.2 %collective-permute-start.6 = (bf16[208,1536]{1,0:T(8,128)(2,1)}, bf16[208,1536]{1,0:T(8,128)(2,1)S(1)}, u32[]{:S(2)}, u32[]{:S(2)}) collective-permute-start(bf16[208,1536]{1,0:T(8,128)(2,1)} %collective-permute-done.1.refs_2_), channel_id=1, source_target_pairs={{0,4},{4,0},{8,12},{12,8},{16,20},{20,16},{24,28},{28,24},{1,5},{5... | collective-permute-start | bytes 1916936 | tf_op jit(solution)/shard_map/ppermute | solution.py:779
  39.2 14.7 %collective-permute-start.5 = (bf16[208,1536]{1,0:T(8,128)(2,1)S(1)}, bf16[208,1536]{1,0:T(8,128)(2,1)S(1)}, u32[]{:S(2)}, u32[]{:S(2)}) collective-permute-start(bf16[208,1536]{1,0:T(8,128)(2,1)S(1)} %pad_maximum_fusion.20.refs_0_), channel_id=1, source_target_pairs={{0,24},{4,28},{8,0},{12,4},{16,8},{20,12},{24,16},{28,20},{1,25},{... | collective-permute-start | bytes 1916936 | tf_op jit(solution)/shard_map/ppermute | solution.py:774
  53.9 13.8 %collective-permute-start.10 = (bf16[208,1536]{1,0:T(8,128)(2,1)S(1)}, bf16[208,1536]{1,0:T(8,128)(2,1)S(1)}, u32[]{:S(2)}, u32[]{:S(2)}) collective-permute-start(bf16[208,1536]{1,0:T(8,128)(2,1)S(1)} %collective-permute-done.5.refs_6_), channel_id=1, source_target_pairs={{0,4},{4,0},{8,12},{12,8},{16,20},{20,16},{24,28},{28,24},{1,5},{5... | collective-permute-start | bytes 1916936 | tf_op jit(solution)/shard_map/ppermute | solution.py:779
  54.5 15.8 %collective-permute-start.9 = (bf16[208,1536]{1,0:T(8,128)(2,1)}, bf16[208,1536]{1,0:T(8,128)(2,1)S(1)}, u32[]{:S(2)}, u32[]{:S(2)}) collective-permute-start(bf16[208,1536]{1,0:T(8,128)(2,1)} %collective-permute-done.1.refs_2_), channel_id=1, source_target_pairs={{0,8},{4,12},{8,16},{12,20},{16,24},{20,28},{24,0},{28,4},{1,9},{5... | collective-permute-start | bytes 1916936 | tf_op jit(solution)/shard_map/ppermute | solution.py:774
  70.3 14.5 %collective-permute-start.13 = (bf16[208,1536]{1,0:T(8,128)(2,1)S(1)}, bf16[208,1536]{1,0:T(8,128)(2,1)S(1)}, u32[]{:S(2)}, u32[]{:S(2)}) collective-permute-start(bf16[208,1536]{1,0:T(8,128)(2,1)S(1)} %collective-permute-done.9.refs_4_), channel_id=1, source_target_pairs={{0,4},{4,0},{8,12},{12,8},{16,20},{20,16},{24,28},{28,24},{1,5},{5... | collective-permute-start | bytes 1916936 | tf_op jit(solution)/shard_map/ppermute | solution.py:779
  84.8 30.1 %collective-permute-start.15 = (bf16[1152,384]{1,0:T(8,128)(2,1)S(1)}, bf16[1152,384]{1,0:T(8,128)(2,1)}, u32[]{:S(2)}, u32[]{:S(2)}) collective-permute-start(bf16[1152,384]{1,0:T(8,128)(2,1)S(1)} %pad_maximum_fusion.8), channel_id=1, source_target_pairs={{0,4},{4,0},{8,12},{12,8},{16,20},{20,16},{24,28},{28,24},{1,5},{5... | collective-permute-start | bytes 2654216 | tf_op jit(solution)/shard_map/ppermute | solution.py:779
  86.0 27.6 %collective-permute-start.17 = (bf16[576,384]{1,0:T(8,128)(2,1)S(1)}, bf16[576,384]{1,0:T(8,128)(2,1)S(1)}, u32[]{:S(2)}, u32[]{:S(2)}) collective-permute-start(bf16[576,384]{1,0:T(8,128)(2,1)S(1)} %collective-permute-done.12), channel_id=1, source_target_pairs={{0,8},{4,12},{8,16},{12,20},{16,24},{20,28},{24,0},{28,4},{1,9},{5... | collective-permute-start | bytes 1327112 | tf_op jit(solution)/shard_map/ppermute | solution.py:774
  86.0 27.6 %collective-permute-start.18 = (bf16[576,384]{1,0:T(8,128)(2,1)S(1)}, bf16[576,384]{1,0:T(8,128)(2,1)}, u32[]{:S(2)}, u32[]{:S(2)}) collective-permute-start(bf16[576,384]{1,0:T(8,128)(2,1)S(1)} %pad_maximum_fusion.25), channel_id=1, source_target_pairs={{0,24},{4,28},{8,0},{12,4},{16,8},{20,12},{24,16},{28,20},{1,25},{... | collective-permute-start | bytes 1327112 | tf_op jit(solution)/shard_map/ppermute | solution.py:774
  90.3 24.5 %collective-permute-start.16 = (bf16[96,2304]{1,0:T(8,128)(2,1)}, bf16[96,2304]{1,0:T(8,128)(2,1)}, u32[]{:S(2)}, u32[]{:S(2)}) collective-permute-start(bf16[96,2304]{1,0:T(8,128)(2,1)} %copy-done.77), channel_id=1, source_target_pairs={{0,4},{4,0},{8,12},{12,8},{16,20},{20,16},{24,28},{28,24},{1,5},{5... | collective-permute-start | bytes 1327112 | tf_op jit(solution)/shard_map/ppermute | solution.py:779
  91.2 23.7 %collective-permute-start.14 = (bf16[96,2304]{1,0:T(8,128)(2,1)}, bf16[96,2304]{1,0:T(8,128)(2,1)}, u32[]{:S(2)}, u32[]{:S(2)}) collective-permute-start(bf16[96,2304]{1,0:T(8,128)(2,1)} %pad_maximum_fusion.24), channel_id=1, source_target_pairs={{0,8},{4,12},{8,16},{12,20},{16,24},{20,28},{24,0},{28,4},{1,9},{5... | collective-permute-start | bytes 1327112 | tf_op jit(solution)/shard_map/ppermute | solution.py:774
  118.0 34.3 %collective-permute-start.20 = (bf16[320,1536]{1,0:T(8,128)(2,1)S(1)}, bf16[320,1536]{1,0:T(8,128)(2,1)S(1)}, u32[]{:S(2)}, u32[]{:S(2)}) collective-permute-start(bf16[320,1536]{1,0:T(8,128)(2,1)S(1)} %add_convert_fusion.1), channel_id=1, source_target_pairs={{0,2},{2,0},{1,3},{3,1},{4,6},{6,4},{5,7},{7,5},{8,10},{10,8},{9,1... | collective-permute-start | bytes 2949128 | tf_op jit(solution)/shard_map/ppermute | solution.py:782
  120.2 14.6 %collective-permute-start.23 = (bf16[96,2304]{1,0:T(8,128)(2,1)S(1)}, bf16[96,2304]{1,0:T(8,128)(2,1)S(1)}, u32[]{:S(2)}, u32[]{:S(2)}) collective-permute-start(bf16[96,2304]{1,0:T(8,128)(2,1)S(1)} %copy-done.79), channel_id=1, source_target_pairs={{0,24},{4,28},{8,0},{12,4},{16,8},{20,12},{24,16},{28,20},{1,25},{... | collective-permute-start | bytes 1327112 | tf_op jit(solution)/shard_map/ppermute | solution.py:774
  124.2 28.0 %collective-permute-start.22 = (bf16[96,2304]{1,0:T(8,128)(2,1)S(1)}, bf16[96,2304]{1,0:T(8,128)(2,1)S(1)}, u32[]{:S(2)}, u32[]{:S(2)}) collective-permute-start(bf16[96,2304]{1,0:T(8,128)(2,1)S(1)} %copy-done.82), channel_id=1, source_target_pairs={{0,16},{4,20},{8,24},{12,28},{16,0},{20,4},{24,8},{28,12},{1,17},{... | collective-permute-start | bytes 1327112 | tf_op jit(solution)/shard_map/ppermute | solution.py:774
  124.2 28.0 %collective-permute-start.21 = (bf16[1152,384]{1,0:T(8,128)(2,1)S(1)}, bf16[1152,384]{1,0:T(8,128)(2,1)S(1)}, u32[]{:S(2)}, u32[]{:S(2)}) collective-permute-start(bf16[1152,384]{1,0:T(8,128)(2,1)S(1)} %pad_maximum_fusion.9), channel_id=1, source_target_pairs={{0,4},{4,0},{8,12},{12,8},{16,20},{20,16},{24,28},{28,24},{1,5},{5... | collective-permute-start | bytes 2654216 | tf_op jit(solution)/shard_map/ppermute | solution.py:779
  152.3 23.3 %collective-permute-start.28 = (bf16[320,1536]{1,0:T(8,128)(2,1)S(1)}, bf16[320,1536]{1,0:T(8,128)(2,1)}, u32[]{:S(2)}, u32[]{:S(2)}) collective-permute-start(bf16[320,1536]{1,0:T(8,128)(2,1)S(1)} %pad_maximum_fusion.5.refs_24_), channel_id=1, source_target_pairs={{0,1},{1,0},{2,3},{3,2},{4,5},{5,4},{6,7},{7,6},{8,9},{9,8},{10,11... | collective-permute-start | bytes 2949128 | tf_op jit(solution)/shard_map/ppermute | solution.py:785
  152.4 22.2 %collective-permute-start.27 = (bf16[192,2304]{1,0:T(8,128)(2,1)S(1)}, bf16[192,2304]{1,0:T(8,128)(2,1)S(1)}, u32[]{:S(2)}, u32[]{:S(2)}) collective-permute-start(bf16[192,2304]{1,0:T(8,128)(2,1)S(1)} %get-tuple-element.464), channel_id=1, source_target_pairs={{0,2},{2,0},{1,3},{3,1},{4,6},{6,4},{5,7},{7,5},{8,10},{10,8},{9,1... | collective-permute-start | bytes 2654216 | tf_op jit(solution)/shard_map/ppermute | solution.py:782
  153.8 21.7 %collective-permute-start.26 = (bf16[192,2304]{1,0:T(8,128)(2,1)S(1)}, bf16[192,2304]{1,0:T(8,128)(2,1)S(1)}, u32[]{:S(2)}, u32[]{:S(2)}) collective-permute-start(bf16[192,2304]{1,0:T(8,128)(2,1)S(1)} %get-tuple-element.498), channel_id=1, source_target_pairs={{0,4},{4,0},{8,12},{12,8},{16,20},{20,16},{24,28},{28,24},{1,5},{5... | collective-permute-start | bytes 2654216 | tf_op jit(solution)/shard_map/ppermute | solution.py:779
  158.0 16.5 %collective-permute-start.25 = (bf16[160,1536]{1,0:T(8,128)(2,1)}, bf16[160,1536]{1,0:T(8,128)(2,1)}, u32[]{:S(2)}, u32[]{:S(2)}) collective-permute-start(bf16[160,1536]{1,0:T(8,128)(2,1)} %dynamic-slice_bitcast_fusion.6.skip_ref), channel_id=1, source_target_pairs={{0,24},{4,28},{8,0},{12,4},{16,8},{20,12},{24,16},{28,20},{1,25},{... | collective-permute-start | bytes 1474568 | tf_op jit(solution)/shard_map/ppermute | solution.py:774
  175.6 12.6 %collective-permute-start.32 = (bf16[96,2304]{1,0:T(8,128)(2,1)S(1)}, bf16[96,2304]{1,0:T(8,128)(2,1)S(1)}, u32[]{:S(2)}, u32[]{:S(2)}) collective-permute-start(bf16[96,2304]{1,0:T(8,128)(2,1)S(1)} %slice.297.refs_12_), channel_id=1, source_target_pairs={{0,4},{4,0},{8,12},{12,8},{16,20},{20,16},{24,28},{28,24},{1,5},{5... | collective-permute-start | bytes 1327112 | tf_op jit(solution)/shard_map/ppermute | solution.py:779
  177.3 15.2 %collective-permute-start.31 = (bf16[160,1536]{1,0:T(8,128)(2,1)S(1)}, bf16[160,1536]{1,0:T(8,128)(2,1)S(1)}, u32[]{:S(2)}, u32[]{:S(2)}) collective-permute-start(bf16[160,1536]{1,0:T(8,128)(2,1)S(1)} %copy-done.73), channel_id=1, source_target_pairs={{0,8},{4,12},{8,16},{12,20},{16,24},{20,28},{24,0},{28,4},{1,9},{5... | collective-permute-start | bytes 1474568 | tf_op jit(solution)/shard_map/ppermute | solution.py:774
  178.2 14.2 %collective-permute-start.30 = (bf16[160,1536]{1,0:T(8,128)(2,1)S(1)}, bf16[160,1536]{1,0:T(8,128)(2,1)S(1)}, u32[]{:S(2)}, u32[]{:S(2)}) collective-permute-start(bf16[160,1536]{1,0:T(8,128)(2,1)S(1)} %add_convert_fusion.14), channel_id=1, source_target_pairs={{0,2},{2,0},{1,3},{3,1},{4,6},{6,4},{5,7},{7,5},{8,10},{10,8},{9,1... | collective-permute-start | bytes 1474568 | tf_op jit(solution)/shard_map/ppermute | solution.py:782
  195.8 26.6 %collective-permute-start.37 = (bf16[480,1536]{1,0:T(8,128)(2,1)S(1)}, bf16[480,1536]{1,0:T(8,128)(2,1)S(1)}, u32[]{:S(2)}, u32[]{:S(2)}) collective-permute-start(bf16[480,1536]{1,0:T(8,128)(2,1)S(1)} %pad_maximum_fusion.2), channel_id=1, source_target_pairs={{0,1},{1,0},{2,3},{3,2},{4,5},{5,4},{6,7},{7,6},{8,9},{9,8},{10,11... | collective-permute-start | bytes 4423688 | tf_op jit(solution)/shard_map/ppermute | solution.py:785
  195.9 26.5 %collective-permute-start.36 = (bf16[192,2304]{1,0:T(8,128)(2,1)S(1)}, bf16[192,2304]{1,0:T(8,128)(2,1)S(1)}, u32[]{:S(2)}, u32[]{:S(2)}) collective-permute-start(bf16[192,2304]{1,0:T(8,128)(2,1)S(1)} %get-tuple-element.484), channel_id=1, source_target_pairs={{0,2},{2,0},{1,3},{3,1},{4,6},{6,4},{5,7},{7,5},{8,10},{10,8},{9,1... | collective-permute-start | bytes 2654216 | tf_op jit(solution)/shard_map/ppermute | solution.py:782
  196.4 25.9 %collective-permute-start.35 = (bf16[192,2304]{1,0:T(8,128)(2,1)S(1)}, bf16[192,2304]{1,0:T(8,128)(2,1)S(1)}, u32[]{:S(2)}, u32[]{:S(2)}) collective-permute-start(bf16[192,2304]{1,0:T(8,128)(2,1)S(1)} %get-tuple-element.501), channel_id=1, source_target_pairs={{0,4},{4,0},{8,12},{12,8},{16,20},{20,16},{24,28},{28,24},{1,5},{5... | collective-permute-start | bytes 2654216 | tf_op jit(solution)/shard_map/ppermute | solution.py:779
  198.3 15.9 %collective-permute-start.33 = (bf16[160,1536]{1,0:T(8,128)(2,1)S(1)}, bf16[160,1536]{1,0:T(8,128)(2,1)S(1)}, u32[]{:S(2)}, u32[]{:S(2)}) collective-permute-start(bf16[160,1536]{1,0:T(8,128)(2,1)S(1)} %get-tuple-element.480.refs_19_), channel_id=1, source_target_pairs={{0,8},{4,12},{8,16},{12,20},{16,24},{20,28},{24,0},{28,4},{1,9},{5... | collective-permute-start | bytes 1474568 | tf_op jit(solution)/shard_map/ppermute | solution.py:774
  198.7 23.7 %collective-permute-start.34 = (bf16[160,1536]{1,0:T(8,128)(2,1)S(1)}, bf16[160,1536]{1,0:T(8,128)(2,1)S(1)}, u32[]{:S(2)}, u32[]{:S(2)}) collective-permute-start(bf16[160,1536]{1,0:T(8,128)(2,1)S(1)} %get-tuple-element.480.refs_19_), channel_id=1, source_target_pairs={{0,24},{4,28},{8,0},{12,4},{16,8},{20,12},{24,16},{28,20},{1,25},{... | collective-permute-start | bytes 1474568 | tf_op jit(solution)/shard_map/ppermute | solution.py:774
  222.5 18.0 %collective-permute-start.40 = (bf16[320,1536]{1,0:T(8,128)(2,1)S(1)}, bf16[320,1536]{1,0:T(8,128)(2,1)S(1)}, u32[]{:S(2)}, u32[]{:S(2)}) collective-permute-start(bf16[320,1536]{1,0:T(8,128)(2,1)S(1)} %pad_maximum_fusion.6), channel_id=1, source_target_pairs={{0,1},{1,0},{2,3},{3,2},{4,5},{5,4},{6,7},{7,6},{8,9},{9,8},{10,11... | collective-permute-start | bytes 2949128 | tf_op jit(solution)/shard_map/ppermute | solution.py:785
  223.6 12.3 %collective-permute-start.39 = (bf16[96,2304]{1,0:T(8,128)(2,1)S(1)}, bf16[96,2304]{1,0:T(8,128)(2,1)S(1)}, u32[]{:S(2)}, u32[]{:S(2)}) collective-permute-start(bf16[96,2304]{1,0:T(8,128)(2,1)S(1)} %get-tuple-element.493.refs_10_), channel_id=1, source_target_pairs={{0,2},{2,0},{1,3},{3,1},{4,6},{6,4},{5,7},{7,5},{8,10},{10,8},{9,1... | collective-permute-start | bytes 1327112 | tf_op jit(solution)/shard_map/ppermute | solution.py:782
  225.1 15.4 %collective-permute-start.38 = (bf16[160,1536]{1,0:T(8,128)(2,1)S(1)}, bf16[160,1536]{1,0:T(8,128)(2,1)S(1)}, u32[]{:S(2)}, u32[]{:S(2)}) collective-permute-start(bf16[160,1536]{1,0:T(8,128)(2,1)S(1)} %collective-permute-done.33.refs_20_), channel_id=1, source_target_pairs={{0,8},{4,12},{8,16},{12,20},{16,24},{20,28},{24,0},{28,4},{1,9},{5... | collective-permute-start | bytes 1474568 | tf_op jit(solution)/shard_map/ppermute | solution.py:774
  279.3 15.7 %collective-permute-start.45 = (bf16[384,768]{1,0:T(8,128)(2,1)S(1)}, bf16[384,768]{1,0:T(8,128)(2,1)S(1)}, u32[]{:S(2)}, u32[]{:S(2)}) collective-permute-start(bf16[384,768]{1,0:T(8,128)(2,1)S(1)} %pad_maximum_fusion.22), channel_id=1, source_target_pairs={{0,2},{2,0},{1,3},{3,1},{4,6},{6,4},{5,7},{7,5},{8,10},{10,8},{9,1... | collective-permute-start | bytes 1769480 | tf_op jit(solution)/shard_map/ppermute | solution.py:782
  280.0 15.3 %collective-permute-start.44 = (bf16[384,768]{1,0:T(8,128)(2,1)S(1)}, bf16[384,768]{1,0:T(8,128)(2,1)S(1)}, u32[]{:S(2)}, u32[]{:S(2)}) collective-permute-start(bf16[384,768]{1,0:T(8,128)(2,1)S(1)} %pad_maximum_fusion.21), channel_id=1, source_target_pairs={{0,4},{4,0},{8,12},{12,8},{16,20},{20,16},{24,28},{28,24},{1,5},{5... | collective-permute-start | bytes 1769480 | tf_op jit(solution)/shard_map/ppermute | solution.py:779
  281.2 13.1 %collective-permute-start.43 = (bf16[160,1536]{1,0:T(8,128)(2,1)S(1)}, bf16[160,1536]{1,0:T(8,128)(2,1)S(1)}, u32[]{:S(2)}, u32[]{:S(2)}) collective-permute-start(bf16[160,1536]{1,0:T(8,128)(2,1)S(1)} %add_convert_fusion.13), channel_id=1, source_target_pairs={{0,24},{4,28},{8,0},{12,4},{16,8},{20,12},{24,16},{28,20},{1,25},{... | collective-permute-start | bytes 1474568 | tf_op jit(solution)/shard_map/ppermute | solution.py:774
  295.8 28.4 %collective-permute-start.49 = (bf16[384,1536]{1,0:T(8,128)(2,1)S(1)}, bf16[384,1536]{1,0:T(8,128)(2,1)S(1)}, u32[]{:S(2)}, u32[]{:S(2)}) collective-permute-start(bf16[384,1536]{1,0:T(8,128)(2,1)S(1)} %pad_maximum_fusion.4), channel_id=1, source_target_pairs={{0,2},{2,0},{1,3},{3,1},{4,6},{6,4},{5,7},{7,5},{8,10},{10,8},{9,1... | collective-permute-start | bytes 3538952 | tf_op jit(solution)/shard_map/ppermute | solution.py:782
  297.4 28.1 %collective-permute-start.48 = (bf16[384,1536]{1,0:T(8,128)(2,1)S(1)}, bf16[384,1536]{1,0:T(8,128)(2,1)S(1)}, u32[]{:S(2)}, u32[]{:S(2)}) collective-permute-start(bf16[384,1536]{1,0:T(8,128)(2,1)S(1)} %pad_maximum_fusion.3), channel_id=1, source_target_pairs={{0,4},{4,0},{8,12},{12,8},{16,20},{20,16},{24,28},{28,24},{1,5},{5... | collective-permute-start | bytes 3538952 | tf_op jit(solution)/shard_map/ppermute | solution.py:779
  298.7 15.9 %collective-permute-start.47 = (bf16[160,1536]{1,0:T(8,128)(2,1)S(1)}, bf16[160,1536]{1,0:T(8,128)(2,1)S(1)}, u32[]{:S(2)}, u32[]{:S(2)}) collective-permute-start(bf16[160,1536]{1,0:T(8,128)(2,1)S(1)} %add_convert_fusion.12), channel_id=1, source_target_pairs={{0,8},{4,12},{8,16},{12,20},{16,24},{20,28},{24,0},{28,4},{1,9},{5... | collective-permute-start | bytes 1474568 | tf_op jit(solution)/shard_map/ppermute | solution.py:774
  298.9 23.6 %collective-permute-start.46 = (bf16[160,1536]{1,0:T(8,128)(2,1)S(1)}, bf16[160,1536]{1,0:T(8,128)(2,1)S(1)}, u32[]{:S(2)}, u32[]{:S(2)}) collective-permute-start(bf16[160,1536]{1,0:T(8,128)(2,1)S(1)} %add_convert_fusion.11), channel_id=1, source_target_pairs={{0,24},{4,28},{8,0},{12,4},{16,8},{20,12},{24,16},{28,20},{1,25},{... | collective-permute-start | bytes 1474568 | tf_op jit(solution)/shard_map/ppermute | solution.py:774
  327.1 12.5 %collective-permute-start.52 = (bf16[160,1536]{1,0:T(8,128)(2,1)S(1)}, bf16[160,1536]{1,0:T(8,128)(2,1)S(1)}, u32[]{:S(2)}, u32[]{:S(2)}) collective-permute-start(bf16[160,1536]{1,0:T(8,128)(2,1)S(1)} %get-tuple-element.566), channel_id=1, source_target_pairs={{0,24},{4,28},{8,0},{12,4},{16,8},{20,12},{24,16},{28,20},{1,25},{... | collective-permute-start | bytes 1474568 | tf_op jit(solution)/shard_map/ppermute | solution.py:774
  332.7 12.3 %collective-permute-start.51 = (bf16[160,1536]{1,0:T(8,128)(2,1)S(1)}, bf16[160,1536]{1,0:T(8,128)(2,1)S(1)}, u32[]{:S(2)}, u32[]{:S(2)}) collective-permute-start(bf16[160,1536]{1,0:T(8,128)(2,1)S(1)} %get-tuple-element.573), channel_id=1, source_target_pairs={{0,2},{2,0},{1,3},{3,1},{4,6},{6,4},{5,7},{7,5},{8,10},{10,8},{9,1... | collective-permute-start | bytes 1474568 | tf_op jit(solution)/shard_map/ppermute | solution.py:782
  346.1 24.4 %collective-permute-start.57 = (bf16[160,1536]{1,0:T(8,128)(2,1)}, bf16[160,1536]{1,0:T(8,128)(2,1)S(1)}, u32[]{:S(2)}, u32[]{:S(2)}) collective-permute-start(bf16[160,1536]{1,0:T(8,128)(2,1)} %add_convert_fusion.8), channel_id=1, source_target_pairs={{0,24},{4,28},{8,0},{12,4},{16,8},{20,12},{24,16},{28,20},{1,25},{... | collective-permute-start | bytes 1474568 | tf_op jit(solution)/shard_map/ppermute | solution.py:774
  346.4 24.1 %collective-permute-start.56 = (bf16[160,1536]{1,0:T(8,128)(2,1)}, bf16[160,1536]{1,0:T(8,128)(2,1)S(1)}, u32[]{:S(2)}, u32[]{:S(2)}) collective-permute-start(bf16[160,1536]{1,0:T(8,128)(2,1)} %get-tuple-element.583), channel_id=1, source_target_pairs={{0,8},{4,12},{8,16},{12,20},{16,24},{20,28},{24,0},{28,4},{1,9},{5... | collective-permute-start | bytes 1474568 | tf_op jit(solution)/shard_map/ppermute | solution.py:774
  348.3 22.2 %collective-permute-start.55 = (bf16[2,96,2304]{2,1,0:T(8,128)(2,1)}, bf16[2,96,2304]{2,1,0:T(8,128)(2,1)S(1)}, u32[]{:S(2)}, u32[]{:S(2)}) collective-permute-start(bf16[2,96,2304]{2,1,0:T(8,128)(2,1)} %pad_maximum_fusion.14), channel_id=1, source_target_pairs={{0,4},{4,0},{8,12},{12,8},{16,20},{20,16},{24,28},{28,24},{1,5},{5... | collective-permute-start | bytes 2654216 | tf_op jit(solution)/shard_map/ppermute | solution.py:779
  349.5 21.4 %collective-permute-start.54 = (bf16[2,96,2304]{2,1,0:T(8,128)(2,1)}, bf16[2,96,2304]{2,1,0:T(8,128)(2,1)S(1)}, u32[]{:S(2)}, u32[]{:S(2)}) collective-permute-start(bf16[2,96,2304]{2,1,0:T(8,128)(2,1)} %pad_maximum_fusion.15), channel_id=1, source_target_pairs={{0,2},{2,0},{1,3},{3,1},{4,6},{6,4},{5,7},{7,5},{8,10},{10,8},{9,1... | collective-permute-start | bytes 2654216 | tf_op jit(solution)/shard_map/ppermute | solution.py:782
  379.6 22.4 %collective-permute-start.62 = (bf16[1152,384]{1,0:T(8,128)(2,1)}, bf16[1152,384]{1,0:T(8,128)(2,1)}, u32[]{:S(2)}, u32[]{:S(2)}) collective-permute-start(bf16[1152,384]{1,0:T(8,128)(2,1)} %pad_maximum_fusion.17), channel_id=1, source_target_pairs={{0,4},{4,0},{8,12},{12,8},{16,20},{20,16},{24,28},{28,24},{1,5},{5... | collective-permute-start | bytes 2654216 | tf_op jit(solution)/shard_map/ppermute | solution.py:779
  381.7 24.1 %collective-permute-start.59 = (bf16[320,1536]{1,0:T(8,128)(2,1)}, bf16[320,1536]{1,0:T(8,128)(2,1)S(1)}, u32[]{:S(2)}, u32[]{:S(2)}) collective-permute-start(bf16[320,1536]{1,0:T(8,128)(2,1)} %add_convert_fusion), channel_id=1, source_target_pairs={{0,2},{2,0},{1,3},{3,1},{4,6},{6,4},{5,7},{7,5},{8,10},{10,8},{9,1... | collective-permute-start | bytes 2949128 | tf_op jit(solution)/shard_map/ppermute | solution.py:782
  382.3 22.3 %collective-permute-start.61 = (bf16[96,2304]{1,0:T(8,128)(2,1)}, bf16[96,2304]{1,0:T(8,128)(2,1)}, u32[]{:S(2)}, u32[]{:S(2)}) collective-permute-start(bf16[96,2304]{1,0:T(8,128)(2,1)} %get-tuple-element.613), channel_id=1, source_target_pairs={{0,24},{4,28},{8,0},{12,4},{16,8},{20,12},{24,16},{28,20},{1,25},{... | collective-permute-start | bytes 1327112 | tf_op jit(solution)/shard_map/ppermute | solution.py:774
  384.4 20.2 %collective-permute-start.60 = (bf16[96,2304]{1,0:T(8,128)(2,1)}, bf16[96,2304]{1,0:T(8,128)(2,1)}, u32[]{:S(2)}, u32[]{:S(2)}) collective-permute-start(bf16[96,2304]{1,0:T(8,128)(2,1)} %get-tuple-element.611), channel_id=1, source_target_pairs={{0,8},{4,12},{8,16},{12,20},{16,24},{20,28},{24,0},{28,4},{1,9},{5... | collective-permute-start | bytes 1327112 | tf_op jit(solution)/shard_map/ppermute | solution.py:774
  412.5 24.5 %collective-permute-start.66 = (bf16[576,384]{1,0:T(8,128)(2,1)}, bf16[576,384]{1,0:T(8,128)(2,1)S(1)}, u32[]{:S(2)}, u32[]{:S(2)}) collective-permute-start(bf16[576,384]{1,0:T(8,128)(2,1)} %get-tuple-element.634), channel_id=1, source_target_pairs={{0,24},{4,28},{8,0},{12,4},{16,8},{20,12},{24,16},{28,20},{1,25},{... | collective-permute-start | bytes 1327112 | tf_op jit(solution)/shard_map/ppermute | solution.py:774
  415.2 29.6 %collective-permute-start.65 = (bf16[1152,384]{1,0:T(8,128)(2,1)S(1)}, bf16[1152,384]{1,0:T(8,128)(2,1)S(1)}, u32[]{:S(2)}, u32[]{:S(2)}) collective-permute-start(bf16[1152,384]{1,0:T(8,128)(2,1)S(1)} %copy-done.61), channel_id=1, source_target_pairs={{0,4},{4,0},{8,12},{12,8},{16,20},{20,16},{24,28},{28,24},{1,5},{5... | collective-permute-start | bytes 2654216 | tf_op jit(solution)/shard_map/ppermute | solution.py:779
  416.4 28.4 %collective-permute-start.64 = (bf16[96,2304]{1,0:T(8,128)(2,1)S(1)}, bf16[96,2304]{1,0:T(8,128)(2,1)S(1)}, u32[]{:S(2)}, u32[]{:S(2)}) collective-permute-start(bf16[96,2304]{1,0:T(8,128)(2,1)S(1)} %copy-done.90), channel_id=1, source_target_pairs={{0,16},{4,20},{8,24},{12,28},{16,0},{20,4},{24,8},{28,12},{1,17},{... | collective-permute-start | bytes 1327112 | tf_op jit(solution)/shard_map/ppermute | solution.py:774
  456.8 15.8 %collective-permute-start.71 = (bf16[192,1536]{1,0:T(8,128)(2,1)S(1)}, bf16[192,1536]{1,0:T(8,128)(2,1)S(1)}, u32[]{:S(2)}, u32[]{:S(2)}) collective-permute-start(bf16[192,1536]{1,0:T(8,128)(2,1)S(1)} %get-tuple-element.664), channel_id=1, source_target_pairs={{0,4},{4,0},{8,12},{12,8},{16,20},{20,16},{24,28},{28,24},{1,5},{5... | collective-permute-start | bytes 1769480 | tf_op jit(solution)/shard_map/ppermute | solution.py:779
  459.0 13.8 %collective-permute-start.72 = (bf16[130,768]{1,0:T(8,128)(2,1)S(1)}, bf16[130,768]{1,0:T(8,128)(2,1)S(1)}, u32[]{:S(2)}, u32[]{:S(2)}) collective-permute-start(bf16[130,768]{1,0:T(8,128)(2,1)S(1)} %get-tuple-element.667), channel_id=1, source_target_pairs={{0,1},{1,0},{2,3},{3,2},{4,5},{5,4},{6,7},{7,6},{8,9},{9,8},{10,11... | collective-permute-start | bytes 599048 | tf_op jit(solution)/shard_map/ppermute | solution.py:785
  459.3 14.8 %collective-permute-start.70 = (bf16[576,384]{1,0:T(8,128)(2,1)S(1)}, bf16[576,384]{1,0:T(8,128)(2,1)S(1)}, u32[]{:S(2)}, u32[]{:S(2)}) collective-permute-start(bf16[576,384]{1,0:T(8,128)(2,1)S(1)} %copy-done.89), channel_id=1, source_target_pairs={{0,8},{4,12},{8,16},{12,20},{16,24},{20,28},{24,0},{28,4},{1,9},{5... | collective-permute-start | bytes 1327112 | tf_op jit(solution)/shard_map/ppermute | solution.py:774
  460.2 21.3 %collective-permute-start.69 = (bf16[576,384]{1,0:T(8,128)(2,1)S(1)}, bf16[576,384]{1,0:T(8,128)(2,1)S(1)}, u32[]{:S(2)}, u32[]{:S(2)}) collective-permute-start(bf16[576,384]{1,0:T(8,128)(2,1)S(1)} %get-tuple-element.660), channel_id=1, source_target_pairs={{0,24},{4,28},{8,0},{12,4},{16,8},{20,12},{24,16},{28,20},{1,25},{... | collective-permute-start | bytes 1327112 | tf_op jit(solution)/shard_map/ppermute | solution.py:774
  463.2 18.3 %collective-permute-start.68 = (bf16[160,1536]{1,0:T(8,128)(2,1)S(1)}, bf16[160,1536]{1,0:T(8,128)(2,1)S(1)}, u32[]{:S(2)}, u32[]{:S(2)}) collective-permute-start(bf16[160,1536]{1,0:T(8,128)(2,1)S(1)} %add_convert_fusion.7), channel_id=1, source_target_pairs={{0,2},{2,0},{1,3},{3,1},{4,6},{6,4},{5,7},{7,5},{8,10},{10,8},{9,1... | collective-permute-start | bytes 1474568 | tf_op jit(solution)/shard_map/ppermute | solution.py:782
  481.8 14.2 %collective-permute-start.73 = (bf16[192,1536]{1,0:T(8,128)(2,1)S(1)}, bf16[192,1536]{1,0:T(8,128)(2,1)S(1)}, u32[]{:S(2)}, u32[]{:S(2)}) collective-permute-start(bf16[192,1536]{1,0:T(8,128)(2,1)S(1)} %get-tuple-element.671), channel_id=1, source_target_pairs={{0,4},{4,0},{8,12},{12,8},{16,20},{20,16},{24,28},{28,24},{1,5},{5... | collective-permute-start | bytes 1769480 | tf_op jit(solution)/shard_map/ppermute | solution.py:779
  482.8 13.3 %collective-permute-start.76 = (f32[160,1536]{1,0:T(8,128)S(1)}, f32[160,1536]{1,0:T(8,128)}, u32[]{:S(2)}, u32[]{:S(2)}) collective-permute-start(f32[160,1536]{1,0:T(8,128)S(1)} %convert_add_fusion.5), channel_id=1, source_target_pairs={{0,1},{1,0},{2,3},{3,2},{4,5},{5,4},{6,7},{7,6},{8,9},{9,8},{10,11... | collective-permute-start | bytes 2949128 | tf_op jit(solution)/shard_map/ppermute | solution.py:785
  483.9 15.9 %collective-permute-start.74 = (bf16[192,1536]{1,0:T(8,128)(2,1)S(1)}, bf16[192,1536]{1,0:T(8,128)(2,1)}, u32[]{:S(2)}, u32[]{:S(2)}) collective-permute-start(bf16[192,1536]{1,0:T(8,128)(2,1)S(1)} %add_convert_fusion.4), channel_id=1, source_target_pairs={{0,24},{4,28},{8,0},{12,4},{16,8},{20,12},{24,16},{28,20},{1,25},{... | collective-permute-start | bytes 1769480 | tf_op jit(solution)/shard_map/ppermute | solution.py:774
  499.8 14.7 %collective-permute-start.77 = (bf16[192,1536]{1,0:T(8,128)(2,1)S(1)}, bf16[192,1536]{1,0:T(8,128)(2,1)S(1)}, u32[]{:S(2)}, u32[]{:S(2)}) collective-permute-start(bf16[192,1536]{1,0:T(8,128)(2,1)S(1)} %get-tuple-element.700), channel_id=1, source_target_pairs={{0,4},{4,0},{8,12},{12,8},{16,20},{20,16},{24,28},{28,24},{1,5},{5... | collective-permute-start | bytes 1769480 | tf_op jit(solution)/shard_map/ppermute | solution.py:779
  502.4 16.8 %collective-permute-start.78 = (bf16[192,1536]{1,0:T(8,128)(2,1)S(1)}, bf16[192,1536]{1,0:T(8,128)(2,1)}, u32[]{:S(2)}, u32[]{:S(2)}) collective-permute-start(bf16[192,1536]{1,0:T(8,128)(2,1)S(1)} %add_convert_fusion.3), channel_id=1, source_target_pairs={{0,8},{4,12},{8,16},{12,20},{16,24},{20,28},{24,0},{28,4},{1,9},{5... | collective-permute-start | bytes 1769480 | tf_op jit(solution)/shard_map/ppermute | solution.py:774
  525.2 15.4 %collective-permute-start.83 = (bf16[192,1536]{1,0:T(8,128)(2,1)}, bf16[192,1536]{1,0:T(8,128)(2,1)S(1)}, u32[]{:S(2)}, u32[]{:S(2)}) collective-permute-start(bf16[192,1536]{1,0:T(8,128)(2,1)} %add_convert_fusion.2), channel_id=1, source_target_pairs={{0,24},{4,28},{8,0},{12,4},{16,8},{20,12},{24,16},{28,20},{1,25},{... | collective-permute-start | bytes 1769480 | tf_op jit(solution)/shard_map/ppermute | solution.py:774
  525.3 15.4 %collective-permute-start.82 = (bf16[192,1536]{1,0:T(8,128)(2,1)S(1)}, bf16[192,1536]{1,0:T(8,128)(2,1)S(1)}, u32[]{:S(2)}, u32[]{:S(2)}) collective-permute-start(bf16[192,1536]{1,0:T(8,128)(2,1)S(1)} %get-tuple-element.712), channel_id=1, source_target_pairs={{0,4},{4,0},{8,12},{12,8},{16,20},{20,16},{24,28},{28,24},{1,5},{5... | collective-permute-start | bytes 1769480 | tf_op jit(solution)/shard_map/ppermute | solution.py:779
  (144 other events, 1219.8 us)

commit v4 on v3

--- a/solution.py
+++ b/solution.py
@@ -70,19 +70,30 @@
 
 
 def pair_forward_kernel(gain_ref, own_ref, over_ref, near_ref, core_ref, far_ref, x_ref, n_ref):
-    rows = own_ref.shape[0]
-    for base, first in ((own_ref, 0), (over_ref, rows)):
-        part, other = slice(first, first + rows), slice(rows - first, 2 * rows - first)
-        values = base[...].astype(F32) + near_ref[part, :]
-        values = values + core_ref[part, :].astype(F32) + far_ref[other, :].astype(F32)
-        x_ref[part, :] = values
-        n_ref[part, :] = (norm_stats(values)[0] * gain_ref[...]).astype(BF16)
+    terms = near_ref[...] + core_ref[...].astype(F32) + far_ref[...].astype(F32)
+    base = jnp.where(pl.program_id(0) == 0, own_ref[...].astype(F32), over_ref[...].astype(F32))
+    values = base + terms
+    x_ref[...] = values
+    n_ref[...] = (norm_stats(values)[0] * gain_ref[...]).astype(BF16)
+
+
+def pair_blocks(rows, width):
+    return (
+        pl.BlockSpec((rows, width), lambda step: (step, 0)),
+        pl.BlockSpec((rows, width), lambda step: (1 - step, 0)),
+        pl.BlockSpec((rows, width), lambda step: (0, 0)),
+        pl.BlockSpec((1, width), lambda step: (0, 0)),
+    )
 
 
 def pair_forward(gain, own, over, near, core, far):
     rows, width = near.shape
+    here, there, fixed, line = pair_blocks(rows // 2, width)
     return pl.pallas_call(
         pair_forward_kernel,
+        grid=(2,),
+        in_specs=[line, fixed, fixed, here, here, there],
+        out_specs=[here, here],
         out_shape=(
             jax.ShapeDtypeStruct((rows, width), F32),
             jax.ShapeDtypeStruct((rows, width), BF16),
@@ -94,28 +105,32 @@
 def pair_backward_kernel(
     gain_ref, x_ref, skip_ref, over_ref, near_ref, core_ref, far_ref, dx_ref, low_ref, dg_ref
 ):
-    rows = skip_ref.shape[0]
-    for skip, first in ((skip_ref, 0), (over_ref, rows)):
-        part, other = slice(first, first + rows), slice(rows - first, 2 * rows - first)
-        upstream = near_ref[part, :] + core_ref[part, :].astype(F32) + far_ref[other, :].astype(F32)
-        unit, rate = norm_stats(x_ref[part, :])
-        scaled = upstream * gain_ref[...]
-        back = rate * (
-            scaled
-            - jnp.mean(scaled, axis=-1, keepdims=True)
-            - unit * jnp.mean(scaled * unit, axis=-1, keepdims=True)
-        )
-        total = skip[...].astype(F32) + back
-        low_ref[part, :] = total.astype(BF16)
-        if first == 0:
-            dx_ref[...] = total
-            dg_ref[...] = jnp.sum(upstream * unit, axis=0, keepdims=True)
+    upstream = near_ref[...] + core_ref[...].astype(F32) + far_ref[...].astype(F32)
+    unit, rate = norm_stats(x_ref[...])
+    scaled = upstream * gain_ref[...]
+    back = rate * (
+        scaled
+        - jnp.mean(scaled, axis=-1, keepdims=True)
+        - unit * jnp.mean(scaled * unit, axis=-1, keepdims=True)
+    )
+    first = pl.program_id(0) == 0
+    total = jnp.where(first, skip_ref[...], over_ref[...].astype(F32)) + back
+    low_ref[...] = total.astype(BF16)
+
+    @pl.when(first)
+    def _():
+        dx_ref[...] = total
+        dg_ref[...] = jnp.sum(upstream * unit, axis=0, keepdims=True)
 
 
 def pair_backward(gain, values, skip, over, near, core, far):
     rows, width = values.shape
+    here, there, fixed, line = pair_blocks(rows // 2, width)
     return pl.pallas_call(
         pair_backward_kernel,
+        grid=(2,),
+        in_specs=[line, here, fixed, fixed, here, here, there],
+        out_specs=[fixed, here, line],
         out_shape=(
             jax.ShapeDtypeStruct((rows // 2, width), F32),
             jax.ShapeDtypeStruct((rows, width), BF16),
@@ -1209,8 +1224,9 @@
     hidden_two_grad, low, third_gain_grad = norm_backward(
         hidden_two, third_norm_gain, upstream, mine, recv, one, three
     )
+    low, out_send = lax.optimization_barrier((low, out_low[0]))
     low_over = over_half(low)
-    out_two = ring(out_low[0], -1)
+    out_two = ring(out_send, -1)
     both_keep, both_move = lanes_second(both_grad, both_lanes)
     both_late_keep, both_late_move = halves_second(both_grad, both_halves)
     low_over, low, out_two, both_keep, both_late_keep, x_send, y_send, out_one = sync(
@@ -1282,7 +1298,9 @@
     def out_of(values, back):
         return lax.dynamic_index_in_dim(values, links.ring_at(back), 0, keepdims=False)
 
-    far_term = over_half((partial + recv.astype(F32)).astype(BF16))
+    half_send = (partial + recv.astype(F32)).astype(BF16)
+    half_send, feed_send, cross_most = lax.optimization_barrier((half_send, feed_send, cross_most))
+    far_term = over_half(half_send)
     feed1_sum, feed3_sum = ring(feed_send[2], 1), ring(feed_send[0], -1)
     cross_most = links.sum_lanes(cross_most)
     block_rows = cross_most.shape[0] // 2
@@ -1312,8 +1330,10 @@
     self_own, self_other = by_back(split_blocks([output_grad, qkv_grad], ring_places, False))
     cross_zero = cross_own[0].astype(F32) + cross_late[:block_rows].astype(F32)
     cross_one = cross_own[1].astype(F32) + cross_late[block_rows:].astype(F32)
-    recv, self_own, self_other, cross_zero, cross_one, backs = sync(
+    cross_three = ring(cross_three, 1)
+    recv, cross_three, self_own, self_other, cross_zero, cross_one, backs = sync(
         over_core(send),
+        cross_three,
         self_own,
         self_other,
         cross_zero,
@@ -1322,18 +1342,21 @@
     )
     cross_key_back, cross_value_back = backs
 
-    far_term = over_half(for_half(partial, recv))
-    cross_one, cross_three = ring(cross_one, -1), ring(cross_three, 1)
-    self2 = links.sum_lanes(self_other[2])
+    half_send = for_half(partial, recv)
+    half_send, cross_one, self_send = lax.optimization_barrier(
+        (half_send, cross_one, self_other[2])
+    )
+    far_term = over_half(half_send)
+    cross_one = ring(cross_one, -1)
+    self2 = links.sum_lanes(self_send)
     context_term = (
         mm_nt(cross_key_back, context_full[:, :cols])
         + mm_nt(cross_value_back, context_full[:, cols:])
     )[:context_count]
     context_recv = over_core(context_term.astype(BF16))
-    far_term, cross_one, cross_three, self2, context_term, context_recv, self_two = sync(
+    far_term, cross_one, self2, context_term, context_recv, self_two = sync(
         far_term,
         cross_one,
-        cross_three,
         self2,
         context_term,
         context_recv,
@@ -1365,6 +1388,8 @@
         ],
         axis=1,
     )
+    gain_grads = gain_grads + over_core(gain_grads)
+    gain_grads = gain_grads + over_half(gain_grads)
     context_grad = context_low_sum.astype(F32) + context_over.astype(F32)
     self3, self_two, context_grad, layer_result, gain_grads, inputs_grad, feed_sums, cross_total, self_three = sync(
         self3,
@@ -1381,37 +1406,38 @@
 
     self1 = links.sum_lanes(self_other[1])
     self_three = ring(self_three, 1)
-    gain_grads = gain_grads + over_core(gain_grads)
-    gain_grads = gain_grads + over_half(gain_grads)
+    gain_lanes = (
+        gain_grads.reshape(3, RING, lane_count, -1).swapaxes(1, 2).reshape(3, -1)
+    )
+    gain_total = slot(gain_lanes, lane_count, links.lane_at(1))
+    for turn in list(range(2, lane_count)) + [0]:
+        gain_total = links.lanes(gain_total) + slot(gain_lanes, lane_count, links.lane_at(turn))
+    gain_ring = [slot(gain_total, RING, links.ring_at(back)) for back in range(RING)]
+    gain_two, gain_three = ring(gain_ring[2], -1), ring(gain_ring[3], 1)
     cross_keep, cross_recv = links.swap_halves(cross_total)
-    self1, self_three, gain_grads, cross_recv, self_one = sync(
+    self1, self_three, gain_two, gain_three, cross_recv, self_one = sync(
         self1,
         self_three,
-        gain_grads,
+        gain_two,
+        gain_three,
         cross_recv,
         (self_own[1].astype(F32) + self1.astype(F32) + self_two.astype(F32)).astype(BF16),
     )
 
     self0 = links.sum_lanes(self_other[0])
     self_one = ring(self_one, -1)
-    gain_ring = [slot(gain_grads, RING, links.ring_at(back)) for back in range(RING)]
-    gain_two, gain_three = ring(gain_ring[2], -1), ring(gain_ring[3], 1)
+    gain_one = ring(gain_ring[1] + gain_two, -1)
     inputs_result = links.both_cores(inputs_grad)
     cross_sums = links.side_by_side(cross_keep, cross_recv)
-    self0, self_one, gain_two, gain_three, inputs_result, cross_sums = sync(
-        self0, self_one, gain_two, gain_three, inputs_result, cross_sums
-    )
-    gain_one = ring(gain_ring[1] + gain_two, -1)
+    gain_sums = slot(gain_ring[0] + gain_one + gain_three, 2, half)
+    self0, self_one, gain_sums, inputs_result, cross_sums = sync(
+        self0, self_one, gain_sums, inputs_result, cross_sums
+    )
 
     self_total = (
         self_own[0].astype(F32) + self0.astype(F32) + self_one.astype(F32) + self_three.astype(F32)
     )
     keep, recv = links.swap_halves(self_total.reshape(2, shard, 4 * cols))
-    gain_grads = gain_ring[0] + gain_one + gain_three
-    gain_total = slot(gain_grads, lane_count, links.lane_at(1))
-    for turn in list(range(2, lane_count)) + [0]:
-        gain_total = links.lanes(gain_total) + slot(gain_grads, lane_count, links.lane_at(turn))
-    gain_sums = slot(gain_total, 2, half)
 
     def of_self(values, n):
         if n == 3:

time: 567 us -> 567 us (level)
  waiting for transfers between devices: 237 us -> 229 us
    ppermute x33, waiting for transfers between devices: 126 us -> 120 us  [ring(): return lax.ppermute(self.begun(value), 'fsdp', pairs)]
    unnamed x241 -> x255, local copies, waits for them, and re-layouts: 14.6 us -> 15.7 us
  transfers between devices with their start and end apart: 90 -> 90, of which waited for: 52 -> 48; matrix products, arithmetic and copies ran while one was open for 18% -> 18% of each run, Pallas kernels for 12% -> 11%
where the time goes in v4:
time: 567 us; the launch traced here: 557 us
  waiting for transfers between devices  229 us (40%)
  Pallas kernels  98.1 us (17%)
  starting transfers between devices  95.7 us (17%)
  other arithmetic  48.4 us (9%)
  local copies, waits for them, and re-layouts  42.9 us (8%)
  matrix products  40.3 us (7%)
    ppermute x33, waiting for transfers between devices, ring(): return lax.ppermute(self.begun(value), 'fsdp', pairs)  120 us
    ppermute x20, waiting for transfers between devices, lanes(): return lax.ppermute(self.begun(value), 'fsdp', pairs)  57.9 us
    ppermute x33, starting transfers between devices, ring(): return lax.ppermute(self.begun(value), 'fsdp', pairs)  50.1 us
    ppermute x19, waiting for transfers between devices, over_half(): return lax.ppermute(self.begun(value), 'ctx', [(0, 1), (1, 0)])  48.1 us
    pallas_call x1, Pallas kernels, feed_forward(): pl.pallas_call(functools.partial(feed_kernel, shard, own, len(held), (tup...  25.5 us
    dot_general x8, matrix products, mm_tn(): lax.dot_general(left, right, (((0,), (0,)), ((), ())), preferred_element_...  23.3 us
    ppermute x20, starting transfers between devices, lanes(): return lax.ppermute(self.begun(value), 'fsdp', pairs)  23.1 us
    pallas_call x1, Pallas kernels, self_forward(): pl.pallas_call(functools.partial(self_forward_kernel, shard), grid=(pairs...  22.4 us
  transfers between devices with their start and end apart: 90, of which 48 were waited for; matrix products, arithmetic and copies ran while one was open for 18% of the time, Pallas kernels for 11%

profile of v4, /device:TPU:0, one launch (start us, length us, event | category | flops | bytes accessed | tf_op | source)
XLA Modules:
  0.0 557.2 jit_solution(13968976798421556711)
XLA Ops:
  2.4 2.9 shard_map.296
  5.3 3.0 collective-permute-start
  12.6 4.1 collective-permute-done
  25.3 8.3 %collective-permute-done.3.refs_9_.over_ref = bf16[160,1536]{1,0:T(8,128)(2,1)S(1)} collective-permute-done((bf16[160,1536]{1,0:T(8,128)(2,1)S(1)}, bf16[160,1536]{1,0:T(8,128)(2,1)S(1)}, u32[]{:S(2)}, u32[]{:S(2)}) %collective-permute-start.3) | collective-permute-done | bytes 491552 | tf_op jit(solution)/shard_map/ppermute | solution.py:797
  33.6 4.1 collective-permute-done.1.refs_2_
  42.3 2.2 fusion.13
  44.4 5.2 collective-permute-done.7
  49.6 3.3 collective-permute-done.6.refs_3_
  56.7 8.2 %collective-permute-done.11 = bf16[96,2304]{1,0:T(8,128)(2,1)S(1)} collective-permute-done((bf16[96,2304]{1,0:T(8,128)(2,1)S(1)}, bf16[96,2304]{1,0:T(8,128)(2,1)S(1)}, u32[]{:S(2)}, u32[]{:S(2)}) %collective-permute-start.11) | collective-permute-done | bytes 442400 | tf_op jit(solution)/shard_map/ppermute | solution.py:797
  64.9 2.8 collective-permute-done.10.refs_7_
  72.2 8.5 %collective-permute-done.12 = bf16[576,384]{1,0:T(8,128)(2,1)S(1)} collective-permute-done((bf16[576,384]{1,0:T(8,128)(2,1)S(1)}, bf16[576,384]{1,0:T(8,128)(2,1)S(1)}, u32[]{:S(2)}, u32[]{:S(2)}) %collective-permute-start.12) | collective-permute-done | bytes 442400 | tf_op jit(solution)/shard_map/ppermute | solution.py:789
  80.8 4.0 collective-permute-done.13.refs_5_
  86.0 3.8 collective-permute-start.18
  91.2 22.4 %shard_map.297 = (bf16[640,1152]{1,0:T(8,128)(2,1)}, bf16[640,384]{1,0:T(8,128)(2,1)}, f32[640,384]{1,0:T(8,128)}, f32[320,1536]{1,0:T(8,128)}, bf16[320,1536]{1...) custom-call(s32[16]{0:T(128)} %xor_add_fusion.place_ref, ...), custom_call_target="tpu_custom_call" | custom-call | flops 3649044480 | bytes 6684672 | tf_op jit(solution)/shard_map/pallas_call | solution.py:306
  120.1 3.8 collective-permute-start.23
  126.5 8.0 %collective-permute-done.23 = bf16[96,2304]{1,0:T(8,128)(2,1)S(1)} collective-permute-done((bf16[96,2304]{1,0:T(8,128)(2,1)S(1)}, bf16[96,2304]{1,0:T(8,128)(2,1)S(1)}, u32[]{:S(2)}, u32[]{:S(2)}) %collective-permute-start.23) | collective-permute-done | bytes 442400 | tf_op jit(solution)/shard_map/ppermute | solution.py:789
  135.8 16.2 %collective-permute-done.22 = bf16[96,2304]{1,0:T(8,128)(2,1)S(1)} collective-permute-done((bf16[96,2304]{1,0:T(8,128)(2,1)S(1)}, bf16[96,2304]{1,0:T(8,128)(2,1)S(1)}, u32[]{:S(2)}, u32[]{:S(2)}) %collective-permute-start.22) | collective-permute-done | bytes 442400 | tf_op jit(solution)/shard_map/ppermute | solution.py:789
  155.2 2.3 shard_map.298
  157.7 4.0 collective-permute-start.25
  169.7 3.5 shard_map.300
  179.5 8.5 %collective-permute-done.32.refs_14_ = bf16[96,2304]{1,0:T(8,128)(2,1)S(1)} collective-permute-done((bf16[96,2304]{1,0:T(8,128)(2,1)S(1)}, bf16[96,2304]{1,0:T(8,128)(2,1)S(1)}, u32[]{:S(2)}, u32[]{:S(2)}) %collective-permute-start.32) | collective-permute-done | bytes 442400 | tf_op jit(solution)/shard_map/ppermute | solution.py:794
  188.2 4.0 collective-permute-done.31.refs_26_
  198.4 3.4 collective-permute-start.34
  202.8 11.0 %collective-permute-done.33.refs_20_ = bf16[160,1536]{1,0:T(8,128)(2,1)S(1)} collective-permute-done((bf16[160,1536]{1,0:T(8,128)(2,1)S(1)}, bf16[160,1536]{1,0:T(8,128)(2,1)S(1)}, u32[]{:S(2)}, u32[]{:S(2)}) %collective-permute-start.33) | collective-permute-done | bytes 491552 | tf_op jit(solution)/shard_map/ppermute | solution.py:789
  213.9 8.2 %collective-permute-done.34.refs_21_ = bf16[160,1536]{1,0:T(8,128)(2,1)S(1)} collective-permute-done((bf16[160,1536]{1,0:T(8,128)(2,1)S(1)}, bf16[160,1536]{1,0:T(8,128)(2,1)S(1)}, u32[]{:S(2)}, u32[]{:S(2)}) %collective-permute-start.34) | collective-permute-done | bytes 491552 | tf_op jit(solution)/shard_map/ppermute | solution.py:789
  227.6 8.1 %collective-permute-done.39.refs_11_ = bf16[96,2304]{1,0:T(8,128)(2,1)S(1)} collective-permute-done((bf16[96,2304]{1,0:T(8,128)(2,1)S(1)}, bf16[96,2304]{1,0:T(8,128)(2,1)S(1)}, u32[]{:S(2)}, u32[]{:S(2)}) %collective-permute-start.39) | collective-permute-done | bytes 442400 | tf_op jit(solution)/shard_map/ppermute | solution.py:797
  235.7 4.0 collective-permute-done.38.refs_22_
  242.4 25.5 %shard_map.302 = (bf16[1280,768]{1,0:T(8,128)(2,1)}, bf16[1280,1536]{1,0:T(8,128)(2,1)}, bf16[640,1536]{1,0:T(8,128)(2,1)}, f32[640,1536]{1,0:T(8,128)}, bf16[12...) custom-call(s32[16]{0:T(128)} %xor_add_fusion.place_ref, bf16[96,2304]{1,0:T(8,128)(2,1)} %copy-done.85, ...), custom_call_target="tpu_custom_call" | custom-call | flops 15099494400 | bytes 22806528 | tf_op jit(solution)/shard_map/pallas_call | solution.py:636
  268.2 6.2 %convolution_convert_fusion.2 = bf16[1536,768]{1,0:T(8,128)(2,1)S(1)} fusion(bf16[1280,1536]{1,0:T(8,128)(2,1)} %get-tuple-element.533, bf16[1280,768]{1,0:T(8,128)(2,1)} %get-tuple-element.549), kind=kOutput, calls=%fused_computation.2 | convolution fusion | flops 3021078528 | bytes 8257536 | tf_op jit(solution)/shard_map/dot_general | solution.py:26
  282.1 6.6 %convolution_convert_fusion.1 = bf16[1536,1536]{1,0:T(8,128)(2,1)S(1)} fusion(bf16[1280,1536]{1,0:T(8,128)(2,1)S(1)} %copy-done.124, bf16[1280,1536]{1,0:T(8,128)(2,1)S(1)} %copy-done.123), kind=kOutput, calls=%fused_computation.1 | convolution fusion | flops 6042157056 | bytes 12582912 | tf_op jit(solution)/shard_map/dot_general | solution.py:26
  289.0 4.5 collective-permute-done.43
  299.0 3.9 collective-permute-start.46
  306.5 8.2 %collective-permute-done.47.refs_3_ = bf16[160,1536]{1,0:T(8,128)(2,1)S(1)} collective-permute-done((bf16[160,1536]{1,0:T(8,128)(2,1)S(1)}, bf16[160,1536]{1,0:T(8,128)(2,1)S(1)}, u32[]{:S(2)}, u32[]{:S(2)}) %collective-permute-start.47) | collective-permute-done | bytes 491552 | tf_op jit(solution)/shard_map/ppermute | solution.py:789
  314.7 7.9 %collective-permute-done.46.refs_2_ = bf16[160,1536]{1,0:T(8,128)(2,1)S(1)} collective-permute-done((bf16[160,1536]{1,0:T(8,128)(2,1)S(1)}, bf16[160,1536]{1,0:T(8,128)(2,1)S(1)}, u32[]{:S(2)}, u32[]{:S(2)}) %collective-permute-start.46) | collective-permute-done | bytes 491552 | tf_op jit(solution)/shard_map/ppermute | solution.py:789
  327.6 2.4 shard_map.303
  335.7 7.1 %collective-permute-done.52 = bf16[160,1536]{1,0:T(8,128)(2,1)S(1)} collective-permute-done((bf16[160,1536]{1,0:T(8,128)(2,1)}, bf16[160,1536]{1,0:T(8,128)(2,1)S(1)}, u32[]{:S(2)}, u32[]{:S(2)}) %collective-permute-start.52) | collective-permute-done | bytes 491552 | tf_op jit(solution)/shard_map/ppermute | solution.py:789
  342.8 2.2 add_convert_fusion.8
  346.2 3.0 collective-permute-start.57
  355.3 9.7 %shard_map.304 = (bf16[640,384]{1,0:T(8,128)(2,1)S(1)}, bf16[256,384]{1,0:T(8,128)(2,1)S(1)}, bf16[256,384]{1,0:T(8,128)(2,1)S(1)}) custom-call(bf16[640,384]{1,0:T(8,128)(2,1)S(1)} %copy-done.39, bf16[256,768]{1,0:T(8,128)(2,1)S(1)} %convolution_convert_fusion.15.k_ref.v_ref, bf16[256,768]{1,0:T(8,128)(2,1)S(1)} %convolution_convert_fusion.15.k_ref.v_ref, ...), custom_call_target="tpu_custom_call" | custom-call | flops 629145600 | bytes 4718592 | tf_op jit(solution)/shard_map/pallas_call | solution.py:466
  368.1 2.4 convolution_convert_fusion.5.refs_1_
  384.8 3.5 collective-permute-start.61
  388.3 16.8 %collective-permute-done.62 = bf16[1152,384]{1,0:T(8,128)(2,1)} collective-permute-done((bf16[1152,384]{1,0:T(8,128)(2,1)}, bf16[1152,384]{1,0:T(8,128)(2,1)}, u32[]{:S(2)}, u32[]{:S(2)}) %collective-permute-start.62) | collective-permute-done | bytes 884768 | tf_op jit(solution)/shard_map/ppermute | solution.py:794
  405.2 2.5 add_convert_fusion.16
  408.4 3.5 shard_map.306
  414.8 3.4 collective-permute-start.66
  422.0 12.3 %shard_map.307 = bf16[640,1152]{1,0:T(8,128)(2,1)S(1)} custom-call(bf16[640,1152]{1,0:T(8,128)(2,1)S(1)} %copy-done.41, bf16[640,384]{1,0:T(8,128)(2,1)S(1)} %copy-done.40, bf16[640,384]{1,0:T(8,128)(2,1)S(1)} %convolution_convert_fusion.12.do_ref, f32[640,384]{1,0:T(8,128)S(1)} %copy-done.42, f32[640,128]{1,0:T(8,128)S(1)} %copy-done.31, ...), custom_call_target="tpu_custom_call" | custom-call | flops 1572864000 | bytes 8847360 | tf_op jit(solution)/shard_map/pallas_call | solution.py:442
  434.2 4.6 convolution_convert_fusion.7
  440.3 7.8 %collective-permute-done.64.refs_2_ = bf16[96,2304]{1,0:T(8,128)(2,1)S(1)} collective-permute-done((bf16[96,2304]{1,0:T(8,128)(2,1)S(1)}, bf16[96,2304]{1,0:T(8,128)(2,1)S(1)}, u32[]{:S(2)}, u32[]{:S(2)}) %collective-permute-start.64) | collective-permute-done | bytes 442400 | tf_op jit(solution)/shard_map/ppermute | solution.py:789
  448.6 4.6 convolution_convert_fusion.refs_1_
  454.6 2.4 shard_map.308
  457.0 3.2 shard_map.310
  464.1 2.4 collective-permute-start.70
  467.4 9.1 %collective-permute-done.71 = bf16[192,1536]{1,0:T(8,128)(2,1)S(1)} collective-permute-done((bf16[192,1536]{1,0:T(8,128)(2,1)S(1)}, bf16[192,1536]{1,0:T(8,128)(2,1)S(1)}, u32[]{:S(2)}, u32[]{:S(2)}) %collective-permute-start.71) | collective-permute-done | bytes 589856 | tf_op jit(solution)/shard_map/ppermute | solution.py:794
  476.9 2.8 collective-permute-done.69.refs_2_
  482.1 2.9 shard_map.309
  490.1 3.2 collective-permute-done.78
  498.0 3.5 collective-permute-done.74
  506.9 9.8 %collective-permute-done.81 = f32[3,768]{1,0:T(4,128)S(1)} collective-permute-done((f32[3,768]{1,0:T(4,128)S(1)}, f32[3,768]{1,0:T(4,128)S(1)}, u32[]{:S(2)}, u32[]{:S(2)}) %collective-permute-start.81) | collective-permute-done | bytes 9248 | tf_op jit(solution)/shard_map/ppermute | solution.py:794
  517.1 3.6 collective-permute-start.82
  521.5 2.3 add_convert_fusion.2
  523.9 2.2 copy.39
  526.2 2.2 collective-permute-start.87
  533.4 10.5 %collective-permute-done.86 = bf16[192,1536]{1,0:T(8,128)(2,1)S(1)} collective-permute-done((bf16[192,1536]{1,0:T(8,128)(2,1)}, bf16[192,1536]{1,0:T(8,128)(2,1)S(1)}, u32[]{:S(2)}, u32[]{:S(2)}) %collective-permute-start.86) | collective-permute-done | bytes 589856 | tf_op jit(solution)/shard_map/ppermute | solution.py:789
  548.8 5.0 collective-permute-done.89
  (555 shorter events, 172.7 us)
Async XLA Ops:
  9.1 16.1 %collective-permute-start.4 = (bf16[160,1536]{1,0:T(8,128)(2,1)}, bf16[160,1536]{1,0:T(8,128)(2,1)S(1)}, u32[]{:S(2)}, u32[]{:S(2)}) collective-permute-start(bf16[160,1536]{1,0:T(8,128)(2,1)} %dynamic-slice_bitcast_fusion.6.skip_ref), channel_id=1, source_target_pairs={{0,8},{4,12},{8,16},{12,20},{16,24},{20,28},{24,0},{28,4},{1,9},{5... | collective-permute-start | bytes 1474568 | tf_op jit(solution)/shard_map/ppermute | solution.py:789
  18.5 19.1 %collective-permute-start.1 = (bf16[208,1536]{1,0:T(8,128)(2,1)S(1)}, bf16[208,1536]{1,0:T(8,128)(2,1)}, u32[]{:S(2)}, u32[]{:S(2)}) collective-permute-start(bf16[208,1536]{1,0:T(8,128)(2,1)S(1)} %pad_maximum_fusion.20.refs_0_), channel_id=1, source_target_pairs={{0,8},{4,12},{8,16},{12,20},{16,24},{20,28},{24,0},{28,4},{1,9},{5... | collective-permute-start | bytes 1916936 | tf_op jit(solution)/shard_map/ppermute | solution.py:789
  20.4 17.3 %collective-permute-start.2 = (bf16[208,1536]{1,0:T(8,128)(2,1)S(1)}, bf16[208,1536]{1,0:T(8,128)(2,1)}, u32[]{:S(2)}, u32[]{:S(2)}) collective-permute-start(bf16[208,1536]{1,0:T(8,128)(2,1)S(1)} %pad_maximum_fusion.20.refs_0_), channel_id=1, source_target_pairs={{0,4},{4,0},{8,12},{12,8},{16,20},{20,16},{24,28},{28,24},{1,5},{5... | collective-permute-start | bytes 1916936 | tf_op jit(solution)/shard_map/ppermute | solution.py:794
  37.7 15.2 %collective-permute-start.6 = (bf16[208,1536]{1,0:T(8,128)(2,1)}, bf16[208,1536]{1,0:T(8,128)(2,1)S(1)}, u32[]{:S(2)}, u32[]{:S(2)}) collective-permute-start(bf16[208,1536]{1,0:T(8,128)(2,1)} %collective-permute-done.1.refs_2_), channel_id=1, source_target_pairs={{0,4},{4,0},{8,12},{12,8},{16,20},{20,16},{24,28},{28,24},{1,5},{5... | collective-permute-start | bytes 1916936 | tf_op jit(solution)/shard_map/ppermute | solution.py:794
  39.2 14.7 %collective-permute-start.5 = (bf16[208,1536]{1,0:T(8,128)(2,1)S(1)}, bf16[208,1536]{1,0:T(8,128)(2,1)S(1)}, u32[]{:S(2)}, u32[]{:S(2)}) collective-permute-start(bf16[208,1536]{1,0:T(8,128)(2,1)S(1)} %pad_maximum_fusion.20.refs_0_), channel_id=1, source_target_pairs={{0,24},{4,28},{8,0},{12,4},{16,8},{20,12},{24,16},{28,20},{1,25},{... | collective-permute-start | bytes 1916936 | tf_op jit(solution)/shard_map/ppermute | solution.py:789
  53.9 13.8 %collective-permute-start.10 = (bf16[208,1536]{1,0:T(8,128)(2,1)S(1)}, bf16[208,1536]{1,0:T(8,128)(2,1)S(1)}, u32[]{:S(2)}, u32[]{:S(2)}) collective-permute-start(bf16[208,1536]{1,0:T(8,128)(2,1)S(1)} %collective-permute-done.5.refs_6_), channel_id=1, source_target_pairs={{0,4},{4,0},{8,12},{12,8},{16,20},{20,16},{24,28},{28,24},{1,5},{5... | collective-permute-start | bytes 1916936 | tf_op jit(solution)/shard_map/ppermute | solution.py:794
  54.4 15.8 %collective-permute-start.9 = (bf16[208,1536]{1,0:T(8,128)(2,1)}, bf16[208,1536]{1,0:T(8,128)(2,1)S(1)}, u32[]{:S(2)}, u32[]{:S(2)}) collective-permute-start(bf16[208,1536]{1,0:T(8,128)(2,1)} %collective-permute-done.1.refs_2_), channel_id=1, source_target_pairs={{0,8},{4,12},{8,16},{12,20},{16,24},{20,28},{24,0},{28,4},{1,9},{5... | collective-permute-start | bytes 1916936 | tf_op jit(solution)/shard_map/ppermute | solution.py:789
  70.3 14.5 %collective-permute-start.13 = (bf16[208,1536]{1,0:T(8,128)(2,1)S(1)}, bf16[208,1536]{1,0:T(8,128)(2,1)S(1)}, u32[]{:S(2)}, u32[]{:S(2)}) collective-permute-start(bf16[208,1536]{1,0:T(8,128)(2,1)S(1)} %collective-permute-done.9.refs_4_), channel_id=1, source_target_pairs={{0,4},{4,0},{8,12},{12,8},{16,20},{20,16},{24,28},{28,24},{1,5},{5... | collective-permute-start | bytes 1916936 | tf_op jit(solution)/shard_map/ppermute | solution.py:794
  84.8 30.1 %collective-permute-start.15 = (bf16[1152,384]{1,0:T(8,128)(2,1)S(1)}, bf16[1152,384]{1,0:T(8,128)(2,1)}, u32[]{:S(2)}, u32[]{:S(2)}) collective-permute-start(bf16[1152,384]{1,0:T(8,128)(2,1)S(1)} %pad_maximum_fusion.8), channel_id=1, source_target_pairs={{0,4},{4,0},{8,12},{12,8},{16,20},{20,16},{24,28},{28,24},{1,5},{5... | collective-permute-start | bytes 2654216 | tf_op jit(solution)/shard_map/ppermute | solution.py:794
  86.0 27.6 %collective-permute-start.17 = (bf16[576,384]{1,0:T(8,128)(2,1)S(1)}, bf16[576,384]{1,0:T(8,128)(2,1)S(1)}, u32[]{:S(2)}, u32[]{:S(2)}) collective-permute-start(bf16[576,384]{1,0:T(8,128)(2,1)S(1)} %collective-permute-done.12), channel_id=1, source_target_pairs={{0,8},{4,12},{8,16},{12,20},{16,24},{20,28},{24,0},{28,4},{1,9},{5... | collective-permute-start | bytes 1327112 | tf_op jit(solution)/shard_map/ppermute | solution.py:789
  86.0 27.6 %collective-permute-start.18 = (bf16[576,384]{1,0:T(8,128)(2,1)S(1)}, bf16[576,384]{1,0:T(8,128)(2,1)}, u32[]{:S(2)}, u32[]{:S(2)}) collective-permute-start(bf16[576,384]{1,0:T(8,128)(2,1)S(1)} %pad_maximum_fusion.25), channel_id=1, source_target_pairs={{0,24},{4,28},{8,0},{12,4},{16,8},{20,12},{24,16},{28,20},{1,25},{... | collective-permute-start | bytes 1327112 | tf_op jit(solution)/shard_map/ppermute | solution.py:789
  90.3 24.5 %collective-permute-start.16 = (bf16[96,2304]{1,0:T(8,128)(2,1)}, bf16[96,2304]{1,0:T(8,128)(2,1)}, u32[]{:S(2)}, u32[]{:S(2)}) collective-permute-start(bf16[96,2304]{1,0:T(8,128)(2,1)} %copy-done.85), channel_id=1, source_target_pairs={{0,4},{4,0},{8,12},{12,8},{16,20},{20,16},{24,28},{28,24},{1,5},{5... | collective-permute-start | bytes 1327112 | tf_op jit(solution)/shard_map/ppermute | solution.py:794
  91.2 23.7 %collective-permute-start.14 = (bf16[96,2304]{1,0:T(8,128)(2,1)}, bf16[96,2304]{1,0:T(8,128)(2,1)}, u32[]{:S(2)}, u32[]{:S(2)}) collective-permute-start(bf16[96,2304]{1,0:T(8,128)(2,1)} %pad_maximum_fusion.24), channel_id=1, source_target_pairs={{0,8},{4,12},{8,16},{12,20},{16,24},{20,28},{24,0},{28,4},{1,9},{5... | collective-permute-start | bytes 1327112 | tf_op jit(solution)/shard_map/ppermute | solution.py:789
  118.0 34.0 %collective-permute-start.20 = (bf16[320,1536]{1,0:T(8,128)(2,1)S(1)}, bf16[320,1536]{1,0:T(8,128)(2,1)S(1)}, u32[]{:S(2)}, u32[]{:S(2)}) collective-permute-start(bf16[320,1536]{1,0:T(8,128)(2,1)S(1)} %add_convert_fusion.1), channel_id=1, source_target_pairs={{0,2},{2,0},{1,3},{3,1},{4,6},{6,4},{5,7},{7,5},{8,10},{10,8},{9,1... | collective-permute-start | bytes 2949128 | tf_op jit(solution)/shard_map/ppermute | solution.py:797
  120.1 14.4 %collective-permute-start.23 = (bf16[96,2304]{1,0:T(8,128)(2,1)S(1)}, bf16[96,2304]{1,0:T(8,128)(2,1)S(1)}, u32[]{:S(2)}, u32[]{:S(2)}) collective-permute-start(bf16[96,2304]{1,0:T(8,128)(2,1)S(1)} %copy-done.87), channel_id=1, source_target_pairs={{0,24},{4,28},{8,0},{12,4},{16,8},{20,12},{24,16},{28,20},{1,25},{... | collective-permute-start | bytes 1327112 | tf_op jit(solution)/shard_map/ppermute | solution.py:789
  124.0 28.0 %collective-permute-start.22 = (bf16[96,2304]{1,0:T(8,128)(2,1)S(1)}, bf16[96,2304]{1,0:T(8,128)(2,1)S(1)}, u32[]{:S(2)}, u32[]{:S(2)}) collective-permute-start(bf16[96,2304]{1,0:T(8,128)(2,1)S(1)} %copy-done.90), channel_id=1, source_target_pairs={{0,16},{4,20},{8,24},{12,28},{16,0},{20,4},{24,8},{28,12},{1,17},{... | collective-permute-start | bytes 1327112 | tf_op jit(solution)/shard_map/ppermute | solution.py:789
  124.0 28.0 %collective-permute-start.21 = (bf16[1152,384]{1,0:T(8,128)(2,1)S(1)}, bf16[1152,384]{1,0:T(8,128)(2,1)S(1)}, u32[]{:S(2)}, u32[]{:S(2)}) collective-permute-start(bf16[1152,384]{1,0:T(8,128)(2,1)S(1)} %pad_maximum_fusion.9), channel_id=1, source_target_pairs={{0,4},{4,0},{8,12},{12,8},{16,20},{20,16},{24,28},{28,24},{1,5},{5... | collective-permute-start | bytes 2654216 | tf_op jit(solution)/shard_map/ppermute | solution.py:794
  152.0 23.3 %collective-permute-start.28 = (bf16[320,1536]{1,0:T(8,128)(2,1)S(1)}, bf16[320,1536]{1,0:T(8,128)(2,1)}, u32[]{:S(2)}, u32[]{:S(2)}) collective-permute-start(bf16[320,1536]{1,0:T(8,128)(2,1)S(1)} %pad_maximum_fusion.5.refs_24_), channel_id=1, source_target_pairs={{0,1},{1,0},{2,3},{3,2},{4,5},{5,4},{6,7},{7,6},{8,9},{9,8},{10,11... | collective-permute-start | bytes 2949128 | tf_op jit(solution)/shard_map/ppermute | solution.py:800
  152.1 22.5 %collective-permute-start.27 = (bf16[192,2304]{1,0:T(8,128)(2,1)S(1)}, bf16[192,2304]{1,0:T(8,128)(2,1)S(1)}, u32[]{:S(2)}, u32[]{:S(2)}) collective-permute-start(bf16[192,2304]{1,0:T(8,128)(2,1)S(1)} %get-tuple-element.472), channel_id=1, source_target_pairs={{0,2},{2,0},{1,3},{3,1},{4,6},{6,4},{5,7},{7,5},{8,10},{10,8},{9,1... | collective-permute-start | bytes 2654216 | tf_op jit(solution)/shard_map/ppermute | solution.py:797
  153.6 21.7 %collective-permute-start.26 = (bf16[192,2304]{1,0:T(8,128)(2,1)S(1)}, bf16[192,2304]{1,0:T(8,128)(2,1)S(1)}, u32[]{:S(2)}, u32[]{:S(2)}) collective-permute-start(bf16[192,2304]{1,0:T(8,128)(2,1)S(1)} %get-tuple-element.506), channel_id=1, source_target_pairs={{0,4},{4,0},{8,12},{12,8},{16,20},{20,16},{24,28},{28,24},{1,5},{5... | collective-permute-start | bytes 2654216 | tf_op jit(solution)/shard_map/ppermute | solution.py:794
  157.7 17.0 %collective-permute-start.25 = (bf16[160,1536]{1,0:T(8,128)(2,1)}, bf16[160,1536]{1,0:T(8,128)(2,1)}, u32[]{:S(2)}, u32[]{:S(2)}) collective-permute-start(bf16[160,1536]{1,0:T(8,128)(2,1)} %dynamic-slice_bitcast_fusion.6.skip_ref), channel_id=1, source_target_pairs={{0,24},{4,28},{8,0},{12,4},{16,8},{20,12},{24,16},{28,20},{1,25},{... | collective-permute-start | bytes 1474568 | tf_op jit(solution)/shard_map/ppermute | solution.py:789
  175.4 12.6 %collective-permute-start.32 = (bf16[96,2304]{1,0:T(8,128)(2,1)S(1)}, bf16[96,2304]{1,0:T(8,128)(2,1)S(1)}, u32[]{:S(2)}, u32[]{:S(2)}) collective-permute-start(bf16[96,2304]{1,0:T(8,128)(2,1)S(1)} %slice.297.refs_12_), channel_id=1, source_target_pairs={{0,4},{4,0},{8,12},{12,8},{16,20},{20,16},{24,28},{28,24},{1,5},{5... | collective-permute-start | bytes 1327112 | tf_op jit(solution)/shard_map/ppermute | solution.py:794
  177.1 15.2 %collective-permute-start.31 = (bf16[160,1536]{1,0:T(8,128)(2,1)S(1)}, bf16[160,1536]{1,0:T(8,128)(2,1)S(1)}, u32[]{:S(2)}, u32[]{:S(2)}) collective-permute-start(bf16[160,1536]{1,0:T(8,128)(2,1)S(1)} %copy-done.81), channel_id=1, source_target_pairs={{0,8},{4,12},{8,16},{12,20},{16,24},{20,28},{24,0},{28,4},{1,9},{5... | collective-permute-start | bytes 1474568 | tf_op jit(solution)/shard_map/ppermute | solution.py:789
  178.0 14.2 %collective-permute-start.30 = (bf16[160,1536]{1,0:T(8,128)(2,1)S(1)}, bf16[160,1536]{1,0:T(8,128)(2,1)S(1)}, u32[]{:S(2)}, u32[]{:S(2)}) collective-permute-start(bf16[160,1536]{1,0:T(8,128)(2,1)S(1)} %add_convert_fusion.14), channel_id=1, source_target_pairs={{0,2},{2,0},{1,3},{3,1},{4,6},{6,4},{5,7},{7,5},{8,10},{10,8},{9,1... | collective-permute-start | bytes 1474568 | tf_op jit(solution)/shard_map/ppermute | solution.py:797
  195.6 26.5 %collective-permute-start.37 = (bf16[480,1536]{1,0:T(8,128)(2,1)S(1)}, bf16[480,1536]{1,0:T(8,128)(2,1)S(1)}, u32[]{:S(2)}, u32[]{:S(2)}) collective-permute-start(bf16[480,1536]{1,0:T(8,128)(2,1)S(1)} %pad_maximum_fusion.2), channel_id=1, source_target_pairs={{0,1},{1,0},{2,3},{3,2},{4,5},{5,4},{6,7},{7,6},{8,9},{9,8},{10,11... | collective-permute-start | bytes 4423688 | tf_op jit(solution)/shard_map/ppermute | solution.py:800
  195.6 26.5 %collective-permute-start.36 = (bf16[192,2304]{1,0:T(8,128)(2,1)S(1)}, bf16[192,2304]{1,0:T(8,128)(2,1)S(1)}, u32[]{:S(2)}, u32[]{:S(2)}) collective-permute-start(bf16[192,2304]{1,0:T(8,128)(2,1)S(1)} %get-tuple-element.492), channel_id=1, source_target_pairs={{0,2},{2,0},{1,3},{3,1},{4,6},{6,4},{5,7},{7,5},{8,10},{10,8},{9,1... | collective-permute-start | bytes 2654216 | tf_op jit(solution)/shard_map/ppermute | solution.py:797
  196.2 25.9 %collective-permute-start.35 = (bf16[192,2304]{1,0:T(8,128)(2,1)S(1)}, bf16[192,2304]{1,0:T(8,128)(2,1)S(1)}, u32[]{:S(2)}, u32[]{:S(2)}) collective-permute-start(bf16[192,2304]{1,0:T(8,128)(2,1)S(1)} %get-tuple-element.509), channel_id=1, source_target_pairs={{0,4},{4,0},{8,12},{12,8},{16,20},{20,16},{24,28},{28,24},{1,5},{5... | collective-permute-start | bytes 2654216 | tf_op jit(solution)/shard_map/ppermute | solution.py:794
  198.0 15.9 %collective-permute-start.33 = (bf16[160,1536]{1,0:T(8,128)(2,1)S(1)}, bf16[160,1536]{1,0:T(8,128)(2,1)S(1)}, u32[]{:S(2)}, u32[]{:S(2)}) collective-permute-start(bf16[160,1536]{1,0:T(8,128)(2,1)S(1)} %get-tuple-element.488.refs_19_), channel_id=1, source_target_pairs={{0,8},{4,12},{8,16},{12,20},{16,24},{20,28},{24,0},{28,4},{1,9},{5... | collective-permute-start | bytes 1474568 | tf_op jit(solution)/shard_map/ppermute | solution.py:789
  198.4 23.7 %collective-permute-start.34 = (bf16[160,1536]{1,0:T(8,128)(2,1)S(1)}, bf16[160,1536]{1,0:T(8,128)(2,1)S(1)}, u32[]{:S(2)}, u32[]{:S(2)}) collective-permute-start(bf16[160,1536]{1,0:T(8,128)(2,1)S(1)} %get-tuple-element.488.refs_19_), channel_id=1, source_target_pairs={{0,24},{4,28},{8,0},{12,4},{16,8},{20,12},{24,16},{28,20},{1,25},{... | collective-permute-start | bytes 1474568 | tf_op jit(solution)/shard_map/ppermute | solution.py:789
  222.2 17.5 %collective-permute-start.40 = (bf16[320,1536]{1,0:T(8,128)(2,1)S(1)}, bf16[320,1536]{1,0:T(8,128)(2,1)S(1)}, u32[]{:S(2)}, u32[]{:S(2)}) collective-permute-start(bf16[320,1536]{1,0:T(8,128)(2,1)S(1)} %pad_maximum_fusion.6), channel_id=1, source_target_pairs={{0,1},{1,0},{2,3},{3,2},{4,5},{5,4},{6,7},{7,6},{8,9},{9,8},{10,11... | collective-permute-start | bytes 2949128 | tf_op jit(solution)/shard_map/ppermute | solution.py:800
  224.8 14.9 %collective-permute-start.38 = (bf16[160,1536]{1,0:T(8,128)(2,1)S(1)}, bf16[160,1536]{1,0:T(8,128)(2,1)S(1)}, u32[]{:S(2)}, u32[]{:S(2)}) collective-permute-start(bf16[160,1536]{1,0:T(8,128)(2,1)S(1)} %collective-permute-done.33.refs_20_), channel_id=1, source_target_pairs={{0,8},{4,12},{8,16},{12,20},{16,24},{20,28},{24,0},{28,4},{1,9},{5... | collective-permute-start | bytes 1474568 | tf_op jit(solution)/shard_map/ppermute | solution.py:789
  278.6 15.7 %collective-permute-start.45 = (bf16[384,768]{1,0:T(8,128)(2,1)S(1)}, bf16[384,768]{1,0:T(8,128)(2,1)S(1)}, u32[]{:S(2)}, u32[]{:S(2)}) collective-permute-start(bf16[384,768]{1,0:T(8,128)(2,1)S(1)} %pad_maximum_fusion.22), channel_id=1, source_target_pairs={{0,2},{2,0},{1,3},{3,1},{4,6},{6,4},{5,7},{7,5},{8,10},{10,8},{9,1... | collective-permute-start | bytes 1769480 | tf_op jit(solution)/shard_map/ppermute | solution.py:797
  279.2 15.3 %collective-permute-start.44 = (bf16[384,768]{1,0:T(8,128)(2,1)S(1)}, bf16[384,768]{1,0:T(8,128)(2,1)S(1)}, u32[]{:S(2)}, u32[]{:S(2)}) collective-permute-start(bf16[384,768]{1,0:T(8,128)(2,1)S(1)} %pad_maximum_fusion.21), channel_id=1, source_target_pairs={{0,4},{4,0},{8,12},{12,8},{16,20},{20,16},{24,28},{28,24},{1,5},{5... | collective-permute-start | bytes 1769480 | tf_op jit(solution)/shard_map/ppermute | solution.py:794
  280.4 13.1 %collective-permute-start.43 = (bf16[160,1536]{1,0:T(8,128)(2,1)S(1)}, bf16[160,1536]{1,0:T(8,128)(2,1)S(1)}, u32[]{:S(2)}, u32[]{:S(2)}) collective-permute-start(bf16[160,1536]{1,0:T(8,128)(2,1)S(1)} %add_convert_fusion.13), channel_id=1, source_target_pairs={{0,24},{4,28},{8,0},{12,4},{16,8},{20,12},{24,16},{28,20},{1,25},{... | collective-permute-start | bytes 1474568 | tf_op jit(solution)/shard_map/ppermute | solution.py:789
  296.0 28.4 %collective-permute-start.49 = (bf16[384,1536]{1,0:T(8,128)(2,1)S(1)}, bf16[384,1536]{1,0:T(8,128)(2,1)S(1)}, u32[]{:S(2)}, u32[]{:S(2)}) collective-permute-start(bf16[384,1536]{1,0:T(8,128)(2,1)S(1)} %pad_maximum_fusion.4), channel_id=1, source_target_pairs={{0,2},{2,0},{1,3},{3,1},{4,6},{6,4},{5,7},{7,5},{8,10},{10,8},{9,1... | collective-permute-start | bytes 3538952 | tf_op jit(solution)/shard_map/ppermute | solution.py:797
  297.6 28.1 %collective-permute-start.48 = (bf16[384,1536]{1,0:T(8,128)(2,1)S(1)}, bf16[384,1536]{1,0:T(8,128)(2,1)S(1)}, u32[]{:S(2)}, u32[]{:S(2)}) collective-permute-start(bf16[384,1536]{1,0:T(8,128)(2,1)S(1)} %pad_maximum_fusion.3), channel_id=1, source_target_pairs={{0,4},{4,0},{8,12},{12,8},{16,20},{20,16},{24,28},{28,24},{1,5},{5... | collective-permute-start | bytes 3538952 | tf_op jit(solution)/shard_map/ppermute | solution.py:794
  298.8 15.9 %collective-permute-start.47 = (bf16[160,1536]{1,0:T(8,128)(2,1)S(1)}, bf16[160,1536]{1,0:T(8,128)(2,1)S(1)}, u32[]{:S(2)}, u32[]{:S(2)}) collective-permute-start(bf16[160,1536]{1,0:T(8,128)(2,1)S(1)} %add_convert_fusion.12), channel_id=1, source_target_pairs={{0,8},{4,12},{8,16},{12,20},{16,24},{20,28},{24,0},{28,4},{1,9},{5... | collective-permute-start | bytes 1474568 | tf_op jit(solution)/shard_map/ppermute | solution.py:789
  299.0 23.6 %collective-permute-start.46 = (bf16[160,1536]{1,0:T(8,128)(2,1)S(1)}, bf16[160,1536]{1,0:T(8,128)(2,1)S(1)}, u32[]{:S(2)}, u32[]{:S(2)}) collective-permute-start(bf16[160,1536]{1,0:T(8,128)(2,1)S(1)} %add_convert_fusion.11), channel_id=1, source_target_pairs={{0,24},{4,28},{8,0},{12,4},{16,8},{20,12},{24,16},{28,20},{1,25},{... | collective-permute-start | bytes 1474568 | tf_op jit(solution)/shard_map/ppermute | solution.py:789
  330.0 12.8 %collective-permute-start.52 = (bf16[160,1536]{1,0:T(8,128)(2,1)}, bf16[160,1536]{1,0:T(8,128)(2,1)S(1)}, u32[]{:S(2)}, u32[]{:S(2)}) collective-permute-start(bf16[160,1536]{1,0:T(8,128)(2,1)} %get-tuple-element.576), channel_id=1, source_target_pairs={{0,24},{4,28},{8,0},{12,4},{16,8},{20,12},{24,16},{28,20},{1,25},{... | collective-permute-start | bytes 1474568 | tf_op jit(solution)/shard_map/ppermute | solution.py:789
  346.2 24.2 %collective-permute-start.57 = (bf16[160,1536]{1,0:T(8,128)(2,1)}, bf16[160,1536]{1,0:T(8,128)(2,1)S(1)}, u32[]{:S(2)}, u32[]{:S(2)}) collective-permute-start(bf16[160,1536]{1,0:T(8,128)(2,1)} %add_convert_fusion.8), channel_id=1, source_target_pairs={{0,24},{4,28},{8,0},{12,4},{16,8},{20,12},{24,16},{28,20},{1,25},{... | collective-permute-start | bytes 1474568 | tf_op jit(solution)/shard_map/ppermute | solution.py:789
  349.2 22.6 %collective-permute-start.56 = (bf16[160,1536]{1,0:T(8,128)(2,1)}, bf16[160,1536]{1,0:T(8,128)(2,1)S(1)}, u32[]{:S(2)}, u32[]{:S(2)}) collective-permute-start(bf16[160,1536]{1,0:T(8,128)(2,1)} %get-tuple-element.593), channel_id=1, source_target_pairs={{0,8},{4,12},{8,16},{12,20},{16,24},{20,28},{24,0},{28,4},{1,9},{5... | collective-permute-start | bytes 1474568 | tf_op jit(solution)/shard_map/ppermute | solution.py:789
  349.4 22.4 %collective-permute-start.55 = (bf16[2,96,2304]{2,1,0:T(8,128)(2,1)}, bf16[2,96,2304]{2,1,0:T(8,128)(2,1)S(1)}, u32[]{:S(2)}, u32[]{:S(2)}) collective-permute-start(bf16[2,96,2304]{2,1,0:T(8,128)(2,1)} %pad_maximum_fusion.14), channel_id=1, source_target_pairs={{0,4},{4,0},{8,12},{12,8},{16,20},{20,16},{24,28},{28,24},{1,5},{5... | collective-permute-start | bytes 2654216 | tf_op jit(solution)/shard_map/ppermute | solution.py:794
  350.7 21.7 %collective-permute-start.54 = (bf16[2,96,2304]{2,1,0:T(8,128)(2,1)}, bf16[2,96,2304]{2,1,0:T(8,128)(2,1)S(1)}, u32[]{:S(2)}, u32[]{:S(2)}) collective-permute-start(bf16[2,96,2304]{2,1,0:T(8,128)(2,1)} %pad_maximum_fusion.15), channel_id=1, source_target_pairs={{0,2},{2,0},{1,3},{3,1},{4,6},{6,4},{5,7},{7,5},{8,10},{10,8},{9,1... | collective-permute-start | bytes 2654216 | tf_op jit(solution)/shard_map/ppermute | solution.py:797
  382.8 22.4 %collective-permute-start.62 = (bf16[1152,384]{1,0:T(8,128)(2,1)}, bf16[1152,384]{1,0:T(8,128)(2,1)}, u32[]{:S(2)}, u32[]{:S(2)}) collective-permute-start(bf16[1152,384]{1,0:T(8,128)(2,1)} %pad_maximum_fusion.17), channel_id=1, source_target_pairs={{0,4},{4,0},{8,12},{12,8},{16,20},{20,16},{24,28},{28,24},{1,5},{5... | collective-permute-start | bytes 2654216 | tf_op jit(solution)/shard_map/ppermute | solution.py:794
  383.6 24.7 %collective-permute-start.59 = (bf16[320,1536]{1,0:T(8,128)(2,1)}, bf16[320,1536]{1,0:T(8,128)(2,1)S(1)}, u32[]{:S(2)}, u32[]{:S(2)}) collective-permute-start(bf16[320,1536]{1,0:T(8,128)(2,1)} %add_convert_fusion), channel_id=1, source_target_pairs={{0,2},{2,0},{1,3},{3,1},{4,6},{6,4},{5,7},{7,5},{8,10},{10,8},{9,1... | collective-permute-start | bytes 2949128 | tf_op jit(solution)/shard_map/ppermute | solution.py:797
  384.8 22.9 %collective-permute-start.61 = (bf16[96,2304]{1,0:T(8,128)(2,1)}, bf16[96,2304]{1,0:T(8,128)(2,1)}, u32[]{:S(2)}, u32[]{:S(2)}) collective-permute-start(bf16[96,2304]{1,0:T(8,128)(2,1)} %get-tuple-element.628), channel_id=1, source_target_pairs={{0,24},{4,28},{8,0},{12,4},{16,8},{20,12},{24,16},{28,20},{1,25},{... | collective-permute-start | bytes 1327112 | tf_op jit(solution)/shard_map/ppermute | solution.py:789
  388.3 20.1 %collective-permute-start.60 = (bf16[96,2304]{1,0:T(8,128)(2,1)}, bf16[96,2304]{1,0:T(8,128)(2,1)}, u32[]{:S(2)}, u32[]{:S(2)}) collective-permute-start(bf16[96,2304]{1,0:T(8,128)(2,1)} %get-tuple-element.626), channel_id=1, source_target_pairs={{0,8},{4,12},{8,16},{12,20},{16,24},{20,28},{24,0},{28,4},{1,9},{5... | collective-permute-start | bytes 1327112 | tf_op jit(solution)/shard_map/ppermute | solution.py:789
  414.8 25.5 %collective-permute-start.66 = (bf16[576,384]{1,0:T(8,128)(2,1)}, bf16[576,384]{1,0:T(8,128)(2,1)S(1)}, u32[]{:S(2)}, u32[]{:S(2)}) collective-permute-start(bf16[576,384]{1,0:T(8,128)(2,1)} %get-tuple-element.649), channel_id=1, source_target_pairs={{0,24},{4,28},{8,0},{12,4},{16,8},{20,12},{24,16},{28,20},{1,25},{... | collective-permute-start | bytes 1327112 | tf_op jit(solution)/shard_map/ppermute | solution.py:789
  418.1 30.0 %collective-permute-start.65 = (bf16[1152,384]{1,0:T(8,128)(2,1)S(1)}, bf16[1152,384]{1,0:T(8,128)(2,1)S(1)}, u32[]{:S(2)}, u32[]{:S(2)}) collective-permute-start(bf16[1152,384]{1,0:T(8,128)(2,1)S(1)} %copy-done.68), channel_id=1, source_target_pairs={{0,4},{4,0},{8,12},{12,8},{16,20},{20,16},{24,28},{28,24},{1,5},{5... | collective-permute-start | bytes 2654216 | tf_op jit(solution)/shard_map/ppermute | solution.py:794
  419.3 28.8 %collective-permute-start.64 = (bf16[96,2304]{1,0:T(8,128)(2,1)S(1)}, bf16[96,2304]{1,0:T(8,128)(2,1)S(1)}, u32[]{:S(2)}, u32[]{:S(2)}) collective-permute-start(bf16[96,2304]{1,0:T(8,128)(2,1)S(1)} %copy-done.97), channel_id=1, source_target_pairs={{0,16},{4,20},{8,24},{12,28},{16,0},{20,4},{24,8},{28,12},{1,17},{... | collective-permute-start | bytes 1327112 | tf_op jit(solution)/shard_map/ppermute | solution.py:789
  448.1 13.8 %collective-permute-start.68 = (bf16[576,384]{1,0:T(8,128)(2,1)}, bf16[576,384]{1,0:T(8,128)(2,1)}, u32[]{:S(2)}, u32[]{:S(2)}) collective-permute-start(bf16[576,384]{1,0:T(8,128)(2,1)} %get-tuple-element.654), channel_id=1, source_target_pairs={{0,8},{4,12},{8,16},{12,20},{16,24},{20,28},{24,0},{28,4},{1,9},{5... | collective-permute-start | bytes 1327112 | tf_op jit(solution)/shard_map/ppermute | solution.py:789
  448.6 13.4 %collective-permute-start.67 = (bf16[320,1536]{1,0:T(8,128)(2,1)}, bf16[320,1536]{1,0:T(8,128)(2,1)S(1)}, u32[]{:S(2)}, u32[]{:S(2)}) collective-permute-start(bf16[320,1536]{1,0:T(8,128)(2,1)} %convolution_convert_fusion.7), channel_id=1, source_target_pairs={{0,1},{1,0},{2,3},{3,2},{4,5},{5,4},{6,7},{7,6},{8,9},{9,8},{10,11... | collective-permute-start | bytes 2949128 | tf_op jit(solution)/shard_map/ppermute | solution.py:800
  462.0 14.5 %collective-permute-start.71 = (bf16[192,1536]{1,0:T(8,128)(2,1)S(1)}, bf16[192,1536]{1,0:T(8,128)(2,1)S(1)}, u32[]{:S(2)}, u32[]{:S(2)}) collective-permute-start(bf16[192,1536]{1,0:T(8,128)(2,1)S(1)} %get-tuple-element.682), channel_id=1, source_target_pairs={{0,4},{4,0},{8,12},{12,8},{16,20},{20,16},{24,28},{28,24},{1,5},{5... | collective-permute-start | bytes 1769480 | tf_op jit(solution)/shard_map/ppermute | solution.py:794
  464.0 12.6 %collective-permute-start.72 = (bf16[130,768]{1,0:T(8,128)(2,1)S(1)}, bf16[130,768]{1,0:T(8,128)(2,1)S(1)}, u32[]{:S(2)}, u32[]{:S(2)}) collective-permute-start(bf16[130,768]{1,0:T(8,128)(2,1)S(1)} %get-tuple-element.685), channel_id=1, source_target_pairs={{0,1},{1,0},{2,3},{3,2},{4,5},{5,4},{6,7},{7,6},{8,9},{9,8},{10,11... | collective-permute-start | bytes 599048 | tf_op jit(solution)/shard_map/ppermute | solution.py:800
  464.1 12.7 %collective-permute-start.70 = (bf16[576,384]{1,0:T(8,128)(2,1)S(1)}, bf16[576,384]{1,0:T(8,128)(2,1)S(1)}, u32[]{:S(2)}, u32[]{:S(2)}) collective-permute-start(bf16[576,384]{1,0:T(8,128)(2,1)S(1)} %get-tuple-element.680), channel_id=1, source_target_pairs={{0,24},{4,28},{8,0},{12,4},{16,8},{20,12},{24,16},{28,20},{1,25},{... | collective-permute-start | bytes 1327112 | tf_op jit(solution)/shard_map/ppermute | solution.py:789
  466.6 13.1 %collective-permute-start.69 = (bf16[160,1536]{1,0:T(8,128)(2,1)S(1)}, bf16[160,1536]{1,0:T(8,128)(2,1)S(1)}, u32[]{:S(2)}, u32[]{:S(2)}) collective-permute-start(bf16[160,1536]{1,0:T(8,128)(2,1)S(1)} %add_convert_fusion.7), channel_id=1, source_target_pairs={{0,2},{2,0},{1,3},{3,1},{4,6},{6,4},{5,7},{7,5},{8,10},{10,8},{9,1... | collective-permute-start | bytes 1474568 | tf_op jit(solution)/shard_map/ppermute | solution.py:797
  481.0 14.5 %collective-permute-start.73 = (bf16[192,1536]{1,0:T(8,128)(2,1)S(1)}, bf16[192,1536]{1,0:T(8,128)(2,1)S(1)}, u32[]{:S(2)}, u32[]{:S(2)}) collective-permute-start(bf16[192,1536]{1,0:T(8,128)(2,1)S(1)} %get-tuple-element.689), channel_id=1, source_target_pairs={{0,4},{4,0},{8,12},{12,8},{16,20},{20,16},{24,28},{28,24},{1,5},{5... | collective-permute-start | bytes 1769480 | tf_op jit(solution)/shard_map/ppermute | solution.py:794
  486.5 15.0 %collective-permute-start.74 = (bf16[192,1536]{1,0:T(8,128)(2,1)S(1)}, bf16[192,1536]{1,0:T(8,128)(2,1)S(1)}, u32[]{:S(2)}, u32[]{:S(2)}) collective-permute-start(bf16[192,1536]{1,0:T(8,128)(2,1)S(1)} %add_convert_fusion.4), channel_id=1, source_target_pairs={{0,24},{4,28},{8,0},{12,4},{16,8},{20,12},{24,16},{28,20},{1,25},{... | collective-permute-start | bytes 1769480 | tf_op jit(solution)/shard_map/ppermute | solution.py:789
  502.3 19.1 %collective-permute-start.79 = (bf16[192,1536]{1,0:T(8,128)(2,1)S(1)}, bf16[192,1536]{1,0:T(8,128)(2,1)}, u32[]{:S(2)}, u32[]{:S(2)}) collective-permute-start(bf16[192,1536]{1,0:T(8,128)(2,1)S(1)} %get-tuple-element.720), channel_id=1, source_target_pairs={{0,4},{4,0},{8,12},{12,8},{16,20},{20,16},{24,28},{28,24},{1,5},{5... | collective-permute-start | bytes 1769480 | tf_op jit(solution)/shard_map/ppermute | solution.py:794
  503.6 13.1 %collective-permute-start.81 = (f32[3,768]{1,0:T(4,128)S(1)}, f32[3,768]{1,0:T(4,128)S(1)}, u32[]{:S(2)}, u32[]{:S(2)}) collective-permute-start(f32[3,768]{1,0:T(4,128)S(1)} %constant_dynamic-slice_fusion.7), channel_id=1, source_target_pairs={{0,4},{4,0},{8,12},{12,8},{16,20},{20,16},{24,28},{28,24},{1,5},{5... | collective-permute-start | bytes 27656 | tf_op jit(solution)/shard_map/ppermute | solution.py:794
  505.7 15.0 %collective-permute-start.84 = (bf16[288,384]{1,0:T(8,128)(2,1)S(1)}, bf16[288,384]{1,0:T(8,128)(2,1)S(1)}, u32[]{:S(2)}, u32[]{:S(2)}) collective-permute-start(bf16[288,384]{1,0:T(8,128)(2,1)S(1)} %fusion.26), channel_id=1, source_target_pairs={{0,2},{2,0},{1,3},{3,1},{4,6},{6,4},{5,7},{7,5},{8,10},{10,8},{9,1... | collective-permute-start | bytes 663560 | tf_op jit(solution)/shard_map/ppermute | solution.py:797
  506.9 16.9 %collective-permute-start.80 = (bf16[192,1536]{1,0:T(8,128)(2,1)}, bf16[192,1536]{1,0:T(8,128)(2,1)}, u32[]{:S(2)}, u32[]{:S(2)}) collective-permute-start(bf16[192,1536]{1,0:T(8,128)(2,1)} %add_convert_fusion.3), channel_id=1, source_target_pairs={{0,8},{4,12},{8,16},{12,20},{16,24},{20,28},{24,0},{28,4},{1,9},{5... | collective-permute-start | bytes 1769480 | tf_op jit(solution)/shard_map/ppermute | solution.py:789
  528.3 15.7 %collective-permute-start.86 = (bf16[192,1536]{1,0:T(8,128)(2,1)}, bf16[192,1536]{1,0:T(8,128)(2,1)S(1)}, u32[]{:S(2)}, u32[]{:S(2)}) collective-permute-start(bf16[192,1536]{1,0:T(8,128)(2,1)} %add_convert_fusion.2), channel_id=1, source_target_pairs={{0,24},{4,28},{8,0},{12,4},{16,8},{20,12},{24,16},{28,20},{1,25},{... | collective-permute-start | bytes 1769480 | tf_op jit(solution)/shard_map/ppermute | solution.py:789
  528.4 15.6 %collective-permute-start.85 = (bf16[192,1536]{1,0:T(8,128)(2,1)S(1)}, bf16[192,1536]{1,0:T(8,128)(2,1)S(1)}, u32[]{:S(2)}, u32[]{:S(2)}) collective-permute-start(bf16[192,1536]{1,0:T(8,128)(2,1)S(1)} %get-tuple-element.733), channel_id=1, source_target_pairs={{0,4},{4,0},{8,12},{12,8},{16,20},{20,16},{24,28},{28,24},{1,5},{5... | collective-permute-start | bytes 1769480 | tf_op jit(solution)/shard_map/ppermute | solution.py:794
  (151 other events, 1317.4 us)

commit v5 on v4

--- a/solution.py
+++ b/solution.py
@@ -744,6 +744,22 @@
     send_ref[rows:, :] = gain_ref[...]
 
 
+def join_early_kernel(keep_ref, recv_ref, gain_ref, out_ref):
+    rows = keep_ref.shape[0]
+    out_ref[:rows, :] = keep_ref[...]
+    out_ref[rows : 2 * rows, :] = recv_ref[:rows, :]
+    marks = gain_ref[...].astype(F32) + recv_ref[rows:, :].astype(F32)
+    out_ref[2 * rows :, :] = marks.astype(BF16)
+
+
+def join_early(keep, recv, gains):
+    return pl.pallas_call(
+        join_early_kernel,
+        out_shape=jax.ShapeDtypeStruct((keep.shape[0] + recv.shape[0], keep.shape[1]), BF16),
+        compiler_params=params(),
+    )(keep, recv, gains)
+
+
 def pack_early(query, key, value, output, gains, half, cols):
     rows, full = query.shape
     vmem = pl.BlockSpec(memory_space=pltpu.VMEM)
@@ -960,7 +976,7 @@
     early_recv, cotangent1 = over_half(early_send), ring(upstream, 1)
     early_keep, early_recv, gains = sync(early_keep, early_recv, gains)
 
-    early0 = jnp.concatenate([early_keep, early_recv[:shard], gains + early_recv[shard:]], axis=0)
+    early0 = join_early(early_keep, early_recv, gains)
     early1, lanes0, own_over = ring(early0, 1), all_lanes(early0), over_half(own)
     early1, lanes0, own_over, late_send, late_keep, cotangent1 = sync(
         early1, lanes0, own_over, late_part(1 - half), late_part(half), cotangent1
@@ -1426,8 +1442,9 @@
 
     self0 = links.sum_lanes(self_other[0])
     self_one = ring(self_one, -1)
-    gain_one = ring(gain_ring[1] + gain_two, -1)
     inputs_result = links.both_cores(inputs_grad)
+    gain_send, inputs_result = lax.optimization_barrier((gain_ring[1] + gain_two, inputs_result))
+    gain_one = ring(gain_send, -1)
     cross_sums = links.side_by_side(cross_keep, cross_recv)
     gain_sums = slot(gain_ring[0] + gain_one + gain_three, 2, half)
     self0, self_one, gain_sums, inputs_result, cross_sums = sync(

time: 567 us -> 566 us (level)
    unnamed x255 -> x251, local copies, waits for them, and re-layouts: 15.7 us -> 15.5 us
  transfers between devices with their start and end apart: 90 -> 90, of which waited for: 48 -> 49; matrix products, arithmetic and copies ran while one was open for 18% -> 18% of each run, Pallas kernels for 11% -> 11%
where the time goes in v5:
time: 566 us; the launch traced here: 556 us
  waiting for transfers between devices  231 us (41%)
  Pallas kernels  98.2 us (17%)
  starting transfers between devices  94.4 us (17%)
  other arithmetic  46.7 us (8%)
  local copies, waits for them, and re-layouts  42.6 us (8%)
  matrix products  40.3 us (7%)
    ppermute x33, waiting for transfers between devices, ring(): return lax.ppermute(self.begun(value), 'fsdp', pairs)  122 us
    ppermute x20, waiting for transfers between devices, lanes(): return lax.ppermute(self.begun(value), 'fsdp', pairs)  58.7 us
    ppermute x33, starting transfers between devices, ring(): return lax.ppermute(self.begun(value), 'fsdp', pairs)  48.8 us
    ppermute x19, waiting for transfers between devices, over_half(): return lax.ppermute(self.begun(value), 'ctx', [(0, 1), (1, 0)])  46.5 us
    pallas_call x1, Pallas kernels, feed_forward(): pl.pallas_call(functools.partial(feed_kernel, shard, own, len(held), (tup...  25.5 us
    ppermute x20, starting transfers between devices, lanes(): return lax.ppermute(self.begun(value), 'fsdp', pairs)  23.3 us
    dot_general x8, matrix products, mm_tn(): lax.dot_general(left, right, (((0,), (0,)), ((), ())), preferred_element_...  23.3 us
    pallas_call x1, Pallas kernels, self_forward(): pl.pallas_call(functools.partial(self_forward_kernel, shard), grid=(pairs...  22.4 us
  transfers between devices with their start and end apart: 90, of which 49 were waited for; matrix products, arithmetic and copies ran while one was open for 18% of the time, Pallas kernels for 11%

profile of v5, /device:TPU:0, one launch (start us, length us, event | category | flops | bytes accessed | tf_op | source)
XLA Modules:
  0.0 555.8 jit_solution(14171889089052513948)
XLA Ops:
  2.4 2.9 shard_map.296
  5.3 3.0 collective-permute-start
  12.6 4.0 collective-permute-done.recv_ref
  25.4 7.5 %collective-permute-done.3.refs_9_.over_ref = bf16[160,1536]{1,0:T(8,128)(2,1)S(1)} collective-permute-done((bf16[160,1536]{1,0:T(8,128)(2,1)S(1)}, bf16[160,1536]{1,0:T(8,128)(2,1)S(1)}, u32[]{:S(2)}, u32[]{:S(2)}) %collective-permute-start.3) | collective-permute-done | bytes 491552 | tf_op jit(solution)/shard_map/ppermute | solution.py:813
  32.9 4.8 collective-permute-done.1.refs_2_
  42.3 2.2 fusion.13
  44.5 5.2 collective-permute-done.7
  49.6 3.3 collective-permute-done.6.refs_3_
  56.9 8.0 %collective-permute-done.11 = bf16[96,2304]{1,0:T(8,128)(2,1)S(1)} collective-permute-done((bf16[96,2304]{1,0:T(8,128)(2,1)S(1)}, bf16[96,2304]{1,0:T(8,128)(2,1)S(1)}, u32[]{:S(2)}, u32[]{:S(2)}) %collective-permute-start.11) | collective-permute-done | bytes 442400 | tf_op jit(solution)/shard_map/ppermute | solution.py:813
  64.9 2.8 collective-permute-done.10.refs_7_
  67.7 2.6 collective-permute-done.9.refs_4_
  72.2 8.5 %collective-permute-done.12 = bf16[576,384]{1,0:T(8,128)(2,1)S(1)} collective-permute-done((bf16[576,384]{1,0:T(8,128)(2,1)S(1)}, bf16[576,384]{1,0:T(8,128)(2,1)S(1)}, u32[]{:S(2)}, u32[]{:S(2)}) %collective-permute-start.12) | collective-permute-done | bytes 442400 | tf_op jit(solution)/shard_map/ppermute | solution.py:805
  80.8 3.1 collective-permute-done.13.refs_5_
  86.3 3.5 collective-permute-start.18
  91.2 22.4 %shard_map.298 = (bf16[640,1152]{1,0:T(8,128)(2,1)}, bf16[640,384]{1,0:T(8,128)(2,1)}, f32[640,384]{1,0:T(8,128)}, f32[320,1536]{1,0:T(8,128)}, bf16[320,1536]{1...) custom-call(s32[16]{0:T(128)} %xor_add_fusion.place_ref, ...), custom_call_target="tpu_custom_call" | custom-call | flops 3649044480 | bytes 6684672 | tf_op jit(solution)/shard_map/pallas_call | solution.py:306
  119.1 3.8 collective-permute-start.23
  125.3 8.2 %collective-permute-done.23 = bf16[96,2304]{1,0:T(8,128)(2,1)S(1)} collective-permute-done((bf16[96,2304]{1,0:T(8,128)(2,1)S(1)}, bf16[96,2304]{1,0:T(8,128)(2,1)S(1)}, u32[]{:S(2)}, u32[]{:S(2)}) %collective-permute-start.23) | collective-permute-done | bytes 442400 | tf_op jit(solution)/shard_map/ppermute | solution.py:805
  134.8 16.2 %collective-permute-done.22 = bf16[96,2304]{1,0:T(8,128)(2,1)S(1)} collective-permute-done((bf16[96,2304]{1,0:T(8,128)(2,1)S(1)}, bf16[96,2304]{1,0:T(8,128)(2,1)S(1)}, u32[]{:S(2)}, u32[]{:S(2)}) %collective-permute-start.22) | collective-permute-done | bytes 442400 | tf_op jit(solution)/shard_map/ppermute | solution.py:805
  154.7 2.3 shard_map.299
  157.1 3.3 collective-permute-start.25
  168.5 3.5 shard_map.301
  178.5 8.8 %collective-permute-done.32.refs_14_ = bf16[96,2304]{1,0:T(8,128)(2,1)S(1)} collective-permute-done((bf16[96,2304]{1,0:T(8,128)(2,1)S(1)}, bf16[96,2304]{1,0:T(8,128)(2,1)S(1)}, u32[]{:S(2)}, u32[]{:S(2)}) %collective-permute-start.32) | collective-permute-done | bytes 442400 | tf_op jit(solution)/shard_map/ppermute | solution.py:810
  187.5 4.3 collective-permute-done.31.refs_26_
  197.2 3.8 collective-permute-start.34
  202.0 11.1 %collective-permute-done.33.refs_20_ = bf16[160,1536]{1,0:T(8,128)(2,1)S(1)} collective-permute-done((bf16[160,1536]{1,0:T(8,128)(2,1)S(1)}, bf16[160,1536]{1,0:T(8,128)(2,1)S(1)}, u32[]{:S(2)}, u32[]{:S(2)}) %collective-permute-start.33) | collective-permute-done | bytes 491552 | tf_op jit(solution)/shard_map/ppermute | solution.py:805
  213.1 8.0 %collective-permute-done.34.refs_21_ = bf16[160,1536]{1,0:T(8,128)(2,1)S(1)} collective-permute-done((bf16[160,1536]{1,0:T(8,128)(2,1)S(1)}, bf16[160,1536]{1,0:T(8,128)(2,1)S(1)}, u32[]{:S(2)}, u32[]{:S(2)}) %collective-permute-start.34) | collective-permute-done | bytes 491552 | tf_op jit(solution)/shard_map/ppermute | solution.py:805
  226.4 8.2 %collective-permute-done.39.refs_11_ = bf16[96,2304]{1,0:T(8,128)(2,1)S(1)} collective-permute-done((bf16[96,2304]{1,0:T(8,128)(2,1)S(1)}, bf16[96,2304]{1,0:T(8,128)(2,1)S(1)}, u32[]{:S(2)}, u32[]{:S(2)}) %collective-permute-start.39) | collective-permute-done | bytes 442400 | tf_op jit(solution)/shard_map/ppermute | solution.py:813
  234.6 3.9 collective-permute-done.38.refs_22_
  241.2 25.5 %shard_map.303 = (bf16[1280,768]{1,0:T(8,128)(2,1)}, bf16[1280,1536]{1,0:T(8,128)(2,1)}, bf16[640,1536]{1,0:T(8,128)(2,1)}, f32[640,1536]{1,0:T(8,128)}, bf16[12...) custom-call(s32[16]{0:T(128)} %xor_add_fusion.place_ref, bf16[96,2304]{1,0:T(8,128)(2,1)} %copy-done.85, ...), custom_call_target="tpu_custom_call" | custom-call | flops 15099494400 | bytes 22806528 | tf_op jit(solution)/shard_map/pallas_call | solution.py:636
  267.0 6.2 %convolution_convert_fusion.2 = bf16[1536,768]{1,0:T(8,128)(2,1)S(1)} fusion(bf16[1280,1536]{1,0:T(8,128)(2,1)} %get-tuple-element.535, bf16[1280,768]{1,0:T(8,128)(2,1)} %get-tuple-element.551), kind=kOutput, calls=%fused_computation.2 | convolution fusion | flops 3021078528 | bytes 8257536 | tf_op jit(solution)/shard_map/dot_general | solution.py:26
  280.9 6.6 %convolution_convert_fusion.1 = bf16[1536,1536]{1,0:T(8,128)(2,1)S(1)} fusion(bf16[1280,1536]{1,0:T(8,128)(2,1)S(1)} %copy-done.122, bf16[1280,1536]{1,0:T(8,128)(2,1)S(1)} %copy-done.121), kind=kOutput, calls=%fused_computation.1 | convolution fusion | flops 6042157056 | bytes 12582912 | tf_op jit(solution)/shard_map/dot_general | solution.py:26
  287.8 4.8 collective-permute-done.43
  298.3 3.9 collective-permute-start.46
  305.8 8.2 %collective-permute-done.47.refs_3_ = bf16[160,1536]{1,0:T(8,128)(2,1)S(1)} collective-permute-done((bf16[160,1536]{1,0:T(8,128)(2,1)S(1)}, bf16[160,1536]{1,0:T(8,128)(2,1)S(1)}, u32[]{:S(2)}, u32[]{:S(2)}) %collective-permute-start.47) | collective-permute-done | bytes 491552 | tf_op jit(solution)/shard_map/ppermute | solution.py:805
  314.0 7.9 %collective-permute-done.46.refs_2_ = bf16[160,1536]{1,0:T(8,128)(2,1)S(1)} collective-permute-done((bf16[160,1536]{1,0:T(8,128)(2,1)S(1)}, bf16[160,1536]{1,0:T(8,128)(2,1)S(1)}, u32[]{:S(2)}, u32[]{:S(2)}) %collective-permute-start.46) | collective-permute-done | bytes 491552 | tf_op jit(solution)/shard_map/ppermute | solution.py:805
  326.4 2.4 shard_map.304
  334.7 6.9 %collective-permute-done.52 = bf16[160,1536]{1,0:T(8,128)(2,1)S(1)} collective-permute-done((bf16[160,1536]{1,0:T(8,128)(2,1)}, bf16[160,1536]{1,0:T(8,128)(2,1)S(1)}, u32[]{:S(2)}, u32[]{:S(2)}) %collective-permute-start.52) | collective-permute-done | bytes 491552 | tf_op jit(solution)/shard_map/ppermute | solution.py:805
  341.6 2.2 add_convert_fusion.8
  345.2 3.0 collective-permute-start.57
  354.1 9.7 %shard_map.305 = (bf16[640,384]{1,0:T(8,128)(2,1)S(1)}, bf16[256,384]{1,0:T(8,128)(2,1)S(1)}, bf16[256,384]{1,0:T(8,128)(2,1)S(1)}) custom-call(bf16[640,384]{1,0:T(8,128)(2,1)S(1)} %copy-done.42, bf16[256,768]{1,0:T(8,128)(2,1)S(1)} %convolution_convert_fusion.15.k_ref.v_ref, bf16[256,768]{1,0:T(8,128)(2,1)S(1)} %convolution_convert_fusion.15.k_ref.v_ref, ...), custom_call_target="tpu_custom_call" | custom-call | flops 629145600 | bytes 4718592 | tf_op jit(solution)/shard_map/pallas_call | solution.py:466
  366.9 2.4 convolution_convert_fusion.5.refs_1_
  383.8 3.5 collective-permute-start.61
  387.3 16.6 %collective-permute-done.62 = bf16[1152,384]{1,0:T(8,128)(2,1)} collective-permute-done((bf16[1152,384]{1,0:T(8,128)(2,1)}, bf16[1152,384]{1,0:T(8,128)(2,1)}, u32[]{:S(2)}, u32[]{:S(2)}) %collective-permute-start.62) | collective-permute-done | bytes 884768 | tf_op jit(solution)/shard_map/ppermute | solution.py:810
  403.9 2.5 add_convert_fusion.16
  407.4 3.5 shard_map.307
  413.8 3.3 collective-permute-start.66
  420.8 12.2 %shard_map.308 = bf16[640,1152]{1,0:T(8,128)(2,1)S(1)} custom-call(bf16[640,1152]{1,0:T(8,128)(2,1)S(1)} %copy-done.44, bf16[640,384]{1,0:T(8,128)(2,1)S(1)} %copy-done.43, bf16[640,384]{1,0:T(8,128)(2,1)S(1)} %convolution_convert_fusion.12.do_ref, f32[640,384]{1,0:T(8,128)S(1)} %copy-done.45, f32[640,128]{1,0:T(8,128)S(1)} %copy-done.33, ...), custom_call_target="tpu_custom_call" | custom-call | flops 1572864000 | bytes 8847360 | tf_op jit(solution)/shard_map/pallas_call | solution.py:442
  433.0 4.6 convolution_convert_fusion.7
  439.1 8.0 %collective-permute-done.64.refs_2_ = bf16[96,2304]{1,0:T(8,128)(2,1)S(1)} collective-permute-done((bf16[96,2304]{1,0:T(8,128)(2,1)S(1)}, bf16[96,2304]{1,0:T(8,128)(2,1)S(1)}, u32[]{:S(2)}, u32[]{:S(2)}) %collective-permute-start.64) | collective-permute-done | bytes 442400 | tf_op jit(solution)/shard_map/ppermute | solution.py:805
  447.4 4.6 convolution_convert_fusion.refs_1_
  453.4 2.4 shard_map.309
  455.8 3.2 shard_map.311
  462.9 2.6 collective-permute-start.70
  466.4 8.9 %collective-permute-done.71 = bf16[192,1536]{1,0:T(8,128)(2,1)S(1)} collective-permute-done((bf16[192,1536]{1,0:T(8,128)(2,1)S(1)}, bf16[192,1536]{1,0:T(8,128)(2,1)S(1)}, u32[]{:S(2)}, u32[]{:S(2)}) %collective-permute-start.71) | collective-permute-done | bytes 589856 | tf_op jit(solution)/shard_map/ppermute | solution.py:810
  475.7 2.8 collective-permute-done.69.refs_2_
  480.9 2.9 shard_map.310
  488.9 3.3 collective-permute-done.78
  496.6 3.8 collective-permute-done.74
  505.8 9.8 %collective-permute-done.81 = f32[3,768]{1,0:T(4,128)S(1)} collective-permute-done((f32[3,768]{1,0:T(4,128)S(1)}, f32[3,768]{1,0:T(4,128)S(1)}, u32[]{:S(2)}, u32[]{:S(2)}) %collective-permute-start.81) | collective-permute-done | bytes 9248 | tf_op jit(solution)/shard_map/ppermute | solution.py:810
  515.7 3.8 collective-permute-start.82
  520.4 2.3 add_convert_fusion.2
  522.8 2.2 copy.39
  532.1 8.9 %collective-permute-done.88 = f32[3,192]{1,0:T(4,128)S(1)} collective-permute-done((f32[3,192]{1,0:T(4,128)S(1)}, f32[3,192]{1,0:T(4,128)S(1)}, u32[]{:S(2)}, u32[]{:S(2)}) %collective-permute-start.88) | collective-permute-done | bytes 2336 | tf_op jit(solution)/shard_map/ppermute | solution.py:805
  547.4 5.0 collective-permute-done.89
  (549 shorter events, 173.3 us)
Async XLA Ops:
  9.1 16.3 %collective-permute-start.4 = (bf16[160,1536]{1,0:T(8,128)(2,1)}, bf16[160,1536]{1,0:T(8,128)(2,1)}, u32[]{:S(2)}, u32[]{:S(2)}) collective-permute-start(bf16[160,1536]{1,0:T(8,128)(2,1)} %dynamic-slice_bitcast_fusion.6.skip_ref), channel_id=1, source_target_pairs={{0,8},{4,12},{8,16},{12,20},{16,24},{20,28},{24,0},{28,4},{1,9},{5... | collective-permute-start | bytes 1474568 | tf_op jit(solution)/shard_map/ppermute | solution.py:805
  16.6 21.0 %collective-permute-start.1 = (bf16[208,1536]{1,0:T(8,128)(2,1)S(1)}, bf16[208,1536]{1,0:T(8,128)(2,1)}, u32[]{:S(2)}, u32[]{:S(2)}) collective-permute-start(bf16[208,1536]{1,0:T(8,128)(2,1)S(1)} %shard_map.297.refs_0_), channel_id=1, source_target_pairs={{0,8},{4,12},{8,16},{12,20},{16,24},{20,28},{24,0},{28,4},{1,9},{5... | collective-permute-start | bytes 1916936 | tf_op jit(solution)/shard_map/ppermute | solution.py:805
  18.5 19.2 %collective-permute-start.2 = (bf16[208,1536]{1,0:T(8,128)(2,1)S(1)}, bf16[208,1536]{1,0:T(8,128)(2,1)}, u32[]{:S(2)}, u32[]{:S(2)}) collective-permute-start(bf16[208,1536]{1,0:T(8,128)(2,1)S(1)} %shard_map.297.refs_0_), channel_id=1, source_target_pairs={{0,4},{4,0},{8,12},{12,8},{16,20},{20,16},{24,28},{28,24},{1,5},{5... | collective-permute-start | bytes 1916936 | tf_op jit(solution)/shard_map/ppermute | solution.py:810
  37.7 15.2 %collective-permute-start.6 = (bf16[208,1536]{1,0:T(8,128)(2,1)}, bf16[208,1536]{1,0:T(8,128)(2,1)S(1)}, u32[]{:S(2)}, u32[]{:S(2)}) collective-permute-start(bf16[208,1536]{1,0:T(8,128)(2,1)} %collective-permute-done.1.refs_2_), channel_id=1, source_target_pairs={{0,4},{4,0},{8,12},{12,8},{16,20},{20,16},{24,28},{28,24},{1,5},{5... | collective-permute-start | bytes 1916936 | tf_op jit(solution)/shard_map/ppermute | solution.py:810
  39.2 14.7 %collective-permute-start.5 = (bf16[208,1536]{1,0:T(8,128)(2,1)S(1)}, bf16[208,1536]{1,0:T(8,128)(2,1)S(1)}, u32[]{:S(2)}, u32[]{:S(2)}) collective-permute-start(bf16[208,1536]{1,0:T(8,128)(2,1)S(1)} %shard_map.297.refs_0_), channel_id=1, source_target_pairs={{0,24},{4,28},{8,0},{12,4},{16,8},{20,12},{24,16},{28,20},{1,25},{... | collective-permute-start | bytes 1916936 | tf_op jit(solution)/shard_map/ppermute | solution.py:805
  53.9 13.8 %collective-permute-start.10 = (bf16[208,1536]{1,0:T(8,128)(2,1)S(1)}, bf16[208,1536]{1,0:T(8,128)(2,1)S(1)}, u32[]{:S(2)}, u32[]{:S(2)}) collective-permute-start(bf16[208,1536]{1,0:T(8,128)(2,1)S(1)} %collective-permute-done.5.refs_6_), channel_id=1, source_target_pairs={{0,4},{4,0},{8,12},{12,8},{16,20},{20,16},{24,28},{28,24},{1,5},{5... | collective-permute-start | bytes 1916936 | tf_op jit(solution)/shard_map/ppermute | solution.py:810
  54.5 15.8 %collective-permute-start.9 = (bf16[208,1536]{1,0:T(8,128)(2,1)}, bf16[208,1536]{1,0:T(8,128)(2,1)S(1)}, u32[]{:S(2)}, u32[]{:S(2)}) collective-permute-start(bf16[208,1536]{1,0:T(8,128)(2,1)} %collective-permute-done.1.refs_2_), channel_id=1, source_target_pairs={{0,8},{4,12},{8,16},{12,20},{16,24},{20,28},{24,0},{28,4},{1,9},{5... | collective-permute-start | bytes 1916936 | tf_op jit(solution)/shard_map/ppermute | solution.py:805
  70.3 13.7 %collective-permute-start.13 = (bf16[208,1536]{1,0:T(8,128)(2,1)S(1)}, bf16[208,1536]{1,0:T(8,128)(2,1)S(1)}, u32[]{:S(2)}, u32[]{:S(2)}) collective-permute-start(bf16[208,1536]{1,0:T(8,128)(2,1)S(1)} %collective-permute-done.9.refs_4_), channel_id=1, source_target_pairs={{0,4},{4,0},{8,12},{12,8},{16,20},{20,16},{24,28},{28,24},{1,5},{5... | collective-permute-start | bytes 1916936 | tf_op jit(solution)/shard_map/ppermute | solution.py:810
  84.8 28.9 %collective-permute-start.15 = (bf16[1152,384]{1,0:T(8,128)(2,1)S(1)}, bf16[1152,384]{1,0:T(8,128)(2,1)}, u32[]{:S(2)}, u32[]{:S(2)}) collective-permute-start(bf16[1152,384]{1,0:T(8,128)(2,1)S(1)} %pad_maximum_fusion.8), channel_id=1, source_target_pairs={{0,4},{4,0},{8,12},{12,8},{16,20},{20,16},{24,28},{28,24},{1,5},{5... | collective-permute-start | bytes 2654216 | tf_op jit(solution)/shard_map/ppermute | solution.py:810
  86.0 27.6 %collective-permute-start.17 = (bf16[576,384]{1,0:T(8,128)(2,1)S(1)}, bf16[576,384]{1,0:T(8,128)(2,1)S(1)}, u32[]{:S(2)}, u32[]{:S(2)}) collective-permute-start(bf16[576,384]{1,0:T(8,128)(2,1)S(1)} %collective-permute-done.12), channel_id=1, source_target_pairs={{0,8},{4,12},{8,16},{12,20},{16,24},{20,28},{24,0},{28,4},{1,9},{5... | collective-permute-start | bytes 1327112 | tf_op jit(solution)/shard_map/ppermute | solution.py:805
  86.3 27.3 %collective-permute-start.18 = (bf16[576,384]{1,0:T(8,128)(2,1)S(1)}, bf16[576,384]{1,0:T(8,128)(2,1)S(1)}, u32[]{:S(2)}, u32[]{:S(2)}) collective-permute-start(bf16[576,384]{1,0:T(8,128)(2,1)S(1)} %pad_maximum_fusion.24), channel_id=1, source_target_pairs={{0,24},{4,28},{8,0},{12,4},{16,8},{20,12},{24,16},{28,20},{1,25},{... | collective-permute-start | bytes 1327112 | tf_op jit(solution)/shard_map/ppermute | solution.py:805
  90.3 23.3 %collective-permute-start.16 = (bf16[96,2304]{1,0:T(8,128)(2,1)}, bf16[96,2304]{1,0:T(8,128)(2,1)}, u32[]{:S(2)}, u32[]{:S(2)}) collective-permute-start(bf16[96,2304]{1,0:T(8,128)(2,1)} %copy-done.85), channel_id=1, source_target_pairs={{0,4},{4,0},{8,12},{12,8},{16,20},{20,16},{24,28},{28,24},{1,5},{5... | collective-permute-start | bytes 1327112 | tf_op jit(solution)/shard_map/ppermute | solution.py:810
  91.2 22.5 %collective-permute-start.14 = (bf16[96,2304]{1,0:T(8,128)(2,1)}, bf16[96,2304]{1,0:T(8,128)(2,1)}, u32[]{:S(2)}, u32[]{:S(2)}) collective-permute-start(bf16[96,2304]{1,0:T(8,128)(2,1)} %pad_maximum_fusion.23), channel_id=1, source_target_pairs={{0,8},{4,12},{8,16},{12,20},{16,24},{20,28},{24,0},{28,4},{1,9},{5... | collective-permute-start | bytes 1327112 | tf_op jit(solution)/shard_map/ppermute | solution.py:805
  116.9 34.1 %collective-permute-start.20 = (bf16[320,1536]{1,0:T(8,128)(2,1)S(1)}, bf16[320,1536]{1,0:T(8,128)(2,1)S(1)}, u32[]{:S(2)}, u32[]{:S(2)}) collective-permute-start(bf16[320,1536]{1,0:T(8,128)(2,1)S(1)} %add_convert_fusion.1), channel_id=1, source_target_pairs={{0,2},{2,0},{1,3},{3,1},{4,6},{6,4},{5,7},{7,5},{8,10},{10,8},{9,1... | collective-permute-start | bytes 2949128 | tf_op jit(solution)/shard_map/ppermute | solution.py:813
  119.1 14.4 %collective-permute-start.23 = (bf16[96,2304]{1,0:T(8,128)(2,1)S(1)}, bf16[96,2304]{1,0:T(8,128)(2,1)S(1)}, u32[]{:S(2)}, u32[]{:S(2)}) collective-permute-start(bf16[96,2304]{1,0:T(8,128)(2,1)S(1)} %copy-done.87), channel_id=1, source_target_pairs={{0,24},{4,28},{8,0},{12,4},{16,8},{20,12},{24,16},{28,20},{1,25},{... | collective-permute-start | bytes 1327112 | tf_op jit(solution)/shard_map/ppermute | solution.py:805
  122.9 28.1 %collective-permute-start.22 = (bf16[96,2304]{1,0:T(8,128)(2,1)S(1)}, bf16[96,2304]{1,0:T(8,128)(2,1)S(1)}, u32[]{:S(2)}, u32[]{:S(2)}) collective-permute-start(bf16[96,2304]{1,0:T(8,128)(2,1)S(1)} %copy-done.90), channel_id=1, source_target_pairs={{0,16},{4,20},{8,24},{12,28},{16,0},{20,4},{24,8},{28,12},{1,17},{... | collective-permute-start | bytes 1327112 | tf_op jit(solution)/shard_map/ppermute | solution.py:805
  122.9 28.1 %collective-permute-start.21 = (bf16[1152,384]{1,0:T(8,128)(2,1)S(1)}, bf16[1152,384]{1,0:T(8,128)(2,1)S(1)}, u32[]{:S(2)}, u32[]{:S(2)}) collective-permute-start(bf16[1152,384]{1,0:T(8,128)(2,1)S(1)} %pad_maximum_fusion.9), channel_id=1, source_target_pairs={{0,4},{4,0},{8,12},{12,8},{16,20},{20,16},{24,28},{28,24},{1,5},{5... | collective-permute-start | bytes 2654216 | tf_op jit(solution)/shard_map/ppermute | solution.py:810
  151.0 23.6 %collective-permute-start.28 = (bf16[320,1536]{1,0:T(8,128)(2,1)S(1)}, bf16[320,1536]{1,0:T(8,128)(2,1)}, u32[]{:S(2)}, u32[]{:S(2)}) collective-permute-start(bf16[320,1536]{1,0:T(8,128)(2,1)S(1)} %pad_maximum_fusion.5.refs_24_), channel_id=1, source_target_pairs={{0,1},{1,0},{2,3},{3,2},{4,5},{5,4},{6,7},{7,6},{8,9},{9,8},{10,11... | collective-permute-start | bytes 2949128 | tf_op jit(solution)/shard_map/ppermute | solution.py:816
  151.1 22.3 %collective-permute-start.27 = (bf16[192,2304]{1,0:T(8,128)(2,1)S(1)}, bf16[192,2304]{1,0:T(8,128)(2,1)S(1)}, u32[]{:S(2)}, u32[]{:S(2)}) collective-permute-start(bf16[192,2304]{1,0:T(8,128)(2,1)S(1)} %get-tuple-element.474), channel_id=1, source_target_pairs={{0,2},{2,0},{1,3},{3,1},{4,6},{6,4},{5,7},{7,5},{8,10},{10,8},{9,1... | collective-permute-start | bytes 2654216 | tf_op jit(solution)/shard_map/ppermute | solution.py:813
  152.7 22.0 %collective-permute-start.26 = (bf16[192,2304]{1,0:T(8,128)(2,1)S(1)}, bf16[192,2304]{1,0:T(8,128)(2,1)S(1)}, u32[]{:S(2)}, u32[]{:S(2)}) collective-permute-start(bf16[192,2304]{1,0:T(8,128)(2,1)S(1)} %get-tuple-element.508), channel_id=1, source_target_pairs={{0,4},{4,0},{8,12},{12,8},{16,20},{20,16},{24,28},{28,24},{1,5},{5... | collective-permute-start | bytes 2654216 | tf_op jit(solution)/shard_map/ppermute | solution.py:810
  157.1 16.3 %collective-permute-start.25 = (bf16[160,1536]{1,0:T(8,128)(2,1)}, bf16[160,1536]{1,0:T(8,128)(2,1)}, u32[]{:S(2)}, u32[]{:S(2)}) collective-permute-start(bf16[160,1536]{1,0:T(8,128)(2,1)} %dynamic-slice_bitcast_fusion.6.skip_ref), channel_id=1, source_target_pairs={{0,24},{4,28},{8,0},{12,4},{16,8},{20,12},{24,16},{28,20},{1,25},{... | collective-permute-start | bytes 1474568 | tf_op jit(solution)/shard_map/ppermute | solution.py:805
  174.7 12.6 %collective-permute-start.32 = (bf16[96,2304]{1,0:T(8,128)(2,1)S(1)}, bf16[96,2304]{1,0:T(8,128)(2,1)S(1)}, u32[]{:S(2)}, u32[]{:S(2)}) collective-permute-start(bf16[96,2304]{1,0:T(8,128)(2,1)S(1)} %slice.289.refs_12_), channel_id=1, source_target_pairs={{0,4},{4,0},{8,12},{12,8},{16,20},{20,16},{24,28},{28,24},{1,5},{5... | collective-permute-start | bytes 1327112 | tf_op jit(solution)/shard_map/ppermute | solution.py:810
  176.5 15.4 %collective-permute-start.31 = (bf16[160,1536]{1,0:T(8,128)(2,1)}, bf16[160,1536]{1,0:T(8,128)(2,1)S(1)}, u32[]{:S(2)}, u32[]{:S(2)}) collective-permute-start(bf16[160,1536]{1,0:T(8,128)(2,1)} %collective-permute-done.4), channel_id=1, source_target_pairs={{0,8},{4,12},{8,16},{12,20},{16,24},{20,28},{24,0},{28,4},{1,9},{5... | collective-permute-start | bytes 1474568 | tf_op jit(solution)/shard_map/ppermute | solution.py:805
  177.3 14.6 %collective-permute-start.30 = (bf16[160,1536]{1,0:T(8,128)(2,1)S(1)}, bf16[160,1536]{1,0:T(8,128)(2,1)S(1)}, u32[]{:S(2)}, u32[]{:S(2)}) collective-permute-start(bf16[160,1536]{1,0:T(8,128)(2,1)S(1)} %add_convert_fusion.14), channel_id=1, source_target_pairs={{0,2},{2,0},{1,3},{3,1},{4,6},{6,4},{5,7},{7,5},{8,10},{10,8},{9,1... | collective-permute-start | bytes 1474568 | tf_op jit(solution)/shard_map/ppermute | solution.py:813
  195.2 25.8 %collective-permute-start.37 = (bf16[480,1536]{1,0:T(8,128)(2,1)S(1)}, bf16[480,1536]{1,0:T(8,128)(2,1)S(1)}, u32[]{:S(2)}, u32[]{:S(2)}) collective-permute-start(bf16[480,1536]{1,0:T(8,128)(2,1)S(1)} %pad_maximum_fusion.2), channel_id=1, source_target_pairs={{0,1},{1,0},{2,3},{3,2},{4,5},{5,4},{6,7},{7,6},{8,9},{9,8},{10,11... | collective-permute-start | bytes 4423688 | tf_op jit(solution)/shard_map/ppermute | solution.py:816
  195.3 25.7 %collective-permute-start.36 = (bf16[192,2304]{1,0:T(8,128)(2,1)S(1)}, bf16[192,2304]{1,0:T(8,128)(2,1)S(1)}, u32[]{:S(2)}, u32[]{:S(2)}) collective-permute-start(bf16[192,2304]{1,0:T(8,128)(2,1)S(1)} %get-tuple-element.494), channel_id=1, source_target_pairs={{0,2},{2,0},{1,3},{3,1},{4,6},{6,4},{5,7},{7,5},{8,10},{10,8},{9,1... | collective-permute-start | bytes 2654216 | tf_op jit(solution)/shard_map/ppermute | solution.py:813
  195.7 25.4 %collective-permute-start.35 = (bf16[192,2304]{1,0:T(8,128)(2,1)S(1)}, bf16[192,2304]{1,0:T(8,128)(2,1)S(1)}, u32[]{:S(2)}, u32[]{:S(2)}) collective-permute-start(bf16[192,2304]{1,0:T(8,128)(2,1)S(1)} %get-tuple-element.511), channel_id=1, source_target_pairs={{0,4},{4,0},{8,12},{12,8},{16,20},{20,16},{24,28},{28,24},{1,5},{5... | collective-permute-start | bytes 2654216 | tf_op jit(solution)/shard_map/ppermute | solution.py:810
  197.2 15.9 %collective-permute-start.33 = (bf16[160,1536]{1,0:T(8,128)(2,1)S(1)}, bf16[160,1536]{1,0:T(8,128)(2,1)S(1)}, u32[]{:S(2)}, u32[]{:S(2)}) collective-permute-start(bf16[160,1536]{1,0:T(8,128)(2,1)S(1)} %get-tuple-element.490.refs_19_), channel_id=1, source_target_pairs={{0,8},{4,12},{8,16},{12,20},{16,24},{20,28},{24,0},{28,4},{1,9},{5... | collective-permute-start | bytes 1474568 | tf_op jit(solution)/shard_map/ppermute | solution.py:805
  197.2 23.9 %collective-permute-start.34 = (bf16[160,1536]{1,0:T(8,128)(2,1)S(1)}, bf16[160,1536]{1,0:T(8,128)(2,1)S(1)}, u32[]{:S(2)}, u32[]{:S(2)}) collective-permute-start(bf16[160,1536]{1,0:T(8,128)(2,1)S(1)} %get-tuple-element.490.refs_19_), channel_id=1, source_target_pairs={{0,24},{4,28},{8,0},{12,4},{16,8},{20,12},{24,16},{28,20},{1,25},{... | collective-permute-start | bytes 1474568 | tf_op jit(solution)/shard_map/ppermute | solution.py:805
  221.1 17.4 %collective-permute-start.40 = (bf16[320,1536]{1,0:T(8,128)(2,1)S(1)}, bf16[320,1536]{1,0:T(8,128)(2,1)S(1)}, u32[]{:S(2)}, u32[]{:S(2)}) collective-permute-start(bf16[320,1536]{1,0:T(8,128)(2,1)S(1)} %pad_maximum_fusion.6), channel_id=1, source_target_pairs={{0,1},{1,0},{2,3},{3,2},{4,5},{5,4},{6,7},{7,6},{8,9},{9,8},{10,11... | collective-permute-start | bytes 2949128 | tf_op jit(solution)/shard_map/ppermute | solution.py:816
  223.6 14.9 %collective-permute-start.38 = (bf16[160,1536]{1,0:T(8,128)(2,1)S(1)}, bf16[160,1536]{1,0:T(8,128)(2,1)S(1)}, u32[]{:S(2)}, u32[]{:S(2)}) collective-permute-start(bf16[160,1536]{1,0:T(8,128)(2,1)S(1)} %collective-permute-done.33.refs_20_), channel_id=1, source_target_pairs={{0,8},{4,12},{8,16},{12,20},{16,24},{20,28},{24,0},{28,4},{1,9},{5... | collective-permute-start | bytes 1474568 | tf_op jit(solution)/shard_map/ppermute | solution.py:805
  277.4 15.7 %collective-permute-start.45 = (bf16[384,768]{1,0:T(8,128)(2,1)S(1)}, bf16[384,768]{1,0:T(8,128)(2,1)S(1)}, u32[]{:S(2)}, u32[]{:S(2)}) collective-permute-start(bf16[384,768]{1,0:T(8,128)(2,1)S(1)} %pad_maximum_fusion.21), channel_id=1, source_target_pairs={{0,2},{2,0},{1,3},{3,1},{4,6},{6,4},{5,7},{7,5},{8,10},{10,8},{9,1... | collective-permute-start | bytes 1769480 | tf_op jit(solution)/shard_map/ppermute | solution.py:813
  278.2 15.3 %collective-permute-start.44 = (bf16[384,768]{1,0:T(8,128)(2,1)S(1)}, bf16[384,768]{1,0:T(8,128)(2,1)S(1)}, u32[]{:S(2)}, u32[]{:S(2)}) collective-permute-start(bf16[384,768]{1,0:T(8,128)(2,1)S(1)} %pad_maximum_fusion.20), channel_id=1, source_target_pairs={{0,4},{4,0},{8,12},{12,8},{16,20},{20,16},{24,28},{28,24},{1,5},{5... | collective-permute-start | bytes 1769480 | tf_op jit(solution)/shard_map/ppermute | solution.py:810
  279.4 13.1 %collective-permute-start.43 = (bf16[160,1536]{1,0:T(8,128)(2,1)S(1)}, bf16[160,1536]{1,0:T(8,128)(2,1)S(1)}, u32[]{:S(2)}, u32[]{:S(2)}) collective-permute-start(bf16[160,1536]{1,0:T(8,128)(2,1)S(1)} %add_convert_fusion.13), channel_id=1, source_target_pairs={{0,24},{4,28},{8,0},{12,4},{16,8},{20,12},{24,16},{28,20},{1,25},{... | collective-permute-start | bytes 1474568 | tf_op jit(solution)/shard_map/ppermute | solution.py:805
  294.9 28.4 %collective-permute-start.49 = (bf16[384,1536]{1,0:T(8,128)(2,1)S(1)}, bf16[384,1536]{1,0:T(8,128)(2,1)S(1)}, u32[]{:S(2)}, u32[]{:S(2)}) collective-permute-start(bf16[384,1536]{1,0:T(8,128)(2,1)S(1)} %pad_maximum_fusion.4), channel_id=1, source_target_pairs={{0,2},{2,0},{1,3},{3,1},{4,6},{6,4},{5,7},{7,5},{8,10},{10,8},{9,1... | collective-permute-start | bytes 3538952 | tf_op jit(solution)/shard_map/ppermute | solution.py:813
  296.4 28.1 %collective-permute-start.48 = (bf16[384,1536]{1,0:T(8,128)(2,1)S(1)}, bf16[384,1536]{1,0:T(8,128)(2,1)S(1)}, u32[]{:S(2)}, u32[]{:S(2)}) collective-permute-start(bf16[384,1536]{1,0:T(8,128)(2,1)S(1)} %pad_maximum_fusion.3), channel_id=1, source_target_pairs={{0,4},{4,0},{8,12},{12,8},{16,20},{20,16},{24,28},{28,24},{1,5},{5... | collective-permute-start | bytes 3538952 | tf_op jit(solution)/shard_map/ppermute | solution.py:810
  298.1 15.9 %collective-permute-start.47 = (bf16[160,1536]{1,0:T(8,128)(2,1)S(1)}, bf16[160,1536]{1,0:T(8,128)(2,1)S(1)}, u32[]{:S(2)}, u32[]{:S(2)}) collective-permute-start(bf16[160,1536]{1,0:T(8,128)(2,1)S(1)} %add_convert_fusion.12), channel_id=1, source_target_pairs={{0,8},{4,12},{8,16},{12,20},{16,24},{20,28},{24,0},{28,4},{1,9},{5... | collective-permute-start | bytes 1474568 | tf_op jit(solution)/shard_map/ppermute | solution.py:805
  298.3 23.6 %collective-permute-start.46 = (bf16[160,1536]{1,0:T(8,128)(2,1)S(1)}, bf16[160,1536]{1,0:T(8,128)(2,1)S(1)}, u32[]{:S(2)}, u32[]{:S(2)}) collective-permute-start(bf16[160,1536]{1,0:T(8,128)(2,1)S(1)} %add_convert_fusion.11), channel_id=1, source_target_pairs={{0,24},{4,28},{8,0},{12,4},{16,8},{20,12},{24,16},{28,20},{1,25},{... | collective-permute-start | bytes 1474568 | tf_op jit(solution)/shard_map/ppermute | solution.py:805
  328.8 12.8 %collective-permute-start.52 = (bf16[160,1536]{1,0:T(8,128)(2,1)}, bf16[160,1536]{1,0:T(8,128)(2,1)S(1)}, u32[]{:S(2)}, u32[]{:S(2)}) collective-permute-start(bf16[160,1536]{1,0:T(8,128)(2,1)} %get-tuple-element.578), channel_id=1, source_target_pairs={{0,24},{4,28},{8,0},{12,4},{16,8},{20,12},{24,16},{28,20},{1,25},{... | collective-permute-start | bytes 1474568 | tf_op jit(solution)/shard_map/ppermute | solution.py:805
  345.2 24.0 %collective-permute-start.57 = (bf16[160,1536]{1,0:T(8,128)(2,1)}, bf16[160,1536]{1,0:T(8,128)(2,1)S(1)}, u32[]{:S(2)}, u32[]{:S(2)}) collective-permute-start(bf16[160,1536]{1,0:T(8,128)(2,1)} %add_convert_fusion.8), channel_id=1, source_target_pairs={{0,24},{4,28},{8,0},{12,4},{16,8},{20,12},{24,16},{28,20},{1,25},{... | collective-permute-start | bytes 1474568 | tf_op jit(solution)/shard_map/ppermute | solution.py:805
  348.2 22.6 %collective-permute-start.56 = (bf16[160,1536]{1,0:T(8,128)(2,1)}, bf16[160,1536]{1,0:T(8,128)(2,1)S(1)}, u32[]{:S(2)}, u32[]{:S(2)}) collective-permute-start(bf16[160,1536]{1,0:T(8,128)(2,1)} %get-tuple-element.595), channel_id=1, source_target_pairs={{0,8},{4,12},{8,16},{12,20},{16,24},{20,28},{24,0},{28,4},{1,9},{5... | collective-permute-start | bytes 1474568 | tf_op jit(solution)/shard_map/ppermute | solution.py:805
  348.5 22.4 %collective-permute-start.55 = (bf16[2,96,2304]{2,1,0:T(8,128)(2,1)}, bf16[2,96,2304]{2,1,0:T(8,128)(2,1)S(1)}, u32[]{:S(2)}, u32[]{:S(2)}) collective-permute-start(bf16[2,96,2304]{2,1,0:T(8,128)(2,1)} %pad_maximum_fusion.14), channel_id=1, source_target_pairs={{0,4},{4,0},{8,12},{12,8},{16,20},{20,16},{24,28},{28,24},{1,5},{5... | collective-permute-start | bytes 2654216 | tf_op jit(solution)/shard_map/ppermute | solution.py:810
  349.5 21.7 %collective-permute-start.54 = (bf16[2,96,2304]{2,1,0:T(8,128)(2,1)}, bf16[2,96,2304]{2,1,0:T(8,128)(2,1)S(1)}, u32[]{:S(2)}, u32[]{:S(2)}) collective-permute-start(bf16[2,96,2304]{2,1,0:T(8,128)(2,1)} %pad_maximum_fusion.15), channel_id=1, source_target_pairs={{0,2},{2,0},{1,3},{3,1},{4,6},{6,4},{5,7},{7,5},{8,10},{10,8},{9,1... | collective-permute-start | bytes 2654216 | tf_op jit(solution)/shard_map/ppermute | solution.py:813
  381.6 22.4 %collective-permute-start.62 = (bf16[1152,384]{1,0:T(8,128)(2,1)}, bf16[1152,384]{1,0:T(8,128)(2,1)}, u32[]{:S(2)}, u32[]{:S(2)}) collective-permute-start(bf16[1152,384]{1,0:T(8,128)(2,1)} %pad_maximum_fusion.17), channel_id=1, source_target_pairs={{0,4},{4,0},{8,12},{12,8},{16,20},{20,16},{24,28},{28,24},{1,5},{5... | collective-permute-start | bytes 2654216 | tf_op jit(solution)/shard_map/ppermute | solution.py:810
  382.6 24.7 %collective-permute-start.59 = (bf16[320,1536]{1,0:T(8,128)(2,1)}, bf16[320,1536]{1,0:T(8,128)(2,1)S(1)}, u32[]{:S(2)}, u32[]{:S(2)}) collective-permute-start(bf16[320,1536]{1,0:T(8,128)(2,1)} %add_convert_fusion), channel_id=1, source_target_pairs={{0,2},{2,0},{1,3},{3,1},{4,6},{6,4},{5,7},{7,5},{8,10},{10,8},{9,1... | collective-permute-start | bytes 2949128 | tf_op jit(solution)/shard_map/ppermute | solution.py:813
  383.8 22.7 %collective-permute-start.61 = (bf16[96,2304]{1,0:T(8,128)(2,1)}, bf16[96,2304]{1,0:T(8,128)(2,1)}, u32[]{:S(2)}, u32[]{:S(2)}) collective-permute-start(bf16[96,2304]{1,0:T(8,128)(2,1)} %get-tuple-element.630), channel_id=1, source_target_pairs={{0,24},{4,28},{8,0},{12,4},{16,8},{20,12},{24,16},{28,20},{1,25},{... | collective-permute-start | bytes 1327112 | tf_op jit(solution)/shard_map/ppermute | solution.py:805
  387.3 20.1 %collective-permute-start.60 = (bf16[96,2304]{1,0:T(8,128)(2,1)}, bf16[96,2304]{1,0:T(8,128)(2,1)}, u32[]{:S(2)}, u32[]{:S(2)}) collective-permute-start(bf16[96,2304]{1,0:T(8,128)(2,1)} %get-tuple-element.628), channel_id=1, source_target_pairs={{0,8},{4,12},{8,16},{12,20},{16,24},{20,28},{24,0},{28,4},{1,9},{5... | collective-permute-start | bytes 1327112 | tf_op jit(solution)/shard_map/ppermute | solution.py:805
  413.8 25.3 %collective-permute-start.66 = (bf16[576,384]{1,0:T(8,128)(2,1)}, bf16[576,384]{1,0:T(8,128)(2,1)S(1)}, u32[]{:S(2)}, u32[]{:S(2)}) collective-permute-start(bf16[576,384]{1,0:T(8,128)(2,1)} %get-tuple-element.651), channel_id=1, source_target_pairs={{0,24},{4,28},{8,0},{12,4},{16,8},{20,12},{24,16},{28,20},{1,25},{... | collective-permute-start | bytes 1327112 | tf_op jit(solution)/shard_map/ppermute | solution.py:805
  417.1 30.0 %collective-permute-start.65 = (bf16[1152,384]{1,0:T(8,128)(2,1)S(1)}, bf16[1152,384]{1,0:T(8,128)(2,1)S(1)}, u32[]{:S(2)}, u32[]{:S(2)}) collective-permute-start(bf16[1152,384]{1,0:T(8,128)(2,1)S(1)} %copy-done.71), channel_id=1, source_target_pairs={{0,4},{4,0},{8,12},{12,8},{16,20},{20,16},{24,28},{28,24},{1,5},{5... | collective-permute-start | bytes 2654216 | tf_op jit(solution)/shard_map/ppermute | solution.py:810
  418.1 29.0 %collective-permute-start.64 = (bf16[96,2304]{1,0:T(8,128)(2,1)S(1)}, bf16[96,2304]{1,0:T(8,128)(2,1)S(1)}, u32[]{:S(2)}, u32[]{:S(2)}) collective-permute-start(bf16[96,2304]{1,0:T(8,128)(2,1)S(1)} %copy-done.96), channel_id=1, source_target_pairs={{0,16},{4,20},{8,24},{12,28},{16,0},{20,4},{24,8},{28,12},{1,17},{... | collective-permute-start | bytes 1327112 | tf_op jit(solution)/shard_map/ppermute | solution.py:805
  447.1 13.7 %collective-permute-start.68 = (bf16[576,384]{1,0:T(8,128)(2,1)}, bf16[576,384]{1,0:T(8,128)(2,1)}, u32[]{:S(2)}, u32[]{:S(2)}) collective-permute-start(bf16[576,384]{1,0:T(8,128)(2,1)} %get-tuple-element.656), channel_id=1, source_target_pairs={{0,8},{4,12},{8,16},{12,20},{16,24},{20,28},{24,0},{28,4},{1,9},{5... | collective-permute-start | bytes 1327112 | tf_op jit(solution)/shard_map/ppermute | solution.py:805
  447.4 13.5 %collective-permute-start.67 = (bf16[320,1536]{1,0:T(8,128)(2,1)}, bf16[320,1536]{1,0:T(8,128)(2,1)S(1)}, u32[]{:S(2)}, u32[]{:S(2)}) collective-permute-start(bf16[320,1536]{1,0:T(8,128)(2,1)} %convolution_convert_fusion.7), channel_id=1, source_target_pairs={{0,1},{1,0},{2,3},{3,2},{4,5},{5,4},{6,7},{7,6},{8,9},{9,8},{10,11... | collective-permute-start | bytes 2949128 | tf_op jit(solution)/shard_map/ppermute | solution.py:816
  460.9 14.3 %collective-permute-start.71 = (bf16[192,1536]{1,0:T(8,128)(2,1)S(1)}, bf16[192,1536]{1,0:T(8,128)(2,1)S(1)}, u32[]{:S(2)}, u32[]{:S(2)}) collective-permute-start(bf16[192,1536]{1,0:T(8,128)(2,1)S(1)} %get-tuple-element.684), channel_id=1, source_target_pairs={{0,4},{4,0},{8,12},{12,8},{16,20},{20,16},{24,28},{28,24},{1,5},{5... | collective-permute-start | bytes 1769480 | tf_op jit(solution)/shard_map/ppermute | solution.py:810
  462.8 12.6 %collective-permute-start.72 = (bf16[130,768]{1,0:T(8,128)(2,1)S(1)}, bf16[130,768]{1,0:T(8,128)(2,1)S(1)}, u32[]{:S(2)}, u32[]{:S(2)}) collective-permute-start(bf16[130,768]{1,0:T(8,128)(2,1)S(1)} %get-tuple-element.687), channel_id=1, source_target_pairs={{0,1},{1,0},{2,3},{3,2},{4,5},{5,4},{6,7},{7,6},{8,9},{9,8},{10,11... | collective-permute-start | bytes 599048 | tf_op jit(solution)/shard_map/ppermute | solution.py:816
  462.9 12.7 %collective-permute-start.70 = (bf16[576,384]{1,0:T(8,128)(2,1)S(1)}, bf16[576,384]{1,0:T(8,128)(2,1)S(1)}, u32[]{:S(2)}, u32[]{:S(2)}) collective-permute-start(bf16[576,384]{1,0:T(8,128)(2,1)S(1)} %get-tuple-element.682), channel_id=1, source_target_pairs={{0,24},{4,28},{8,0},{12,4},{16,8},{20,12},{24,16},{28,20},{1,25},{... | collective-permute-start | bytes 1327112 | tf_op jit(solution)/shard_map/ppermute | solution.py:805
  465.6 12.9 %collective-permute-start.69 = (bf16[160,1536]{1,0:T(8,128)(2,1)S(1)}, bf16[160,1536]{1,0:T(8,128)(2,1)S(1)}, u32[]{:S(2)}, u32[]{:S(2)}) collective-permute-start(bf16[160,1536]{1,0:T(8,128)(2,1)S(1)} %add_convert_fusion.7), channel_id=1, source_target_pairs={{0,2},{2,0},{1,3},{3,1},{4,6},{6,4},{5,7},{7,5},{8,10},{10,8},{9,1... | collective-permute-start | bytes 1474568 | tf_op jit(solution)/shard_map/ppermute | solution.py:813
  479.8 14.2 %collective-permute-start.73 = (bf16[192,1536]{1,0:T(8,128)(2,1)S(1)}, bf16[192,1536]{1,0:T(8,128)(2,1)S(1)}, u32[]{:S(2)}, u32[]{:S(2)}) collective-permute-start(bf16[192,1536]{1,0:T(8,128)(2,1)S(1)} %get-tuple-element.691), channel_id=1, source_target_pairs={{0,4},{4,0},{8,12},{12,8},{16,20},{20,16},{24,28},{28,24},{1,5},{5... | collective-permute-start | bytes 1769480 | tf_op jit(solution)/shard_map/ppermute | solution.py:810
  485.4 15.0 %collective-permute-start.74 = (bf16[192,1536]{1,0:T(8,128)(2,1)S(1)}, bf16[192,1536]{1,0:T(8,128)(2,1)S(1)}, u32[]{:S(2)}, u32[]{:S(2)}) collective-permute-start(bf16[192,1536]{1,0:T(8,128)(2,1)S(1)} %add_convert_fusion.4), channel_id=1, source_target_pairs={{0,24},{4,28},{8,0},{12,4},{16,8},{20,12},{24,16},{28,20},{1,25},{... | collective-permute-start | bytes 1769480 | tf_op jit(solution)/shard_map/ppermute | solution.py:805
  501.2 19.1 %collective-permute-start.79 = (bf16[192,1536]{1,0:T(8,128)(2,1)S(1)}, bf16[192,1536]{1,0:T(8,128)(2,1)}, u32[]{:S(2)}, u32[]{:S(2)}) collective-permute-start(bf16[192,1536]{1,0:T(8,128)(2,1)S(1)} %get-tuple-element.722), channel_id=1, source_target_pairs={{0,4},{4,0},{8,12},{12,8},{16,20},{20,16},{24,28},{28,24},{1,5},{5... | collective-permute-start | bytes 1769480 | tf_op jit(solution)/shard_map/ppermute | solution.py:810
  502.4 13.2 %collective-permute-start.81 = (f32[3,768]{1,0:T(4,128)S(1)}, f32[3,768]{1,0:T(4,128)S(1)}, u32[]{:S(2)}, u32[]{:S(2)}) collective-permute-start(f32[3,768]{1,0:T(4,128)S(1)} %constant_dynamic-slice_fusion.7), channel_id=1, source_target_pairs={{0,4},{4,0},{8,12},{12,8},{16,20},{20,16},{24,28},{28,24},{1,5},{5... | collective-permute-start | bytes 27656 | tf_op jit(solution)/shard_map/ppermute | solution.py:810
  504.6 15.0 %collective-permute-start.84 = (bf16[288,384]{1,0:T(8,128)(2,1)S(1)}, bf16[288,384]{1,0:T(8,128)(2,1)S(1)}, u32[]{:S(2)}, u32[]{:S(2)}) collective-permute-start(bf16[288,384]{1,0:T(8,128)(2,1)S(1)} %fusion.26), channel_id=1, source_target_pairs={{0,2},{2,0},{1,3},{3,1},{4,6},{6,4},{5,7},{7,5},{8,10},{10,8},{9,1... | collective-permute-start | bytes 663560 | tf_op jit(solution)/shard_map/ppermute | solution.py:813
  505.8 16.9 %collective-permute-start.80 = (bf16[192,1536]{1,0:T(8,128)(2,1)}, bf16[192,1536]{1,0:T(8,128)(2,1)}, u32[]{:S(2)}, u32[]{:S(2)}) collective-permute-start(bf16[192,1536]{1,0:T(8,128)(2,1)} %add_convert_fusion.3), channel_id=1, source_target_pairs={{0,8},{4,12},{8,16},{12,20},{16,24},{20,28},{24,0},{28,4},{1,9},{5... | collective-permute-start | bytes 1769480 | tf_op jit(solution)/shard_map/ppermute | solution.py:805
  525.0 16.1 %collective-permute-start.86 = (bf16[192,1536]{1,0:T(8,128)(2,1)}, bf16[192,1536]{1,0:T(8,128)(2,1)S(1)}, u32[]{:S(2)}, u32[]{:S(2)}) collective-permute-start(bf16[192,1536]{1,0:T(8,128)(2,1)} %add_convert_fusion.2), channel_id=1, source_target_pairs={{0,24},{4,28},{8,0},{12,4},{16,8},{20,12},{24,16},{28,20},{1,25},{... | collective-permute-start | bytes 1769480 | tf_op jit(solution)/shard_map/ppermute | solution.py:805
  527.1 15.5 %collective-permute-start.85 = (bf16[192,1536]{1,0:T(8,128)(2,1)S(1)}, bf16[192,1536]{1,0:T(8,128)(2,1)S(1)}, u32[]{:S(2)}, u32[]{:S(2)}) collective-permute-start(bf16[192,1536]{1,0:T(8,128)(2,1)S(1)} %get-tuple-element.735), channel_id=1, source_target_pairs={{0,4},{4,0},{8,12},{12,8},{16,20},{20,16},{24,28},{28,24},{1,5},{5... | collective-permute-start | bytes 1769480 | tf_op jit(solution)/shard_map/ppermute | solution.py:810
  (149 other events, 1236.9 us)
